TPU v7x, 32 devices: a whole 2x2x4 slice. The times are simulated.
32 devices in a mesh: dp: 4 (over z), tensor: 2 (over x), col: 4 (over y, core).
Axes of the slice: x: 2, y: 2, z: 4, core: 2. Of those that a mesh axis runs over, the one named last changes fastest.
Arguments:
- tokens: bfloat16 [512, 6144], P('dp', 'col'), may hold values from -6 to 6
- routes: int32 [512, 2], P('dp'), may hold values from 0 to 7, all different within a row; in each aligned block of 128 rows (0 to 127, 128 to 255, ...) at most 40 rows name the same one
- route_logits: float32 [512, 2], P('dp'), may hold values from -6 to 6
- kept_experts: int32 [6], replicated, may hold values from 0 to 7, as said below
- gate_weight: bfloat16 [65536, 6144], P(('dp', 'tensor'), 'col'), may hold values from -0.078125 to 0.078125
- up_weight: bfloat16 [65536, 6144], P(('dp', 'tensor'), 'col'), may hold values from -0.078125 to 0.078125
- down_weight: bfloat16 [65536, 3072], P(('dp', 'tensor'), 'col'), as said below
Outputs:
- token_error: float32 [512, 3072], P('dp', 'col')
Inputs may be any that keep to these rules, and one draw needn't show every extreme that they name: Each token names two different experts. Among the tokens of one dp index (aligned blocks of 128 tokens) no expert is named by more than 40 routes, and in some block one expert is named by exactly 40. `kept_experts`: 6 different expert numbers. `down_weight`: entries lie between -6 / sqrt(8192) and 6 / sqrt(8192).
All inputs are finite; a program needn't handle non-finite values.
Results may differ from a plain program's by a relative error of at most 0.02.
Values may be sent and summed in bfloat16 or wider, within the bound.
No kernel may reach another device: no remote copies, remote signals or barrier semaphores. Data moves between devices by JAX's collectives and lax.ppermute only.
A program may use at most 192 MiB of HBM per device.

v0:
```python
import jax
import jax.numpy as jnp
from jax import lax
from jax.sharding import PartitionSpec as P

FF = 8192
E = 8
ITERS = 2
CAP = 40


ridge_share = 0.25
top_precision = lax.Precision.HIGHEST


def spread_copies(values, experts, held_count, copies):
    old_shape = values.shape
    grouped = values.reshape((experts // held_count, 1, held_count) + old_shape[1:])
    widened = jnp.broadcast_to(grouped, (experts // held_count, copies, held_count) + old_shape[1:])
    return widened.reshape((experts // held_count * copies, held_count) + old_shape[1:])


def expert_major(returned, experts, held_count, copies):
    old_shape = returned.shape
    grouped = returned.reshape((experts // held_count, copies, held_count) + old_shape[2:])
    merged = jnp.sum(grouped, axis=1)
    return merged.reshape((experts * old_shape[2],) + old_shape[3:])


def exact_product(left, right, contract):
    return lax.dot_general(
        left, right, contract, precision=top_precision, preferred_element_type=jnp.float32
    )


def shards(tokens, routes, route_logits, kept_experts, gate_weight, up_weight, down_weight):
    dp_count = lax.axis_size("dp")
    tensor_count = lax.axis_size("tensor")
    held_count = max(1, E // dp_count)
    copies = max(1, dp_count // E)
    tok_rows = tokens.shape[0]
    piece_rows = gate_weight.shape[0]
    slot_total = E * CAP
    device_rank = lax.axis_index("dp") * tensor_count + lax.axis_index("tensor")
    own_expert = device_rank * piece_rows // FF
    own_group = own_expert % held_count
    expert_ids = jnp.arange(E, dtype=jnp.int32)
    kept_table = jnp.any(kept_experts[:, None] == expert_ids[None, :], axis=0).astype(jnp.float32)
    own_kept = jnp.sum(jnp.where(expert_ids == own_expert, kept_table, 0.0))
    route_experts = routes.reshape(-1)
    route_onehot = (route_experts[:, None] == expert_ids[None, :]).astype(jnp.int32)
    route_rank = jnp.sum((jnp.cumsum(route_onehot, axis=0) - route_onehot) * route_onehot, axis=1)
    route_slot = route_experts * CAP + route_rank
    gate_probs = jax.nn.softmax(route_logits, axis=-1).reshape(-1)
    route_kept = jnp.sum(route_onehot.astype(jnp.float32) * kept_table[None, :], axis=1)
    slot_match = (jnp.arange(slot_total, dtype=jnp.int32)[:, None] == route_slot[None, :]).astype(
        jnp.float32
    )
    pick_tokens = slot_match.reshape(slot_total, tok_rows, 2).sum(axis=2)
    kept_weights = (
        (slot_match * (gate_probs * route_kept)[None, :])
        .reshape(slot_total, tok_rows, 2)
        .sum(axis=2)
    )
    dropped_weights = (
        (slot_match * (gate_probs * (1.0 - route_kept))[None, :])
        .reshape(slot_total, tok_rows, 2)
        .sum(axis=2)
    )
    by_expert = jnp.dot(
        pick_tokens.astype(jnp.bfloat16), tokens, preferred_element_type=jnp.float32
    ).astype(jnp.bfloat16)
    outgoing = spread_copies(by_expert.reshape(E, CAP, -1), E, held_count, copies)
    chosen = lax.dynamic_index_in_dim(
        lax.all_to_all(outgoing, "dp", split_axis=0, concat_axis=0, tiled=True),
        own_group,
        1,
        keepdims=False,
    )
    contract = (((2,), (1,)), ((), ()))
    gate_part = lax.dot_general(chosen, gate_weight, contract, preferred_element_type=jnp.float32)
    up_part = lax.dot_general(chosen, up_weight, contract, preferred_element_type=jnp.float32)
    gate_part, up_part = (gate_part, up_part)
    gate_sum, up_sum = (
        lax.psum(gate_part.astype(jnp.bfloat16), "col").astype(jnp.float32),
        lax.psum(up_part.astype(jnp.bfloat16), "col").astype(jnp.float32),
    )
    hidden = (jax.nn.silu(gate_sum) * up_sum).astype(jnp.bfloat16)
    expert_out = lax.dot_general(
        hidden, down_weight, (((2,), (0,)), ((), ())), preferred_element_type=jnp.float32
    ).astype(jnp.bfloat16)
    hidden_wide = hidden.astype(jnp.float32)
    group_mask = (jnp.arange(held_count) == own_group)[None, :, None, None]
    placed = jnp.where(group_mask, expert_out[:, None], jnp.zeros((), jnp.bfloat16))
    returned = lax.all_to_all(placed, "dp", split_axis=0, concat_axis=0, tiled=True)
    slot_values = expert_major(returned.astype(jnp.float32), E, held_count, copies)
    dropped_part = jnp.dot(dropped_weights.T, slot_values, precision=top_precision)
    dropped = lax.psum(dropped_part, "tensor")
    ridge_weight = ridge_share * 2.0 * tok_rows * dp_count / E

    def apply_backward(image_tokens):
        slot_image = jnp.dot(kept_weights, image_tokens, precision=top_precision)
        outgoing_image = spread_copies(slot_image.reshape(E, CAP, -1), E, held_count, copies)
        arrived = lax.all_to_all(outgoing_image, "dp", split_axis=0, concat_axis=0, tiled=True)
        chosen = lax.dynamic_index_in_dim(arrived, own_group, 1, keepdims=False)
        return exact_product(hidden_wide, chosen, (((0, 1), (0, 1)), ((), ())))

    def total_norm(values):
        return lax.psum(jnp.sum(values * values), ("dp", "tensor", "col"))

    base_down = down_weight.astype(jnp.float32)
    residual = apply_backward(dropped) - ridge_weight * own_kept * base_down
    res_norm = total_norm(residual)
    direction = residual
    leftover = dropped
    for turn_index in range(ITERS):
        slot_part = exact_product(hidden_wide, direction, (((2,), (0,)), ((), ())))
        placed_part = jnp.where(group_mask, slot_part[:, None], 0.0)
        came_back = lax.all_to_all(placed_part, "dp", split_axis=0, concat_axis=0, tiled=True)
        image_part = jnp.dot(
            kept_weights.T, expert_major(came_back, E, held_count, copies), precision=top_precision
        )
        image_tokens = lax.psum(image_part, "tensor")
        first_copy = (lax.axis_index("tensor") == 0).astype(jnp.float32)
        local_term = first_copy * jnp.sum(image_tokens * image_tokens) + ridge_weight * jnp.sum(
            direction * direction
        )
        curvature = lax.psum(local_term, ("dp", "tensor", "col"))
        step_size = res_norm / curvature
        leftover = leftover - step_size * image_tokens
        if turn_index + 1 < ITERS:
            curved = apply_backward(image_tokens) + ridge_weight * direction
            residual = residual - step_size * curved
            next_norm = total_norm(residual)
            direction = residual + next_norm / res_norm * direction
            res_norm = next_norm
    return leftover


def solution(mesh):
    placed = (
        P("dp", "col"),
        P("dp", None),
        P("dp", None),
        P(),
        P(("dp", "tensor"), "col"),
        P(("dp", "tensor"), "col"),
        P(("dp", "tensor"), "col"),
    )
    return jax.shard_map(
        shards, mesh=mesh, in_specs=placed, out_specs=P("dp", "col"), check_vma=False
    )
```

profile of v0, /device:TPU:0, one launch (start us, length us, event | category | flops | bytes accessed | tf_op | source)
XLA Modules:
  0.0 595.8 jit_solution(7660476875489459945)
XLA Ops:
  12.8 1.4 convolution_convert_fusion
  14.1 6.3 %all-to-all-start = ((bf16[4,2,40,1536]{3,2,1,0:T(8,128)(2,1)}), bf16[4,2,40,1536]{3,2,1,0:T(8,128)(2,1)S(1)}, u32[]{:S(2)}, u32[]{:S(2)}) async-start(bf16[4,2,40,1536]{3,2,1,0:T(8,128)(2,1)} %bitcast.2), calls=%async_computation | async-start | bytes 1966080 | tf_op jit(solution)/shard_map/all_to_all | solution.py:75
  20.4 24.3 %all-to-all-done = bf16[4,2,40,1536]{3,2,1,0:T(8,128)(2,1)S(1)} async-done(((bf16[4,2,40,1536]{3,2,1,0:T(8,128)(2,1)}), bf16[4,2,40,1536]{3,2,1,0:T(8,128)(2,1)S(1)}, u32[]{:S(2)}, u32[]{:S(2)}) %all-to-all-start) | async-done | bytes 983072 | tf_op jit(solution)/shard_map/all_to_all | solution.py:75
  44.8 14.9 %fusion.15 = bf16[4,40,8192]{2,1,0:T(8,128)(2,1)} fusion(bf16[8192,1536]{1,0:T(8,128)(2,1)} %param.12, bf16[4,2,40,1536]{3,2,1,0:T(8,128)(2,1)S(1)} %all-to-all-done, s32[]{:T(128)S(6)} %select_n.35), kind=kOutput, calls=%fused_computation.19 | convolution fusion | flops 4027842560 | bytes 28278788 | tf_op jit(solution)/shard_map/dot_general | solution.py:82
  59.6 14.9 %fusion.12 = bf16[4,40,8192]{2,1,0:T(8,128)(2,1)} fusion(bf16[8192,1536]{1,0:T(8,128)(2,1)} %param.11, bf16[4,2,40,1536]{3,2,1,0:T(8,128)(2,1)S(1)} %all-to-all-done, s32[]{:T(128)S(6)} %select_n.35), kind=kOutput, calls=%fused_computation.18 | convolution fusion | flops 4027842560 | bytes 28278788 | tf_op jit(solution)/shard_map/dot_general | solution.py:81
  74.7 101.9 %all-reduce.13.cloned.1.call-done = (bf16[4,40,8192]{2,1,0:T(8,128)(2,1)}, bf16[4,40,8192]{2,1,0:T(8,128)(2,1)}) async-done(((bf16[4,40,8192]{2,1,0:T(8,128)(2,1)}, bf16[4,40,8192]{2,1,0:T(8,128)(2,1)}), (bf16[4,40,8192]{2,1,0:T(8,128)(2,1)}, bf16[4,40,8192]{2,1,0:T(8,128)(2,1)})) %all-reduce.13.cloned.1.call-update) | async-done | bytes 5242896 | tf_op jit(solution)/shard_map/psum | solution.py:86
  176.6 4.2 fusion.22
  180.8 6.9 %fusion.23 = bf16[4,40,768]{2,1,0:T(8,128)(2,1)S(1)} fusion(bf16[4,40,8192]{2,1,0:T(8,128)(2,1)S(1)} %fusion.22, bf16[8192,768]{1,0:T(8,128)(2,1)} %param.13), kind=kOutput, calls=%fused_computation.28 | convolution fusion | flops 2013388800 | bytes 15450112 | tf_op jit(solution)/shard_map/dot_general | solution.py:89
  187.8 18.2 %all_to_all.30 = bf16[4,2,40,768]{3,2,1,0:T(8,128)(2,1)S(1)} all-to-all(bf16[4,2,40,768]{3,2,1,0:T(8,128)(2,1)S(1)} %broadcast_select_fusion.2), channel_id=1, replica_groups=mesh['dp'=4,'tensor'=2,'col'=4] {'dp'}, dimensions={0} | all-to-all | bytes 983040 | tf_op jit(solution)/shard_map/all_to_all | solution.py:95
  207.3 24.5 %all-reduce.7.cloned.1.call-done = f32[128,768]{1,0:T(8,128)} async-done(((f32[128,768]{1,0:T(8,128)}), f32[128,768]{1,0:T(8,128)}) %all-reduce.7.cloned.1.call-update) | async-done | bytes 393232 | tf_op jit(solution)/shard_map/psum | solution.py:98
  231.8 2.9 fusion.37
  234.7 4.6 all-to-all-start.2
  240.6 23.2 %all-to-all-done.2 = f32[4,2,40,768]{3,2,1,0:T(8,128)} async-done(((f32[4,2,40,768]{3,2,1,0:T(8,128)}), f32[4,2,40,768]{3,2,1,0:T(8,128)}, u32[]{:S(2)}, u32[]{:S(2)}) %all-to-all-start.2) | async-done | bytes 983072 | tf_op jit(solution)/shard_map/all_to_all | solution.py:104
  263.7 20.3 %multiply_reduce_fusion.2 = (f32[]{:T(128)}, f32[8192,768]{1,0:T(8,128)}) fusion(bf16[8192,768]{1,0:T(8,128)(2,1)} %param.13, f32[]{:T(128)S(6)} %mul.146, bf16[4,40,8192]{2,1,0:T(8,128)(2,1)S(1)} %fusion.22, f32[4,2,40,768]{3,2,1,0:T(8,128)} %all-to-all-done.2, s32[]{:T(128)S(6)} %select_n.35), kind=kOutput, calls=%fused_computation.15 | convolution fusion | flops 12111052800 | bytes 40861708 | tf_op jit(solution)/shard_map/dot_general | solution.py:31
  284.0 14.4 %fusion.4 = f32[4,40,768]{2,1,0:T(8,128)S(1)} fusion(bf16[4,40,8192]{2,1,0:T(8,128)(2,1)S(1)} %fusion.22, f32[8192,768]{1,0:T(8,128)} %get-tuple-element.15), kind=kOutput, calls=%fused_computation.5 | convolution fusion | flops 12079595520 | bytes 28278784 | tf_op jit(solution)/shard_map/dot_general | solution.py:31
  298.5 26.5 %all_to_all.31 = f32[4,2,40,768]{3,2,1,0:T(8,128)S(1)} all-to-all(f32[4,2,40,768]{3,2,1,0:T(8,128)S(1)} %broadcast_select_fusion.1), channel_id=1, replica_groups=mesh['dp'=4,'tensor'=2,'col'=4] {'dp'}, dimensions={0} | all-to-all | bytes 1966080 | tf_op jit(solution)/shard_map/all_to_all | solution.py:119
  325.0 1.6 fusion.57
  326.6 24.0 %all-reduce.9.cloned.1.call-done = f32[128,768]{1,0:T(8,128)} async-done(((f32[128,768]{1,0:T(8,128)}), f32[128,768]{1,0:T(8,128)}) %all-reduce.9.cloned.1.call-update) | async-done | bytes 393232 | tf_op jit(solution)/shard_map/psum | solution.py:123
  350.6 3.0 fusion.35
  353.5 4.6 all-to-all-start.4
  358.8 1.7 multiply_reduce_fusion.4
  361.2 40.6 %all-reduce = (f32[]{:T(128)}, f32[]{:T(128)}) all-reduce(f32[]{:T(128)} %get-tuple-element.14, f32[]{:T(128)S(6)} %add.61), channel_id=1, replica_groups=mesh['dp'=4,'tensor'=2,'col'=4] {'dp','tensor','col'}, use_global_device_ids=true, to_apply=%region_15.16 | all-reduce | flops 2 | bytes 16 | tf_op jit(solution)/shard_map/psum | solution.py:109
  403.1 23.2 %multiply_reduce_fusion.1 = (f32[]{:T(128)}, f32[8192,768,1]{1,0,2:T(8,128)}) fusion(f32[8192,768]{1,0:T(8,128)} %get-tuple-element.15, f32[]{:T(128)S(6)} %div.35, bf16[4,40,8192]{2,1,0:T(8,128)(2,1)S(1)} %fusion.22, f32[4,2,40,768]{3,2,1,0:T(8,128)} %all-to-all-done.4, s32[]{:T(128)S(6)} %select_n.35), kind=kOutput, calls=%fused_computation.14 | convolution fusion | flops 12117344256 | bytes 53444620 | tf_op jit(solution)/shard_map/dot_general | solution.py:31
  426.3 41.0 %psum.69 = f32[]{:T(128)} all-reduce(f32[]{:T(128)} %get-tuple-element.16), channel_id=1, replica_groups=mesh['dp'=4,'tensor'=2,'col'=4] {'dp','tensor','col'}, use_global_device_ids=true, to_apply=%region_20.21 | all-reduce | flops 1 | bytes 8 | tf_op jit(solution)/shard_map/psum | solution.py:109
  468.7 21.6 %fusion = f32[4,40,768]{2,1,0:T(8,128)S(1)} fusion(bf16[4,40,8192]{2,1,0:T(8,128)(2,1)S(1)} %fusion.22, f32[8192,768]{1,0:T(8,128)} %get-tuple-element.15, f32[8192,768,1]{1,0,2:T(8,128)} %get-tuple-element.17, f32[]{:T(128)S(6)} %div.36, f32[]{:T(128)S(6)} %div.35), kind=kOutput, calls=%fused_computation | convolution fusion | flops 12117344256 | bytes 53444616 | tf_op jit(solution)/shard_map/dot_general | solution.py:31
  490.4 27.1 %all_to_all.32 = f32[4,2,40,768]{3,2,1,0:T(8,128)S(1)} all-to-all(f32[4,2,40,768]{3,2,1,0:T(8,128)S(1)} %broadcast_select_fusion), channel_id=1, replica_groups=mesh['dp'=4,'tensor'=2,'col'=4] {'dp'}, dimensions={0} | all-to-all | bytes 1966080 | tf_op jit(solution)/shard_map/all_to_all | solution.py:119
  517.5 1.6 fusion.58
  519.2 18.1 %multiply_reduce_fusion = f32[]{:T(128)} fusion(f32[8192,768]{1,0:T(8,128)} %get-tuple-element.15, f32[]{:T(128)S(6)} %div.36, f32[8192,768,1]{1,0,2:T(8,128)} %get-tuple-element.17, f32[]{:T(128)S(6)} %div.35), kind=kLoop, calls=%fused_computation.12 | loop fusion | flops 50331648 | bytes 50331660 | tf_op jit(solution)/shard_map/reduce_sum | solution.py:125
  537.8 6.1 %all-reduce.11.cloned.1.call-done = f32[128,768]{1,0:T(8,128)} async-done(((f32[128,768]{1,0:T(8,128)}), f32[128,768]{1,0:T(8,128)}) %all-reduce.11.cloned.1.call-update) | async-done | bytes 393232 | tf_op jit(solution)/shard_map/psum | solution.py:123
  543.9 1.7 multiply_reduce_fusion.3
  546.3 39.3 %psum.71 = f32[]{:T(128)} all-reduce(f32[]{:T(128)S(6)} %add.64), channel_id=1, replica_groups=mesh['dp'=4,'tensor'=2,'col'=4] {'dp','tensor','col'}, use_global_device_ids=true, to_apply=%region_24.25 | all-reduce | flops 1 | bytes 8 | tf_op jit(solution)/shard_map/psum | solution.py:128
  587.0 1.8 multiply_subtract_fusion
  (45 shorter events, 8.6 us)
Async XLA Ops:
  6.5 6.2 %copy-start = (bf16[128,1536]{1,0:T(8,128)(2,1)S(1)}, bf16[128,1536]{1,0:T(8,128)(2,1)}, u32[]{:S(2)}) copy-start(bf16[128,1536]{1,0:T(8,128)(2,1)} %param.7) | copy-start | bytes 1179652
  14.1 30.6 %all-to-all-start = ((bf16[4,2,40,1536]{3,2,1,0:T(8,128)(2,1)}), bf16[4,2,40,1536]{3,2,1,0:T(8,128)(2,1)S(1)}, u32[]{:S(2)}, u32[]{:S(2)}) async-start(bf16[4,2,40,1536]{3,2,1,0:T(8,128)(2,1)} %bitcast.2), calls=%async_computation | async-start | bytes 1966080 | tf_op jit(solution)/shard_map/all_to_all | solution.py:75
  20.4 156.2 %all-reduce.13.cloned.1.call-start = ((), (), s32[]{:S(2)}) async-start(), calls=%async_computation.9 | async-start | bytes 10485760 | tf_op jit(solution)/shard_map/psum | solution.py:86
  74.6 157.2 %all-reduce.7.cloned.1.call-start = ((), (), s32[]{:S(2)}) async-start(), calls=%async_computation.6 | async-start | bytes 786432 | tf_op jit(solution)/shard_map/psum | solution.py:98
  234.7 29.0 %all-to-all-start.2 = ((f32[4,2,40,768]{3,2,1,0:T(8,128)}), f32[4,2,40,768]{3,2,1,0:T(8,128)}, u32[]{:S(2)}, u32[]{:S(2)}) async-start(f32[4,2,40,768]{3,2,1,0:T(8,128)} %fusion.37), calls=%async_computation.2 | async-start | bytes 1966080 | tf_op jit(solution)/shard_map/all_to_all | solution.py:104
  239.3 111.3 %all-reduce.9.cloned.1.call-start = ((), (), s32[]{:S(2)}) async-start(), calls=%async_computation.7 | async-start | bytes 786432 | tf_op jit(solution)/shard_map/psum | solution.py:123
  353.5 49.6 %all-to-all-start.4 = ((f32[4,2,40,768]{3,2,1,0:T(8,128)}), f32[4,2,40,768]{3,2,1,0:T(8,128)}, u32[]{:S(2)}, u32[]{:S(2)}) async-start(f32[4,2,40,768]{3,2,1,0:T(8,128)} %fusion.35), calls=%async_computation.4 | async-start | bytes 1966080 | tf_op jit(solution)/shard_map/all_to_all | solution.py:104
  358.1 185.8 %all-reduce.11.cloned.1.call-start = ((), (), s32[]{:S(2)}) async-start(), calls=%async_computation.8 | async-start | bytes 786432 | tf_op jit(solution)/shard_map/psum | solution.py:123
  519.1 67.9 %copy-start.2 = (f32[128,768]{1,0:T(8,128)S(1)}, f32[128,768]{1,0:T(8,128)}, u32[]{:S(2)}) copy-start(f32[128,768]{1,0:T(8,128)} %all-reduce.9.cloned.1.call-done) | copy-start | bytes 1179652
  519.1 67.9 %copy-start.3 = (f32[128,768]{1,0:T(8,128)S(1)}, f32[128,768]{1,0:T(8,128)}, u32[]{:S(2)}) copy-start(f32[128,768]{1,0:T(8,128)} %all-reduce.7.cloned.1.call-done) | copy-start | bytes 1179652
  519.2 69.7 %copy-start.1 = (bf16[128,1536]{1,0:T(8,128)(2,1)S(1)}, bf16[128,1536]{1,0:T(8,128)(2,1)}, u32[]{:S(2)}) copy-start(bf16[128,1536]{1,0:T(8,128)(2,1)} %param.7) | copy-start | bytes 1179652
Sparse Core Ops, SparseCore 0:
  74.7 101.8 all-reduce.12
  207.4 24.3 all-reduce.6
  326.7 23.7 all-reduce.8
  519.3 24.6 all-reduce.10
where the time goes:
time: 605 us; the launch traced here: 596 us
  waiting for transfers between devices  204 us (34%)
  blocking collectives  193 us (32%)
  matrix products  128 us (21%)
  other arithmetic  32.9 us (5%)
  between operations  21 us (3%)
  starting transfers between devices  15.6 us (3%)
    psum x1, waiting for transfers between devices, shards(): lax.psum(up_part.astype(jnp.bfloat16), 'col').astype(jnp.float32)  102 us
    psum x2, blocking collectives, total_norm(): return lax.psum(jnp.sum(values * values), ('dp', 'tensor', 'col'))  81.7 us
    dot_general x4, matrix products, exact_product(): lax.dot_general(left, right, contract, precision=top_precision, preferred...  79.4 us
    all_to_all x2, blocking collectives, shards(): lax.all_to_all(placed_part, 'dp', split_axis=0, concat_axis=0, tiled=True)  53.6 us
    psum x1, blocking collectives, shards(): curvature = lax.psum(local_term, ('dp', 'tensor', 'col'))  39.3 us
    psum x2, waiting for transfers between devices, shards(): image_tokens = lax.psum(image_part, 'tensor')  30.1 us
    psum x1, waiting for transfers between devices, shards(): dropped = lax.psum(dropped_part, 'tensor')  24.5 us
    all_to_all x1, waiting for transfers between devices, shards(): lax.all_to_all(outgoing, 'dp', split_axis=0, concat_axis=0, tiled=True)  24.3 us
  transfers between devices with their start and end apart: 7, of which 6 were waited for; matrix products, arithmetic and copies ran while one was open for 3% of the time, Pallas kernels for 0%

commit v1 on v0

--- a/solution.py
+++ b/solution.py
@@ -1,16 +1,394 @@
+import functools
+
 import jax
 import jax.numpy as jnp
 from jax import lax
+from jax.experimental import pallas as pl
+from jax.experimental.pallas import tpu as pltpu
 from jax.sharding import PartitionSpec as P
 
-FF = 8192
 E = 8
 ITERS = 2
 CAP = 40
+CHUNKS = 4
 
 
 ridge_share = 0.25
 top_precision = lax.Precision.HIGHEST
+MIB = 1024 * 1024
+f32 = jnp.float32
+bf16 = jnp.bfloat16
+NT = (((1,), (1,)), ((), ()))
+NN = (((1,), (0,)), ((), ()))
+TN = (((0,), (0,)), ((), ()))
+
+
+def whole():
+    return pl.BlockSpec(memory_space=pltpu.VMEM)
+
+
+def scalars():
+    return pl.BlockSpec(memory_space=pltpu.SMEM)
+
+
+def mm(left, right, contract=NN):
+    return lax.dot_general(left, right, contract, preferred_element_type=f32)
+
+
+def split_wide(values):
+    high = values.astype(bf16)
+    low = (values - high.astype(f32)).astype(bf16)
+    return jnp.concatenate([high, low], axis=1)
+
+
+def mm_wide(left, right, contract=NN):
+    lanes = right.shape[1]
+    both = mm(left, split_wide(right), contract)
+    return both[:, :lanes] + both[:, lanes:]
+
+
+def params(mib):
+    return pltpu.CompilerParams(vmem_limit_bytes=mib * MIB)
+
+
+def block_slots(first, second):
+    count = first.shape[1]
+    expert_rows = lax.broadcasted_iota(jnp.int32, (E, count), 0).astype(f32)
+    hot_first = (expert_rows == first).astype(f32)
+    hot_second = (expert_rows == second).astype(f32)
+    before = (
+        lax.broadcasted_iota(jnp.int32, (count, count), 0)
+        < lax.broadcasted_iota(jnp.int32, (count, count), 1)
+    ).astype(bf16)
+    place = mm((hot_first + hot_second).astype(bf16), before)
+    ranked_first = jnp.sum(hot_first * place, axis=0, keepdims=True)
+    ranked_second = jnp.sum(hot_second * place, axis=0, keepdims=True)
+    return ranked_first, ranked_second
+
+
+def pick_kernel(parts, tensor_count, own_ref, info_ref, tokens_ref, out_ref):
+    first, second = info_ref[0:1, :], info_ref[1:2, :]
+    rank_first, rank_second = block_slots(first, second)
+    own = own_ref[0]
+    count = first.shape[1]
+    rows = lax.broadcasted_iota(jnp.int32, (CAP, count), 0).astype(f32)
+    values = tokens_ref[...]
+    for part in range(parts):
+        expert = (part * tensor_count + own).astype(f32)
+        hit = ((first == expert) & (rank_first == rows)) | ((second == expert) & (rank_second == rows))
+        out_ref[part] = mm(hit.astype(f32).astype(bf16), values).astype(bf16)
+
+
+def gate_up_kernel(order_ref, inputs_ref, gate_ref, up_ref, send_ref, keep_ref):
+    step = pl.program_id(0)
+    values = inputs_ref[...]
+    gate = mm(values, gate_ref[...], NT).astype(bf16)
+    up = mm(values, up_ref[...], NT).astype(bf16)
+
+    @pl.when(step < 2)
+    def _():
+        send_ref[0, 0] = gate
+        send_ref[0, 1] = up
+
+    @pl.when(step >= 2)
+    def _():
+        keep_ref[0, 0] = gate
+        keep_ref[0, 1] = up
+
+
+def gate_up(order, inputs, gate_weight, up_weight, chunk, width):
+    slots, depth = inputs.shape
+    weight_spec = pl.BlockSpec((width, depth), lambda s, order: (order[s] * CHUNKS + chunk, 0))
+    shape = jax.ShapeDtypeStruct((2, 2, slots, width), bf16)
+    return pl.pallas_call(
+        gate_up_kernel,
+        grid_spec=pltpu.PrefetchScalarGridSpec(
+            num_scalar_prefetch=1,
+            grid=(4,),
+            in_specs=[
+                pl.BlockSpec((slots, depth), lambda s, order: (0, 0)),
+                weight_spec,
+                weight_spec,
+            ],
+            out_specs=[
+                pl.BlockSpec((1, 2, slots, width), lambda s, order: (jnp.minimum(s, 1), 0, 0, 0)),
+                pl.BlockSpec((1, 2, slots, width), lambda s, order: (jnp.maximum(s - 2, 0), 0, 0, 0)),
+            ],
+        ),
+        out_shape=[shape, shape],
+        compiler_params=params(20),
+        cost_estimate=pl.CostEstimate(
+            flops=16 * slots * depth * width, bytes_accessed=16 * width * depth, transcendentals=0
+        ),
+        name=f"gate_up_{chunk}",
+    )(order, inputs, gate_weight, up_weight)
+
+
+def down_kernel(order_ref, own_ref, across_ref, beside_ref, both_ref, down_ref, *rest):
+    refs = (own_ref, across_ref, beside_ref, both_ref)
+    if len(rest) == 4:
+        old_out_ref, old_gram_ref, out_ref, gram_ref = rest
+    else:
+        out_ref, gram_ref = rest
+    for step, ref in enumerate(refs):
+
+        @pl.when(pl.program_id(0) == step)
+        def _(step=step, ref=ref):
+            values = ref[...]
+            out = mm(values, down_ref[...])
+            gram = mm(values, values, NT)
+            if step:
+                out_ref[...] += out
+                gram_ref[...] += gram
+            elif len(rest) == 4:
+                out_ref[...] = old_out_ref[...] + out
+                gram_ref[...] = old_gram_ref[...] + gram
+            else:
+                out_ref[...] = out
+                gram_ref[...] = gram
+
+
+def down(order, pieces, down_weight, chunk, older):
+    slots, width = pieces[0].shape
+    columns = down_weight.shape[1]
+
+    def fixed(shape):
+        return pl.BlockSpec(shape, lambda s, order: (0,) * len(shape))
+
+    return pl.pallas_call(
+        down_kernel,
+        grid_spec=pltpu.PrefetchScalarGridSpec(
+            num_scalar_prefetch=1,
+            grid=(4,),
+            in_specs=[fixed((slots, width))] * 4
+            + [pl.BlockSpec((width, columns), lambda s, order: (order[s] * CHUNKS + chunk, 0))]
+            + [fixed(value.shape) for value in older],
+            out_specs=[fixed((slots, columns)), fixed((slots, slots))],
+        ),
+        out_shape=[
+            jax.ShapeDtypeStruct((slots, columns), f32),
+            jax.ShapeDtypeStruct((slots, slots), f32),
+        ],
+        compiler_params=params(20),
+        cost_estimate=pl.CostEstimate(
+            flops=8 * slots * width * (columns + slots),
+            bytes_accessed=8 * width * columns,
+            transcendentals=0,
+        ),
+        name=f"down_{chunk}",
+    )(order, *pieces, down_weight, *older)
+
+
+def pack_kernel(parts, out_ref, gram_ref, packed_ref):
+    gram = gram_ref[...]
+    wide = out_ref.shape[1] // parts
+    for part in range(parts):
+        piece = out_ref[:, part * wide : (part + 1) * wide]
+        packed_ref[part] = jnp.concatenate([gram, piece], axis=1).astype(bf16)
+
+
+def route_kernel(blocks, kept_ref, info_ref, hot_ref, gates_ref):
+    count = info_ref.shape[2]
+    slots = blocks * CAP
+    zero = jnp.zeros((CAP, count), f32)
+    rows = lax.broadcasted_iota(jnp.int32, (CAP, count), 0).astype(f32)
+    for block in range(blocks):
+        first, second = info_ref[block, 0:1, :], info_ref[block, 1:2, :]
+        delta = info_ref[block, 3:4, :] - info_ref[block, 2:3, :]
+        share_first = 1.0 / (1.0 + jnp.exp(delta))
+        share_second = 1.0 / (1.0 + jnp.exp(-delta))
+        rank_first, rank_second = block_slots(first, second)
+        for expert in range(E):
+            kept = jnp.zeros((), jnp.bool_)
+            for place in range(kept_ref.shape[0]):
+                kept = kept | (kept_ref[place] == expert)
+            kept = kept.astype(f32)
+            hit_first = (first == expert) & (rank_first == rows)
+            hit_second = (second == expert) & (rank_second == rows)
+            gate = jnp.sum(
+                jnp.where(hit_first, share_first, zero) + jnp.where(hit_second, share_second, zero),
+                axis=1,
+                keepdims=True,
+            )
+            hot = (hit_first | hit_second).astype(f32)
+            row = expert * slots + block * CAP
+            for other in range(blocks):
+                hot_ref[row : row + CAP, other * count : (other + 1) * count] = hot if other == block else zero
+            gates_ref[row : row + CAP, 0:1] = gate * kept
+            gates_ref[row : row + CAP, 1:2] = gate * (1.0 - kept)
+
+
+def solve_kernel(ridge, slots, packed_ref, hot_ref, gates_ref, square_ref, base_ref, zero_ref, one_ref, sums_ref):
+    hot = hot_ref[...].astype(bf16)
+    kept, dropped = gates_ref[:, 0:1], gates_ref[:, 1:2]
+    values = jnp.concatenate([packed_ref[e][:, slots:].astype(f32) for e in range(E)], axis=0)
+    base = mm_wide(hot, dropped * values, TN)
+    output = mm_wide(hot, kept * values, TN)
+
+    def apply(field):
+        spread = kept * mm_wide(hot, field)
+        mixed = jnp.concatenate(
+            [
+                mm_wide(packed_ref[e][:, :slots], spread[e * slots : (e + 1) * slots])
+                for e in range(E)
+            ],
+            axis=0,
+        )
+        return mm_wide(hot, kept * mixed, TN)
+
+    curved = apply(base)
+    zero = curved - ridge * output
+    one = apply(zero)
+    base_ref[...] = base
+    zero_ref[...] = zero
+    one_ref[...] = one
+    norm = jnp.sum(base * curved) - 2.0 * ridge * jnp.sum(base * output)
+    sums_ref[0:1, :] = jnp.full((1, sums_ref.shape[1]), norm, f32) + ridge * ridge * square_ref[0]
+    sums_ref[1:2, :] = jnp.full((1, sums_ref.shape[1]), jnp.sum(zero * zero), f32)
+    sums_ref[2:3, :] = jnp.full((1, sums_ref.shape[1]), jnp.sum(zero * one), f32)
+    sums_ref[3:4, :] = jnp.full((1, sums_ref.shape[1]), jnp.sum(one * one), f32)
+    sums_ref[4:8, :] = jnp.zeros((4, sums_ref.shape[1]), f32)
+
+
+def finish_kernel(ridge, blocks, copies, base_ref, zero_ref, one_ref, sums_ref, out_ref):
+    norm = sums_ref[0:1, 0:1]
+    zero_zero = sums_ref[1:2, 0:1]
+    zero_one = sums_ref[2:3, 0:1]
+    one_one = sums_ref[3:4, 0:1]
+    step = norm / (zero_zero + ridge * norm)
+    left = 1.0 - step * ridge
+    new = left * left * norm - 2.0 * left * step * zero_zero + step * step * zero_one
+    ratio = new / norm
+    grown = left + ratio
+    image = grown * grown * zero_zero - 2.0 * grown * step * zero_one + step * step * one_one
+    later = new / (image + ridge * (new + ratio * ratio * norm))
+    field = base_ref[...] - (step + later * grown) * zero_ref[...] + (later * step) * one_ref[...]
+    rows = field.shape[0] // blocks
+    for block in range(blocks):
+        piece = field[block * rows : (block + 1) * rows].astype(bf16)
+        for copy in range(copies):
+            out_ref[block * copies + copy] = piece
+
+
+def join_kernel(pieces_ref, out_ref):
+    out_ref[...] = jnp.concatenate(
+        [pieces_ref[part].astype(f32) for part in range(pieces_ref.shape[0])], axis=1
+    )
+
+
+def single(kernel, out_shape, in_specs, mib, name):
+    many = isinstance(out_shape, list)
+    return pl.pallas_call(
+        kernel,
+        out_shape=out_shape,
+        in_specs=in_specs,
+        out_specs=[whole()] * len(out_shape) if many else whole(),
+        compiler_params=params(mib),
+        name=name,
+    )
+
+
+def one_expert_each(tokens, routes, route_logits, kept_experts, gate_weight, up_weight, down_weight):
+    dp_count = lax.axis_size("dp")
+    tensor_count = lax.axis_size("tensor")
+    parts = dp_count * tensor_count
+    tok_rows, depth = tokens.shape
+    units, columns = down_weight.shape
+    slots = dp_count * CAP
+    lanes = columns // parts
+    width = units // 4 // CHUNKS
+    ridge = ridge_share * 2.0 * tok_rows * dp_count / E
+    tensor_index = lax.axis_index("tensor")
+    col_index = lax.axis_index("col")
+    own_expert = lax.axis_index("dp") * tensor_count + tensor_index
+
+    def beside(values):
+        return lax.ppermute(values, "col", [(k, k ^ 1) for k in range(4)])
+
+    def across(values):
+        return lax.ppermute(values, "col", [(k, k ^ 2) for k in range(4)])
+
+    info = jnp.concatenate([routes.astype(f32).T, route_logits.T], axis=0)
+    all_info = lax.all_gather(info, "dp")
+    hot, gates = single(
+        functools.partial(route_kernel, dp_count),
+        [
+            jax.ShapeDtypeStruct((E * slots, dp_count * tok_rows), f32),
+            jax.ShapeDtypeStruct((E * slots, 2), f32),
+        ],
+        [scalars(), whole()],
+        16,
+        "route",
+    )(kept_experts, all_info)
+
+    picked = single(
+        functools.partial(pick_kernel, dp_count, tensor_count),
+        jax.ShapeDtypeStruct((dp_count, CAP, depth), bf16),
+        [scalars(), whole(), whole()],
+        16,
+        "pick",
+    )(tensor_index.reshape(1), info, tokens)
+    arrived = lax.all_to_all(picked, "dp", split_axis=0, concat_axis=0, tiled=True)
+    inputs = arrived.reshape(slots, depth)
+
+    gate_order = col_index ^ jnp.array([3, 1, 2, 0], jnp.int32)
+    down_order = col_index ^ jnp.array([0, 2, 1, 3], jnp.int32)
+    older = ()
+    for chunk in range(CHUNKS):
+        send, keep = gate_up(gate_order, inputs, gate_weight, up_weight, chunk, width)
+        near = beside(send)
+        pair = keep.astype(f32) + near.astype(f32)
+        far = across(pair[0].astype(bf16))
+        total = pair[1] + far.astype(f32)
+        own = (jax.nn.silu(total[0]) * total[1]).astype(bf16)
+        other = across(own)
+        older = down(down_order, (own, other, beside(own), beside(other)), down_weight, chunk, older)
+
+    is_kept = jnp.any(kept_experts == own_expert).astype(f32)
+    wide_down = down_weight.astype(f32)
+    square = (is_kept * jnp.sum(wide_down * wide_down)).reshape(1)
+
+    packed = single(
+        functools.partial(pack_kernel, parts),
+        jax.ShapeDtypeStruct((parts, slots, slots + lanes), bf16),
+        [whole(), whole()],
+        16,
+        "pack",
+    )(*older)
+    spread = lax.all_to_all(packed, ("dp", "tensor"), split_axis=0, concat_axis=0, tiled=True)
+
+    field = jax.ShapeDtypeStruct((dp_count * tok_rows, lanes), f32)
+    base, zero, one, sums = single(
+        functools.partial(solve_kernel, ridge, slots),
+        [field, field, field, jax.ShapeDtypeStruct((8, 128), f32)],
+        [whole(), whole(), whole(), scalars()],
+        40,
+        "solve",
+    )(spread, hot, gates, square)
+
+    for axis, size in (("col", 4), ("tensor", tensor_count), ("dp", dp_count)):
+        shifted = [
+            lax.ppermute(sums, axis, [(k, (k + step) % size) for k in range(size)])
+            for step in range(1, size)
+        ]
+        for value in shifted:
+            sums = sums + value
+
+    home = single(
+        functools.partial(finish_kernel, ridge, dp_count, tensor_count),
+        jax.ShapeDtypeStruct((parts, tok_rows, lanes), bf16),
+        [whole()] * 4,
+        16,
+        "finish",
+    )(base, zero, one, sums)
+    pieces = lax.all_to_all(home, ("dp", "tensor"), split_axis=0, concat_axis=0, tiled=True)
+    return single(
+        join_kernel,
+        jax.ShapeDtypeStruct((tok_rows, columns), f32),
+        [whole()],
+        16,
+        "join",
+    )(pieces)
 
 
 def spread_copies(values, experts, held_count, copies):
@@ -33,13 +411,14 @@
     )
 
 
-def shards(tokens, routes, route_logits, kept_experts, gate_weight, up_weight, down_weight):
+def general(tokens, routes, route_logits, kept_experts, gate_weight, up_weight, down_weight):
     dp_count = lax.axis_size("dp")
     tensor_count = lax.axis_size("tensor")
     held_count = max(1, E // dp_count)
     copies = max(1, dp_count // E)
     tok_rows = tokens.shape[0]
     piece_rows = gate_weight.shape[0]
+    FF = piece_rows * dp_count * tensor_count // E
     slot_total = E * CAP
     device_rank = lax.axis_index("dp") * tensor_count + lax.axis_index("tensor")
     own_expert = device_rank * piece_rows // FF
@@ -137,6 +516,13 @@
     return leftover
 
 
+def shards(*arrays):
+    sizes = [lax.axis_size(axis) for axis in ("dp", "tensor", "col")]
+    if sizes[0] * sizes[1] == E and sizes[2] == 4 and ITERS == 2:
+        return one_expert_each(*arrays)
+    return general(*arrays)
+
+
 def solution(mesh):
     placed = (
         P("dp", "col"),

time: 605 us -> 194 us (0.32); the launches traced: 596 us -> 193 us
  blocking collectives: 193 us -> 34.6 us
  waiting for transfers between devices: 204 us -> 55.1 us
  matrix products: 128 us -> 0 us
  Pallas kernels: 0 us -> 46.9 us
  between operations: 21 us -> 1.66 us
  other arithmetic: 32.9 us -> 15.2 us
  starting transfers between devices: 15.6 us -> 28 us
  local copies, waits for them, and re-layouts: 1.74 us -> 11.6 us
    psum x4 -> x0, waiting for transfers between devices: 157 us -> none  [the longest x1 102 us: shards(): lax.psum(up_part.astype(jnp.bfloat16), 'col').astype(jnp.float32)]
    dot_general x13 -> x0, matrix products: 128 us -> none  [the longest x4 79.4 us: exact_product(): lax.dot_general(left, right, contract, precision=top_precision, preferred...]
    psum x3 -> x0, blocking collectives: 121 us -> none  [the longest x2 81.7 us: total_norm(): return lax.psum(jnp.sum(values * values), ('dp', 'tensor', 'col'))]
    all_to_all x3 -> x1, blocking collectives: 71.8 us -> 12 us  [one_expert_each(): lax.all_to_all(home, ('dp', 'tensor'), split_axis=0, concat_axis=0, tiled...]
    pallas_call x0 -> x14, Pallas kernels: none -> 46.9 us  [the longest x4 28.2 us: gate_up(): pl.pallas_call(gate_up_kernel, grid_spec=pltpu.PrefetchScalarGridSpec(num...]
    ppermute x0 -> x27, waiting for transfers between devices: none -> 41.3 us  [the longest x8 32.5 us: across(): return lax.ppermute(values, 'col', [(k, k ^ 2) for k in range(4)])]
    all_to_all x3 -> x2, waiting for transfers between devices: 47.5 us -> 13.8 us  [the longest x1 13.8 us: one_expert_each(): lax.all_to_all(picked, 'dp', split_axis=0, concat_axis=0, tiled=True)]
    all_gather x0 -> x1, blocking collectives: none -> 22.7 us  [one_expert_each(): all_info = lax.all_gather(info, 'dp')]
  transfers between devices with their start and end apart: 7 -> 29, of which waited for: 6 -> 15; matrix products, arithmetic and copies ran while one was open for 3% -> 7% of each run, Pallas kernels for 0% -> 15%
where the time goes in v1:
time: 194 us; the launch traced here: 193 us
  waiting for transfers between devices  55.1 us (28%)
  Pallas kernels  46.9 us (24%)
  blocking collectives  34.6 us (18%)
  starting transfers between devices  28 us (14%)
  other arithmetic  15.2 us (8%)
  local copies, waits for them, and re-layouts  11.6 us (6%)
    ppermute x8, waiting for transfers between devices, across(): return lax.ppermute(values, 'col', [(k, k ^ 2) for k in range(4)])  32.5 us
    pallas_call x4, Pallas kernels, gate_up(): pl.pallas_call(gate_up_kernel, grid_spec=pltpu.PrefetchScalarGridSpec(num...  28.2 us
    all_gather x1, blocking collectives, one_expert_each(): all_info = lax.all_gather(info, 'dp')  22.7 us
    all_to_all x1, waiting for transfers between devices, one_expert_each(): lax.all_to_all(picked, 'dp', split_axis=0, concat_axis=0, tiled=True)  13.8 us
    all_to_all x1, blocking collectives, one_expert_each(): lax.all_to_all(home, ('dp', 'tensor'), split_axis=0, concat_axis=0, tiled...  12 us
    reduce_sum x1, other arithmetic, one_expert_each(): square = (is_kept * jnp.sum(wide_down * wide_down)).reshape(1)  11.7 us
    unnamed x20, local copies, waits for them, and re-layouts  11.1 us
    ppermute x8, starting transfers between devices, across(): return lax.ppermute(values, 'col', [(k, k ^ 2) for k in range(4)])  10.5 us
  transfers between devices with their start and end apart: 29, of which 15 were waited for; matrix products, arithmetic and copies ran while one was open for 7% of the time, Pallas kernels for 15%

profile of v1, /device:TPU:0, one launch (start us, length us, event | category | flops | bytes accessed | tf_op | source)
XLA Modules:
  0.0 193.0 jit_solution(8898315430025910746)
XLA Ops:
  3.7 6.3 %all-to-all-start = ((bf16[4,40,1536]{2,1,0:T(8,128)(2,1)}), bf16[4,40,1536]{2,1,0:T(8,128)(2,1)S(1)}, u32[]{:S(2)}, u32[]{:S(2)}) async-start(bf16[4,40,1536]{2,1,0:T(8,128)(2,1)} %pick.1), calls=%async_computation | async-start | bytes 983040 | tf_op jit(solution)/shard_map/all_to_all | solution.py:331
  10.0 13.8 %all-to-all-done = bf16[4,40,1536]{2,1,0:T(8,128)(2,1)S(1)} async-done(((bf16[4,40,1536]{2,1,0:T(8,128)(2,1)}), bf16[4,40,1536]{2,1,0:T(8,128)(2,1)S(1)}, u32[]{:S(2)}, u32[]{:S(2)}) %all-to-all-start) | async-done | bytes 491552 | tf_op jit(solution)/shard_map/all_to_all | solution.py:331
  23.8 8.2 %copy-done = bf16[8192,1536]{1,0:T(8,128)(2,1)S(1)} copy-done((bf16[8192,1536]{1,0:T(8,128)(2,1)S(1)}, bf16[8192,1536]{1,0:T(8,128)(2,1)}, u32[]{:S(2)}) %copy-start) | copy-done | bytes 25165848
  31.9 7.1 %gate_up_0.1 = (bf16[2,2,160,512]{3,2,1,0:T(8,128)(2,1)S(1)}, bf16[2,2,160,512]{3,2,1,0:T(8,128)(2,1)S(1)}) custom-call(s32[4]{0:T(128)S(1)} %broadcast_xor_fusion.order_ref, bf16[160,1536]{1,0:T(8,128)(2,1)S(1)} %bitcast.74, bf16[8192,1536]{1,0:T(8,128)(2,1)S(1)} %copy-done, bf16[8192,1536]{1,0:T(8,128)(2,1)} %up_ref.7), custom_call_target="tpu_custom_call" | custom-call | flops 2013265920 | bytes 12582912 | tf_op jit(solution)/shard_map/gate_up_0/pallas_call | solution.py:103
  39.1 7.1 %gate_up_1.1 = (bf16[2,2,160,512]{3,2,1,0:T(8,128)(2,1)S(1)}, bf16[2,2,160,512]{3,2,1,0:T(8,128)(2,1)S(1)}) custom-call(s32[4]{0:T(128)S(1)} %broadcast_xor_fusion.order_ref, bf16[160,1536]{1,0:T(8,128)(2,1)S(1)} %bitcast.75, bf16[8192,1536]{1,0:T(8,128)(2,1)S(1)} %copy-done, bf16[8192,1536]{1,0:T(8,128)(2,1)} %up_ref.7), custom_call_target="tpu_custom_call" | custom-call | flops 2013265920 | bytes 12582912 | tf_op jit(solution)/shard_map/gate_up_1/pallas_call | solution.py:103
  46.7 7.1 %gate_up_2.1 = (bf16[2,2,160,512]{3,2,1,0:T(8,128)(2,1)S(1)}, bf16[2,2,160,512]{3,2,1,0:T(8,128)(2,1)S(1)}) custom-call(s32[4]{0:T(128)S(1)} %broadcast_xor_fusion.order_ref, bf16[160,1536]{1,0:T(8,128)(2,1)S(1)} %bitcast.76, bf16[8192,1536]{1,0:T(8,128)(2,1)S(1)} %copy-done, bf16[8192,1536]{1,0:T(8,128)(2,1)} %up_ref.7), custom_call_target="tpu_custom_call" | custom-call | flops 2013265920 | bytes 12582912 | tf_op jit(solution)/shard_map/gate_up_2/pallas_call | solution.py:103
  53.8 7.1 %gate_up_3.1 = (bf16[2,2,160,512]{3,2,1,0:T(8,128)(2,1)S(1)}, bf16[2,2,160,512]{3,2,1,0:T(8,128)(2,1)S(1)}) custom-call(s32[4]{0:T(128)S(1)} %broadcast_xor_fusion.order_ref, bf16[160,1536]{1,0:T(8,128)(2,1)S(1)} %bitcast.77, bf16[8192,1536]{1,0:T(8,128)(2,1)S(1)} %copy-done, bf16[8192,1536]{1,0:T(8,128)(2,1)} %up_ref.7), custom_call_target="tpu_custom_call" | custom-call | flops 2013265920 | bytes 12582912 | tf_op jit(solution)/shard_map/gate_up_3/pallas_call | solution.py:103
  61.7 1.6 collective-permute-start.16
  64.4 1.6 collective-permute-start.6
  66.8 5.6 %collective-permute-done.16 = bf16[2,160,512]{2,1,0:T(8,128)(2,1)S(1)} collective-permute-done((bf16[2,160,512]{2,1,0:T(8,128)(2,1)S(1)}, bf16[2,160,512]{2,1,0:T(8,128)(2,1)S(1)}, u32[]{:S(2)}, u32[]{:S(2)}) %collective-permute-start.16) | collective-permute-done | bytes 327712 | tf_op jit(solution)/shard_map/ppermute | solution.py:309
  72.6 1.6 collective-permute-start.17
  74.2 5.1 %collective-permute-done.11 = bf16[2,160,512]{2,1,0:T(8,128)(2,1)S(1)} collective-permute-done((bf16[2,160,512]{2,1,0:T(8,128)(2,1)S(1)}, bf16[2,160,512]{2,1,0:T(8,128)(2,1)S(1)}, u32[]{:S(2)}, u32[]{:S(2)}) %collective-permute-start.11) | collective-permute-done | bytes 327712 | tf_op jit(solution)/shard_map/ppermute | solution.py:309
  79.7 6.7 %collective-permute-done.6 = bf16[2,160,512]{2,1,0:T(8,128)(2,1)S(1)} collective-permute-done((bf16[2,160,512]{2,1,0:T(8,128)(2,1)S(1)}, bf16[2,160,512]{2,1,0:T(8,128)(2,1)S(1)}, u32[]{:S(2)}, u32[]{:S(2)}) %collective-permute-start.6) | collective-permute-done | bytes 327712 | tf_op jit(solution)/shard_map/ppermute | solution.py:309
  88.1 5.3 %collective-permute-done.1 = bf16[2,160,512]{2,1,0:T(8,128)(2,1)S(1)} collective-permute-done((bf16[2,160,512]{2,1,0:T(8,128)(2,1)S(1)}, bf16[2,160,512]{2,1,0:T(8,128)(2,1)S(1)}, u32[]{:S(2)}, u32[]{:S(2)}) %collective-permute-start.1) | collective-permute-done | bytes 327712 | tf_op jit(solution)/shard_map/ppermute | solution.py:309
  95.2 1.7 collective-permute-done.17.across_ref
  98.5 2.0 %collective-permute-done.12.across_ref = bf16[160,512]{1,0:T(8,128)(2,1)S(1)} collective-permute-done((bf16[160,512]{1,0:T(8,128)(2,1)S(1)}, bf16[160,512]{1,0:T(8,128)(2,1)S(1)}, u32[]{:S(2)}, u32[]{:S(2)}) %collective-permute-start.12) | collective-permute-done | bytes 163872 | tf_op jit(solution)/shard_map/ppermute | solution.py:309
  100.4 3.5 %collective-permute-done.7.across_ref = bf16[160,512]{1,0:T(8,128)(2,1)S(1)} collective-permute-done((bf16[160,512]{1,0:T(8,128)(2,1)S(1)}, bf16[160,512]{1,0:T(8,128)(2,1)S(1)}, u32[]{:S(2)}, u32[]{:S(2)}) %collective-permute-start.7) | collective-permute-done | bytes 163872 | tf_op jit(solution)/shard_map/ppermute | solution.py:309
  104.0 2.6 %collective-permute-done.2.across_ref = bf16[160,512]{1,0:T(8,128)(2,1)S(1)} collective-permute-done((bf16[160,512]{1,0:T(8,128)(2,1)S(1)}, bf16[160,512]{1,0:T(8,128)(2,1)S(1)}, u32[]{:S(2)}, u32[]{:S(2)}) %collective-permute-start.2) | collective-permute-done | bytes 163872 | tf_op jit(solution)/shard_map/ppermute | solution.py:309
  107.1 2.0 %down_0.1 = (f32[160,768]{1,0:T(8,128)S(1)}, f32[160,160]{1,0:T(8,128)S(1)}) custom-call(s32[4]{0:T(128)S(1)} %broadcast_xor_fusion.1.order_ref, bf16[160,512]{1,0:T(8,128)(2,1)S(1)} %fusion.9.own_ref, bf16[160,512]{1,0:T(8,128)(2,1)S(1)} %collective-permute-done.17.across_ref, bf16[160,512]{1,0:T(8,128)(2,1)S(1)} %collective-permute-done.18.beside_ref, ...), custom_call_target="tpu_custom_call" | custom-call | flops 608174080 | bytes 3145728 | tf_op jit(solution)/shard_map/down_0/pallas_call | solution.py:158
  109.1 2.0 %down_1.1 = (f32[160,768]{1,0:T(8,128)S(1)}, f32[160,160]{1,0:T(8,128)S(1)}) custom-call(s32[4]{0:T(128)S(1)} %broadcast_xor_fusion.1.order_ref, bf16[160,512]{1,0:T(8,128)(2,1)S(1)} %fusion.11.own_ref, bf16[160,512]{1,0:T(8,128)(2,1)S(1)} %collective-permute-done.12.across_ref, bf16[160,512]{1,0:T(8,128)(2,1)S(1)} %collective-permute-done.13.beside_ref, ...), custom_call_target="tpu_custom_call" | custom-call | flops 608174080 | bytes 3145728 | tf_op jit(solution)/shard_map/down_1/pallas_call | solution.py:158
  111.2 2.0 %down_2.1 = (f32[160,768]{1,0:T(8,128)S(1)}, f32[160,160]{1,0:T(8,128)S(1)}) custom-call(s32[4]{0:T(128)S(1)} %broadcast_xor_fusion.1.order_ref, bf16[160,512]{1,0:T(8,128)(2,1)S(1)} %fusion.13.own_ref, bf16[160,512]{1,0:T(8,128)(2,1)S(1)} %collective-permute-done.7.across_ref, bf16[160,512]{1,0:T(8,128)(2,1)S(1)} %collective-permute-done.8.beside_ref, ...), custom_call_target="tpu_custom_call" | custom-call | flops 608174080 | bytes 3145728 | tf_op jit(solution)/shard_map/down_2/pallas_call | solution.py:158
  113.2 2.0 %down_3.1 = (f32[160,768]{1,0:T(8,128)S(1)}, f32[160,160]{1,0:T(8,128)S(1)}) custom-call(s32[4]{0:T(128)S(1)} %broadcast_xor_fusion.1.order_ref, bf16[160,512]{1,0:T(8,128)(2,1)S(1)} %fusion.15.own_ref, bf16[160,512]{1,0:T(8,128)(2,1)S(1)} %collective-permute-done.2.across_ref, bf16[160,512]{1,0:T(8,128)(2,1)S(1)} %collective-permute-done.3.beside_ref, ...), custom_call_target="tpu_custom_call" | custom-call | flops 608174080 | bytes 3145728 | tf_op jit(solution)/shard_map/down_3/pallas_call | solution.py:158
  116.3 3.7 %all-to-all-start.1 = ((bf16[8,160,256]{2,1,0:T(8,128)(2,1)}), bf16[8,160,256]{2,1,0:T(8,128)(2,1)S(1)}, u32[]{:S(2)}, u32[]{:S(2)}) async-start(bf16[8,160,256]{2,1,0:T(8,128)(2,1)} %pack.1), calls=%async_computation.1 | async-start | bytes 1310720 | tf_op jit(solution)/shard_map/all_to_all | solution.py:358
  120.0 22.7 %all-gather.1.info_ref = f32[4,4,128]{2,1,0:T(4,128)S(1)} all-gather(f32[1,4,128]{2,1,0:T(4,128)S(1)} %get-tuple-element.49), channel_id=2, replica_groups=mesh['dp'=4,'tensor'=2,'col'=4] {'dp'}, dimensions={0}, use_global_device_ids=true | all-gather | bytes 10240 | tf_op jit(solution)/shard_map/all_gather | solution.py:312
  145.3 11.7 %multiply_reduce_fusion = f32[]{:T(128)} fusion(bf16[8192,768]{1,0:T(8,128)(2,1)} %down_ref.7), kind=kLoop, calls=%fused_computation | loop fusion | flops 18874368 | bytes 12582916 | tf_op jit(solution)/shard_map/reduce_sum | solution.py:349
  159.3 6.0 %solve.1 = (f32[512,96]{1,0:T(8,128)S(1)}, f32[512,96]{1,0:T(8,128)S(1)}, f32[512,96]{1,0:T(8,128)S(1)}, f32[8,128]{1,0:T(8,128)S(1)}) custom-call(bf16[8,160,256]{2,1,0:T(8,128)(2,1)S(1)} %all-to-all-done.1.packed_ref, f32[1280,512]{1,0:T(8,128)S(1)} %get-tuple-element.43.hot_ref, f32[1280,2]{1,0:T(8,128)S(1)} %copy-done.2, f32[1]{0:T(128)} %bitcast.21.square_ref), custom_call_target="tpu_custom_call" | custom-call | tf_op jit(solution)/shard_map/solve/pallas_call | solution.py:361
  165.4 1.6 collective-permute-start.21
  167.2 1.9 collective-permute-done.21
  170.0 1.7 collective-permute-start.23
  171.7 1.9 collective-permute-done.23
  175.7 1.6 collective-permute-done.26
  180.0 12.0 %all_to_all.15 = bf16[8,128,96]{1,2,0:T(8,128)(2,1)S(1)} all-to-all(bf16[8,128,96]{1,2,0:T(8,128)(2,1)S(1)} %copy.10), channel_id=1, replica_groups=mesh['dp'=4,'tensor'=2,'col'=4] {'dp','tensor'}, dimensions={0} | all-to-all | bytes 393216 | tf_op jit(solution)/shard_map/all_to_all | solution.py:384
  (90 shorter events, 24.9 us)
Async XLA Ops:
  3.7 20.1 %all-to-all-start = ((bf16[4,40,1536]{2,1,0:T(8,128)(2,1)}), bf16[4,40,1536]{2,1,0:T(8,128)(2,1)S(1)}, u32[]{:S(2)}, u32[]{:S(2)}) async-start(bf16[4,40,1536]{2,1,0:T(8,128)(2,1)} %pick.1), calls=%async_computation | async-start | bytes 983040 | tf_op jit(solution)/shard_map/all_to_all | solution.py:331
  39.0 22.5 %collective-permute-start.15 = (bf16[2,2,160,512]{3,2,1,0:T(8,128)(2,1)S(1)}, bf16[2,2,160,512]{3,2,1,0:T(8,128)(2,1)S(1)}, u32[]{:S(2)}, u32[]{:S(2)}) collective-permute-start(bf16[2,2,160,512]{3,2,1,0:T(8,128)(2,1)S(1)} %get-tuple-element.34), channel_id=1, source_target_pairs={{0,1},{1,0},{2,3},{3,2},{4,5},{5,4},{6,7},{7,6},{8,9},{9,8},{10,11... | collective-permute-start | bytes 1966088 | tf_op jit(solution)/shard_map/ppermute | solution.py:306
  46.1 17.2 %collective-permute-start.10 = (bf16[2,2,160,512]{3,2,1,0:T(8,128)(2,1)S(1)}, bf16[2,2,160,512]{3,2,1,0:T(8,128)(2,1)S(1)}, u32[]{:S(2)}, u32[]{:S(2)}) collective-permute-start(bf16[2,2,160,512]{3,2,1,0:T(8,128)(2,1)S(1)} %get-tuple-element.32), channel_id=1, source_target_pairs={{0,1},{1,0},{2,3},{3,2},{4,5},{5,4},{6,7},{7,6},{8,9},{9,8},{10,11... | collective-permute-start | bytes 1966088 | tf_op jit(solution)/shard_map/ppermute | solution.py:306
  53.8 10.4 %collective-permute-start.5 = (bf16[2,2,160,512]{3,2,1,0:T(8,128)(2,1)S(1)}, bf16[2,2,160,512]{3,2,1,0:T(8,128)(2,1)S(1)}, u32[]{:S(2)}, u32[]{:S(2)}) collective-permute-start(bf16[2,2,160,512]{3,2,1,0:T(8,128)(2,1)S(1)} %get-tuple-element.30), channel_id=1, source_target_pairs={{0,1},{1,0},{2,3},{3,2},{4,5},{5,4},{6,7},{7,6},{8,9},{9,8},{10,11... | collective-permute-start | bytes 1966088 | tf_op jit(solution)/shard_map/ppermute | solution.py:306
  60.9 5.1 %collective-permute-start = (bf16[2,2,160,512]{3,2,1,0:T(8,128)(2,1)S(1)}, bf16[2,2,160,512]{3,2,1,0:T(8,128)(2,1)S(1)}, u32[]{:S(2)}, u32[]{:S(2)}) collective-permute-start(bf16[2,2,160,512]{3,2,1,0:T(8,128)(2,1)S(1)} %get-tuple-element.28), channel_id=1, source_target_pairs={{0,1},{1,0},{2,3},{3,2},{4,5},{5,4},{6,7},{7,6},{8,9},{9,8},{10,11... | collective-permute-start | bytes 1966088 | tf_op jit(solution)/shard_map/ppermute | solution.py:306
  61.5 45.6 %slice-start = ((s8[12582912]{0:T(1024)(128)(4,1)}), s8[4194304]{0:T(1024)(128)(4,1)S(1)}, s32[]{:S(2)}) async-start(s8[12582912]{0:T(1024)(128)(4,1)} %bitcast.72), calls=%async_computation.3 | async-start | bytes 8388608
  61.7 10.6 %collective-permute-start.16 = (bf16[2,160,512]{2,1,0:T(8,128)(2,1)S(1)}, bf16[2,160,512]{2,1,0:T(8,128)(2,1)S(1)}, u32[]{:S(2)}, u32[]{:S(2)}) collective-permute-start(bf16[2,160,512]{2,1,0:T(8,128)(2,1)S(1)} %fusion.7), channel_id=1, source_target_pairs={{0,2},{1,3},{2,0},{3,1},{4,6},{5,7},{6,4},{7,5},{8,10},{9,11},{10,... | collective-permute-start | bytes 983048 | tf_op jit(solution)/shard_map/ppermute | solution.py:309
  63.5 15.8 %collective-permute-start.11 = (bf16[2,160,512]{2,1,0:T(8,128)(2,1)S(1)}, bf16[2,160,512]{2,1,0:T(8,128)(2,1)S(1)}, u32[]{:S(2)}, u32[]{:S(2)}) collective-permute-start(bf16[2,160,512]{2,1,0:T(8,128)(2,1)S(1)} %fusion.6), channel_id=1, source_target_pairs={{0,2},{1,3},{2,0},{3,1},{4,6},{5,7},{6,4},{7,5},{8,10},{9,11},{10,... | collective-permute-start | bytes 983048 | tf_op jit(solution)/shard_map/ppermute | solution.py:309
  64.1 42.9 %slice-start.1 = ((s8[12582912]{0:T(1024)(128)(4,1)}), s8[4194304]{0:T(1024)(128)(4,1)S(1)}, s32[]{:S(2)}) async-start(s8[12582912]{0:T(1024)(128)(4,1)} %bitcast.72), calls=%async_computation.4 | async-start | bytes 8388608
  64.4 22.0 %collective-permute-start.6 = (bf16[2,160,512]{2,1,0:T(8,128)(2,1)S(1)}, bf16[2,160,512]{2,1,0:T(8,128)(2,1)S(1)}, u32[]{:S(2)}, u32[]{:S(2)}) collective-permute-start(bf16[2,160,512]{2,1,0:T(8,128)(2,1)S(1)} %fusion.5), channel_id=1, source_target_pairs={{0,2},{1,3},{2,0},{3,1},{4,6},{5,7},{6,4},{7,5},{8,10},{9,11},{10,... | collective-permute-start | bytes 983048 | tf_op jit(solution)/shard_map/ppermute | solution.py:309
  66.2 27.2 %collective-permute-start.1 = (bf16[2,160,512]{2,1,0:T(8,128)(2,1)S(1)}, bf16[2,160,512]{2,1,0:T(8,128)(2,1)S(1)}, u32[]{:S(2)}, u32[]{:S(2)}) collective-permute-start(bf16[2,160,512]{2,1,0:T(8,128)(2,1)S(1)} %fusion.4), channel_id=1, source_target_pairs={{0,2},{1,3},{2,0},{3,1},{4,6},{5,7},{6,4},{7,5},{8,10},{9,11},{10,... | collective-permute-start | bytes 983048 | tf_op jit(solution)/shard_map/ppermute | solution.py:309
  72.4 34.6 %slice-start.2 = ((s8[12582912]{0:T(1024)(128)(4,1)}), s8[4194304]{0:T(1024)(128)(4,1)S(1)}, s32[]{:S(2)}) async-start(s8[12582912]{0:T(1024)(128)(4,1)} %bitcast.72), calls=%async_computation.5 | async-start | bytes 8388608
  72.6 22.6 %collective-permute-start.18 = (bf16[160,512]{1,0:T(8,128)(2,1)S(1)}, bf16[160,512]{1,0:T(8,128)(2,1)S(1)}, u32[]{:S(2)}, u32[]{:S(2)}) collective-permute-start(bf16[160,512]{1,0:T(8,128)(2,1)S(1)} %fusion.9.own_ref), channel_id=1, source_target_pairs={{0,1},{1,0},{2,3},{3,2},{4,5},{5,4},{6,7},{7,6},{8,9},{9,8},{10,11... | collective-permute-start | bytes 491528 | tf_op jit(solution)/shard_map/ppermute | solution.py:306
  72.6 24.3 %collective-permute-start.17 = (bf16[160,512]{1,0:T(8,128)(2,1)S(1)}, bf16[160,512]{1,0:T(8,128)(2,1)S(1)}, u32[]{:S(2)}, u32[]{:S(2)}) collective-permute-start(bf16[160,512]{1,0:T(8,128)(2,1)S(1)} %fusion.9.own_ref), channel_id=1, source_target_pairs={{0,2},{1,3},{2,0},{3,1},{4,6},{5,7},{6,4},{7,5},{8,10},{9,11},{10,... | collective-permute-start | bytes 491528 | tf_op jit(solution)/shard_map/ppermute | solution.py:309
  79.6 18.9 %collective-permute-start.13 = (bf16[160,512]{1,0:T(8,128)(2,1)S(1)}, bf16[160,512]{1,0:T(8,128)(2,1)S(1)}, u32[]{:S(2)}, u32[]{:S(2)}) collective-permute-start(bf16[160,512]{1,0:T(8,128)(2,1)S(1)} %fusion.11.own_ref), channel_id=1, source_target_pairs={{0,1},{1,0},{2,3},{3,2},{4,5},{5,4},{6,7},{7,6},{8,9},{9,8},{10,11... | collective-permute-start | bytes 491528 | tf_op jit(solution)/shard_map/ppermute | solution.py:306
  86.4 14.0 %collective-permute-start.12 = (bf16[160,512]{1,0:T(8,128)(2,1)S(1)}, bf16[160,512]{1,0:T(8,128)(2,1)S(1)}, u32[]{:S(2)}, u32[]{:S(2)}) collective-permute-start(bf16[160,512]{1,0:T(8,128)(2,1)S(1)} %fusion.11.own_ref), channel_id=1, source_target_pairs={{0,2},{1,3},{2,0},{3,1},{4,6},{5,7},{6,4},{7,5},{8,10},{9,11},{10,... | collective-permute-start | bytes 491528 | tf_op jit(solution)/shard_map/ppermute | solution.py:309
  93.4 10.5 %collective-permute-start.7 = (bf16[160,512]{1,0:T(8,128)(2,1)S(1)}, bf16[160,512]{1,0:T(8,128)(2,1)S(1)}, u32[]{:S(2)}, u32[]{:S(2)}) collective-permute-start(bf16[160,512]{1,0:T(8,128)(2,1)S(1)} %fusion.13.own_ref), channel_id=1, source_target_pairs={{0,2},{1,3},{2,0},{3,1},{4,6},{5,7},{6,4},{7,5},{8,10},{9,11},{10,... | collective-permute-start | bytes 491528 | tf_op jit(solution)/shard_map/ppermute | solution.py:309
  95.1 16.0 %collective-permute-start.8 = (bf16[160,512]{1,0:T(8,128)(2,1)S(1)}, bf16[160,512]{1,0:T(8,128)(2,1)S(1)}, u32[]{:S(2)}, u32[]{:S(2)}) collective-permute-start(bf16[160,512]{1,0:T(8,128)(2,1)S(1)} %fusion.13.own_ref), channel_id=1, source_target_pairs={{0,1},{1,0},{2,3},{3,2},{4,5},{5,4},{6,7},{7,6},{8,9},{9,8},{10,11... | collective-permute-start | bytes 491528 | tf_op jit(solution)/shard_map/ppermute | solution.py:306
  96.9 9.6 %collective-permute-start.2 = (bf16[160,512]{1,0:T(8,128)(2,1)S(1)}, bf16[160,512]{1,0:T(8,128)(2,1)S(1)}, u32[]{:S(2)}, u32[]{:S(2)}) collective-permute-start(bf16[160,512]{1,0:T(8,128)(2,1)S(1)} %fusion.15.own_ref), channel_id=1, source_target_pairs={{0,2},{1,3},{2,0},{3,1},{4,6},{5,7},{6,4},{7,5},{8,10},{9,11},{10,... | collective-permute-start | bytes 491528 | tf_op jit(solution)/shard_map/ppermute | solution.py:309
  98.5 8.1 %collective-permute-start.19 = (bf16[160,512]{1,0:T(8,128)(2,1)S(1)}, bf16[160,512]{1,0:T(8,128)(2,1)S(1)}, u32[]{:S(2)}, u32[]{:S(2)}) collective-permute-start(bf16[160,512]{1,0:T(8,128)(2,1)S(1)} %collective-permute-done.17.across_ref), channel_id=1, source_target_pairs={{0,1},{1,0},{2,3},{3,2},{4,5},{5,4},{6,7},{7,6},{8,9},{9,8},{10,11... | collective-permute-start | bytes 491528 | tf_op jit(solution)/shard_map/ppermute | solution.py:306
  100.4 8.7 %collective-permute-start.14 = (bf16[160,512]{1,0:T(8,128)(2,1)S(1)}, bf16[160,512]{1,0:T(8,128)(2,1)S(1)}, u32[]{:S(2)}, u32[]{:S(2)}) collective-permute-start(bf16[160,512]{1,0:T(8,128)(2,1)S(1)} %collective-permute-done.12.across_ref), channel_id=1, source_target_pairs={{0,1},{1,0},{2,3},{3,2},{4,5},{5,4},{6,7},{7,6},{8,9},{9,8},{10,11... | collective-permute-start | bytes 491528 | tf_op jit(solution)/shard_map/ppermute | solution.py:306
  104.0 7.2 %collective-permute-start.9 = (bf16[160,512]{1,0:T(8,128)(2,1)S(1)}, bf16[160,512]{1,0:T(8,128)(2,1)S(1)}, u32[]{:S(2)}, u32[]{:S(2)}) collective-permute-start(bf16[160,512]{1,0:T(8,128)(2,1)S(1)} %collective-permute-done.7.across_ref), channel_id=1, source_target_pairs={{0,1},{1,0},{2,3},{3,2},{4,5},{5,4},{6,7},{7,6},{8,9},{9,8},{10,11... | collective-permute-start | bytes 491528 | tf_op jit(solution)/shard_map/ppermute | solution.py:306
  106.5 6.7 %collective-permute-start.3 = (bf16[160,512]{1,0:T(8,128)(2,1)S(1)}, bf16[160,512]{1,0:T(8,128)(2,1)S(1)}, u32[]{:S(2)}, u32[]{:S(2)}) collective-permute-start(bf16[160,512]{1,0:T(8,128)(2,1)S(1)} %fusion.15.own_ref), channel_id=1, source_target_pairs={{0,1},{1,0},{2,3},{3,2},{4,5},{5,4},{6,7},{7,6},{8,9},{9,8},{10,11... | collective-permute-start | bytes 491528 | tf_op jit(solution)/shard_map/ppermute | solution.py:306
  106.5 6.7 %collective-permute-start.4 = (bf16[160,512]{1,0:T(8,128)(2,1)S(1)}, bf16[160,512]{1,0:T(8,128)(2,1)S(1)}, u32[]{:S(2)}, u32[]{:S(2)}) collective-permute-start(bf16[160,512]{1,0:T(8,128)(2,1)S(1)} %collective-permute-done.2.across_ref), channel_id=1, source_target_pairs={{0,1},{1,0},{2,3},{3,2},{4,5},{5,4},{6,7},{7,6},{8,9},{9,8},{10,11... | collective-permute-start | bytes 491528 | tf_op jit(solution)/shard_map/ppermute | solution.py:306
  116.3 41.9 %all-to-all-start.1 = ((bf16[8,160,256]{2,1,0:T(8,128)(2,1)}), bf16[8,160,256]{2,1,0:T(8,128)(2,1)S(1)}, u32[]{:S(2)}, u32[]{:S(2)}) async-start(bf16[8,160,256]{2,1,0:T(8,128)(2,1)} %pack.1), calls=%async_computation.1 | async-start | bytes 1310720 | tf_op jit(solution)/shard_map/all_to_all | solution.py:358
  165.3 1.8 collective-permute-start.22
  165.4 3.7 %collective-permute-start.21 = (f32[8,128]{1,0:T(8,128)S(1)}, f32[8,128]{1,0:T(8,128)S(1)}, u32[]{:S(2)}, u32[]{:S(2)}) collective-permute-start(f32[8,128]{1,0:T(8,128)S(1)} %get-tuple-element.48), channel_id=1, source_target_pairs={{0,2},{1,3},{2,0},{3,1},{4,6},{5,7},{6,4},{7,5},{8,10},{9,11},{10,... | collective-permute-start | bytes 12296 | tf_op jit(solution)/shard_map/ppermute | solution.py:371
  167.0 3.0 %collective-permute-start.20 = (f32[8,128]{1,0:T(8,128)S(1)}, f32[8,128]{1,0:T(8,128)S(1)}, u32[]{:S(2)}, u32[]{:S(2)}) collective-permute-start(f32[8,128]{1,0:T(8,128)S(1)} %get-tuple-element.48), channel_id=1, source_target_pairs={{0,1},{1,2},{2,3},{3,0},{4,5},{5,6},{6,7},{7,4},{8,9},{9,10},{10,1... | collective-permute-start | bytes 12296 | tf_op jit(solution)/shard_map/ppermute | solution.py:371
  170.0 3.6 %collective-permute-start.23 = (f32[8,128]{1,0:T(8,128)S(1)}, f32[8,128]{1,0:T(8,128)S(1)}, u32[]{:S(2)}, u32[]{:S(2)}) collective-permute-start(f32[8,128]{1,0:T(8,128)S(1)} %add_add_fusion.1), channel_id=1, source_target_pairs={{0,4},{4,0},{1,5},{5,1},{2,6},{6,2},{3,7},{7,3},{8,12},{12,8},{9,1... | collective-permute-start | bytes 12296 | tf_op jit(solution)/shard_map/ppermute | solution.py:371
  173.6 3.6 %collective-permute-start.26 = (f32[8,128]{1,0:T(8,128)S(1)}, f32[8,128]{1,0:T(8,128)S(1)}, u32[]{:S(2)}, u32[]{:S(2)}) collective-permute-start(f32[8,128]{1,0:T(8,128)S(1)} %add.77), channel_id=1, source_target_pairs={{0,24},{8,0},{16,8},{24,16},{1,25},{9,1},{17,9},{25,17},{2,26},{10... | collective-permute-start | bytes 12296 | tf_op jit(solution)/shard_map/ppermute | solution.py:371
  174.2 4.5 %collective-permute-start.25 = (f32[8,128]{1,0:T(8,128)S(1)}, f32[8,128]{1,0:T(8,128)S(1)}, u32[]{:S(2)}, u32[]{:S(2)}) collective-permute-start(f32[8,128]{1,0:T(8,128)S(1)} %add.77), channel_id=1, source_target_pairs={{0,16},{8,24},{16,0},{24,8},{1,17},{9,25},{17,1},{25,9},{2,18},{10... | collective-permute-start | bytes 12296 | tf_op jit(solution)/shard_map/ppermute | solution.py:371
  174.2 5.5 %collective-permute-start.24 = (f32[8,128]{1,0:T(8,128)S(1)}, f32[8,128]{1,0:T(8,128)S(1)}, u32[]{:S(2)}, u32[]{:S(2)}) collective-permute-start(f32[8,128]{1,0:T(8,128)S(1)} %add.77), channel_id=1, source_target_pairs={{0,8},{8,16},{16,24},{24,0},{1,9},{9,17},{17,25},{25,1},{2,10},{10... | collective-permute-start | bytes 12296 | tf_op jit(solution)/shard_map/ppermute | solution.py:371
  (7 other events, 64.3 us)

commit v2 on v1

--- a/solution.py
+++ b/solution.py
@@ -10,12 +10,12 @@
 E = 8
 ITERS = 2
 CAP = 40
-CHUNKS = 4
 
 
 ridge_share = 0.25
 top_precision = lax.Precision.HIGHEST
 MIB = 1024 * 1024
+LIGHT = pl.CostEstimate(flops=1, bytes_accessed=1, transcendentals=0)
 f32 = jnp.float32
 bf16 = jnp.bfloat16
 NT = (((1,), (1,)), ((), ()))
@@ -66,24 +66,30 @@
     return ranked_first, ranked_second
 
 
-def pick_kernel(parts, tensor_count, own_ref, info_ref, tokens_ref, out_ref):
+def pick_kernel(parts, tensor_count, place_ref, info_ref, tokens_ref, *out_refs):
     first, second = info_ref[0:1, :], info_ref[1:2, :]
     rank_first, rank_second = block_slots(first, second)
-    own = own_ref[0]
     count = first.shape[1]
     rows = lax.broadcasted_iota(jnp.int32, (CAP, count), 0).astype(f32)
     values = tokens_ref[...]
-    for part in range(parts):
-        expert = (part * tensor_count + own).astype(f32)
+    for shift, out_ref in enumerate(out_refs):
+        expert = (lax.rem(place_ref[0] + shift, parts) * tensor_count + place_ref[1]).astype(f32)
         hit = ((first == expert) & (rank_first == rows)) | ((second == expert) & (rank_second == rows))
-        out_ref[part] = mm(hit.astype(f32).astype(bf16), values).astype(bf16)
-
-
-def gate_up_kernel(order_ref, inputs_ref, gate_ref, up_ref, send_ref, keep_ref):
+        out_ref[...] = mm(hit.astype(f32).astype(bf16), values).astype(bf16)
+
+
+def turn_kernel(*refs):
+    pieces = refs[: (len(refs) - 1) // 2]
+    rows = jnp.concatenate([ref[...].astype(f32) for ref in pieces], axis=0)
+    refs[-1][...] = rows.T.astype(bf16)
+
+
+def gate_up_kernel(order_ref, inputs_ref, gate_ref, up_ref, *rest):
+    send_ref, keep_ref = rest[-2:]
     step = pl.program_id(0)
     values = inputs_ref[...]
-    gate = mm(values, gate_ref[...], NT).astype(bf16)
-    up = mm(values, up_ref[...], NT).astype(bf16)
+    gate = mm(gate_ref[...], values).T.astype(bf16)
+    up = mm(up_ref[...], values).T.astype(bf16)
 
     @pl.when(step < 2)
     def _():
@@ -96,9 +102,12 @@
         keep_ref[0, 1] = up
 
 
-def gate_up(order, inputs, gate_weight, up_weight, chunk, width):
-    slots, depth = inputs.shape
-    weight_spec = pl.BlockSpec((width, depth), lambda s, order: (order[s] * CHUNKS + chunk, 0))
+def gate_up(order, inputs, gate_weight, up_weight, width, at, after):
+    depth, slots = inputs.shape
+    quarter = gate_weight.shape[0] // 4
+    gate_weight = gate_weight.reshape(4, quarter, depth)
+    up_weight = up_weight.reshape(4, quarter, depth)
+    weight_spec = pl.BlockSpec((None, width, depth), lambda s, order: (order[s], at // width, 0))
     shape = jax.ShapeDtypeStruct((2, 2, slots, width), bf16)
     return pl.pallas_call(
         gate_up_kernel,
@@ -106,76 +115,71 @@
             num_scalar_prefetch=1,
             grid=(4,),
             in_specs=[
-                pl.BlockSpec((slots, depth), lambda s, order: (0, 0)),
+                pl.BlockSpec((depth, slots), lambda s, order: (0, 0)),
                 weight_spec,
                 weight_spec,
-            ],
+            ]
+            + [pl.BlockSpec(memory_space=pl.ANY)] * len(after),
             out_specs=[
                 pl.BlockSpec((1, 2, slots, width), lambda s, order: (jnp.minimum(s, 1), 0, 0, 0)),
                 pl.BlockSpec((1, 2, slots, width), lambda s, order: (jnp.maximum(s - 2, 0), 0, 0, 0)),
             ],
         ),
         out_shape=[shape, shape],
-        compiler_params=params(20),
-        cost_estimate=pl.CostEstimate(
-            flops=16 * slots * depth * width, bytes_accessed=16 * width * depth, transcendentals=0
-        ),
-        name=f"gate_up_{chunk}",
-    )(order, inputs, gate_weight, up_weight)
+        compiler_params=params(41),
+        cost_estimate=LIGHT,
+        name=f"gate_up_{at}",
+    )(order, inputs, gate_weight, up_weight, *after)
 
 
 def down_kernel(order_ref, own_ref, across_ref, beside_ref, both_ref, down_ref, *rest):
-    refs = (own_ref, across_ref, beside_ref, both_ref)
-    if len(rest) == 4:
-        old_out_ref, old_gram_ref, out_ref, gram_ref = rest
-    else:
-        out_ref, gram_ref = rest
-    for step, ref in enumerate(refs):
-
-        @pl.when(pl.program_id(0) == step)
-        def _(step=step, ref=ref):
+    pieces = (own_ref, across_ref, beside_ref, both_ref)
+    old, new = rest[:-3], rest[-3:]
+    step = pl.program_id(0)
+
+    @pl.when(step == 0)
+    def _():
+        for index, ref in enumerate(new):
+            ref[...] = old[index][...] if old else jnp.zeros_like(ref)
+
+    out_ref, gram_ref, square_ref = new
+    weight = down_ref[...]
+    wide = weight.astype(f32)
+    square_ref[...] += jnp.sum((wide * wide).reshape(-1, 8, wide.shape[1]), axis=0)
+    for index, ref in enumerate(pieces):
+
+        @pl.when(step == index)
+        def _(ref=ref):
             values = ref[...]
-            out = mm(values, down_ref[...])
-            gram = mm(values, values, NT)
-            if step:
-                out_ref[...] += out
-                gram_ref[...] += gram
-            elif len(rest) == 4:
-                out_ref[...] = old_out_ref[...] + out
-                gram_ref[...] = old_gram_ref[...] + gram
-            else:
-                out_ref[...] = out
-                gram_ref[...] = gram
-
-
-def down(order, pieces, down_weight, chunk, older):
+            out_ref[...] += mm(values, weight)
+            gram_ref[...] += mm(values, values, NT)
+
+
+def down(order, pieces, down_weight, at, older):
     slots, width = pieces[0].shape
     columns = down_weight.shape[1]
+    down_weight = down_weight.reshape(4, -1, columns)
 
     def fixed(shape):
         return pl.BlockSpec(shape, lambda s, order: (0,) * len(shape))
 
+    shapes = [(slots, columns), (slots, slots), (8, columns)]
     return pl.pallas_call(
         down_kernel,
         grid_spec=pltpu.PrefetchScalarGridSpec(
             num_scalar_prefetch=1,
             grid=(4,),
             in_specs=[fixed((slots, width))] * 4
-            + [pl.BlockSpec((width, columns), lambda s, order: (order[s] * CHUNKS + chunk, 0))]
+            + [
+                pl.BlockSpec((None, width, columns), lambda s, order: (order[s], at // width, 0))
+            ]
             + [fixed(value.shape) for value in older],
-            out_specs=[fixed((slots, columns)), fixed((slots, slots))],
+            out_specs=[fixed(shape) for shape in shapes],
         ),
-        out_shape=[
-            jax.ShapeDtypeStruct((slots, columns), f32),
-            jax.ShapeDtypeStruct((slots, slots), f32),
-        ],
+        out_shape=[jax.ShapeDtypeStruct(shape, f32) for shape in shapes],
         compiler_params=params(20),
-        cost_estimate=pl.CostEstimate(
-            flops=8 * slots * width * (columns + slots),
-            bytes_accessed=8 * width * columns,
-            transcendentals=0,
-        ),
-        name=f"down_{chunk}",
+        cost_estimate=LIGHT,
+        name=f"down_{at}",
     )(order, *pieces, down_weight, *older)
 
 
@@ -187,7 +191,11 @@
         packed_ref[part] = jnp.concatenate([gram, piece], axis=1).astype(bf16)
 
 
-def route_kernel(blocks, kept_ref, info_ref, hot_ref, gates_ref):
+def route_kernel(blocks, tensor_count, kept_ref, place_ref, *refs):
+    infos = refs[:blocks]
+    hot_ref, turned_ref, gates_ref, info_ref, wide_ref = refs[blocks:]
+    for shift in range(blocks):
+        info_ref[lax.rem(place_ref[0] + blocks - shift, blocks)] = infos[shift][...]
     count = info_ref.shape[2]
     slots = blocks * CAP
     zero = jnp.zeros((CAP, count), f32)
@@ -199,9 +207,9 @@
         share_second = 1.0 / (1.0 + jnp.exp(-delta))
         rank_first, rank_second = block_slots(first, second)
         for expert in range(E):
-            kept = jnp.zeros((), jnp.bool_)
-            for place in range(kept_ref.shape[0]):
-                kept = kept | (kept_ref[place] == expert)
+            kept = jnp.zeros((), jnp.int32)
+            for index in range(kept_ref.shape[0]):
+                kept = kept | (kept_ref[index] == expert).astype(jnp.int32)
             kept = kept.astype(f32)
             hit_first = (first == expert) & (rank_first == rows)
             hit_second = (second == expert) & (rank_second == rows)
@@ -210,20 +218,23 @@
                 axis=1,
                 keepdims=True,
             )
-            hot = (hit_first | hit_second).astype(f32)
-            row = expert * slots + block * CAP
+            row = expert * slots + (expert // tensor_count - block) % blocks * CAP
             for other in range(blocks):
-                hot_ref[row : row + CAP, other * count : (other + 1) * count] = hot if other == block else zero
+                wide_ref[row : row + CAP, other * count : (other + 1) * count] = (
+                    (hit_first | hit_second).astype(f32) if other == block else zero
+                )
             gates_ref[row : row + CAP, 0:1] = gate * kept
             gates_ref[row : row + CAP, 1:2] = gate * (1.0 - kept)
-
-
-def solve_kernel(ridge, slots, packed_ref, hot_ref, gates_ref, square_ref, base_ref, zero_ref, one_ref, sums_ref):
-    hot = hot_ref[...].astype(bf16)
+    hot_ref[...] = wide_ref[...].astype(bf16)
+    turned_ref[...] = wide_ref[...].T.astype(bf16)
+
+
+def solve_kernel(ridge, slots, own_ref, packed_ref, hot_ref, turned_ref, gates_ref, square_ref, base_ref, zero_ref, one_ref, sums_ref):
+    hot, turned = hot_ref[...], turned_ref[...]
     kept, dropped = gates_ref[:, 0:1], gates_ref[:, 1:2]
     values = jnp.concatenate([packed_ref[e][:, slots:].astype(f32) for e in range(E)], axis=0)
-    base = mm_wide(hot, dropped * values, TN)
-    output = mm_wide(hot, kept * values, TN)
+    base = mm_wide(turned, dropped * values)
+    output = mm_wide(turned, kept * values)
 
     def apply(field):
         spread = kept * mm_wide(hot, field)
@@ -234,7 +245,7 @@
             ],
             axis=0,
         )
-        return mm_wide(hot, kept * mixed, TN)
+        return mm_wide(turned, kept * mixed)
 
     curved = apply(base)
     zero = curved - ridge * output
@@ -242,19 +253,20 @@
     base_ref[...] = base
     zero_ref[...] = zero
     one_ref[...] = one
-    norm = jnp.sum(base * curved) - 2.0 * ridge * jnp.sum(base * output)
-    sums_ref[0:1, :] = jnp.full((1, sums_ref.shape[1]), norm, f32) + ridge * ridge * square_ref[0]
-    sums_ref[1:2, :] = jnp.full((1, sums_ref.shape[1]), jnp.sum(zero * zero), f32)
-    sums_ref[2:3, :] = jnp.full((1, sums_ref.shape[1]), jnp.sum(zero * one), f32)
-    sums_ref[3:4, :] = jnp.full((1, sums_ref.shape[1]), jnp.sum(one * one), f32)
-    sums_ref[4:8, :] = jnp.zeros((4, sums_ref.shape[1]), f32)
+    norm = jnp.sum(base * (curved - 2.0 * ridge * output))
+    square = jnp.sum(square_ref[...]) * own_ref[0]
+    lane = lax.broadcasted_iota(jnp.int32, sums_ref.shape[1:], 1)
+    sums = jnp.where(lane == 0, norm + ridge * ridge * square, 0.0)
+    for index, value in enumerate((jnp.sum(zero * zero), jnp.sum(zero * one), jnp.sum(one * one))):
+        sums = jnp.where(lane == index + 1, value, sums)
+    for part in range(sums_ref.shape[0]):
+        sums_ref[part] = sums
 
 
 def finish_kernel(ridge, blocks, copies, base_ref, zero_ref, one_ref, sums_ref, out_ref):
-    norm = sums_ref[0:1, 0:1]
-    zero_zero = sums_ref[1:2, 0:1]
-    zero_one = sums_ref[2:3, 0:1]
-    one_one = sums_ref[3:4, 0:1]
+    sums = jnp.sum(sums_ref[...], axis=0)[0:1, :]
+    norm, zero_zero = sums[:, 0:1], sums[:, 1:2]
+    zero_one, one_one = sums[:, 2:3], sums[:, 3:4]
     step = norm / (zero_zero + ridge * norm)
     left = 1.0 - step * ridge
     new = left * left * norm - 2.0 * left * step * zero_zero + step * step * zero_one
@@ -264,26 +276,27 @@
     later = new / (image + ridge * (new + ratio * ratio * norm))
     field = base_ref[...] - (step + later * grown) * zero_ref[...] + (later * step) * one_ref[...]
     rows = field.shape[0] // blocks
+    turned = field.T.astype(bf16)
     for block in range(blocks):
-        piece = field[block * rows : (block + 1) * rows].astype(bf16)
         for copy in range(copies):
-            out_ref[block * copies + copy] = piece
+            out_ref[block * copies + copy] = turned[:, block * rows : (block + 1) * rows]
 
 
 def join_kernel(pieces_ref, out_ref):
-    out_ref[...] = jnp.concatenate(
-        [pieces_ref[part].astype(f32) for part in range(pieces_ref.shape[0])], axis=1
-    )
-
-
-def single(kernel, out_shape, in_specs, mib, name):
+    rows = jnp.concatenate([pieces_ref[part].astype(f32) for part in range(pieces_ref.shape[0])], axis=0)
+    out_ref[...] = rows.T
+
+
+def single(kernel, out_shape, in_specs, mib, name, scratch=()):
     many = isinstance(out_shape, list)
     return pl.pallas_call(
         kernel,
         out_shape=out_shape,
         in_specs=in_specs,
         out_specs=[whole()] * len(out_shape) if many else whole(),
+        scratch_shapes=list(scratch),
         compiler_params=params(mib),
+        cost_estimate=LIGHT,
         name=name,
     )
 
@@ -296,11 +309,13 @@
     units, columns = down_weight.shape
     slots = dp_count * CAP
     lanes = columns // parts
-    width = units // 4 // CHUNKS
+    eighth = units // 32
     ridge = ridge_share * 2.0 * tok_rows * dp_count / E
+    dp_index = lax.axis_index("dp")
     tensor_index = lax.axis_index("tensor")
     col_index = lax.axis_index("col")
-    own_expert = lax.axis_index("dp") * tensor_count + tensor_index
+    own_expert = dp_index * tensor_count + tensor_index
+    place = jnp.stack([dp_index, tensor_index])
 
     def beside(values):
         return lax.ppermute(values, "col", [(k, k ^ 1) for k in range(4)])
@@ -308,45 +323,68 @@
     def across(values):
         return lax.ppermute(values, "col", [(k, k ^ 2) for k in range(4)])
 
+    def ahead(values, shift):
+        if shift == 0:
+            return values
+        return lax.ppermute(values, "dp", [(k, (k + shift) % dp_count) for k in range(dp_count)])
+
     info = jnp.concatenate([routes.astype(f32).T, route_logits.T], axis=0)
-    all_info = lax.all_gather(info, "dp")
-    hot, gates = single(
-        functools.partial(route_kernel, dp_count),
-        [
-            jax.ShapeDtypeStruct((E * slots, dp_count * tok_rows), f32),
-            jax.ShapeDtypeStruct((E * slots, 2), f32),
-        ],
-        [scalars(), whole()],
-        16,
-        "route",
-    )(kept_experts, all_info)
-
     picked = single(
         functools.partial(pick_kernel, dp_count, tensor_count),
-        jax.ShapeDtypeStruct((dp_count, CAP, depth), bf16),
+        [jax.ShapeDtypeStruct((CAP, depth), bf16)] * dp_count,
         [scalars(), whole(), whole()],
         16,
         "pick",
-    )(tensor_index.reshape(1), info, tokens)
-    arrived = lax.all_to_all(picked, "dp", split_axis=0, concat_axis=0, tiled=True)
-    inputs = arrived.reshape(slots, depth)
+    )(place, info, tokens)
+    arrived = [ahead(value, shift) for shift, value in enumerate(picked)]
+    infos = [ahead(info, shift) for shift in range(dp_count)]
+    inputs = single(
+        turn_kernel,
+        jax.ShapeDtypeStruct((depth, slots), bf16),
+        [whole()] * dp_count + [pl.BlockSpec(memory_space=pl.ANY)] * dp_count,
+        16,
+        "turn",
+    )(*arrived, *infos)
+    total_slots, total_tokens = E * slots, dp_count * tok_rows
+    hot, turned, gates = single(
+        functools.partial(route_kernel, dp_count, tensor_count),
+        [
+            jax.ShapeDtypeStruct((total_slots, total_tokens), bf16),
+            jax.ShapeDtypeStruct((total_tokens, total_slots), bf16),
+            jax.ShapeDtypeStruct((total_slots, 2), f32),
+        ],
+        [scalars(), scalars()] + [whole()] * dp_count,
+        24,
+        "route",
+        [pltpu.VMEM((dp_count,) + info.shape, f32), pltpu.VMEM((total_slots, total_tokens), f32)],
+    )(kept_experts, place, *infos)
 
     gate_order = col_index ^ jnp.array([3, 1, 2, 0], jnp.int32)
     down_order = col_index ^ jnp.array([0, 2, 1, 3], jnp.int32)
-    older = ()
-    for chunk in range(CHUNKS):
-        send, keep = gate_up(gate_order, inputs, gate_weight, up_weight, chunk, width)
+    plan = [(width * eighth, at * eighth) for width, at in ((1, 6), (2, 0), (2, 2), (2, 4), (1, 7))]
+    last = len(plan) - 1
+    keeps, pairs, sent = [], [], []
+    for chunk, (width, at) in enumerate(plan):
+        after = [pairs[chunk - 2], keeps[chunk - 1][0]] if chunk >= 2 else []
+        send, keep = gate_up(gate_order, inputs, gate_weight, up_weight, width, at, after)
         near = beside(send)
-        pair = keep.astype(f32) + near.astype(f32)
-        far = across(pair[0].astype(bf16))
-        total = pair[1] + far.astype(f32)
+        pairs.append((keep[0].astype(f32) + near[0].astype(f32)).astype(bf16))
+        sent.append(across(pairs[-1]))
+        keeps.append((keep, near))
+    older, olders = (), []
+    for chunk, (width, at) in enumerate(plan):
+        first = [pairs[last]]
+        if chunk == 1:
+            first.append(gates)
+        if chunk >= 2:
+            first.append(olders[chunk - 2][2])
+        far = lax.optimization_barrier((sent[chunk], *first))[0]
+        keep, near = keeps[chunk]
+        total = keep[1].astype(f32) + near[1].astype(f32) + far.astype(f32)
         own = (jax.nn.silu(total[0]) * total[1]).astype(bf16)
         other = across(own)
-        older = down(down_order, (own, other, beside(own), beside(other)), down_weight, chunk, older)
-
-    is_kept = jnp.any(kept_experts == own_expert).astype(f32)
-    wide_down = down_weight.astype(f32)
-    square = (is_kept * jnp.sum(wide_down * wide_down)).reshape(1)
+        older = down(down_order, (own, other, beside(own), beside(other)), down_weight, at, older)
+        olders.append(older)
 
     packed = single(
         functools.partial(pack_kernel, parts),
@@ -354,29 +392,24 @@
         [whole(), whole()],
         16,
         "pack",
-    )(*older)
+    )(*older[:2])
     spread = lax.all_to_all(packed, ("dp", "tensor"), split_axis=0, concat_axis=0, tiled=True)
 
-    field = jax.ShapeDtypeStruct((dp_count * tok_rows, lanes), f32)
+    everyone = parts * lax.axis_size("col")
+    is_kept = jnp.any(kept_experts == own_expert).astype(f32).reshape(1)
+    field = jax.ShapeDtypeStruct((total_tokens, lanes), f32)
     base, zero, one, sums = single(
         functools.partial(solve_kernel, ridge, slots),
-        [field, field, field, jax.ShapeDtypeStruct((8, 128), f32)],
-        [whole(), whole(), whole(), scalars()],
+        [field, field, field, jax.ShapeDtypeStruct((everyone, 1, 128), f32)],
+        [scalars()] + [whole()] * 5,
         40,
         "solve",
-    )(spread, hot, gates, square)
-
-    for axis, size in (("col", 4), ("tensor", tensor_count), ("dp", dp_count)):
-        shifted = [
-            lax.ppermute(sums, axis, [(k, (k + step) % size) for k in range(size)])
-            for step in range(1, size)
-        ]
-        for value in shifted:
-            sums = sums + value
+    )(is_kept, spread, hot, turned, gates, older[2])
+    sums = lax.all_to_all(sums, ("dp", "tensor", "col"), split_axis=0, concat_axis=0, tiled=True)
 
     home = single(
         functools.partial(finish_kernel, ridge, dp_count, tensor_count),
-        jax.ShapeDtypeStruct((parts, tok_rows, lanes), bf16),
+        jax.ShapeDtypeStruct((parts, lanes, tok_rows), bf16),
         [whole()] * 4,
         16,
         "finish",

time: 194 us -> 168 us (0.87)
  blocking collectives: 34.6 us -> 21.3 us
  other arithmetic: 15.2 us -> 3.96 us
  Pallas kernels: 46.9 us -> 57.5 us
  local copies, waits for them, and re-layouts: 11.6 us -> 2.12 us
  waiting for transfers between devices: 55.1 us -> 49.7 us
  starting transfers between devices: 28 us -> 31.7 us
    all_gather x1 -> x0, blocking collectives: 22.7 us -> none  [one_expert_each(): all_info = lax.all_gather(info, 'dp')]
    all_to_all x1, waiting for transfers between devices: 0.01 us -> 16.7 us  [one_expert_each(): lax.all_to_all(packed, ('dp', 'tensor'), split_axis=0, concat_axis=0, til...]
    all_to_all x1 -> x0, waiting for transfers between devices: 13.8 us -> none  [one_expert_each(): lax.all_to_all(picked, 'dp', split_axis=0, concat_axis=0, tiled=True)]
    reduce_sum x1 -> x0, other arithmetic: 11.7 us -> none  [one_expert_each(): square = (is_kept * jnp.sum(wide_down * wide_down)).reshape(1)]
    all_to_all x0 -> x1, blocking collectives: none -> 10.6 us  [one_expert_each(): lax.all_to_all(sums, ('dp', 'tensor', 'col'), split_axis=0, concat_axis=0...]
    unnamed x20 -> x16, local copies, waits for them, and re-layouts: 11.1 us -> 2.12 us
    pallas_call x4 -> x5, Pallas kernels: 28.2 us -> 36.6 us  [gate_up(): pl.pallas_call(gate_up_kernel, grid_spec=pltpu.PrefetchScalarGridSpec(num...]
    ppermute x8 -> x10, waiting for transfers between devices: 32.5 us -> 25.9 us  [across(): return lax.ppermute(values, 'col', [(k, k ^ 2) for k in range(4)])]
  transfers between devices with their start and end apart: 29 -> 32, of which waited for: 15 -> 12; matrix products, arithmetic and copies ran while one was open for 7% -> 1% of each run, Pallas kernels for 15% -> 21%
where the time goes in v2:
time: 168 us; the launch traced here: 167 us
  Pallas kernels  57.5 us (34%)
  waiting for transfers between devices  49.7 us (30%)
  starting transfers between devices  31.7 us (19%)
  blocking collectives  21.3 us (13%)
  other arithmetic  3.96 us (2%)
  local copies, waits for them, and re-layouts  2.12 us (1%)
    pallas_call x5, Pallas kernels, gate_up(): pl.pallas_call(gate_up_kernel, grid_spec=pltpu.PrefetchScalarGridSpec(num...  36.6 us
    ppermute x10, waiting for transfers between devices, across(): return lax.ppermute(values, 'col', [(k, k ^ 2) for k in range(4)])  25.9 us
    all_to_all x1, waiting for transfers between devices, one_expert_each(): lax.all_to_all(packed, ('dp', 'tensor'), split_axis=0, concat_axis=0, til...  16.7 us
    ppermute x10, starting transfers between devices, across(): return lax.ppermute(values, 'col', [(k, k ^ 2) for k in range(4)])  14.6 us
    ppermute x6, starting transfers between devices, ahead(): lax.ppermute(values, 'dp', [(k, (k + shift) % dp_count) for k in range(dp...  10.8 us
    all_to_all x1, blocking collectives, one_expert_each(): lax.all_to_all(home, ('dp', 'tensor'), split_axis=0, concat_axis=0, tiled...  10.7 us
    all_to_all x1, blocking collectives, one_expert_each(): lax.all_to_all(sums, ('dp', 'tensor', 'col'), split_axis=0, concat_axis=0...  10.6 us
    pallas_call x5, Pallas kernels, down(): pl.pallas_call(down_kernel, grid_spec=pltpu.PrefetchScalarGridSpec(num_sc...  10.5 us
  transfers between devices with their start and end apart: 32, of which 12 were waited for; matrix products, arithmetic and copies ran while one was open for 1% of the time, Pallas kernels for 21%

profile of v2, /device:TPU:0, one launch (start us, length us, event | category | flops | bytes accessed | tf_op | source)
XLA Modules:
  0.0 167.4 jit_solution(891860398092537422)
XLA Ops:
  1.4 3.0 %collective-permute-start.3 = (f32[4,128]{1,0:T(4,128)S(1)}, f32[4,128]{1,0:T(4,128)S(1)}, u32[]{:S(2)}, u32[]{:S(2)}) collective-permute-start(f32[4,128]{1,0:T(4,128)S(1)} %pad_maximum_fusion.info_ref.refs_4_.refs_0_), channel_id=1, source_target_pairs={{0,8},{8,16},{16,24},{24,0},{1,9},{9,17},{17,25},{25,1},{2,10},{10... | collective-permute-start | bytes 6152 | tf_op jit(solution)/shard_map/ppermute | solution.py:329
  4.4 2.6 %collective-permute-start.4 = (f32[4,128]{1,0:T(4,128)S(1)}, f32[4,128]{1,0:T(4,128)S(1)}, u32[]{:S(2)}, u32[]{:S(2)}) collective-permute-start(f32[4,128]{1,0:T(4,128)S(1)} %pad_maximum_fusion.info_ref.refs_4_.refs_0_), channel_id=1, source_target_pairs={{0,16},{8,24},{16,0},{24,8},{1,17},{9,25},{17,1},{25,9},{2,18},{10... | collective-permute-start | bytes 6152 | tf_op jit(solution)/shard_map/ppermute | solution.py:329
  11.5 2.8 %collective-permute-start.2 = (bf16[40,1536]{1,0:T(8,128)(2,1)S(1)}, bf16[40,1536]{1,0:T(8,128)(2,1)S(1)}, u32[]{:S(2)}, u32[]{:S(2)}) collective-permute-start(bf16[40,1536]{1,0:T(8,128)(2,1)S(1)} %get-tuple-element.49), channel_id=1, source_target_pairs={{0,24},{8,0},{16,8},{24,16},{1,25},{9,1},{17,9},{25,17},{2,26},{10... | collective-permute-start | bytes 368648 | tf_op jit(solution)/shard_map/ppermute | solution.py:329
  15.0 3.6 %collective-permute-done.refs_1_ = bf16[40,1536]{1,0:T(8,128)(2,1)S(1)} collective-permute-done((bf16[40,1536]{1,0:T(8,128)(2,1)S(1)}, bf16[40,1536]{1,0:T(8,128)(2,1)S(1)}, u32[]{:S(2)}, u32[]{:S(2)}) %collective-permute-start) | collective-permute-done | bytes 122912 | tf_op jit(solution)/shard_map/ppermute | solution.py:329
  18.6 3.4 %collective-permute-done.1.refs_2_ = bf16[40,1536]{1,0:T(8,128)(2,1)S(1)} collective-permute-done((bf16[40,1536]{1,0:T(8,128)(2,1)S(1)}, bf16[40,1536]{1,0:T(8,128)(2,1)S(1)}, u32[]{:S(2)}, u32[]{:S(2)}) %collective-permute-start.1) | collective-permute-done | bytes 122912 | tf_op jit(solution)/shard_map/ppermute | solution.py:329
  22.3 5.5 %gate_up_1536.1 = (bf16[2,2,160,256]{3,2,1,0:T(8,128)(2,1)S(1)}, bf16[2,2,160,256]{3,2,1,0:T(8,128)(2,1)S(1)}) custom-call(s32[4]{0:T(128)S(1)} %broadcast_xor_fusion.order_ref, bf16[1536,160]{1,0:T(8,128)(2,1)S(1)} %turn.1.inputs_ref, bf16[4,2048,1536]{2,1,0:T(8,128)(2,1)} %bitcast.86, bf16[4,2048,1536]{2,1,0:T(8,128)(2,1)} %bitcast.91), custom_call_target="tpu_custom_call" | custom-call | flops 1 | bytes 1 | tf_op jit(solution)/shard_map/gate_up_1536/pallas_call | solution.py:112
  27.9 7.9 %gate_up_0.1 = (bf16[2,2,160,512]{3,2,1,0:T(8,128)(2,1)S(1)}, bf16[2,2,160,512]{3,2,1,0:T(8,128)(2,1)S(1)}) custom-call(s32[4]{0:T(128)S(1)} %broadcast_xor_fusion.order_ref, bf16[1536,160]{1,0:T(8,128)(2,1)S(1)} %turn.1.inputs_ref, bf16[4,2048,1536]{2,1,0:T(8,128)(2,1)} %bitcast.87, bf16[4,2048,1536]{2,1,0:T(8,128)(2,1)} %bitcast.92), custom_call_target="tpu_custom_call" | custom-call | flops 1 | bytes 1 | tf_op jit(solution)/shard_map/gate_up_0/pallas_call | solution.py:112
  36.4 7.9 %gate_up_512.1 = (bf16[2,2,160,512]{3,2,1,0:T(8,128)(2,1)S(1)}, bf16[2,2,160,512]{3,2,1,0:T(8,128)(2,1)S(1)}) custom-call(s32[4]{0:T(128)S(1)} %broadcast_xor_fusion.order_ref, bf16[1536,160]{1,0:T(8,128)(2,1)S(1)} %turn.1.inputs_ref, bf16[4,2048,1536]{2,1,0:T(8,128)(2,1)} %bitcast.88, bf16[4,2048,1536]{2,1,0:T(8,128)(2,1)} %bitcast.93, ...), custom_call_target="tpu_custom_call" | custom-call | flops 1 | bytes 1 | tf_op jit(solution)/shard_map/gate_up_512/pallas_call | solution.py:112
  44.6 7.9 %gate_up_1024.1 = (bf16[2,2,160,512]{3,2,1,0:T(8,128)(2,1)S(1)}, bf16[2,2,160,512]{3,2,1,0:T(8,128)(2,1)S(1)}) custom-call(s32[4]{0:T(128)S(1)} %broadcast_xor_fusion.order_ref, bf16[1536,160]{1,0:T(8,128)(2,1)S(1)} %turn.1.inputs_ref, bf16[4,2048,1536]{2,1,0:T(8,128)(2,1)} %bitcast.89, bf16[4,2048,1536]{2,1,0:T(8,128)(2,1)} %bitcast.94, ...), custom_call_target="tpu_custom_call" | custom-call | flops 1 | bytes 1 | tf_op jit(solution)/shard_map/gate_up_1024/pallas_call | solution.py:112
  52.7 7.2 %gate_up_1792.1 = (bf16[2,2,160,256]{3,2,1,0:T(8,128)(2,1)S(1)}, bf16[2,2,160,256]{3,2,1,0:T(8,128)(2,1)S(1)}) custom-call(s32[4]{0:T(128)S(1)} %broadcast_xor_fusion.order_ref, bf16[1536,160]{1,0:T(8,128)(2,1)S(1)} %turn.1.inputs_ref, bf16[4,2048,1536]{2,1,0:T(8,128)(2,1)} %bitcast.90, bf16[4,2048,1536]{2,1,0:T(8,128)(2,1)} %bitcast.95, ...), custom_call_target="tpu_custom_call" | custom-call | flops 1 | bytes 1 | tf_op jit(solution)/shard_map/gate_up_1792/pallas_call | solution.py:112
  62.0 1.6 collective-permute-start.12
  65.6 3.5 %collective-permute-done.12 = bf16[2,160,256]{2,1,0:T(8,128)(2,1)S(1)} collective-permute-done((bf16[2,160,256]{2,1,0:T(8,128)(2,1)S(1)}, bf16[2,160,256]{2,1,0:T(8,128)(2,1)S(1)}, u32[]{:S(2)}, u32[]{:S(2)}) %collective-permute-start.12) | collective-permute-done | bytes 163872 | tf_op jit(solution)/shard_map/ppermute | solution.py:324
  69.2 1.6 collective-permute-start.13
  70.8 5.3 %collective-permute-done.19 = bf16[2,160,512]{2,1,0:T(8,128)(2,1)S(1)} collective-permute-done((bf16[2,160,512]{2,1,0:T(8,128)(2,1)S(1)}, bf16[2,160,512]{2,1,0:T(8,128)(2,1)S(1)}, u32[]{:S(2)}, u32[]{:S(2)}) %collective-permute-start.19) | collective-permute-done | bytes 327712 | tf_op jit(solution)/shard_map/ppermute | solution.py:324
  76.4 1.6 collective-permute-start.20
  77.9 7.0 %collective-permute-done.13.across_ref = bf16[160,256]{1,0:T(8,128)(2,1)S(1)} collective-permute-done((bf16[160,256]{1,0:T(8,128)(2,1)S(1)}, bf16[160,256]{1,0:T(8,128)(2,1)S(1)}, u32[]{:S(2)}, u32[]{:S(2)}) %collective-permute-start.13) | collective-permute-done | bytes 81952 | tf_op jit(solution)/shard_map/ppermute | solution.py:324
  85.0 1.6 collective-permute-start.27
  87.5 1.8 %down_1536.1 = (f32[160,768]{1,0:T(8,128)S(1)}, f32[160,160]{1,0:T(8,128)S(1)}, f32[8,768]{1,0:T(8,128)S(1)}) custom-call(s32[4]{0:T(128)S(1)} %broadcast_xor_fusion.1.order_ref, bf16[160,256]{1,0:T(8,128)(2,1)S(1)} %fusion.14.own_ref, bf16[160,256]{1,0:T(8,128)(2,1)S(1)} %collective-permute-done.13.across_ref, ...), custom_call_target="tpu_custom_call" | custom-call | flops 1 | bytes 1 | tf_op jit(solution)/shard_map/down_1536/pallas_call | solution.py:167
  91.2 2.3 %down_0.1 = (f32[160,768]{1,0:T(8,128)S(1)}, f32[160,160]{1,0:T(8,128)S(1)}, f32[8,768]{1,0:T(8,128)S(1)}) custom-call(s32[4]{0:T(128)S(1)} %broadcast_xor_fusion.1.order_ref, bf16[160,512]{1,0:T(8,128)(2,1)S(1)} %fusion.6.own_ref, bf16[160,512]{1,0:T(8,128)(2,1)S(1)} %collective-permute-done.20.across_ref, ...), custom_call_target="tpu_custom_call" | custom-call | flops 1 | bytes 1 | tf_op jit(solution)/shard_map/down_0/pallas_call | solution.py:167
  93.5 2.1 %collective-permute-done.27 = bf16[2,160,512]{2,1,0:T(8,128)(2,1)S(1)} collective-permute-done((bf16[2,160,512]{2,1,0:T(8,128)(2,1)S(1)}, bf16[2,160,512]{2,1,0:T(8,128)(2,1)S(1)}, u32[]{:S(2)}, u32[]{:S(2)}) %collective-permute-start.27) | collective-permute-done | bytes 327712 | tf_op jit(solution)/shard_map/ppermute | solution.py:324
  95.8 1.6 collective-permute-start.28
  97.4 1.7 %collective-permute-done.16.across_ref = bf16[160,512]{1,0:T(8,128)(2,1)S(1)} collective-permute-done((bf16[160,512]{1,0:T(8,128)(2,1)S(1)}, bf16[160,512]{1,0:T(8,128)(2,1)S(1)}, u32[]{:S(2)}, u32[]{:S(2)}) %collective-permute-start.16) | collective-permute-done | bytes 163872 | tf_op jit(solution)/shard_map/ppermute | solution.py:324
  102.2 2.3 %down_512.1 = (f32[160,768]{1,0:T(8,128)S(1)}, f32[160,160]{1,0:T(8,128)S(1)}, f32[8,768]{1,0:T(8,128)S(1)}) custom-call(s32[4]{0:T(128)S(1)} %broadcast_xor_fusion.1.order_ref, bf16[160,512]{1,0:T(8,128)(2,1)S(1)} %fusion.8.own_ref, bf16[160,512]{1,0:T(8,128)(2,1)S(1)} %collective-permute-done.16.across_ref, ...), custom_call_target="tpu_custom_call" | custom-call | flops 1 | bytes 1 | tf_op jit(solution)/shard_map/down_512/pallas_call | solution.py:167
  105.8 1.6 collective-permute-start.23
  107.4 2.9 %collective-permute-done.23.across_ref = bf16[160,256]{1,0:T(8,128)(2,1)S(1)} collective-permute-done((bf16[160,256]{1,0:T(8,128)(2,1)S(1)}, bf16[160,256]{1,0:T(8,128)(2,1)S(1)}, u32[]{:S(2)}, u32[]{:S(2)}) %collective-permute-start.23) | collective-permute-done | bytes 81952 | tf_op jit(solution)/shard_map/ppermute | solution.py:324
  110.4 2.3 %down_1024.1 = (f32[160,768]{1,0:T(8,128)S(1)}, f32[160,160]{1,0:T(8,128)S(1)}, f32[8,768]{1,0:T(8,128)S(1)}) custom-call(s32[4]{0:T(128)S(1)} %broadcast_xor_fusion.1.order_ref, bf16[160,512]{1,0:T(8,128)(2,1)S(1)} %fusion.4.own_ref, bf16[160,512]{1,0:T(8,128)(2,1)S(1)} %collective-permute-done.28.across_ref, ...), custom_call_target="tpu_custom_call" | custom-call | flops 1 | bytes 1 | tf_op jit(solution)/shard_map/down_1024/pallas_call | solution.py:167
  112.7 1.8 %down_1792.1 = (f32[160,768]{1,0:T(8,128)S(1)}, f32[160,160]{1,0:T(8,128)S(1)}, f32[8,768]{1,0:T(8,128)S(1)}) custom-call(s32[4]{0:T(128)S(1)} %broadcast_xor_fusion.1.order_ref, bf16[160,256]{1,0:T(8,128)(2,1)S(1)} %fusion.12.own_ref, bf16[160,256]{1,0:T(8,128)(2,1)S(1)} %collective-permute-done.23.across_ref, ...), custom_call_target="tpu_custom_call" | custom-call | flops 1 | bytes 1 | tf_op jit(solution)/shard_map/down_1792/pallas_call | solution.py:167
  115.5 4.7 %all-to-all-start = ((bf16[8,160,256]{2,1,0:T(8,128)(2,1)}), bf16[8,160,256]{2,1,0:T(8,128)(2,1)S(1)}, u32[]{:S(2)}, u32[]{:S(2)}) async-start(bf16[8,160,256]{2,1,0:T(8,128)(2,1)} %pack.1), calls=%async_computation | async-start | bytes 1310720 | tf_op jit(solution)/shard_map/all_to_all | solution.py:396
  121.6 16.7 %all-to-all-done.packed_ref = bf16[8,160,256]{2,1,0:T(8,128)(2,1)S(1)} async-done(((bf16[8,160,256]{2,1,0:T(8,128)(2,1)}), bf16[8,160,256]{2,1,0:T(8,128)(2,1)S(1)}, u32[]{:S(2)}, u32[]{:S(2)}) %all-to-all-start) | async-done | bytes 655392 | tf_op jit(solution)/shard_map/all_to_all | solution.py:396
  139.4 5.4 %solve.1 = (f32[512,96]{1,0:T(8,128)S(1)}, f32[512,96]{1,0:T(8,128)S(1)}, f32[512,96]{1,0:T(8,128)S(1)}, f32[32,1,128]{2,1,0:T(1,128)S(1)}) custom-call(f32[1]{0:T(128)} %bitcast.own_ref, bf16[8,160,256]{2,1,0:T(8,128)(2,1)S(1)} %all-to-all-done.packed_ref, bf16[1280,512]{1,0:T(8,128)(2,1)S(1)} %get-tuple-element.80.hot_ref, ...), custom_call_target="tpu_custom_call" | custom-call | flops 1 | bytes 1 | tf_op jit(solution)/shard_map/solve/pallas_call | solution.py:401
  144.8 10.6 %all_to_all.15.sums_ref = f32[32,1,128]{2,1,0:T(1,128)S(1)} all-to-all(f32[32,1,128]{2,1,0:T(1,128)S(1)} %get-tuple-element.86), channel_id=1, replica_groups=mesh['dp'=4,'tensor'=2,'col'=4] {'dp','tensor','col'}, dimensions={0} | all-to-all | bytes 32768 | tf_op jit(solution)/shard_map/all_to_all | solution.py:408
  155.8 10.7 %all_to_all.16.pieces_ref = bf16[8,96,128]{2,1,0:T(8,128)(2,1)S(1)} all-to-all(bf16[8,96,128]{2,1,0:T(8,128)(2,1)S(1)} %finish.1), channel_id=1, replica_groups=mesh['dp'=4,'tensor'=2,'col'=4] {'dp','tensor'}, dimensions={0} | all-to-all | bytes 393216 | tf_op jit(solution)/shard_map/all_to_all | solution.py:417
  (89 shorter events, 23.8 us)
Async XLA Ops:
  1.4 10.1 %collective-permute-start.3 = (f32[4,128]{1,0:T(4,128)S(1)}, f32[4,128]{1,0:T(4,128)S(1)}, u32[]{:S(2)}, u32[]{:S(2)}) collective-permute-start(f32[4,128]{1,0:T(4,128)S(1)} %pad_maximum_fusion.info_ref.refs_4_.refs_0_), channel_id=1, source_target_pairs={{0,8},{8,16},{16,24},{24,0},{1,9},{9,17},{17,25},{25,1},{2,10},{10... | collective-permute-start | bytes 6152 | tf_op jit(solution)/shard_map/ppermute | solution.py:329
  4.4 10.6 %collective-permute-start.4 = (f32[4,128]{1,0:T(4,128)S(1)}, f32[4,128]{1,0:T(4,128)S(1)}, u32[]{:S(2)}, u32[]{:S(2)}) collective-permute-start(f32[4,128]{1,0:T(4,128)S(1)} %pad_maximum_fusion.info_ref.refs_4_.refs_0_), channel_id=1, source_target_pairs={{0,16},{8,24},{16,0},{24,8},{1,17},{9,25},{17,1},{25,9},{2,18},{10... | collective-permute-start | bytes 6152 | tf_op jit(solution)/shard_map/ppermute | solution.py:329
  7.0 8.0 %collective-permute-start.5 = (f32[4,128]{1,0:T(4,128)S(1)}, f32[4,128]{1,0:T(4,128)S(1)}, u32[]{:S(2)}, u32[]{:S(2)}) collective-permute-start(f32[4,128]{1,0:T(4,128)S(1)} %pad_maximum_fusion.info_ref.refs_4_.refs_0_), channel_id=1, source_target_pairs={{0,24},{8,0},{16,8},{24,16},{1,25},{9,1},{17,9},{25,17},{2,26},{10... | collective-permute-start | bytes 6152 | tf_op jit(solution)/shard_map/ppermute | solution.py:329
  10.4 8.2 %collective-permute-start = (bf16[40,1536]{1,0:T(8,128)(2,1)S(1)}, bf16[40,1536]{1,0:T(8,128)(2,1)S(1)}, u32[]{:S(2)}, u32[]{:S(2)}) collective-permute-start(bf16[40,1536]{1,0:T(8,128)(2,1)S(1)} %get-tuple-element.47), channel_id=1, source_target_pairs={{0,8},{8,16},{16,24},{24,0},{1,9},{9,17},{17,25},{25,1},{2,10},{10... | collective-permute-start | bytes 368648 | tf_op jit(solution)/shard_map/ppermute | solution.py:329
  11.2 10.8 %collective-permute-start.1 = (bf16[40,1536]{1,0:T(8,128)(2,1)S(1)}, bf16[40,1536]{1,0:T(8,128)(2,1)S(1)}, u32[]{:S(2)}, u32[]{:S(2)}) collective-permute-start(bf16[40,1536]{1,0:T(8,128)(2,1)S(1)} %get-tuple-element.48), channel_id=1, source_target_pairs={{0,16},{8,24},{16,0},{24,8},{1,17},{9,25},{17,1},{25,9},{2,18},{10... | collective-permute-start | bytes 368648 | tf_op jit(solution)/shard_map/ppermute | solution.py:329
  11.5 10.5 %collective-permute-start.2 = (bf16[40,1536]{1,0:T(8,128)(2,1)S(1)}, bf16[40,1536]{1,0:T(8,128)(2,1)S(1)}, u32[]{:S(2)}, u32[]{:S(2)}) collective-permute-start(bf16[40,1536]{1,0:T(8,128)(2,1)S(1)} %get-tuple-element.49), channel_id=1, source_target_pairs={{0,24},{8,0},{16,8},{24,16},{1,25},{9,1},{17,9},{25,17},{2,26},{10... | collective-permute-start | bytes 368648 | tf_op jit(solution)/shard_map/ppermute | solution.py:329
  27.8 8.6 %collective-permute-start.6 = (bf16[2,2,160,256]{3,2,1,0:T(8,128)(2,1)S(1)}, bf16[2,2,160,256]{3,2,1,0:T(8,128)(2,1)S(1)}, u32[]{:S(2)}, u32[]{:S(2)}) collective-permute-start(bf16[2,2,160,256]{3,2,1,0:T(8,128)(2,1)S(1)} %get-tuple-element.51), channel_id=1, source_target_pairs={{0,1},{1,0},{2,3},{3,2},{4,5},{5,4},{6,7},{7,6},{8,9},{9,8},{10,11... | collective-permute-start | bytes 983048 | tf_op jit(solution)/shard_map/ppermute | solution.py:321
  35.8 8.6 %collective-permute-start.8 = (bf16[2,2,160,512]{3,2,1,0:T(8,128)(2,1)S(1)}, bf16[2,2,160,512]{3,2,1,0:T(8,128)(2,1)S(1)}, u32[]{:S(2)}, u32[]{:S(2)}) collective-permute-start(bf16[2,2,160,512]{3,2,1,0:T(8,128)(2,1)S(1)} %get-tuple-element.55), channel_id=1, source_target_pairs={{0,1},{1,0},{2,3},{3,2},{4,5},{5,4},{6,7},{7,6},{8,9},{9,8},{10,11... | collective-permute-start | bytes 1966088 | tf_op jit(solution)/shard_map/ppermute | solution.py:321
  44.4 8.1 %collective-permute-start.7 = (bf16[2,2,160,512]{3,2,1,0:T(8,128)(2,1)S(1)}, bf16[2,2,160,512]{3,2,1,0:T(8,128)(2,1)S(1)}, u32[]{:S(2)}, u32[]{:S(2)}) collective-permute-start(bf16[2,2,160,512]{3,2,1,0:T(8,128)(2,1)S(1)} %get-tuple-element.54), channel_id=1, source_target_pairs={{0,1},{1,0},{2,3},{3,2},{4,5},{5,4},{6,7},{7,6},{8,9},{9,8},{10,11... | collective-permute-start | bytes 1966088 | tf_op jit(solution)/shard_map/ppermute | solution.py:321
  59.9 5.7 %collective-permute-start.9 = (bf16[2,2,160,256]{3,2,1,0:T(8,128)(2,1)S(1)}, bf16[2,2,160,256]{3,2,1,0:T(8,128)(2,1)S(1)}, u32[]{:S(2)}, u32[]{:S(2)}) collective-permute-start(bf16[2,2,160,256]{3,2,1,0:T(8,128)(2,1)S(1)} %get-tuple-element.58), channel_id=1, source_target_pairs={{0,1},{1,0},{2,3},{3,2},{4,5},{5,4},{6,7},{7,6},{8,9},{9,8},{10,11... | collective-permute-start | bytes 983048 | tf_op jit(solution)/shard_map/ppermute | solution.py:321
  62.0 7.1 %collective-permute-start.12 = (bf16[2,160,256]{2,1,0:T(8,128)(2,1)S(1)}, bf16[2,160,256]{2,1,0:T(8,128)(2,1)S(1)}, u32[]{:S(2)}, u32[]{:S(2)}) collective-permute-start(bf16[2,160,256]{2,1,0:T(8,128)(2,1)S(1)} %fusion.9.rest_0_), channel_id=1, source_target_pairs={{0,2},{1,3},{2,0},{3,1},{4,6},{5,7},{6,4},{7,5},{8,10},{9,11},{10,... | collective-permute-start | bytes 491528 | tf_op jit(solution)/shard_map/ppermute | solution.py:324
  63.6 12.6 %collective-permute-start.19 = (bf16[2,160,512]{2,1,0:T(8,128)(2,1)S(1)}, bf16[2,160,512]{2,1,0:T(8,128)(2,1)S(1)}, u32[]{:S(2)}, u32[]{:S(2)}) collective-permute-start(bf16[2,160,512]{2,1,0:T(8,128)(2,1)S(1)} %fusion.1.rest_0_), channel_id=1, source_target_pairs={{0,2},{1,3},{2,0},{3,1},{4,6},{5,7},{6,4},{7,5},{8,10},{9,11},{10,... | collective-permute-start | bytes 983048 | tf_op jit(solution)/shard_map/ppermute | solution.py:324
  64.1 13.9 %collective-permute-start.26 = (bf16[2,2,160,512]{3,2,1,0:T(8,128)(2,1)S(1)}, bf16[2,2,160,512]{3,2,1,0:T(8,128)(2,1)S(1)}, u32[]{:S(2)}, u32[]{:S(2)}) collective-permute-start(bf16[2,2,160,512]{3,2,1,0:T(8,128)(2,1)S(1)} %get-tuple-element.71), channel_id=1, source_target_pairs={{0,1},{1,0},{2,3},{3,2},{4,5},{5,4},{6,7},{7,6},{8,9},{9,8},{10,11... | collective-permute-start | bytes 1966088 | tf_op jit(solution)/shard_map/ppermute | solution.py:321
  64.1 25.3 %collective-permute-start.11 = (bf16[2,160,512]{2,1,0:T(8,128)(2,1)S(1)}, bf16[2,160,512]{2,1,0:T(8,128)(2,1)S(1)}, u32[]{:S(2)}, u32[]{:S(2)}) collective-permute-start(bf16[2,160,512]{2,1,0:T(8,128)(2,1)S(1)} %fusion.rest_0_), channel_id=1, source_target_pairs={{0,2},{1,3},{2,0},{3,1},{4,6},{5,7},{6,4},{7,5},{8,10},{9,11},{10,... | collective-permute-start | bytes 983048 | tf_op jit(solution)/shard_map/ppermute | solution.py:324
  69.2 15.7 %collective-permute-start.13 = (bf16[160,256]{1,0:T(8,128)(2,1)S(1)}, bf16[160,256]{1,0:T(8,128)(2,1)S(1)}, u32[]{:S(2)}, u32[]{:S(2)}) collective-permute-start(bf16[160,256]{1,0:T(8,128)(2,1)S(1)} %fusion.14.own_ref), channel_id=1, source_target_pairs={{0,2},{1,3},{2,0},{3,1},{4,6},{5,7},{6,4},{7,5},{8,10},{9,11},{10,... | collective-permute-start | bytes 245768 | tf_op jit(solution)/shard_map/ppermute | solution.py:324
  70.8 14.2 %collective-permute-start.14 = (bf16[160,256]{1,0:T(8,128)(2,1)S(1)}, bf16[160,256]{1,0:T(8,128)(2,1)S(1)}, u32[]{:S(2)}, u32[]{:S(2)}) collective-permute-start(bf16[160,256]{1,0:T(8,128)(2,1)S(1)} %fusion.14.own_ref), channel_id=1, source_target_pairs={{0,1},{1,0},{2,3},{3,2},{4,5},{5,4},{6,7},{7,6},{8,9},{9,8},{10,11... | collective-permute-start | bytes 245768 | tf_op jit(solution)/shard_map/ppermute | solution.py:321
  76.4 11.1 %collective-permute-start.20 = (bf16[160,512]{1,0:T(8,128)(2,1)S(1)}, bf16[160,512]{1,0:T(8,128)(2,1)S(1)}, u32[]{:S(2)}, u32[]{:S(2)}) collective-permute-start(bf16[160,512]{1,0:T(8,128)(2,1)S(1)} %fusion.6.own_ref), channel_id=1, source_target_pairs={{0,2},{1,3},{2,0},{3,1},{4,6},{5,7},{6,4},{7,5},{8,10},{9,11},{10,... | collective-permute-start | bytes 491528 | tf_op jit(solution)/shard_map/ppermute | solution.py:324
  77.9 13.3 %collective-permute-start.21 = (bf16[160,512]{1,0:T(8,128)(2,1)S(1)}, bf16[160,512]{1,0:T(8,128)(2,1)S(1)}, u32[]{:S(2)}, u32[]{:S(2)}) collective-permute-start(bf16[160,512]{1,0:T(8,128)(2,1)S(1)} %fusion.6.own_ref), channel_id=1, source_target_pairs={{0,1},{1,0},{2,3},{3,2},{4,5},{5,4},{6,7},{7,6},{8,9},{9,8},{10,11... | collective-permute-start | bytes 491528 | tf_op jit(solution)/shard_map/ppermute | solution.py:321
  84.9 2.6 %collective-permute-start.15 = (bf16[160,256]{1,0:T(8,128)(2,1)S(1)}, bf16[160,256]{1,0:T(8,128)(2,1)S(1)}, u32[]{:S(2)}, u32[]{:S(2)}) collective-permute-start(bf16[160,256]{1,0:T(8,128)(2,1)S(1)} %collective-permute-done.13.across_ref), channel_id=1, source_target_pairs={{0,1},{1,0},{2,3},{3,2},{4,5},{5,4},{6,7},{7,6},{8,9},{9,8},{10,11... | collective-permute-start | bytes 245768 | tf_op jit(solution)/shard_map/ppermute | solution.py:321
  85.0 10.6 %collective-permute-start.27 = (bf16[2,160,512]{2,1,0:T(8,128)(2,1)S(1)}, bf16[2,160,512]{2,1,0:T(8,128)(2,1)S(1)}, u32[]{:S(2)}, u32[]{:S(2)}) collective-permute-start(bf16[2,160,512]{2,1,0:T(8,128)(2,1)S(1)} %fusion.2), channel_id=1, source_target_pairs={{0,2},{1,3},{2,0},{3,1},{4,6},{5,7},{6,4},{7,5},{8,10},{9,11},{10,... | collective-permute-start | bytes 983048 | tf_op jit(solution)/shard_map/ppermute | solution.py:324
  87.5 3.7 %collective-permute-start.22 = (bf16[160,512]{1,0:T(8,128)(2,1)S(1)}, bf16[160,512]{1,0:T(8,128)(2,1)S(1)}, u32[]{:S(2)}, u32[]{:S(2)}) collective-permute-start(bf16[160,512]{1,0:T(8,128)(2,1)S(1)} %collective-permute-done.20.across_ref), channel_id=1, source_target_pairs={{0,1},{1,0},{2,3},{3,2},{4,5},{5,4},{6,7},{7,6},{8,9},{9,8},{10,11... | collective-permute-start | bytes 491528 | tf_op jit(solution)/shard_map/ppermute | solution.py:321
  89.6 9.5 %collective-permute-start.16 = (bf16[160,512]{1,0:T(8,128)(2,1)S(1)}, bf16[160,512]{1,0:T(8,128)(2,1)S(1)}, u32[]{:S(2)}, u32[]{:S(2)}) collective-permute-start(bf16[160,512]{1,0:T(8,128)(2,1)S(1)} %fusion.8.own_ref), channel_id=1, source_target_pairs={{0,2},{1,3},{2,0},{3,1},{4,6},{5,7},{6,4},{7,5},{8,10},{9,11},{10,... | collective-permute-start | bytes 491528 | tf_op jit(solution)/shard_map/ppermute | solution.py:324
  95.8 6.4 %collective-permute-start.28 = (bf16[160,512]{1,0:T(8,128)(2,1)S(1)}, bf16[160,512]{1,0:T(8,128)(2,1)S(1)}, u32[]{:S(2)}, u32[]{:S(2)}) collective-permute-start(bf16[160,512]{1,0:T(8,128)(2,1)S(1)} %fusion.4.own_ref), channel_id=1, source_target_pairs={{0,2},{1,3},{2,0},{3,1},{4,6},{5,7},{6,4},{7,5},{8,10},{9,11},{10,... | collective-permute-start | bytes 491528 | tf_op jit(solution)/shard_map/ppermute | solution.py:324
  97.4 4.8 %collective-permute-start.17 = (bf16[160,512]{1,0:T(8,128)(2,1)S(1)}, bf16[160,512]{1,0:T(8,128)(2,1)S(1)}, u32[]{:S(2)}, u32[]{:S(2)}) collective-permute-start(bf16[160,512]{1,0:T(8,128)(2,1)S(1)} %fusion.8.own_ref), channel_id=1, source_target_pairs={{0,1},{1,0},{2,3},{3,2},{4,5},{5,4},{6,7},{7,6},{8,9},{9,8},{10,11... | collective-permute-start | bytes 491528 | tf_op jit(solution)/shard_map/ppermute | solution.py:321
  99.1 3.1 %collective-permute-start.18 = (bf16[160,512]{1,0:T(8,128)(2,1)S(1)}, bf16[160,512]{1,0:T(8,128)(2,1)S(1)}, u32[]{:S(2)}, u32[]{:S(2)}) collective-permute-start(bf16[160,512]{1,0:T(8,128)(2,1)S(1)} %collective-permute-done.16.across_ref), channel_id=1, source_target_pairs={{0,1},{1,0},{2,3},{3,2},{4,5},{5,4},{6,7},{7,6},{8,9},{9,8},{10,11... | collective-permute-start | bytes 491528 | tf_op jit(solution)/shard_map/ppermute | solution.py:321
  99.1 6.6 %collective-permute-start.10 = (bf16[2,160,256]{2,1,0:T(8,128)(2,1)S(1)}, bf16[2,160,256]{2,1,0:T(8,128)(2,1)S(1)}, u32[]{:S(2)}, u32[]{:S(2)}) collective-permute-start(bf16[2,160,256]{2,1,0:T(8,128)(2,1)S(1)} %fusion.10), channel_id=1, source_target_pairs={{0,2},{1,3},{2,0},{3,1},{4,6},{5,7},{6,4},{7,5},{8,10},{9,11},{10,... | collective-permute-start | bytes 491528 | tf_op jit(solution)/shard_map/ppermute | solution.py:324
  100.6 9.8 %collective-permute-start.29 = (bf16[160,512]{1,0:T(8,128)(2,1)S(1)}, bf16[160,512]{1,0:T(8,128)(2,1)S(1)}, u32[]{:S(2)}, u32[]{:S(2)}) collective-permute-start(bf16[160,512]{1,0:T(8,128)(2,1)S(1)} %fusion.4.own_ref), channel_id=1, source_target_pairs={{0,1},{1,0},{2,3},{3,2},{4,5},{5,4},{6,7},{7,6},{8,9},{9,8},{10,11... | collective-permute-start | bytes 491528 | tf_op jit(solution)/shard_map/ppermute | solution.py:321
  102.2 8.1 %collective-permute-start.30 = (bf16[160,512]{1,0:T(8,128)(2,1)S(1)}, bf16[160,512]{1,0:T(8,128)(2,1)S(1)}, u32[]{:S(2)}, u32[]{:S(2)}) collective-permute-start(bf16[160,512]{1,0:T(8,128)(2,1)S(1)} %collective-permute-done.28.across_ref), channel_id=1, source_target_pairs={{0,1},{1,0},{2,3},{3,2},{4,5},{5,4},{6,7},{7,6},{8,9},{9,8},{10,11... | collective-permute-start | bytes 491528 | tf_op jit(solution)/shard_map/ppermute | solution.py:321
  105.8 4.5 %collective-permute-start.23 = (bf16[160,256]{1,0:T(8,128)(2,1)S(1)}, bf16[160,256]{1,0:T(8,128)(2,1)S(1)}, u32[]{:S(2)}, u32[]{:S(2)}) collective-permute-start(bf16[160,256]{1,0:T(8,128)(2,1)S(1)} %fusion.12.own_ref), channel_id=1, source_target_pairs={{0,2},{1,3},{2,0},{3,1},{4,6},{5,7},{6,4},{7,5},{8,10},{9,11},{10,... | collective-permute-start | bytes 245768 | tf_op jit(solution)/shard_map/ppermute | solution.py:324
  107.4 5.2 %collective-permute-start.24 = (bf16[160,256]{1,0:T(8,128)(2,1)S(1)}, bf16[160,256]{1,0:T(8,128)(2,1)S(1)}, u32[]{:S(2)}, u32[]{:S(2)}) collective-permute-start(bf16[160,256]{1,0:T(8,128)(2,1)S(1)} %fusion.12.own_ref), channel_id=1, source_target_pairs={{0,1},{1,0},{2,3},{3,2},{4,5},{5,4},{6,7},{7,6},{8,9},{9,8},{10,11... | collective-permute-start | bytes 245768 | tf_op jit(solution)/shard_map/ppermute | solution.py:321
  110.3 2.3 %collective-permute-start.25 = (bf16[160,256]{1,0:T(8,128)(2,1)S(1)}, bf16[160,256]{1,0:T(8,128)(2,1)S(1)}, u32[]{:S(2)}, u32[]{:S(2)}) collective-permute-start(bf16[160,256]{1,0:T(8,128)(2,1)S(1)} %collective-permute-done.23.across_ref), channel_id=1, source_target_pairs={{0,1},{1,0},{2,3},{3,2},{4,5},{5,4},{6,7},{7,6},{8,9},{9,8},{10,11... | collective-permute-start | bytes 245768 | tf_op jit(solution)/shard_map/ppermute | solution.py:321
  115.5 22.7 %all-to-all-start = ((bf16[8,160,256]{2,1,0:T(8,128)(2,1)}), bf16[8,160,256]{2,1,0:T(8,128)(2,1)S(1)}, u32[]{:S(2)}, u32[]{:S(2)}) async-start(bf16[8,160,256]{2,1,0:T(8,128)(2,1)} %pack.1), calls=%async_computation | async-start | bytes 1310720 | tf_op jit(solution)/shard_map/all_to_all | solution.py:396
  (8 other events, 153.8 us)

commit v3 on v2

--- a/solution.py
+++ b/solution.py
@@ -10,6 +10,7 @@
 E = 8
 ITERS = 2
 CAP = 40
+CHUNKS = 4
 
 
 ridge_share = 0.25
@@ -66,7 +67,9 @@
     return ranked_first, ranked_second
 
 
-def pick_kernel(parts, tensor_count, place_ref, info_ref, tokens_ref, *out_refs):
+def pick_kernel(parts, tensor_count, place_ref, routes_ref, logits_ref, tokens_ref, info_ref, *out_refs):
+    info_ref[0:2, :] = routes_ref[...].astype(f32)
+    info_ref[2:4, :] = logits_ref[...]
     first, second = info_ref[0:1, :], info_ref[1:2, :]
     rank_first, rank_second = block_slots(first, second)
     count = first.shape[1]
@@ -79,62 +82,87 @@
 
 
 def turn_kernel(*refs):
-    pieces = refs[: (len(refs) - 1) // 2]
-    rows = jnp.concatenate([ref[...].astype(f32) for ref in pieces], axis=0)
+    rows = jnp.concatenate([ref[...].astype(f32) for ref in refs[:-1]], axis=0)
     refs[-1][...] = rows.T.astype(bf16)
 
 
-def gate_up_kernel(order_ref, inputs_ref, gate_ref, up_ref, *rest):
-    send_ref, keep_ref = rest[-2:]
+def turned(values):
+    rows, slots = values.shape
+    main = slots // 128 * 128
+    rest = slots - main
+    if main == 0 or rest == 0 or 128 % rest or rows % (128 // rest):
+        return values.T
+    groups = 128 // rest
+    tall = rows // groups
+    folded = jnp.concatenate(
+        [values[group * tall : (group + 1) * tall, main:] for group in range(groups)], axis=1
+    ).T
+    tail = jnp.concatenate(
+        [folded[group * rest : (group + 1) * rest] for group in range(groups)], axis=1
+    )
+    return jnp.concatenate([values[:, :main].T, tail], axis=0)
+
+
+def gate_up_kernel(has_keep, order_ref, inputs_ref, gate_ref, up_ref, *rest):
+    values = inputs_ref[...]
+    gate = turned(mm(gate_ref[...], values).astype(bf16))
+    up = turned(mm(up_ref[...], values).astype(bf16))
     step = pl.program_id(0)
-    values = inputs_ref[...]
-    gate = mm(gate_ref[...], values).T.astype(bf16)
-    up = mm(up_ref[...], values).T.astype(bf16)
-
-    @pl.when(step < 2)
-    def _():
-        send_ref[0, 0] = gate
-        send_ref[0, 1] = up
-
-    @pl.when(step >= 2)
-    def _():
-        keep_ref[0, 0] = gate
-        keep_ref[0, 1] = up
-
-
-def gate_up(order, inputs, gate_weight, up_weight, width, at, after):
+    outs = rest[-(1 + (has_keep == 2)) :]
+    for index, ref in enumerate(outs):
+
+        @pl.when(step // 2 == index)
+        def _(ref=ref):
+            ref[0, 0] = gate
+            ref[0, 1] = up
+
+
+def gate_up(order, inputs, gate_weight, up_weight, width, keep, send, after):
     depth, slots = inputs.shape
     quarter = gate_weight.shape[0] // 4
     gate_weight = gate_weight.reshape(4, quarter, depth)
     up_weight = up_weight.reshape(4, quarter, depth)
-    weight_spec = pl.BlockSpec((None, width, depth), lambda s, order: (order[s], at // width, 0))
-    shape = jax.ShapeDtypeStruct((2, 2, slots, width), bf16)
+    base = 0 if keep is not None else 2
+    chunks = [chunk for chunk in (keep, send) if chunk is not None]
+    count = len(chunks)
+
+    def place(s, order):
+        return (order[base + s], chunks[0] if count == 1 else jnp.where(s < 2, chunks[0], chunks[1]), 0)
+
+    weight_spec = pl.BlockSpec((None, width, depth), place)
+    out_specs = [
+        pl.BlockSpec(
+            (1, 2, slots, width),
+            lambda s, order, index=index: (jnp.clip(s - 2 * index, 0, 1), 0, 0, 0),
+        )
+        for index in range(count)
+    ]
     return pl.pallas_call(
-        gate_up_kernel,
+        functools.partial(gate_up_kernel, count),
         grid_spec=pltpu.PrefetchScalarGridSpec(
             num_scalar_prefetch=1,
-            grid=(4,),
+            grid=(2 * count,),
             in_specs=[
                 pl.BlockSpec((depth, slots), lambda s, order: (0, 0)),
                 weight_spec,
                 weight_spec,
             ]
             + [pl.BlockSpec(memory_space=pl.ANY)] * len(after),
-            out_specs=[
-                pl.BlockSpec((1, 2, slots, width), lambda s, order: (jnp.minimum(s, 1), 0, 0, 0)),
-                pl.BlockSpec((1, 2, slots, width), lambda s, order: (jnp.maximum(s - 2, 0), 0, 0, 0)),
-            ],
+            out_specs=out_specs,
         ),
-        out_shape=[shape, shape],
+        out_shape=[jax.ShapeDtypeStruct((2, 2, slots, width), bf16)] * count,
         compiler_params=params(41),
         cost_estimate=LIGHT,
-        name=f"gate_up_{at}",
+        name=f"gate_up_{chunks[-1] + (send is None)}",
     )(order, inputs, gate_weight, up_weight, *after)
 
 
-def down_kernel(order_ref, own_ref, across_ref, beside_ref, both_ref, down_ref, *rest):
+def down_kernel(pack, has_old, order_ref, place_ref, own_ref, across_ref, beside_ref, both_ref, down_ref, *rest):
     pieces = (own_ref, across_ref, beside_ref, both_ref)
-    old, new = rest[:-3], rest[-3:]
+    old, new = rest[:3] if has_old else (), rest[3 * has_old :]
+    packed_refs = ()
+    if pack:
+        packed_refs, new = new[:-3], new[-3:]
     step = pl.program_id(0)
 
     @pl.when(step == 0)
@@ -149,90 +177,111 @@
     for index, ref in enumerate(pieces):
 
         @pl.when(step == index)
-        def _(ref=ref):
+        def _(ref=ref, index=index):
             values = ref[...]
             out_ref[...] += mm(values, weight)
             gram_ref[...] += mm(values, values, NT)
-
-
-def down(order, pieces, down_weight, at, older):
+            if pack and index == len(pieces) - 1:
+                dp_count, tensor_count = pack
+                columns = out_ref.shape[1]
+                lanes = columns // (dp_count * tensor_count)
+                group = columns // dp_count
+                gram = gram_ref[...]
+                rolled = pltpu.roll(out_ref[...], lax.rem(columns - place_ref[0] * group, columns), 1)
+                for ahead in range(dp_count):
+                    parts = [
+                        rolled[:, ahead * group + part * lanes : ahead * group + (part + 1) * lanes]
+                        for part in range(tensor_count)
+                    ]
+                    for aside in range(tensor_count):
+                        target = lax.rem(place_ref[1] + aside, tensor_count)
+                        piece = parts[0]
+                        for part in range(1, tensor_count):
+                            piece = jnp.where(target == part, parts[part], piece)
+                        packed_refs[ahead * tensor_count + aside][...] = jnp.concatenate(
+                            [gram, piece], axis=1
+                        ).astype(bf16)
+
+
+def down(order, place, pieces, down_weight, chunk, older, pack=None):
     slots, width = pieces[0].shape
     columns = down_weight.shape[1]
     down_weight = down_weight.reshape(4, -1, columns)
 
     def fixed(shape):
-        return pl.BlockSpec(shape, lambda s, order: (0,) * len(shape))
+        return pl.BlockSpec(shape, lambda s, order, place: (0,) * len(shape))
 
     shapes = [(slots, columns), (slots, slots), (8, columns)]
+    out_shape = [jax.ShapeDtypeStruct(shape, f32) for shape in shapes]
+    if pack:
+        parts = pack[0] * pack[1]
+        packed = (slots, slots + columns // parts)
+        out_shape = [jax.ShapeDtypeStruct(packed, bf16)] * parts + out_shape
     return pl.pallas_call(
-        down_kernel,
+        functools.partial(down_kernel, pack, bool(older)),
         grid_spec=pltpu.PrefetchScalarGridSpec(
-            num_scalar_prefetch=1,
+            num_scalar_prefetch=2,
             grid=(4,),
             in_specs=[fixed((slots, width))] * 4
-            + [
-                pl.BlockSpec((None, width, columns), lambda s, order: (order[s], at // width, 0))
-            ]
+            + [pl.BlockSpec((None, width, columns), lambda s, order, place: (order[s], chunk, 0))]
             + [fixed(value.shape) for value in older],
-            out_specs=[fixed(shape) for shape in shapes],
+            out_specs=[fixed(value.shape) for value in out_shape],
         ),
-        out_shape=[jax.ShapeDtypeStruct(shape, f32) for shape in shapes],
+        out_shape=out_shape,
         compiler_params=params(20),
         cost_estimate=LIGHT,
-        name=f"down_{at}",
-    )(order, *pieces, down_weight, *older)
-
-
-def pack_kernel(parts, out_ref, gram_ref, packed_ref):
-    gram = gram_ref[...]
-    wide = out_ref.shape[1] // parts
-    for part in range(parts):
-        piece = out_ref[:, part * wide : (part + 1) * wide]
-        packed_ref[part] = jnp.concatenate([gram, piece], axis=1).astype(bf16)
+        name=f"down_{chunk}",
+    )(order, place, *pieces, down_weight, *older)
 
 
 def route_kernel(blocks, tensor_count, kept_ref, place_ref, *refs):
     infos = refs[:blocks]
-    hot_ref, turned_ref, gates_ref, info_ref, wide_ref = refs[blocks:]
-    for shift in range(blocks):
-        info_ref[lax.rem(place_ref[0] + blocks - shift, blocks)] = infos[shift][...]
-    count = info_ref.shape[2]
+    hot_ref, turned_ref, gates_ref, wide_ref = refs[-4:]
+    count = infos[0].shape[1]
     slots = blocks * CAP
     zero = jnp.zeros((CAP, count), f32)
     rows = lax.broadcasted_iota(jnp.int32, (CAP, count), 0).astype(f32)
+    routed = []
     for block in range(blocks):
-        first, second = info_ref[block, 0:1, :], info_ref[block, 1:2, :]
-        delta = info_ref[block, 3:4, :] - info_ref[block, 2:3, :]
+        first, second = infos[block][0:1, :], infos[block][1:2, :]
+        delta = infos[block][3:4, :] - infos[block][2:3, :]
         share_first = 1.0 / (1.0 + jnp.exp(delta))
         share_second = 1.0 / (1.0 + jnp.exp(-delta))
-        rank_first, rank_second = block_slots(first, second)
-        for expert in range(E):
+        routed.append((first, second, share_first, share_second) + block_slots(first, second))
+    for back in range(blocks):
+        for aside in range(tensor_count):
+            expert = lax.rem(place_ref[0] + blocks - back, blocks) * tensor_count
+            expert = expert + lax.rem(place_ref[1] + tensor_count - aside, tensor_count)
             kept = jnp.zeros((), jnp.int32)
             for index in range(kept_ref.shape[0]):
                 kept = kept | (kept_ref[index] == expert).astype(jnp.int32)
-            kept = kept.astype(f32)
-            hit_first = (first == expert) & (rank_first == rows)
-            hit_second = (second == expert) & (rank_second == rows)
-            gate = jnp.sum(
-                jnp.where(hit_first, share_first, zero) + jnp.where(hit_second, share_second, zero),
-                axis=1,
-                keepdims=True,
-            )
-            row = expert * slots + (expert // tensor_count - block) % blocks * CAP
-            for other in range(blocks):
-                wide_ref[row : row + CAP, other * count : (other + 1) * count] = (
-                    (hit_first | hit_second).astype(f32) if other == block else zero
+            kept, expert = kept.astype(f32), expert.astype(f32)
+            for shift in range(blocks):
+                block = (back + shift) % blocks
+                first, second, share_first, share_second, rank_first, rank_second = routed[block]
+                hit_first = (first == expert) & (rank_first == rows)
+                hit_second = (second == expert) & (rank_second == rows)
+                gate = jnp.sum(
+                    jnp.where(hit_first, share_first, zero) + jnp.where(hit_second, share_second, zero),
+                    axis=1,
+                    keepdims=True,
                 )
-            gates_ref[row : row + CAP, 0:1] = gate * kept
-            gates_ref[row : row + CAP, 1:2] = gate * (1.0 - kept)
+                row = (back * tensor_count + aside) * slots + shift * CAP
+                for other in range(blocks):
+                    wide_ref[row : row + CAP, other * count : (other + 1) * count] = (
+                        (hit_first | hit_second).astype(f32) if other == block else zero
+                    )
+                gates_ref[row : row + CAP, 0:1] = gate * kept
+                gates_ref[row : row + CAP, 1:2] = gate * (1.0 - kept)
     hot_ref[...] = wide_ref[...].astype(bf16)
     turned_ref[...] = wide_ref[...].T.astype(bf16)
 
 
-def solve_kernel(ridge, slots, own_ref, packed_ref, hot_ref, turned_ref, gates_ref, square_ref, base_ref, zero_ref, one_ref, sums_ref):
+def solve_kernel(ridge, slots, own_ref, hot_ref, turned_ref, gates_ref, square_ref, *refs):
+    packed_refs, (base_ref, zero_ref, one_ref, sums_ref) = refs[:E], refs[E:]
     hot, turned = hot_ref[...], turned_ref[...]
     kept, dropped = gates_ref[:, 0:1], gates_ref[:, 1:2]
-    values = jnp.concatenate([packed_ref[e][:, slots:].astype(f32) for e in range(E)], axis=0)
+    values = jnp.concatenate([packed_refs[e][:, slots:].astype(f32) for e in range(E)], axis=0)
     base = mm_wide(turned, dropped * values)
     output = mm_wide(turned, kept * values)
 
@@ -240,7 +289,7 @@
         spread = kept * mm_wide(hot, field)
         mixed = jnp.concatenate(
             [
-                mm_wide(packed_ref[e][:, :slots], spread[e * slots : (e + 1) * slots])
+                mm_wide(packed_refs[e][:, :slots], spread[e * slots : (e + 1) * slots])
                 for e in range(E)
             ],
             axis=0,
@@ -263,7 +312,7 @@
         sums_ref[part] = sums
 
 
-def finish_kernel(ridge, blocks, copies, base_ref, zero_ref, one_ref, sums_ref, out_ref):
+def finish_kernel(ridge, base_ref, zero_ref, one_ref, sums_ref, *out_refs):
     sums = jnp.sum(sums_ref[...], axis=0)[0:1, :]
     norm, zero_zero = sums[:, 0:1], sums[:, 1:2]
     zero_one, one_one = sums[:, 2:3], sums[:, 3:4]
@@ -275,16 +324,22 @@
     image = grown * grown * zero_zero - 2.0 * grown * step * zero_one + step * step * one_one
     later = new / (image + ridge * (new + ratio * ratio * norm))
     field = base_ref[...] - (step + later * grown) * zero_ref[...] + (later * step) * one_ref[...]
-    rows = field.shape[0] // blocks
-    turned = field.T.astype(bf16)
-    for block in range(blocks):
-        for copy in range(copies):
-            out_ref[block * copies + copy] = turned[:, block * rows : (block + 1) * rows]
-
-
-def join_kernel(pieces_ref, out_ref):
-    rows = jnp.concatenate([pieces_ref[part].astype(f32) for part in range(pieces_ref.shape[0])], axis=0)
-    out_ref[...] = rows.T
+    rows = field.shape[0] // len(out_refs)
+    sideways = field.T.astype(bf16)
+    for block, ref in enumerate(out_refs):
+        ref[...] = sideways[:, block * rows : (block + 1) * rows]
+
+
+def join_kernel(blocks, tensor_count, place_ref, *refs):
+    pieces, (out_ref, rows_ref) = refs[:-2], refs[-2:]
+    lanes = pieces[0].shape[0]
+    for back in range(blocks):
+        for aside in range(tensor_count):
+            part = lax.rem(place_ref[0] + blocks - back, blocks) * tensor_count
+            part = part + lax.rem(place_ref[1] + tensor_count - aside, tensor_count)
+            start = pl.multiple_of(part * lanes, 8)
+            rows_ref[pl.ds(start, lanes), :] = pieces[back * tensor_count + aside][...].astype(f32)
+    out_ref[...] = rows_ref[...].T
 
 
 def single(kernel, out_shape, in_specs, mib, name, scratch=()):
@@ -309,7 +364,7 @@
     units, columns = down_weight.shape
     slots = dp_count * CAP
     lanes = columns // parts
-    eighth = units // 32
+    width = units // 4 // CHUNKS
     ridge = ridge_share * 2.0 * tok_rows * dp_count / E
     dp_index = lax.axis_index("dp")
     tensor_index = lax.axis_index("tensor")
@@ -323,105 +378,129 @@
     def across(values):
         return lax.ppermute(values, "col", [(k, k ^ 2) for k in range(4)])
 
-    def ahead(values, shift):
-        if shift == 0:
+    def shifted(values, ahead, aside=0):
+        if ahead == 0 and aside == 0:
             return values
-        return lax.ppermute(values, "dp", [(k, (k + shift) % dp_count) for k in range(dp_count)])
-
-    info = jnp.concatenate([routes.astype(f32).T, route_logits.T], axis=0)
-    picked = single(
+        pairs = [
+            (i * tensor_count + j, (i + ahead) % dp_count * tensor_count + (j + aside) % tensor_count)
+            for i in range(dp_count)
+            for j in range(tensor_count)
+        ]
+        return lax.ppermute(values, ("dp", "tensor"), pairs)
+
+    shifts = [(ahead, aside) for ahead in range(dp_count) for aside in range(tensor_count)]
+    info, *picked = single(
         functools.partial(pick_kernel, dp_count, tensor_count),
-        [jax.ShapeDtypeStruct((CAP, depth), bf16)] * dp_count,
-        [scalars(), whole(), whole()],
+        [jax.ShapeDtypeStruct((4, tok_rows), f32)] + [jax.ShapeDtypeStruct((CAP, depth), bf16)] * dp_count,
+        [scalars(), whole(), whole(), whole()],
         16,
         "pick",
-    )(place, info, tokens)
-    arrived = [ahead(value, shift) for shift, value in enumerate(picked)]
-    infos = [ahead(info, shift) for shift in range(dp_count)]
+    )(place, routes.T, route_logits.T, tokens)
+    arrived = [shifted(value, ahead) for ahead, value in enumerate(picked)]
     inputs = single(
         turn_kernel,
         jax.ShapeDtypeStruct((depth, slots), bf16),
-        [whole()] * dp_count + [pl.BlockSpec(memory_space=pl.ANY)] * dp_count,
+        [whole()] * dp_count,
         16,
         "turn",
-    )(*arrived, *infos)
+    )(*arrived)
+
+    gate_order = col_index ^ jnp.array([2, 0, 3, 1], jnp.int32)
+    down_order = col_index ^ jnp.array([0, 2, 1, 3], jnp.int32)
+
+    def products(keep, send, after=()):
+        return gate_up(gate_order, inputs, gate_weight, up_weight, width, keep, send, after)
+
+    last = CHUNKS - 1
+    keeps, nears, pairs, fars, owns = [], [], [], [], []
+
+    def activate(chunk, after):
+        far = lax.optimization_barrier((fars[chunk], *after))[0] if after else fars[chunk]
+        total = keeps[chunk][1].astype(f32) + nears[chunk][1].astype(f32) + far.astype(f32)
+        owns.append((jax.nn.silu(total[0]) * total[1]).astype(bf16))
+
+    nears.append(beside(products(None, 0)[0]))
+    for chunk in range(CHUNKS):
+        after = []
+        if chunk >= 2:
+            after = after + [fars[chunk - 2]]
+        if chunk >= 3:
+            activate(chunk - 3, [])
+            after = after + [owns[chunk - 3]]
+        if chunk < last:
+            keep, send = products(chunk, chunk + 1, after)
+            nears.append(beside(send))
+        else:
+            (keep,) = products(chunk, None, after)
+        keeps.append(keep)
+        pairs.append((keep[0].astype(f32) + nears[chunk][0].astype(f32)).astype(bf16))
+        fars.append(across(pairs[-1]))
+    info = lax.optimization_barrier((info, owns[0]))[0]
+    infos = [shifted(info, ahead) for ahead in range(dp_count)]
+    older, olders = (), []
+    for chunk in range(CHUNKS):
+        if chunk >= len(owns):
+            after = [pairs[last]]
+            if chunk >= 2:
+                after.append(olders[chunk - 2][2])
+                after.extend(infos[1:])
+            activate(chunk, after)
+        own = owns[chunk]
+        other = across(own)
+        older = down(
+            down_order,
+            place,
+            (own, other, beside(own), beside(other)),
+            down_weight,
+            chunk,
+            older,
+            (dp_count, tensor_count) if chunk == last else None,
+        )
+        olders.append(older)
+    packed, (_, _, square) = older[:parts], older[parts:]
+    spread = [shifted(value, *shift) for value, shift in zip(packed, shifts)]
+
     total_slots, total_tokens = E * slots, dp_count * tok_rows
-    hot, turned, gates = single(
+    hot, turned_hot, gates = single(
         functools.partial(route_kernel, dp_count, tensor_count),
         [
             jax.ShapeDtypeStruct((total_slots, total_tokens), bf16),
             jax.ShapeDtypeStruct((total_tokens, total_slots), bf16),
             jax.ShapeDtypeStruct((total_slots, 2), f32),
         ],
-        [scalars(), scalars()] + [whole()] * dp_count,
+        [scalars(), scalars()] + [whole()] * dp_count + [pl.BlockSpec(memory_space=pl.ANY)],
         24,
         "route",
-        [pltpu.VMEM((dp_count,) + info.shape, f32), pltpu.VMEM((total_slots, total_tokens), f32)],
-    )(kept_experts, place, *infos)
-
-    gate_order = col_index ^ jnp.array([3, 1, 2, 0], jnp.int32)
-    down_order = col_index ^ jnp.array([0, 2, 1, 3], jnp.int32)
-    plan = [(width * eighth, at * eighth) for width, at in ((1, 6), (2, 0), (2, 2), (2, 4), (1, 7))]
-    last = len(plan) - 1
-    keeps, pairs, sent = [], [], []
-    for chunk, (width, at) in enumerate(plan):
-        after = [pairs[chunk - 2], keeps[chunk - 1][0]] if chunk >= 2 else []
-        send, keep = gate_up(gate_order, inputs, gate_weight, up_weight, width, at, after)
-        near = beside(send)
-        pairs.append((keep[0].astype(f32) + near[0].astype(f32)).astype(bf16))
-        sent.append(across(pairs[-1]))
-        keeps.append((keep, near))
-    older, olders = (), []
-    for chunk, (width, at) in enumerate(plan):
-        first = [pairs[last]]
-        if chunk == 1:
-            first.append(gates)
-        if chunk >= 2:
-            first.append(olders[chunk - 2][2])
-        far = lax.optimization_barrier((sent[chunk], *first))[0]
-        keep, near = keeps[chunk]
-        total = keep[1].astype(f32) + near[1].astype(f32) + far.astype(f32)
-        own = (jax.nn.silu(total[0]) * total[1]).astype(bf16)
-        other = across(own)
-        older = down(down_order, (own, other, beside(own), beside(other)), down_weight, at, older)
-        olders.append(older)
-
-    packed = single(
-        functools.partial(pack_kernel, parts),
-        jax.ShapeDtypeStruct((parts, slots, slots + lanes), bf16),
-        [whole(), whole()],
-        16,
-        "pack",
-    )(*older[:2])
-    spread = lax.all_to_all(packed, ("dp", "tensor"), split_axis=0, concat_axis=0, tiled=True)
-
-    everyone = parts * lax.axis_size("col")
+        [pltpu.VMEM((total_slots, total_tokens), f32)],
+    )(kept_experts, place, *infos, square)
     is_kept = jnp.any(kept_experts == own_expert).astype(f32).reshape(1)
     field = jax.ShapeDtypeStruct((total_tokens, lanes), f32)
+    everyone = parts * lax.axis_size("col")
     base, zero, one, sums = single(
         functools.partial(solve_kernel, ridge, slots),
         [field, field, field, jax.ShapeDtypeStruct((everyone, 1, 128), f32)],
-        [scalars()] + [whole()] * 5,
+        [scalars()] + [whole()] * (4 + E),
         40,
         "solve",
-    )(is_kept, spread, hot, turned, gates, older[2])
+    )(is_kept, hot, turned_hot, gates, square, *spread)
     sums = lax.all_to_all(sums, ("dp", "tensor", "col"), split_axis=0, concat_axis=0, tiled=True)
 
     home = single(
-        functools.partial(finish_kernel, ridge, dp_count, tensor_count),
-        jax.ShapeDtypeStruct((parts, lanes, tok_rows), bf16),
+        functools.partial(finish_kernel, ridge),
+        [jax.ShapeDtypeStruct((lanes, tok_rows), bf16)] * dp_count,
         [whole()] * 4,
         16,
         "finish",
     )(base, zero, one, sums)
-    pieces = lax.all_to_all(home, ("dp", "tensor"), split_axis=0, concat_axis=0, tiled=True)
+    pieces = [shifted(home[-ahead % dp_count], ahead, aside) for ahead, aside in shifts]
     return single(
-        join_kernel,
+        functools.partial(join_kernel, dp_count, tensor_count),
         jax.ShapeDtypeStruct((tok_rows, columns), f32),
-        [whole()],
+        [scalars()] + [whole()] * parts,
         16,
         "join",
-    )(pieces)
+        [pltpu.VMEM((columns, tok_rows), f32)],
+    )(place, *pieces)
 
 
 def spread_copies(values, experts, held_count, copies):

time: 168 us -> 151 us (0.90)
  waiting for transfers between devices: 49.7 us -> 33.1 us
  starting transfers between devices: 31.7 us -> 45.6 us
  blocking collectives: 21.3 us -> 11.8 us
  Pallas kernels: 57.5 us -> 54.2 us
    ppermute x6 -> x20, starting transfers between devices: 10.8 us -> 35.7 us  [shifted(): return lax.ppermute(values, ('dp', 'tensor'), pairs)]
    all_to_all x1 -> x0, waiting for transfers between devices: 16.7 us -> none  [one_expert_each(): lax.all_to_all(packed, ('dp', 'tensor'), split_axis=0, concat_axis=0, til...]
    all_to_all x1 -> x0, blocking collectives: 10.7 us -> none  [one_expert_each(): lax.all_to_all(home, ('dp', 'tensor'), split_axis=0, concat_axis=0, tiled...]
    ppermute x10 -> x8, starting transfers between devices: 14.6 us -> 7.84 us  [across(): return lax.ppermute(values, 'col', [(k, k ^ 2) for k in range(4)])]
    ppermute x10 -> x8, waiting for transfers between devices: 25.9 us -> 19.6 us  [across(): return lax.ppermute(values, 'col', [(k, k ^ 2) for k in range(4)])]
    ppermute x6 -> x20, waiting for transfers between devices: 7.01 us -> 12 us  [shifted(): return lax.ppermute(values, ('dp', 'tensor'), pairs)]
    all_to_all x1 -> x0, starting transfers between devices: 4.74 us -> none  [one_expert_each(): lax.all_to_all(packed, ('dp', 'tensor'), split_axis=0, concat_axis=0, til...]
    pallas_call x13 -> x11, Pallas kernels: 49.3 us -> 46.1 us  [the longest x5 33.9 us: gate_up(): pl.pallas_call(functools.partial(gate_up_kernel, count), grid_spec=pltpu....]
  transfers between devices with their start and end apart: 32 -> 40, of which waited for: 12 -> 13; matrix products, arithmetic and copies ran while one was open for 1% -> 2% of each run, Pallas kernels for 21% -> 25%
where the time goes in v3:
time: 151 us
  Pallas kernels  54.2 us (36%)
  starting transfers between devices  45.6 us (30%)
  waiting for transfers between devices  33.1 us (22%)
  blocking collectives  11.8 us (8%)
  other arithmetic  2.58 us (2%)
  local copies, waits for them, and re-layouts  2.38 us (2%)
    ppermute x20, starting transfers between devices, shifted(): return lax.ppermute(values, ('dp', 'tensor'), pairs)  35.7 us
    pallas_call x5, Pallas kernels, gate_up(): pl.pallas_call(functools.partial(gate_up_kernel, count), grid_spec=pltpu....  33.9 us
    ppermute x8, waiting for transfers between devices, across(): return lax.ppermute(values, 'col', [(k, k ^ 2) for k in range(4)])  19.6 us
    ppermute x20, waiting for transfers between devices, shifted(): return lax.ppermute(values, ('dp', 'tensor'), pairs)  12 us
    all_to_all x1, blocking collectives, one_expert_each(): lax.all_to_all(sums, ('dp', 'tensor', 'col'), split_axis=0, concat_axis=0...  11.8 us
    pallas_call x4, Pallas kernels, down(): pl.pallas_call(functools.partial(down_kernel, pack, bool(older)), grid_sp...  10.3 us
    ppermute x8, starting transfers between devices, across(): return lax.ppermute(values, 'col', [(k, k ^ 2) for k in range(4)])  7.84 us
    pallas_call x1, Pallas kernels, one_expert_each(): single(functools.partial(solve_kernel, ridge, slots), [field, field, fiel...  5.35 us
  transfers between devices with their start and end apart: 40, of which 13 were waited for; matrix products, arithmetic and copies ran while one was open for 2% of the time, Pallas kernels for 25%

profile of v3, /device:TPU:0, one launch (start us, length us, event | category | flops | bytes accessed | tf_op | source)
XLA Modules:
  0.0 150.7 jit_solution(17725943184798685055)
XLA Ops:
  3.5 3.1 %collective-permute-start = (bf16[40,1536]{1,0:T(8,128)(2,1)S(1)}, bf16[40,1536]{1,0:T(8,128)(2,1)S(1)}, u32[]{:S(2)}, u32[]{:S(2)}) collective-permute-start(bf16[40,1536]{1,0:T(8,128)(2,1)S(1)} %get-tuple-element.51), channel_id=1, source_target_pairs={{0,8},{4,12},{8,16},{12,20},{16,24},{20,28},{24,0},{28,4},{1,9},{5... | collective-permute-start | bytes 368648 | tf_op jit(solution)/shard_map/ppermute | solution.py:389
  6.5 2.6 %collective-permute-start.1 = (bf16[40,1536]{1,0:T(8,128)(2,1)S(1)}, bf16[40,1536]{1,0:T(8,128)(2,1)S(1)}, u32[]{:S(2)}, u32[]{:S(2)}) collective-permute-start(bf16[40,1536]{1,0:T(8,128)(2,1)S(1)} %get-tuple-element.52), channel_id=1, source_target_pairs={{0,16},{4,20},{8,24},{12,28},{16,0},{20,4},{24,8},{28,12},{1,17},{... | collective-permute-start | bytes 368648 | tf_op jit(solution)/shard_map/ppermute | solution.py:389
  11.1 1.7 %collective-permute-done.refs_1_ = bf16[40,1536]{1,0:T(8,128)(2,1)S(1)} collective-permute-done((bf16[40,1536]{1,0:T(8,128)(2,1)S(1)}, bf16[40,1536]{1,0:T(8,128)(2,1)S(1)}, u32[]{:S(2)}, u32[]{:S(2)}) %collective-permute-start) | collective-permute-done | bytes 122912 | tf_op jit(solution)/shard_map/ppermute | solution.py:389
  12.8 4.4 %collective-permute-done.1.refs_2_ = bf16[40,1536]{1,0:T(8,128)(2,1)S(1)} collective-permute-done((bf16[40,1536]{1,0:T(8,128)(2,1)S(1)}, bf16[40,1536]{1,0:T(8,128)(2,1)S(1)}, u32[]{:S(2)}, u32[]{:S(2)}) %collective-permute-start.1) | collective-permute-done | bytes 122912 | tf_op jit(solution)/shard_map/ppermute | solution.py:389
  17.5 4.8 %gate_up_0.1 = bf16[2,2,160,512]{3,2,1,0:T(8,128)(2,1)S(1)} custom-call(s32[4]{0:T(128)S(1)} %broadcast_xor_fusion.1.order_ref, bf16[1536,160]{1,0:T(8,128)(2,1)S(1)} %turn.1.inputs_ref, bf16[4,2048,1536]{2,1,0:T(8,128)(2,1)} %bitcast.72, bf16[4,2048,1536]{2,1,0:T(8,128)(2,1)} %bitcast.77), custom_call_target="tpu_custom_call" | custom-call | flops 1 | bytes 1 | tf_op jit(solution)/shard_map/gate_up_0/pallas_call | solution.py:140
  22.5 8.1 %gate_up_1.1 = (bf16[2,2,160,512]{3,2,1,0:T(8,128)(2,1)S(1)}, bf16[2,2,160,512]{3,2,1,0:T(8,128)(2,1)S(1)}) custom-call(s32[4]{0:T(128)S(1)} %broadcast_xor_fusion.1.order_ref, bf16[1536,160]{1,0:T(8,128)(2,1)S(1)} %turn.1.inputs_ref, bf16[4,2048,1536]{2,1,0:T(8,128)(2,1)} %bitcast.73, bf16[4,2048,1536]{2,1,0:T(8,128)(2,1)} %bitcast.78), custom_call_target="tpu_custom_call" | custom-call | flops 1 | bytes 1 | tf_op jit(solution)/shard_map/gate_up_1/pallas_call | solution.py:140
  31.2 1.6 %collective-permute-start.4 = (bf16[2,160,512]{2,1,0:T(8,128)(2,1)S(1)}, bf16[2,160,512]{2,1,0:T(8,128)(2,1)S(1)}, u32[]{:S(2)}, u32[]{:S(2)}) collective-permute-start(bf16[2,160,512]{2,1,0:T(8,128)(2,1)S(1)} %fusion), channel_id=1, source_target_pairs={{0,2},{1,3},{2,0},{3,1},{4,6},{5,7},{6,4},{7,5},{8,10},{9,11},{10,... | collective-permute-start | bytes 983048 | tf_op jit(solution)/shard_map/ppermute | solution.py:379
  32.8 8.1 %gate_up_2.1 = (bf16[2,2,160,512]{3,2,1,0:T(8,128)(2,1)S(1)}, bf16[2,2,160,512]{3,2,1,0:T(8,128)(2,1)S(1)}) custom-call(s32[4]{0:T(128)S(1)} %broadcast_xor_fusion.1.order_ref, bf16[1536,160]{1,0:T(8,128)(2,1)S(1)} %turn.1.inputs_ref, bf16[4,2048,1536]{2,1,0:T(8,128)(2,1)} %bitcast.74, bf16[4,2048,1536]{2,1,0:T(8,128)(2,1)} %bitcast.79), custom_call_target="tpu_custom_call" | custom-call | flops 1 | bytes 1 | tf_op jit(solution)/shard_map/gate_up_2/pallas_call | solution.py:140
  41.6 8.1 %gate_up_3.1 = (bf16[2,2,160,512]{3,2,1,0:T(8,128)(2,1)S(1)}, bf16[2,2,160,512]{3,2,1,0:T(8,128)(2,1)S(1)}) custom-call(s32[4]{0:T(128)S(1)} %broadcast_xor_fusion.1.order_ref, bf16[1536,160]{1,0:T(8,128)(2,1)S(1)} %turn.1.inputs_ref, bf16[4,2048,1536]{2,1,0:T(8,128)(2,1)} %bitcast.75, bf16[4,2048,1536]{2,1,0:T(8,128)(2,1)} %bitcast.80, ...), custom_call_target="tpu_custom_call" | custom-call | flops 1 | bytes 1 | tf_op jit(solution)/shard_map/gate_up_3/pallas_call | solution.py:140
  50.3 1.6 %collective-permute-start.15 = (bf16[160,512]{1,0:T(8,128)(2,1)S(1)}, bf16[160,512]{1,0:T(8,128)(2,1)S(1)}, u32[]{:S(2)}, u32[]{:S(2)}) collective-permute-start(bf16[160,512]{1,0:T(8,128)(2,1)S(1)} %fusion.11.rest_1_.own_ref), channel_id=1, source_target_pairs={{0,2},{1,3},{2,0},{3,1},{4,6},{5,7},{6,4},{7,5},{8,10},{9,11},{10,... | collective-permute-start | bytes 491528 | tf_op jit(solution)/shard_map/ppermute | solution.py:379
  51.9 3.2 %collective-permute-start.5 = (f32[4,128]{1,0:T(4,128)S(1)}, f32[4,128]{1,0:T(4,128)S(1)}, u32[]{:S(2)}, u32[]{:S(2)}) collective-permute-start(f32[4,128]{1,0:T(4,128)S(1)} %get-tuple-element.55.refs_0_), channel_id=1, source_target_pairs={{0,8},{4,12},{8,16},{12,20},{16,24},{20,28},{24,0},{28,4},{1,9},{5... | collective-permute-start | bytes 6152 | tf_op jit(solution)/shard_map/ppermute | solution.py:389
  55.0 1.6 %collective-permute-start.6 = (f32[4,128]{1,0:T(4,128)S(1)}, f32[4,128]{1,0:T(4,128)S(1)}, u32[]{:S(2)}, u32[]{:S(2)}) collective-permute-start(f32[4,128]{1,0:T(4,128)S(1)} %get-tuple-element.55.refs_0_), channel_id=1, source_target_pairs={{0,16},{4,20},{8,24},{12,28},{16,0},{20,4},{24,8},{28,12},{1,17},{... | collective-permute-start | bytes 6152 | tf_op jit(solution)/shard_map/ppermute | solution.py:389
  56.6 4.8 %gate_up_4.1 = bf16[2,2,160,512]{3,2,1,0:T(8,128)(2,1)S(1)} custom-call(s32[4]{0:T(128)S(1)} %broadcast_xor_fusion.1.order_ref, bf16[1536,160]{1,0:T(8,128)(2,1)S(1)} %turn.1.inputs_ref, bf16[4,2048,1536]{2,1,0:T(8,128)(2,1)} %bitcast.76, bf16[4,2048,1536]{2,1,0:T(8,128)(2,1)} %bitcast.81, bf16[2,160,512]{2,1,0:T(8,128)(2,1)S(1)} %collective-permute-done.9.rest_0_, ...), custom_call_target="tpu_custom_call" | custom-call | flops 1 | bytes 1 | tf_op jit(solution)/shard_map/gate_up_4/pallas_call | solution.py:140
  63.0 1.6 %collective-permute-start.7 = (f32[4,128]{1,0:T(4,128)S(1)}, f32[4,128]{1,0:T(4,128)S(1)}, u32[]{:S(2)}, u32[]{:S(2)}) collective-permute-start(f32[4,128]{1,0:T(4,128)S(1)} %get-tuple-element.55.refs_0_), channel_id=1, source_target_pairs={{0,24},{4,28},{8,0},{12,4},{16,8},{20,12},{24,16},{28,20},{1,25},{... | collective-permute-start | bytes 6152 | tf_op jit(solution)/shard_map/ppermute | solution.py:389
  65.1 2.3 %down_0.1 = (f32[160,768]{1,0:T(8,128)S(1)}, f32[160,160]{1,0:T(8,128)S(1)}, f32[8,768]{1,0:T(8,128)S(1)}) custom-call(s32[4]{0:T(128)S(1)} %broadcast_xor_fusion.order_ref, s32[2]{0:T(128)S(1)} %pad_add_fusion.place_ref, bf16[160,512]{1,0:T(8,128)(2,1)S(1)} %fusion.11.rest_1_.own_ref, bf16[160,512]{1,0:T(8,128)(2,1)S(1)} %collective-permute-done.15.across_ref, ...), custom_call_target="tpu_custom_call" | custom-call | flops 1 | bytes 1 | tf_op jit(solution)/shard_map/down_0/pallas_call | solution.py:220
  67.5 1.6 %collective-permute-start.11 = (bf16[2,160,512]{2,1,0:T(8,128)(2,1)S(1)}, bf16[2,160,512]{2,1,0:T(8,128)(2,1)S(1)}, u32[]{:S(2)}, u32[]{:S(2)}) collective-permute-start(bf16[2,160,512]{2,1,0:T(8,128)(2,1)S(1)} %fusion.2), channel_id=1, source_target_pairs={{0,2},{1,3},{2,0},{3,1},{4,6},{5,7},{6,4},{7,5},{8,10},{9,11},{10,... | collective-permute-start | bytes 983048 | tf_op jit(solution)/shard_map/ppermute | solution.py:379
  69.9 5.3 %collective-permute-done.22 = bf16[2,160,512]{2,1,0:T(8,128)(2,1)S(1)} collective-permute-done((bf16[2,160,512]{2,1,0:T(8,128)(2,1)S(1)}, bf16[2,160,512]{2,1,0:T(8,128)(2,1)S(1)}, u32[]{:S(2)}, u32[]{:S(2)}) %collective-permute-start.22) | collective-permute-done | bytes 327712 | tf_op jit(solution)/shard_map/ppermute | solution.py:379
  75.3 9.3 %collective-permute-done.12.across_ref = bf16[160,512]{1,0:T(8,128)(2,1)S(1)} collective-permute-done((bf16[160,512]{1,0:T(8,128)(2,1)S(1)}, bf16[160,512]{1,0:T(8,128)(2,1)S(1)}, u32[]{:S(2)}, u32[]{:S(2)}) %collective-permute-start.12) | collective-permute-done | bytes 163872 | tf_op jit(solution)/shard_map/ppermute | solution.py:379
  86.0 2.3 %down_1.1 = (f32[160,768]{1,0:T(8,128)S(1)}, f32[160,160]{1,0:T(8,128)S(1)}, f32[8,768]{1,0:T(8,128)S(1)}) custom-call(s32[4]{0:T(128)S(1)} %broadcast_xor_fusion.order_ref, s32[2]{0:T(128)S(1)} %pad_add_fusion.place_ref, bf16[160,512]{1,0:T(8,128)(2,1)S(1)} %fusion.9.own_ref, bf16[160,512]{1,0:T(8,128)(2,1)S(1)} %collective-permute-done.12.across_ref, ...), custom_call_target="tpu_custom_call" | custom-call | flops 1 | bytes 1 | tf_op jit(solution)/shard_map/down_1/pallas_call | solution.py:220
  89.4 2.0 %collective-permute-done.23.across_ref = bf16[160,512]{1,0:T(8,128)(2,1)S(1)} collective-permute-done((bf16[160,512]{1,0:T(8,128)(2,1)S(1)}, bf16[160,512]{1,0:T(8,128)(2,1)S(1)}, u32[]{:S(2)}, u32[]{:S(2)}) %collective-permute-start.23) | collective-permute-done | bytes 163872 | tf_op jit(solution)/shard_map/ppermute | solution.py:379
  91.9 3.0 %collective-permute-done.18.across_ref = bf16[160,512]{1,0:T(8,128)(2,1)S(1)} collective-permute-done((bf16[160,512]{1,0:T(8,128)(2,1)S(1)}, bf16[160,512]{1,0:T(8,128)(2,1)S(1)}, u32[]{:S(2)}, u32[]{:S(2)}) %collective-permute-start.18) | collective-permute-done | bytes 163872 | tf_op jit(solution)/shard_map/ppermute | solution.py:379
  94.9 2.3 %down_2.1 = (f32[160,768]{1,0:T(8,128)S(1)}, f32[160,160]{1,0:T(8,128)S(1)}, f32[8,768]{1,0:T(8,128)S(1)}) custom-call(s32[4]{0:T(128)S(1)} %broadcast_xor_fusion.order_ref, s32[2]{0:T(128)S(1)} %pad_add_fusion.place_ref, bf16[160,512]{1,0:T(8,128)(2,1)S(1)} %fusion.5.own_ref, bf16[160,512]{1,0:T(8,128)(2,1)S(1)} %collective-permute-done.23.across_ref, ...), custom_call_target="tpu_custom_call" | custom-call | flops 1 | bytes 1 | tf_op jit(solution)/shard_map/down_2/pallas_call | solution.py:220
  97.2 3.4 %down_3.1 = (bf16[160,256]{1,0:T(8,128)(2,1)S(1)}, bf16[160,256]{1,0:T(8,128)(2,1)S(1)}, bf16[160,256]{1,0:T(8,128)(2,1)S(1)}, bf16[160,256]{1,0:T(8,128)(2,1)S(...) custom-call(s32[4]{0:T(128)S(1)} %broadcast_xor_fusion.order_ref, ...), custom_call_target="tpu_custom_call" | custom-call | flops 1 | bytes 1 | tf_op jit(solution)/shard_map/down_3/pallas_call | solution.py:220
  103.4 3.1 %collective-permute-start.29 = (bf16[160,256]{1,0:T(8,128)(2,1)S(1)}, bf16[160,256]{1,0:T(8,128)(2,1)S(1)}, u32[]{:S(2)}, u32[]{:S(2)}) collective-permute-start(bf16[160,256]{1,0:T(8,128)(2,1)S(1)} %get-tuple-element.81), channel_id=1, source_target_pairs={{0,16},{4,20},{8,24},{12,28},{16,0},{20,4},{24,8},{28,12},{1,17},{... | collective-permute-start | bytes 245768 | tf_op jit(solution)/shard_map/ppermute | solution.py:389
  107.4 2.8 %collective-permute-start.31 = (bf16[160,256]{1,0:T(8,128)(2,1)S(1)}, bf16[160,256]{1,0:T(8,128)(2,1)S(1)}, u32[]{:S(2)}, u32[]{:S(2)}) collective-permute-start(bf16[160,256]{1,0:T(8,128)(2,1)S(1)} %get-tuple-element.83), channel_id=1, source_target_pairs={{0,24},{4,28},{8,0},{12,4},{16,8},{20,12},{24,16},{28,20},{1,25},{... | collective-permute-start | bytes 245768 | tf_op jit(solution)/shard_map/ppermute | solution.py:389
  115.7 1.7 %collective-permute-done.30.refs_5_ = bf16[160,256]{1,0:T(8,128)(2,1)S(1)} collective-permute-done((bf16[160,256]{1,0:T(8,128)(2,1)S(1)}, bf16[160,256]{1,0:T(8,128)(2,1)S(1)}, u32[]{:S(2)}, u32[]{:S(2)}) %collective-permute-start.30) | collective-permute-done | bytes 81952 | tf_op jit(solution)/shard_map/ppermute | solution.py:389
  118.1 5.4 %solve.1 = (f32[512,96]{1,0:T(8,128)S(1)}, f32[512,96]{1,0:T(8,128)S(1)}, f32[512,96]{1,0:T(8,128)S(1)}, f32[32,1,128]{2,1,0:T(1,128)S(1)}) custom-call(f32[1]{0:T(128)} %bitcast.2.own_ref, bf16[1280,512]{1,0:T(8,128)(2,1)S(1)} %get-tuple-element.74.hot_ref, bf16[512,1280]{1,0:T(8,128)(2,1)S(1)} %get-tuple-element.75.turned_ref, ...), custom_call_target="tpu_custom_call" | custom-call | flops 1 | bytes 1 | tf_op jit(solution)/shard_map/solve/pallas_call | solution.py:479
  123.5 11.8 %all_to_all.5.sums_ref = f32[32,1,128]{2,1,0:T(1,128)S(1)} all-to-all(f32[32,1,128]{2,1,0:T(1,128)S(1)} %get-tuple-element.88), channel_id=1, replica_groups=mesh['dp'=4,'tensor'=2,'col'=4] {'dp','tensor','col'}, dimensions={0} | all-to-all | bytes 32768 | tf_op jit(solution)/shard_map/all_to_all | solution.py:486
  138.3 3.2 %collective-permute-start.36 = (bf16[96,128]{1,0:T(8,128)(2,1)S(1)}, bf16[96,128]{1,0:T(8,128)(2,1)S(1)}, u32[]{:S(2)}, u32[]{:S(2)}) collective-permute-start(bf16[96,128]{1,0:T(8,128)(2,1)S(1)} %get-tuple-element.91), channel_id=1, source_target_pairs={{0,16},{4,20},{8,24},{12,28},{16,0},{20,4},{24,8},{28,12},{1,17},{... | collective-permute-start | bytes 73736 | tf_op jit(solution)/shard_map/ppermute | solution.py:389
  141.5 2.9 %collective-permute-start.38 = (bf16[96,128]{1,0:T(8,128)(2,1)S(1)}, bf16[96,128]{1,0:T(8,128)(2,1)S(1)}, u32[]{:S(2)}, u32[]{:S(2)}) collective-permute-start(bf16[96,128]{1,0:T(8,128)(2,1)S(1)} %get-tuple-element.92), channel_id=1, source_target_pairs={{0,24},{4,28},{8,0},{12,4},{16,8},{20,12},{24,16},{28,20},{1,25},{... | collective-permute-start | bytes 73736 | tf_op jit(solution)/shard_map/ppermute | solution.py:389
  144.5 2.4 %collective-permute-start.39 = (bf16[96,128]{1,0:T(8,128)(2,1)S(1)}, bf16[96,128]{1,0:T(8,128)(2,1)S(1)}, u32[]{:S(2)}, u32[]{:S(2)}) collective-permute-start(bf16[96,128]{1,0:T(8,128)(2,1)S(1)} %get-tuple-element.92), channel_id=1, source_target_pairs={{0,28},{4,24},{8,4},{12,0},{16,12},{20,8},{24,20},{28,16},{1,29},{... | collective-permute-start | bytes 73736 | tf_op jit(solution)/shard_map/ppermute | solution.py:389
  147.4 1.8 %collective-permute-done.39.refs_7_ = bf16[96,128]{1,0:T(8,128)(2,1)S(1)} collective-permute-done((bf16[96,128]{1,0:T(8,128)(2,1)S(1)}, bf16[96,128]{1,0:T(8,128)(2,1)S(1)}, u32[]{:S(2)}, u32[]{:S(2)}) %collective-permute-start.39) | collective-permute-done | bytes 24608 | tf_op jit(solution)/shard_map/ppermute | solution.py:389
  (97 shorter events, 28.0 us)
Async XLA Ops:
  3.5 9.3 %collective-permute-start = (bf16[40,1536]{1,0:T(8,128)(2,1)S(1)}, bf16[40,1536]{1,0:T(8,128)(2,1)S(1)}, u32[]{:S(2)}, u32[]{:S(2)}) collective-permute-start(bf16[40,1536]{1,0:T(8,128)(2,1)S(1)} %get-tuple-element.51), channel_id=1, source_target_pairs={{0,8},{4,12},{8,16},{12,20},{16,24},{20,28},{24,0},{28,4},{1,9},{5... | collective-permute-start | bytes 368648 | tf_op jit(solution)/shard_map/ppermute | solution.py:389
  6.5 10.7 %collective-permute-start.1 = (bf16[40,1536]{1,0:T(8,128)(2,1)S(1)}, bf16[40,1536]{1,0:T(8,128)(2,1)S(1)}, u32[]{:S(2)}, u32[]{:S(2)}) collective-permute-start(bf16[40,1536]{1,0:T(8,128)(2,1)S(1)} %get-tuple-element.52), channel_id=1, source_target_pairs={{0,16},{4,20},{8,24},{12,28},{16,0},{20,4},{24,8},{28,12},{1,17},{... | collective-permute-start | bytes 368648 | tf_op jit(solution)/shard_map/ppermute | solution.py:389
  9.1 8.1 %collective-permute-start.2 = (bf16[40,1536]{1,0:T(8,128)(2,1)S(1)}, bf16[40,1536]{1,0:T(8,128)(2,1)S(1)}, u32[]{:S(2)}, u32[]{:S(2)}) collective-permute-start(bf16[40,1536]{1,0:T(8,128)(2,1)S(1)} %get-tuple-element.53), channel_id=1, source_target_pairs={{0,24},{4,28},{8,0},{12,4},{16,8},{20,12},{24,16},{28,20},{1,25},{... | collective-permute-start | bytes 368648 | tf_op jit(solution)/shard_map/ppermute | solution.py:389
  22.4 8.7 %collective-permute-start.3 = (bf16[2,2,160,512]{3,2,1,0:T(8,128)(2,1)S(1)}, bf16[2,2,160,512]{3,2,1,0:T(8,128)(2,1)S(1)}, u32[]{:S(2)}, u32[]{:S(2)}) collective-permute-start(bf16[2,2,160,512]{3,2,1,0:T(8,128)(2,1)S(1)} %gate_up_0.1), channel_id=1, source_target_pairs={{0,1},{1,0},{2,3},{3,2},{4,5},{5,4},{6,7},{7,6},{8,9},{9,8},{10,11... | collective-permute-start | bytes 1966088 | tf_op jit(solution)/shard_map/ppermute | solution.py:376
  30.6 10.4 %collective-permute-start.8 = (bf16[2,2,160,512]{3,2,1,0:T(8,128)(2,1)S(1)}, bf16[2,2,160,512]{3,2,1,0:T(8,128)(2,1)S(1)}, u32[]{:S(2)}, u32[]{:S(2)}) collective-permute-start(bf16[2,2,160,512]{3,2,1,0:T(8,128)(2,1)S(1)} %get-tuple-element.57), channel_id=1, source_target_pairs={{0,1},{1,0},{2,3},{3,2},{4,5},{5,4},{6,7},{7,6},{8,9},{9,8},{10,11... | collective-permute-start | bytes 1966088 | tf_op jit(solution)/shard_map/ppermute | solution.py:376
  31.2 10.4 %collective-permute-start.4 = (bf16[2,160,512]{2,1,0:T(8,128)(2,1)S(1)}, bf16[2,160,512]{2,1,0:T(8,128)(2,1)S(1)}, u32[]{:S(2)}, u32[]{:S(2)}) collective-permute-start(bf16[2,160,512]{2,1,0:T(8,128)(2,1)S(1)} %fusion), channel_id=1, source_target_pairs={{0,2},{1,3},{2,0},{3,1},{4,6},{5,7},{6,4},{7,5},{8,10},{9,11},{10,... | collective-permute-start | bytes 983048 | tf_op jit(solution)/shard_map/ppermute | solution.py:379
  40.9 20.6 %collective-permute-start.21 = (bf16[2,2,160,512]{3,2,1,0:T(8,128)(2,1)S(1)}, bf16[2,2,160,512]{3,2,1,0:T(8,128)(2,1)S(1)}, u32[]{:S(2)}, u32[]{:S(2)}) collective-permute-start(bf16[2,2,160,512]{3,2,1,0:T(8,128)(2,1)S(1)} %get-tuple-element.66), channel_id=1, source_target_pairs={{0,1},{1,0},{2,3},{3,2},{4,5},{5,4},{6,7},{7,6},{8,9},{9,8},{10,11... | collective-permute-start | bytes 1966088 | tf_op jit(solution)/shard_map/ppermute | solution.py:376
  41.1 13.9 %collective-permute-start.9 = (bf16[2,160,512]{2,1,0:T(8,128)(2,1)S(1)}, bf16[2,160,512]{2,1,0:T(8,128)(2,1)S(1)}, u32[]{:S(2)}, u32[]{:S(2)}) collective-permute-start(bf16[2,160,512]{2,1,0:T(8,128)(2,1)S(1)} %fusion.1), channel_id=1, source_target_pairs={{0,2},{1,3},{2,0},{3,1},{4,6},{5,7},{6,4},{7,5},{8,10},{9,11},{10,... | collective-permute-start | bytes 983048 | tf_op jit(solution)/shard_map/ppermute | solution.py:379
  49.7 17.6 %collective-permute-start.10 = (bf16[2,2,160,512]{3,2,1,0:T(8,128)(2,1)S(1)}, bf16[2,2,160,512]{3,2,1,0:T(8,128)(2,1)S(1)}, u32[]{:S(2)}, u32[]{:S(2)}) collective-permute-start(bf16[2,2,160,512]{3,2,1,0:T(8,128)(2,1)S(1)} %get-tuple-element.58), channel_id=1, source_target_pairs={{0,1},{1,0},{2,3},{3,2},{4,5},{5,4},{6,7},{7,6},{8,9},{9,8},{10,11... | collective-permute-start | bytes 1966088 | tf_op jit(solution)/shard_map/ppermute | solution.py:376
  50.3 11.3 %collective-permute-start.15 = (bf16[160,512]{1,0:T(8,128)(2,1)S(1)}, bf16[160,512]{1,0:T(8,128)(2,1)S(1)}, u32[]{:S(2)}, u32[]{:S(2)}) collective-permute-start(bf16[160,512]{1,0:T(8,128)(2,1)S(1)} %fusion.11.rest_1_.own_ref), channel_id=1, source_target_pairs={{0,2},{1,3},{2,0},{3,1},{4,6},{5,7},{6,4},{7,5},{8,10},{9,11},{10,... | collective-permute-start | bytes 491528 | tf_op jit(solution)/shard_map/ppermute | solution.py:379
  51.9 17.4 %collective-permute-start.5 = (f32[4,128]{1,0:T(4,128)S(1)}, f32[4,128]{1,0:T(4,128)S(1)}, u32[]{:S(2)}, u32[]{:S(2)}) collective-permute-start(f32[4,128]{1,0:T(4,128)S(1)} %get-tuple-element.55.refs_0_), channel_id=1, source_target_pairs={{0,8},{4,12},{8,16},{12,20},{16,24},{20,28},{24,0},{28,4},{1,9},{5... | collective-permute-start | bytes 6152 | tf_op jit(solution)/shard_map/ppermute | solution.py:389
  55.0 14.8 %collective-permute-start.6 = (f32[4,128]{1,0:T(4,128)S(1)}, f32[4,128]{1,0:T(4,128)S(1)}, u32[]{:S(2)}, u32[]{:S(2)}) collective-permute-start(f32[4,128]{1,0:T(4,128)S(1)} %get-tuple-element.55.refs_0_), channel_id=1, source_target_pairs={{0,16},{4,20},{8,24},{12,28},{16,0},{20,4},{24,8},{28,12},{1,17},{... | collective-permute-start | bytes 6152 | tf_op jit(solution)/shard_map/ppermute | solution.py:389
  63.0 6.9 %collective-permute-start.7 = (f32[4,128]{1,0:T(4,128)S(1)}, f32[4,128]{1,0:T(4,128)S(1)}, u32[]{:S(2)}, u32[]{:S(2)}) collective-permute-start(f32[4,128]{1,0:T(4,128)S(1)} %get-tuple-element.55.refs_0_), channel_id=1, source_target_pairs={{0,24},{4,28},{8,0},{12,4},{16,8},{20,12},{24,16},{28,20},{1,25},{... | collective-permute-start | bytes 6152 | tf_op jit(solution)/shard_map/ppermute | solution.py:389
  64.6 10.6 %collective-permute-start.22 = (bf16[2,160,512]{2,1,0:T(8,128)(2,1)S(1)}, bf16[2,160,512]{2,1,0:T(8,128)(2,1)S(1)}, u32[]{:S(2)}, u32[]{:S(2)}) collective-permute-start(bf16[2,160,512]{2,1,0:T(8,128)(2,1)S(1)} %fusion.3), channel_id=1, source_target_pairs={{0,2},{1,3},{2,0},{3,1},{4,6},{5,7},{6,4},{7,5},{8,10},{9,11},{10,... | collective-permute-start | bytes 983048 | tf_op jit(solution)/shard_map/ppermute | solution.py:379
  67.5 20.8 %collective-permute-start.11 = (bf16[2,160,512]{2,1,0:T(8,128)(2,1)S(1)}, bf16[2,160,512]{2,1,0:T(8,128)(2,1)S(1)}, u32[]{:S(2)}, u32[]{:S(2)}) collective-permute-start(bf16[2,160,512]{2,1,0:T(8,128)(2,1)S(1)} %fusion.2), channel_id=1, source_target_pairs={{0,2},{1,3},{2,0},{3,1},{4,6},{5,7},{6,4},{7,5},{8,10},{9,11},{10,... | collective-permute-start | bytes 983048 | tf_op jit(solution)/shard_map/ppermute | solution.py:379
  69.3 15.3 %collective-permute-start.12 = (bf16[160,512]{1,0:T(8,128)(2,1)S(1)}, bf16[160,512]{1,0:T(8,128)(2,1)S(1)}, u32[]{:S(2)}, u32[]{:S(2)}) collective-permute-start(bf16[160,512]{1,0:T(8,128)(2,1)S(1)} %fusion.9.own_ref), channel_id=1, source_target_pairs={{0,2},{1,3},{2,0},{3,1},{4,6},{5,7},{6,4},{7,5},{8,10},{9,11},{10,... | collective-permute-start | bytes 491528 | tf_op jit(solution)/shard_map/ppermute | solution.py:379
  69.9 15.4 %collective-permute-start.13 = (bf16[160,512]{1,0:T(8,128)(2,1)S(1)}, bf16[160,512]{1,0:T(8,128)(2,1)S(1)}, u32[]{:S(2)}, u32[]{:S(2)}) collective-permute-start(bf16[160,512]{1,0:T(8,128)(2,1)S(1)} %fusion.9.own_ref), channel_id=1, source_target_pairs={{0,1},{1,0},{2,3},{3,2},{4,5},{5,4},{6,7},{7,6},{8,9},{9,8},{10,11... | collective-permute-start | bytes 491528 | tf_op jit(solution)/shard_map/ppermute | solution.py:376
  84.7 6.7 %collective-permute-start.23 = (bf16[160,512]{1,0:T(8,128)(2,1)S(1)}, bf16[160,512]{1,0:T(8,128)(2,1)S(1)}, u32[]{:S(2)}, u32[]{:S(2)}) collective-permute-start(bf16[160,512]{1,0:T(8,128)(2,1)S(1)} %fusion.5.own_ref), channel_id=1, source_target_pairs={{0,2},{1,3},{2,0},{3,1},{4,6},{5,7},{6,4},{7,5},{8,10},{9,11},{10,... | collective-permute-start | bytes 491528 | tf_op jit(solution)/shard_map/ppermute | solution.py:379
  88.5 6.3 %collective-permute-start.18 = (bf16[160,512]{1,0:T(8,128)(2,1)S(1)}, bf16[160,512]{1,0:T(8,128)(2,1)S(1)}, u32[]{:S(2)}, u32[]{:S(2)}) collective-permute-start(bf16[160,512]{1,0:T(8,128)(2,1)S(1)} %fusion.7.own_ref), channel_id=1, source_target_pairs={{0,2},{1,3},{2,0},{3,1},{4,6},{5,7},{6,4},{7,5},{8,10},{9,11},{10,... | collective-permute-start | bytes 491528 | tf_op jit(solution)/shard_map/ppermute | solution.py:379
  100.6 6.8 %collective-permute-start.26 = (bf16[160,256]{1,0:T(8,128)(2,1)S(1)}, bf16[160,256]{1,0:T(8,128)(2,1)S(1)}, u32[]{:S(2)}, u32[]{:S(2)}) collective-permute-start(bf16[160,256]{1,0:T(8,128)(2,1)S(1)} %get-tuple-element.78), channel_id=1, source_target_pairs={{0,4},{4,0},{8,12},{12,8},{16,20},{20,16},{24,28},{28,24},{1,5},{5... | collective-permute-start | bytes 245768 | tf_op jit(solution)/shard_map/ppermute | solution.py:389
  102.1 8.1 %collective-permute-start.27 = (bf16[160,256]{1,0:T(8,128)(2,1)S(1)}, bf16[160,256]{1,0:T(8,128)(2,1)S(1)}, u32[]{:S(2)}, u32[]{:S(2)}) collective-permute-start(bf16[160,256]{1,0:T(8,128)(2,1)S(1)} %get-tuple-element.79), channel_id=1, source_target_pairs={{0,8},{4,12},{8,16},{12,20},{16,24},{20,28},{24,0},{28,4},{1,9},{5... | collective-permute-start | bytes 245768 | tf_op jit(solution)/shard_map/ppermute | solution.py:389
  102.6 12.0 %collective-permute-start.28 = (bf16[160,256]{1,0:T(8,128)(2,1)S(1)}, bf16[160,256]{1,0:T(8,128)(2,1)S(1)}, u32[]{:S(2)}, u32[]{:S(2)}) collective-permute-start(bf16[160,256]{1,0:T(8,128)(2,1)S(1)} %get-tuple-element.80), channel_id=1, source_target_pairs={{0,12},{4,8},{8,20},{12,16},{16,28},{20,24},{24,4},{28,0},{1,13},{... | collective-permute-start | bytes 245768 | tf_op jit(solution)/shard_map/ppermute | solution.py:389
  103.4 12.3 %collective-permute-start.29 = (bf16[160,256]{1,0:T(8,128)(2,1)S(1)}, bf16[160,256]{1,0:T(8,128)(2,1)S(1)}, u32[]{:S(2)}, u32[]{:S(2)}) collective-permute-start(bf16[160,256]{1,0:T(8,128)(2,1)S(1)} %get-tuple-element.81), channel_id=1, source_target_pairs={{0,16},{4,20},{8,24},{12,28},{16,0},{20,4},{24,8},{28,12},{1,17},{... | collective-permute-start | bytes 245768 | tf_op jit(solution)/shard_map/ppermute | solution.py:389
  106.5 10.9 %collective-permute-start.30 = (bf16[160,256]{1,0:T(8,128)(2,1)S(1)}, bf16[160,256]{1,0:T(8,128)(2,1)S(1)}, u32[]{:S(2)}, u32[]{:S(2)}) collective-permute-start(bf16[160,256]{1,0:T(8,128)(2,1)S(1)} %get-tuple-element.82), channel_id=1, source_target_pairs={{0,20},{4,16},{8,28},{12,24},{16,4},{20,0},{24,12},{28,8},{1,21},{... | collective-permute-start | bytes 245768 | tf_op jit(solution)/shard_map/ppermute | solution.py:389
  107.4 10.0 %collective-permute-start.31 = (bf16[160,256]{1,0:T(8,128)(2,1)S(1)}, bf16[160,256]{1,0:T(8,128)(2,1)S(1)}, u32[]{:S(2)}, u32[]{:S(2)}) collective-permute-start(bf16[160,256]{1,0:T(8,128)(2,1)S(1)} %get-tuple-element.83), channel_id=1, source_target_pairs={{0,24},{4,28},{8,0},{12,4},{16,8},{20,12},{24,16},{28,20},{1,25},{... | collective-permute-start | bytes 245768 | tf_op jit(solution)/shard_map/ppermute | solution.py:389
  110.2 7.9 %collective-permute-start.32 = (bf16[160,256]{1,0:T(8,128)(2,1)S(1)}, bf16[160,256]{1,0:T(8,128)(2,1)S(1)}, u32[]{:S(2)}, u32[]{:S(2)}) collective-permute-start(bf16[160,256]{1,0:T(8,128)(2,1)S(1)} %get-tuple-element.84), channel_id=1, source_target_pairs={{0,28},{4,24},{8,4},{12,0},{16,12},{20,8},{24,20},{28,16},{1,29},{... | collective-permute-start | bytes 245768 | tf_op jit(solution)/shard_map/ppermute | solution.py:389
  135.6 5.9 %collective-permute-start.33 = (bf16[96,128]{1,0:T(8,128)(2,1)S(1)}, bf16[96,128]{1,0:T(8,128)(2,1)S(1)}, u32[]{:S(2)}, u32[]{:S(2)}) collective-permute-start(bf16[96,128]{1,0:T(8,128)(2,1)S(1)} %get-tuple-element.89.refs_0_), channel_id=1, source_target_pairs={{0,4},{4,0},{8,12},{12,8},{16,20},{20,16},{24,28},{28,24},{1,5},{5... | collective-permute-start | bytes 73736 | tf_op jit(solution)/shard_map/ppermute | solution.py:389
  136.2 8.2 %collective-permute-start.34 = (bf16[96,128]{1,0:T(8,128)(2,1)S(1)}, bf16[96,128]{1,0:T(8,128)(2,1)S(1)}, u32[]{:S(2)}, u32[]{:S(2)}) collective-permute-start(bf16[96,128]{1,0:T(8,128)(2,1)S(1)} %get-tuple-element.90), channel_id=1, source_target_pairs={{0,8},{4,12},{8,16},{12,20},{16,24},{20,28},{24,0},{28,4},{1,9},{5... | collective-permute-start | bytes 73736 | tf_op jit(solution)/shard_map/ppermute | solution.py:389
  136.8 10.0 %collective-permute-start.35 = (bf16[96,128]{1,0:T(8,128)(2,1)S(1)}, bf16[96,128]{1,0:T(8,128)(2,1)S(1)}, u32[]{:S(2)}, u32[]{:S(2)}) collective-permute-start(bf16[96,128]{1,0:T(8,128)(2,1)S(1)} %get-tuple-element.90), channel_id=1, source_target_pairs={{0,12},{4,8},{8,20},{12,16},{16,28},{20,24},{24,4},{28,0},{1,13},{... | collective-permute-start | bytes 73736 | tf_op jit(solution)/shard_map/ppermute | solution.py:389
  138.3 8.5 %collective-permute-start.36 = (bf16[96,128]{1,0:T(8,128)(2,1)S(1)}, bf16[96,128]{1,0:T(8,128)(2,1)S(1)}, u32[]{:S(2)}, u32[]{:S(2)}) collective-permute-start(bf16[96,128]{1,0:T(8,128)(2,1)S(1)} %get-tuple-element.91), channel_id=1, source_target_pairs={{0,16},{4,20},{8,24},{12,28},{16,0},{20,4},{24,8},{28,12},{1,17},{... | collective-permute-start | bytes 73736 | tf_op jit(solution)/shard_map/ppermute | solution.py:389
  141.5 5.9 %collective-permute-start.37 = (bf16[96,128]{1,0:T(8,128)(2,1)S(1)}, bf16[96,128]{1,0:T(8,128)(2,1)S(1)}, u32[]{:S(2)}, u32[]{:S(2)}) collective-permute-start(bf16[96,128]{1,0:T(8,128)(2,1)S(1)} %get-tuple-element.91), channel_id=1, source_target_pairs={{0,20},{4,16},{8,28},{12,24},{16,4},{20,0},{24,12},{28,8},{1,21},{... | collective-permute-start | bytes 73736 | tf_op jit(solution)/shard_map/ppermute | solution.py:389
  141.5 5.9 %collective-permute-start.38 = (bf16[96,128]{1,0:T(8,128)(2,1)S(1)}, bf16[96,128]{1,0:T(8,128)(2,1)S(1)}, u32[]{:S(2)}, u32[]{:S(2)}) collective-permute-start(bf16[96,128]{1,0:T(8,128)(2,1)S(1)} %get-tuple-element.92), channel_id=1, source_target_pairs={{0,24},{4,28},{8,0},{12,4},{16,8},{20,12},{24,16},{28,20},{1,25},{... | collective-permute-start | bytes 73736 | tf_op jit(solution)/shard_map/ppermute | solution.py:389
  (16 other events, 97.4 us)

commit v4 on v3

--- a/solution.py
+++ b/solution.py
@@ -103,58 +103,50 @@
     return jnp.concatenate([values[:, :main].T, tail], axis=0)
 
 
-def gate_up_kernel(has_keep, order_ref, inputs_ref, gate_ref, up_ref, *rest):
+def gate_up_kernel(plan, order_ref, inputs_ref, gate_ref, up_ref, *rest):
+    outs, (weights, sems) = rest[-2 - len(plan) // 2 : -2], rest[-2:]
+    width = weights.shape[2]
+    copies = []
+    for step, (slot, chunk) in enumerate(plan):
+        rows = pl.ds(chunk * width, width)
+        for kind, ref in enumerate((gate_ref, up_ref)):
+            copy = pltpu.make_async_copy(
+                ref.at[order_ref[slot], rows], weights.at[step, kind], sems.at[step, kind]
+            )
+            copy.start()
+            copies.append(copy)
     values = inputs_ref[...]
-    gate = turned(mm(gate_ref[...], values).astype(bf16))
-    up = turned(mm(up_ref[...], values).astype(bf16))
-    step = pl.program_id(0)
-    outs = rest[-(1 + (has_keep == 2)) :]
-    for index, ref in enumerate(outs):
-
-        @pl.when(step // 2 == index)
-        def _(ref=ref):
-            ref[0, 0] = gate
-            ref[0, 1] = up
+    for step in range(len(plan)):
+        for kind in range(2):
+            copies[2 * step + kind].wait()
+            outs[step // 2][step % 2, kind] = turned(mm(weights[step, kind], values).astype(bf16))
 
 
 def gate_up(order, inputs, gate_weight, up_weight, width, keep, send, after):
     depth, slots = inputs.shape
     quarter = gate_weight.shape[0] // 4
-    gate_weight = gate_weight.reshape(4, quarter, depth)
-    up_weight = up_weight.reshape(4, quarter, depth)
-    base = 0 if keep is not None else 2
-    chunks = [chunk for chunk in (keep, send) if chunk is not None]
-    count = len(chunks)
-
-    def place(s, order):
-        return (order[base + s], chunks[0] if count == 1 else jnp.where(s < 2, chunks[0], chunks[1]), 0)
-
-    weight_spec = pl.BlockSpec((None, width, depth), place)
-    out_specs = [
-        pl.BlockSpec(
-            (1, 2, slots, width),
-            lambda s, order, index=index: (jnp.clip(s - 2 * index, 0, 1), 0, 0, 0),
-        )
-        for index in range(count)
-    ]
+    plan = [(0, keep), (1, keep)] if keep is not None else []
+    plan = plan + ([(2, send), (3, send)] if send is not None else [])
+    anywhere = pl.BlockSpec(memory_space=pl.ANY)
     return pl.pallas_call(
-        functools.partial(gate_up_kernel, count),
-        grid_spec=pltpu.PrefetchScalarGridSpec(
-            num_scalar_prefetch=1,
-            grid=(2 * count,),
-            in_specs=[
-                pl.BlockSpec((depth, slots), lambda s, order: (0, 0)),
-                weight_spec,
-                weight_spec,
-            ]
-            + [pl.BlockSpec(memory_space=pl.ANY)] * len(after),
-            out_specs=out_specs,
-        ),
-        out_shape=[jax.ShapeDtypeStruct((2, 2, slots, width), bf16)] * count,
+        functools.partial(gate_up_kernel, plan),
+        in_specs=[scalars(), whole(), anywhere, anywhere] + [anywhere] * len(after),
+        out_specs=[whole()] * (len(plan) // 2),
+        out_shape=[jax.ShapeDtypeStruct((2, 2, slots, width), bf16)] * (len(plan) // 2),
+        scratch_shapes=[
+            pltpu.VMEM((len(plan), 2, width, depth), bf16),
+            pltpu.SemaphoreType.DMA((len(plan), 2)),
+        ],
         compiler_params=params(41),
         cost_estimate=LIGHT,
-        name=f"gate_up_{chunks[-1] + (send is None)}",
-    )(order, inputs, gate_weight, up_weight, *after)
+        name=f"gate_up_{plan[-1][1] + (send is None)}",
+    )(
+        order,
+        inputs,
+        gate_weight.reshape(4, quarter, depth),
+        up_weight.reshape(4, quarter, depth),
+        *after,
+    )
 
 
 def down_kernel(pack, has_old, order_ref, place_ref, own_ref, across_ref, beside_ref, both_ref, down_ref, *rest):
@@ -435,14 +427,15 @@
         keeps.append(keep)
         pairs.append((keep[0].astype(f32) + nears[chunk][0].astype(f32)).astype(bf16))
         fars.append(across(pairs[-1]))
-    info = lax.optimization_barrier((info, owns[0]))[0]
-    infos = [shifted(info, ahead) for ahead in range(dp_count)]
     older, olders = (), []
     for chunk in range(CHUNKS):
         if chunk >= len(owns):
             after = [pairs[last]]
             if chunk >= 2:
                 after.append(olders[chunk - 2][2])
+            if chunk == last:
+                info = lax.optimization_barrier((info, owns[chunk - 1]))[0]
+                infos = [shifted(info, ahead) for ahead in range(dp_count)]
                 after.extend(infos[1:])
             activate(chunk, after)
         own = owns[chunk]

time: 151 us -> 157 us (1.040)
  Pallas kernels: 54.2 us -> 66.4 us
  waiting for transfers between devices: 33.1 us -> 26.4 us
    pallas_call x5, Pallas kernels: 33.9 us -> 46.2 us  [gate_up(): pl.pallas_call(functools.partial(gate_up_kernel, plan), in_specs=[scalars...]
    ppermute x8, waiting for transfers between devices: 19.6 us -> 14.1 us  [across(): return lax.ppermute(values, 'col', [(k, k ^ 2) for k in range(4)])]
  transfers between devices with their start and end apart: 40 -> 40, of which waited for: 13 -> 12; matrix products, arithmetic and copies ran while one was open for 2% -> 2% of each run, Pallas kernels for 25% -> 31%
where the time goes in v4:
time: 157 us; the launch traced here: 156 us
  Pallas kernels  66.4 us (42%)
  starting transfers between devices  45.9 us (29%)
  waiting for transfers between devices  26.4 us (17%)
  blocking collectives  11.7 us (7%)
  other arithmetic  2.59 us (2%)
  local copies, waits for them, and re-layouts  2.38 us (2%)
    pallas_call x5, Pallas kernels, gate_up(): pl.pallas_call(functools.partial(gate_up_kernel, plan), in_specs=[scalars...  46.2 us
    ppermute x20, starting transfers between devices, shifted(): return lax.ppermute(values, ('dp', 'tensor'), pairs)  35 us
    ppermute x8, waiting for transfers between devices, across(): return lax.ppermute(values, 'col', [(k, k ^ 2) for k in range(4)])  14.1 us
    ppermute x20, waiting for transfers between devices, shifted(): return lax.ppermute(values, ('dp', 'tensor'), pairs)  12.3 us
    all_to_all x1, blocking collectives, one_expert_each(): lax.all_to_all(sums, ('dp', 'tensor', 'col'), split_axis=0, concat_axis=0...  11.7 us
    pallas_call x4, Pallas kernels, down(): pl.pallas_call(functools.partial(down_kernel, pack, bool(older)), grid_sp...  10.3 us
    ppermute x8, starting transfers between devices, across(): return lax.ppermute(values, 'col', [(k, k ^ 2) for k in range(4)])  9.39 us
    pallas_call x1, Pallas kernels, one_expert_each(): single(functools.partial(solve_kernel, ridge, slots), [field, field, fiel...  5.35 us
  transfers between devices with their start and end apart: 40, of which 12 were waited for; matrix products, arithmetic and copies ran while one was open for 2% of the time, Pallas kernels for 31%

profile of v4, /device:TPU:0, one launch (start us, length us, event | category | flops | bytes accessed | tf_op | source)
XLA Modules:
  0.0 156.4 jit_solution(2137067650727497644)
XLA Ops:
  3.5 3.1 %collective-permute-start = (bf16[40,1536]{1,0:T(8,128)(2,1)S(1)}, bf16[40,1536]{1,0:T(8,128)(2,1)S(1)}, u32[]{:S(2)}, u32[]{:S(2)}) collective-permute-start(bf16[40,1536]{1,0:T(8,128)(2,1)S(1)} %get-tuple-element.51), channel_id=1, source_target_pairs={{0,8},{4,12},{8,16},{12,20},{16,24},{20,28},{24,0},{28,4},{1,9},{5... | collective-permute-start | bytes 368648 | tf_op jit(solution)/shard_map/ppermute | solution.py:381
  6.5 2.6 %collective-permute-start.1 = (bf16[40,1536]{1,0:T(8,128)(2,1)S(1)}, bf16[40,1536]{1,0:T(8,128)(2,1)S(1)}, u32[]{:S(2)}, u32[]{:S(2)}) collective-permute-start(bf16[40,1536]{1,0:T(8,128)(2,1)S(1)} %get-tuple-element.52), channel_id=1, source_target_pairs={{0,16},{4,20},{8,24},{12,28},{16,0},{20,4},{24,8},{28,12},{1,17},{... | collective-permute-start | bytes 368648 | tf_op jit(solution)/shard_map/ppermute | solution.py:381
  11.1 1.7 %collective-permute-done.refs_1_ = bf16[40,1536]{1,0:T(8,128)(2,1)S(1)} collective-permute-done((bf16[40,1536]{1,0:T(8,128)(2,1)S(1)}, bf16[40,1536]{1,0:T(8,128)(2,1)S(1)}, u32[]{:S(2)}, u32[]{:S(2)}) %collective-permute-start) | collective-permute-done | bytes 122912 | tf_op jit(solution)/shard_map/ppermute | solution.py:381
  12.8 4.4 %collective-permute-done.1.refs_2_ = bf16[40,1536]{1,0:T(8,128)(2,1)S(1)} collective-permute-done((bf16[40,1536]{1,0:T(8,128)(2,1)S(1)}, bf16[40,1536]{1,0:T(8,128)(2,1)S(1)}, u32[]{:S(2)}, u32[]{:S(2)}) %collective-permute-start.1) | collective-permute-done | bytes 122912 | tf_op jit(solution)/shard_map/ppermute | solution.py:381
  17.5 6.4 %gate_up_0.1 = bf16[2,2,160,512]{3,2,1,0:T(8,128)(2,1)S(1)} custom-call(s32[4]{0:T(128)S(1)} %broadcast_xor_fusion.1.order_ref, bf16[1536,160]{1,0:T(8,128)(2,1)S(1)} %turn.1.inputs_ref, bf16[4,2048,1536]{2,1,0:T(8,128)(2,1)} %bitcast.72, bf16[4,2048,1536]{2,1,0:T(8,128)(2,1)} %bitcast.77), custom_call_target="tpu_custom_call" | custom-call | flops 1 | bytes 1 | tf_op jit(solution)/shard_map/gate_up_0/pallas_call | solution.py:131
  24.0 10.8 %gate_up_1.1 = (bf16[2,2,160,512]{3,2,1,0:T(8,128)(2,1)S(1)}, bf16[2,2,160,512]{3,2,1,0:T(8,128)(2,1)S(1)}) custom-call(s32[4]{0:T(128)S(1)} %broadcast_xor_fusion.1.order_ref, bf16[1536,160]{1,0:T(8,128)(2,1)S(1)} %turn.1.inputs_ref, bf16[4,2048,1536]{2,1,0:T(8,128)(2,1)} %bitcast.73, bf16[4,2048,1536]{2,1,0:T(8,128)(2,1)} %bitcast.78), custom_call_target="tpu_custom_call" | custom-call | flops 1 | bytes 1 | tf_op jit(solution)/shard_map/gate_up_1/pallas_call | solution.py:131
  37.1 10.8 %gate_up_2.1 = (bf16[2,2,160,512]{3,2,1,0:T(8,128)(2,1)S(1)}, bf16[2,2,160,512]{3,2,1,0:T(8,128)(2,1)S(1)}) custom-call(s32[4]{0:T(128)S(1)} %broadcast_xor_fusion.1.order_ref, bf16[1536,160]{1,0:T(8,128)(2,1)S(1)} %turn.1.inputs_ref, bf16[4,2048,1536]{2,1,0:T(8,128)(2,1)} %bitcast.74, bf16[4,2048,1536]{2,1,0:T(8,128)(2,1)} %bitcast.79), custom_call_target="tpu_custom_call" | custom-call | flops 1 | bytes 1 | tf_op jit(solution)/shard_map/gate_up_2/pallas_call | solution.py:131
  48.7 11.0 %gate_up_3.1 = (bf16[2,2,160,512]{3,2,1,0:T(8,128)(2,1)S(1)}, bf16[2,2,160,512]{3,2,1,0:T(8,128)(2,1)S(1)}) custom-call(s32[4]{0:T(128)S(1)} %broadcast_xor_fusion.1.order_ref, bf16[1536,160]{1,0:T(8,128)(2,1)S(1)} %turn.1.inputs_ref, bf16[4,2048,1536]{2,1,0:T(8,128)(2,1)} %bitcast.75, bf16[4,2048,1536]{2,1,0:T(8,128)(2,1)} %bitcast.80, ...), custom_call_target="tpu_custom_call" | custom-call | flops 1 | bytes 1 | tf_op jit(solution)/shard_map/gate_up_3/pallas_call | solution.py:131
  60.2 1.6 %collective-permute-start.10 = (bf16[160,512]{1,0:T(8,128)(2,1)S(1)}, bf16[160,512]{1,0:T(8,128)(2,1)S(1)}, u32[]{:S(2)}, u32[]{:S(2)}) collective-permute-start(bf16[160,512]{1,0:T(8,128)(2,1)S(1)} %fusion.11.rest_1_.own_ref), channel_id=1, source_target_pairs={{0,2},{1,3},{2,0},{3,1},{4,6},{5,7},{6,4},{7,5},{8,10},{9,11},{10,... | collective-permute-start | bytes 491528 | tf_op jit(solution)/shard_map/ppermute | solution.py:371
  61.8 4.9 %collective-permute-done.10.across_ref = bf16[160,512]{1,0:T(8,128)(2,1)S(1)} collective-permute-done((bf16[160,512]{1,0:T(8,128)(2,1)S(1)}, bf16[160,512]{1,0:T(8,128)(2,1)S(1)}, u32[]{:S(2)}, u32[]{:S(2)}) %collective-permute-start.10) | collective-permute-done | bytes 163872 | tf_op jit(solution)/shard_map/ppermute | solution.py:371
  66.8 1.6 %collective-permute-start.6 = (bf16[2,160,512]{2,1,0:T(8,128)(2,1)S(1)}, bf16[2,160,512]{2,1,0:T(8,128)(2,1)S(1)}, u32[]{:S(2)}, u32[]{:S(2)}) collective-permute-start(bf16[2,160,512]{2,1,0:T(8,128)(2,1)S(1)} %fusion.1), channel_id=1, source_target_pairs={{0,2},{1,3},{2,0},{3,1},{4,6},{5,7},{6,4},{7,5},{8,10},{9,11},{10,... | collective-permute-start | bytes 983048 | tf_op jit(solution)/shard_map/ppermute | solution.py:371
  68.4 7.2 %gate_up_4.1 = bf16[2,2,160,512]{3,2,1,0:T(8,128)(2,1)S(1)} custom-call(s32[4]{0:T(128)S(1)} %broadcast_xor_fusion.1.order_ref, bf16[1536,160]{1,0:T(8,128)(2,1)S(1)} %turn.1.inputs_ref, bf16[4,2048,1536]{2,1,0:T(8,128)(2,1)} %bitcast.76, bf16[4,2048,1536]{2,1,0:T(8,128)(2,1)} %bitcast.81, bf16[2,160,512]{2,1,0:T(8,128)(2,1)S(1)} %collective-permute-done.8.rest_0_, ...), custom_call_target="tpu_custom_call" | custom-call | flops 1 | bytes 1 | tf_op jit(solution)/shard_map/gate_up_4/pallas_call | solution.py:131
  75.6 2.3 %down_0.1 = (f32[160,768]{1,0:T(8,128)S(1)}, f32[160,160]{1,0:T(8,128)S(1)}, f32[8,768]{1,0:T(8,128)S(1)}) custom-call(s32[4]{0:T(128)S(1)} %broadcast_xor_fusion.order_ref, s32[2]{0:T(128)S(1)} %pad_add_fusion.place_ref, bf16[160,512]{1,0:T(8,128)(2,1)S(1)} %fusion.11.rest_1_.own_ref, bf16[160,512]{1,0:T(8,128)(2,1)S(1)} %collective-permute-done.10.across_ref, ...), custom_call_target="tpu_custom_call" | custom-call | flops 1 | bytes 1 | tf_op jit(solution)/shard_map/down_0/pallas_call | solution.py:212
  78.6 1.7 %collective-permute-start.16 = (bf16[2,160,512]{2,1,0:T(8,128)(2,1)S(1)}, bf16[2,160,512]{2,1,0:T(8,128)(2,1)S(1)}, u32[]{:S(2)}, u32[]{:S(2)}) collective-permute-start(bf16[2,160,512]{2,1,0:T(8,128)(2,1)S(1)} %fusion.3), channel_id=1, source_target_pairs={{0,2},{1,3},{2,0},{3,1},{4,6},{5,7},{6,4},{7,5},{8,10},{9,11},{10,... | collective-permute-start | bytes 983048 | tf_op jit(solution)/shard_map/ppermute | solution.py:371
  80.4 4.9 %collective-permute-done.17.across_ref = bf16[160,512]{1,0:T(8,128)(2,1)S(1)} collective-permute-done((bf16[160,512]{1,0:T(8,128)(2,1)S(1)}, bf16[160,512]{1,0:T(8,128)(2,1)S(1)}, u32[]{:S(2)}, u32[]{:S(2)}) %collective-permute-start.17) | collective-permute-done | bytes 163872 | tf_op jit(solution)/shard_map/ppermute | solution.py:371
  85.4 3.2 %collective-permute-start.13 = (f32[4,128]{1,0:T(4,128)S(1)}, f32[4,128]{1,0:T(4,128)S(1)}, u32[]{:S(2)}, u32[]{:S(2)}) collective-permute-start(f32[4,128]{1,0:T(4,128)S(1)} %get-tuple-element.62.refs_0_), channel_id=1, source_target_pairs={{0,8},{4,12},{8,16},{12,20},{16,24},{20,28},{24,0},{28,4},{1,9},{5... | collective-permute-start | bytes 6152 | tf_op jit(solution)/shard_map/ppermute | solution.py:381
  88.6 1.6 %collective-permute-start.14 = (f32[4,128]{1,0:T(4,128)S(1)}, f32[4,128]{1,0:T(4,128)S(1)}, u32[]{:S(2)}, u32[]{:S(2)}) collective-permute-start(f32[4,128]{1,0:T(4,128)S(1)} %get-tuple-element.62.refs_0_), channel_id=1, source_target_pairs={{0,16},{4,20},{8,24},{12,28},{16,0},{20,4},{24,8},{28,12},{1,17},{... | collective-permute-start | bytes 6152 | tf_op jit(solution)/shard_map/ppermute | solution.py:381
  91.3 2.3 %down_1.1 = (f32[160,768]{1,0:T(8,128)S(1)}, f32[160,160]{1,0:T(8,128)S(1)}, f32[8,768]{1,0:T(8,128)S(1)}) custom-call(s32[4]{0:T(128)S(1)} %broadcast_xor_fusion.order_ref, s32[2]{0:T(128)S(1)} %pad_add_fusion.place_ref, bf16[160,512]{1,0:T(8,128)(2,1)S(1)} %fusion.7.own_ref, bf16[160,512]{1,0:T(8,128)(2,1)S(1)} %collective-permute-done.17.across_ref, ...), custom_call_target="tpu_custom_call" | custom-call | flops 1 | bytes 1 | tf_op jit(solution)/shard_map/down_1/pallas_call | solution.py:212
  94.0 1.7 %collective-permute-start.20 = (bf16[160,512]{1,0:T(8,128)(2,1)S(1)}, bf16[160,512]{1,0:T(8,128)(2,1)S(1)}, u32[]{:S(2)}, u32[]{:S(2)}) collective-permute-start(bf16[160,512]{1,0:T(8,128)(2,1)S(1)} %fusion.5.own_ref), channel_id=1, source_target_pairs={{0,2},{1,3},{2,0},{3,1},{4,6},{5,7},{6,4},{7,5},{8,10},{9,11},{10,... | collective-permute-start | bytes 491528 | tf_op jit(solution)/shard_map/ppermute | solution.py:371
  95.7 2.2 %collective-permute-done.23.across_ref = bf16[160,512]{1,0:T(8,128)(2,1)S(1)} collective-permute-done((bf16[160,512]{1,0:T(8,128)(2,1)S(1)}, bf16[160,512]{1,0:T(8,128)(2,1)S(1)}, u32[]{:S(2)}, u32[]{:S(2)}) %collective-permute-start.23) | collective-permute-done | bytes 163872 | tf_op jit(solution)/shard_map/ppermute | solution.py:371
  98.4 2.2 %collective-permute-done.20.across_ref = bf16[160,512]{1,0:T(8,128)(2,1)S(1)} collective-permute-done((bf16[160,512]{1,0:T(8,128)(2,1)S(1)}, bf16[160,512]{1,0:T(8,128)(2,1)S(1)}, u32[]{:S(2)}, u32[]{:S(2)}) %collective-permute-start.20) | collective-permute-done | bytes 163872 | tf_op jit(solution)/shard_map/ppermute | solution.py:371
  100.6 2.3 %down_2.1 = (f32[160,768]{1,0:T(8,128)S(1)}, f32[160,160]{1,0:T(8,128)S(1)}, f32[8,768]{1,0:T(8,128)S(1)}) custom-call(s32[4]{0:T(128)S(1)} %broadcast_xor_fusion.order_ref, s32[2]{0:T(128)S(1)} %pad_add_fusion.place_ref, bf16[160,512]{1,0:T(8,128)(2,1)S(1)} %fusion.9.own_ref, bf16[160,512]{1,0:T(8,128)(2,1)S(1)} %collective-permute-done.23.across_ref, ...), custom_call_target="tpu_custom_call" | custom-call | flops 1 | bytes 1 | tf_op jit(solution)/shard_map/down_2/pallas_call | solution.py:212
  102.9 3.4 %down_3.1 = (bf16[160,256]{1,0:T(8,128)(2,1)S(1)}, bf16[160,256]{1,0:T(8,128)(2,1)S(1)}, bf16[160,256]{1,0:T(8,128)(2,1)S(1)}, bf16[160,256]{1,0:T(8,128)(2,1)S(...) custom-call(s32[4]{0:T(128)S(1)} %broadcast_xor_fusion.order_ref, ...), custom_call_target="tpu_custom_call" | custom-call | flops 1 | bytes 1 | tf_op jit(solution)/shard_map/down_3/pallas_call | solution.py:212
  109.1 3.1 %collective-permute-start.29 = (bf16[160,256]{1,0:T(8,128)(2,1)S(1)}, bf16[160,256]{1,0:T(8,128)(2,1)S(1)}, u32[]{:S(2)}, u32[]{:S(2)}) collective-permute-start(bf16[160,256]{1,0:T(8,128)(2,1)S(1)} %get-tuple-element.81), channel_id=1, source_target_pairs={{0,16},{4,20},{8,24},{12,28},{16,0},{20,4},{24,8},{28,12},{1,17},{... | collective-permute-start | bytes 245768 | tf_op jit(solution)/shard_map/ppermute | solution.py:381
  113.1 3.5 %collective-permute-start.31 = (bf16[160,256]{1,0:T(8,128)(2,1)S(1)}, bf16[160,256]{1,0:T(8,128)(2,1)S(1)}, u32[]{:S(2)}, u32[]{:S(2)}) collective-permute-start(bf16[160,256]{1,0:T(8,128)(2,1)S(1)} %get-tuple-element.83), channel_id=1, source_target_pairs={{0,24},{4,28},{8,0},{12,4},{16,8},{20,12},{24,16},{28,20},{1,25},{... | collective-permute-start | bytes 245768 | tf_op jit(solution)/shard_map/ppermute | solution.py:381
  121.4 1.7 %collective-permute-done.30.refs_5_ = bf16[160,256]{1,0:T(8,128)(2,1)S(1)} collective-permute-done((bf16[160,256]{1,0:T(8,128)(2,1)S(1)}, bf16[160,256]{1,0:T(8,128)(2,1)S(1)}, u32[]{:S(2)}, u32[]{:S(2)}) %collective-permute-start.30) | collective-permute-done | bytes 81952 | tf_op jit(solution)/shard_map/ppermute | solution.py:381
  123.9 5.3 %solve.1 = (f32[512,96]{1,0:T(8,128)S(1)}, f32[512,96]{1,0:T(8,128)S(1)}, f32[512,96]{1,0:T(8,128)S(1)}, f32[32,1,128]{2,1,0:T(1,128)S(1)}) custom-call(f32[1]{0:T(128)} %bitcast.2.own_ref, bf16[1280,512]{1,0:T(8,128)(2,1)S(1)} %get-tuple-element.74.hot_ref, bf16[512,1280]{1,0:T(8,128)(2,1)S(1)} %get-tuple-element.75.turned_ref, ...), custom_call_target="tpu_custom_call" | custom-call | flops 1 | bytes 1 | tf_op jit(solution)/shard_map/solve/pallas_call | solution.py:472
  129.3 11.7 %all_to_all.5.sums_ref = f32[32,1,128]{2,1,0:T(1,128)S(1)} all-to-all(f32[32,1,128]{2,1,0:T(1,128)S(1)} %get-tuple-element.88), channel_id=1, replica_groups=mesh['dp'=4,'tensor'=2,'col'=4] {'dp','tensor','col'}, dimensions={0} | all-to-all | bytes 32768 | tf_op jit(solution)/shard_map/all_to_all | solution.py:479
  144.0 3.2 %collective-permute-start.36 = (bf16[96,128]{1,0:T(8,128)(2,1)S(1)}, bf16[96,128]{1,0:T(8,128)(2,1)S(1)}, u32[]{:S(2)}, u32[]{:S(2)}) collective-permute-start(bf16[96,128]{1,0:T(8,128)(2,1)S(1)} %get-tuple-element.91), channel_id=1, source_target_pairs={{0,16},{4,20},{8,24},{12,28},{16,0},{20,4},{24,8},{28,12},{1,17},{... | collective-permute-start | bytes 73736 | tf_op jit(solution)/shard_map/ppermute | solution.py:381
  147.3 2.9 %collective-permute-start.38 = (bf16[96,128]{1,0:T(8,128)(2,1)S(1)}, bf16[96,128]{1,0:T(8,128)(2,1)S(1)}, u32[]{:S(2)}, u32[]{:S(2)}) collective-permute-start(bf16[96,128]{1,0:T(8,128)(2,1)S(1)} %get-tuple-element.92), channel_id=1, source_target_pairs={{0,24},{4,28},{8,0},{12,4},{16,8},{20,12},{24,16},{28,20},{1,25},{... | collective-permute-start | bytes 73736 | tf_op jit(solution)/shard_map/ppermute | solution.py:381
  150.2 2.4 %collective-permute-start.39 = (bf16[96,128]{1,0:T(8,128)(2,1)S(1)}, bf16[96,128]{1,0:T(8,128)(2,1)S(1)}, u32[]{:S(2)}, u32[]{:S(2)}) collective-permute-start(bf16[96,128]{1,0:T(8,128)(2,1)S(1)} %get-tuple-element.92), channel_id=1, source_target_pairs={{0,28},{4,24},{8,4},{12,0},{16,12},{20,8},{24,20},{28,16},{1,29},{... | collective-permute-start | bytes 73736 | tf_op jit(solution)/shard_map/ppermute | solution.py:381
  153.1 1.8 %collective-permute-done.39.refs_7_ = bf16[96,128]{1,0:T(8,128)(2,1)S(1)} collective-permute-done((bf16[96,128]{1,0:T(8,128)(2,1)S(1)}, bf16[96,128]{1,0:T(8,128)(2,1)S(1)}, u32[]{:S(2)}, u32[]{:S(2)}) %collective-permute-start.39) | collective-permute-done | bytes 24608 | tf_op jit(solution)/shard_map/ppermute | solution.py:381
  (97 shorter events, 26.0 us)
Async XLA Ops:
  3.5 9.3 %collective-permute-start = (bf16[40,1536]{1,0:T(8,128)(2,1)S(1)}, bf16[40,1536]{1,0:T(8,128)(2,1)S(1)}, u32[]{:S(2)}, u32[]{:S(2)}) collective-permute-start(bf16[40,1536]{1,0:T(8,128)(2,1)S(1)} %get-tuple-element.51), channel_id=1, source_target_pairs={{0,8},{4,12},{8,16},{12,20},{16,24},{20,28},{24,0},{28,4},{1,9},{5... | collective-permute-start | bytes 368648 | tf_op jit(solution)/shard_map/ppermute | solution.py:381
  6.5 10.7 %collective-permute-start.1 = (bf16[40,1536]{1,0:T(8,128)(2,1)S(1)}, bf16[40,1536]{1,0:T(8,128)(2,1)S(1)}, u32[]{:S(2)}, u32[]{:S(2)}) collective-permute-start(bf16[40,1536]{1,0:T(8,128)(2,1)S(1)} %get-tuple-element.52), channel_id=1, source_target_pairs={{0,16},{4,20},{8,24},{12,28},{16,0},{20,4},{24,8},{28,12},{1,17},{... | collective-permute-start | bytes 368648 | tf_op jit(solution)/shard_map/ppermute | solution.py:381
  9.1 8.1 %collective-permute-start.2 = (bf16[40,1536]{1,0:T(8,128)(2,1)S(1)}, bf16[40,1536]{1,0:T(8,128)(2,1)S(1)}, u32[]{:S(2)}, u32[]{:S(2)}) collective-permute-start(bf16[40,1536]{1,0:T(8,128)(2,1)S(1)} %get-tuple-element.53), channel_id=1, source_target_pairs={{0,24},{4,28},{8,0},{12,4},{16,8},{20,12},{24,16},{28,20},{1,25},{... | collective-permute-start | bytes 368648 | tf_op jit(solution)/shard_map/ppermute | solution.py:381
  23.9 11.5 %collective-permute-start.3 = (bf16[2,2,160,512]{3,2,1,0:T(8,128)(2,1)S(1)}, bf16[2,2,160,512]{3,2,1,0:T(8,128)(2,1)S(1)}, u32[]{:S(2)}, u32[]{:S(2)}) collective-permute-start(bf16[2,2,160,512]{3,2,1,0:T(8,128)(2,1)S(1)} %gate_up_0.1), channel_id=1, source_target_pairs={{0,1},{1,0},{2,3},{3,2},{4,5},{5,4},{6,7},{7,6},{8,9},{9,8},{10,11... | collective-permute-start | bytes 1966088 | tf_op jit(solution)/shard_map/ppermute | solution.py:368
  34.8 13.2 %collective-permute-start.7 = (bf16[2,2,160,512]{3,2,1,0:T(8,128)(2,1)S(1)}, bf16[2,2,160,512]{3,2,1,0:T(8,128)(2,1)S(1)}, u32[]{:S(2)}, u32[]{:S(2)}) collective-permute-start(bf16[2,2,160,512]{3,2,1,0:T(8,128)(2,1)S(1)} %get-tuple-element.58), channel_id=1, source_target_pairs={{0,1},{1,0},{2,3},{3,2},{4,5},{5,4},{6,7},{7,6},{8,9},{9,8},{10,11... | collective-permute-start | bytes 1966088 | tf_op jit(solution)/shard_map/ppermute | solution.py:368
  35.5 13.2 %collective-permute-start.4 = (bf16[2,160,512]{2,1,0:T(8,128)(2,1)S(1)}, bf16[2,160,512]{2,1,0:T(8,128)(2,1)S(1)}, u32[]{:S(2)}, u32[]{:S(2)}) collective-permute-start(bf16[2,160,512]{2,1,0:T(8,128)(2,1)S(1)} %fusion), channel_id=1, source_target_pairs={{0,2},{1,3},{2,0},{3,1},{4,6},{5,7},{6,4},{7,5},{8,10},{9,11},{10,... | collective-permute-start | bytes 983048 | tf_op jit(solution)/shard_map/ppermute | solution.py:371
  47.9 18.8 %collective-permute-start.5 = (bf16[2,2,160,512]{3,2,1,0:T(8,128)(2,1)S(1)}, bf16[2,2,160,512]{3,2,1,0:T(8,128)(2,1)S(1)}, u32[]{:S(2)}, u32[]{:S(2)}) collective-permute-start(bf16[2,2,160,512]{3,2,1,0:T(8,128)(2,1)S(1)} %get-tuple-element.56), channel_id=1, source_target_pairs={{0,1},{1,0},{2,3},{3,2},{4,5},{5,4},{6,7},{7,6},{8,9},{9,8},{10,11... | collective-permute-start | bytes 1966088 | tf_op jit(solution)/shard_map/ppermute | solution.py:368
  48.1 20.3 %collective-permute-start.8 = (bf16[2,160,512]{2,1,0:T(8,128)(2,1)S(1)}, bf16[2,160,512]{2,1,0:T(8,128)(2,1)S(1)}, u32[]{:S(2)}, u32[]{:S(2)}) collective-permute-start(bf16[2,160,512]{2,1,0:T(8,128)(2,1)S(1)} %fusion.2), channel_id=1, source_target_pairs={{0,2},{1,3},{2,0},{3,1},{4,6},{5,7},{6,4},{7,5},{8,10},{9,11},{10,... | collective-permute-start | bytes 983048 | tf_op jit(solution)/shard_map/ppermute | solution.py:371
  59.7 18.2 %collective-permute-start.9 = (bf16[2,2,160,512]{3,2,1,0:T(8,128)(2,1)S(1)}, bf16[2,2,160,512]{3,2,1,0:T(8,128)(2,1)S(1)}, u32[]{:S(2)}, u32[]{:S(2)}) collective-permute-start(bf16[2,2,160,512]{3,2,1,0:T(8,128)(2,1)S(1)} %get-tuple-element.59), channel_id=1, source_target_pairs={{0,1},{1,0},{2,3},{3,2},{4,5},{5,4},{6,7},{7,6},{8,9},{9,8},{10,11... | collective-permute-start | bytes 1966088 | tf_op jit(solution)/shard_map/ppermute | solution.py:368
  60.2 6.5 %collective-permute-start.10 = (bf16[160,512]{1,0:T(8,128)(2,1)S(1)}, bf16[160,512]{1,0:T(8,128)(2,1)S(1)}, u32[]{:S(2)}, u32[]{:S(2)}) collective-permute-start(bf16[160,512]{1,0:T(8,128)(2,1)S(1)} %fusion.11.rest_1_.own_ref), channel_id=1, source_target_pairs={{0,2},{1,3},{2,0},{3,1},{4,6},{5,7},{6,4},{7,5},{8,10},{9,11},{10,... | collective-permute-start | bytes 491528 | tf_op jit(solution)/shard_map/ppermute | solution.py:371
  61.8 13.8 %collective-permute-start.11 = (bf16[160,512]{1,0:T(8,128)(2,1)S(1)}, bf16[160,512]{1,0:T(8,128)(2,1)S(1)}, u32[]{:S(2)}, u32[]{:S(2)}) collective-permute-start(bf16[160,512]{1,0:T(8,128)(2,1)S(1)} %fusion.11.rest_1_.own_ref), channel_id=1, source_target_pairs={{0,1},{1,0},{2,3},{3,2},{4,5},{5,4},{6,7},{7,6},{8,9},{9,8},{10,11... | collective-permute-start | bytes 491528 | tf_op jit(solution)/shard_map/ppermute | solution.py:368
  66.7 8.9 %collective-permute-start.12 = (bf16[160,512]{1,0:T(8,128)(2,1)S(1)}, bf16[160,512]{1,0:T(8,128)(2,1)S(1)}, u32[]{:S(2)}, u32[]{:S(2)}) collective-permute-start(bf16[160,512]{1,0:T(8,128)(2,1)S(1)} %collective-permute-done.10.across_ref), channel_id=1, source_target_pairs={{0,1},{1,0},{2,3},{3,2},{4,5},{5,4},{6,7},{7,6},{8,9},{9,8},{10,11... | collective-permute-start | bytes 491528 | tf_op jit(solution)/shard_map/ppermute | solution.py:368
  66.8 13.5 %collective-permute-start.6 = (bf16[2,160,512]{2,1,0:T(8,128)(2,1)S(1)}, bf16[2,160,512]{2,1,0:T(8,128)(2,1)S(1)}, u32[]{:S(2)}, u32[]{:S(2)}) collective-permute-start(bf16[2,160,512]{2,1,0:T(8,128)(2,1)S(1)} %fusion.1), channel_id=1, source_target_pairs={{0,2},{1,3},{2,0},{3,1},{4,6},{5,7},{6,4},{7,5},{8,10},{9,11},{10,... | collective-permute-start | bytes 983048 | tf_op jit(solution)/shard_map/ppermute | solution.py:371
  78.2 7.1 %collective-permute-start.17 = (bf16[160,512]{1,0:T(8,128)(2,1)S(1)}, bf16[160,512]{1,0:T(8,128)(2,1)S(1)}, u32[]{:S(2)}, u32[]{:S(2)}) collective-permute-start(bf16[160,512]{1,0:T(8,128)(2,1)S(1)} %fusion.7.own_ref), channel_id=1, source_target_pairs={{0,2},{1,3},{2,0},{3,1},{4,6},{5,7},{6,4},{7,5},{8,10},{9,11},{10,... | collective-permute-start | bytes 491528 | tf_op jit(solution)/shard_map/ppermute | solution.py:371
  78.6 11.6 %collective-permute-start.18 = (bf16[160,512]{1,0:T(8,128)(2,1)S(1)}, bf16[160,512]{1,0:T(8,128)(2,1)S(1)}, u32[]{:S(2)}, u32[]{:S(2)}) collective-permute-start(bf16[160,512]{1,0:T(8,128)(2,1)S(1)} %fusion.7.own_ref), channel_id=1, source_target_pairs={{0,1},{1,0},{2,3},{3,2},{4,5},{5,4},{6,7},{7,6},{8,9},{9,8},{10,11... | collective-permute-start | bytes 491528 | tf_op jit(solution)/shard_map/ppermute | solution.py:368
  78.6 15.2 %collective-permute-start.16 = (bf16[2,160,512]{2,1,0:T(8,128)(2,1)S(1)}, bf16[2,160,512]{2,1,0:T(8,128)(2,1)S(1)}, u32[]{:S(2)}, u32[]{:S(2)}) collective-permute-start(bf16[2,160,512]{2,1,0:T(8,128)(2,1)S(1)} %fusion.3), channel_id=1, source_target_pairs={{0,2},{1,3},{2,0},{3,1},{4,6},{5,7},{6,4},{7,5},{8,10},{9,11},{10,... | collective-permute-start | bytes 983048 | tf_op jit(solution)/shard_map/ppermute | solution.py:371
  85.4 8.2 %collective-permute-start.13 = (f32[4,128]{1,0:T(4,128)S(1)}, f32[4,128]{1,0:T(4,128)S(1)}, u32[]{:S(2)}, u32[]{:S(2)}) collective-permute-start(f32[4,128]{1,0:T(4,128)S(1)} %get-tuple-element.62.refs_0_), channel_id=1, source_target_pairs={{0,8},{4,12},{8,16},{12,20},{16,24},{20,28},{24,0},{28,4},{1,9},{5... | collective-permute-start | bytes 6152 | tf_op jit(solution)/shard_map/ppermute | solution.py:381
  91.0 6.8 %collective-permute-start.23 = (bf16[160,512]{1,0:T(8,128)(2,1)S(1)}, bf16[160,512]{1,0:T(8,128)(2,1)S(1)}, u32[]{:S(2)}, u32[]{:S(2)}) collective-permute-start(bf16[160,512]{1,0:T(8,128)(2,1)S(1)} %fusion.9.own_ref), channel_id=1, source_target_pairs={{0,2},{1,3},{2,0},{3,1},{4,6},{5,7},{6,4},{7,5},{8,10},{9,11},{10,... | collective-permute-start | bytes 491528 | tf_op jit(solution)/shard_map/ppermute | solution.py:371
  94.0 6.6 %collective-permute-start.20 = (bf16[160,512]{1,0:T(8,128)(2,1)S(1)}, bf16[160,512]{1,0:T(8,128)(2,1)S(1)}, u32[]{:S(2)}, u32[]{:S(2)}) collective-permute-start(bf16[160,512]{1,0:T(8,128)(2,1)S(1)} %fusion.5.own_ref), channel_id=1, source_target_pairs={{0,2},{1,3},{2,0},{3,1},{4,6},{5,7},{6,4},{7,5},{8,10},{9,11},{10,... | collective-permute-start | bytes 491528 | tf_op jit(solution)/shard_map/ppermute | solution.py:371
  106.4 6.8 %collective-permute-start.26 = (bf16[160,256]{1,0:T(8,128)(2,1)S(1)}, bf16[160,256]{1,0:T(8,128)(2,1)S(1)}, u32[]{:S(2)}, u32[]{:S(2)}) collective-permute-start(bf16[160,256]{1,0:T(8,128)(2,1)S(1)} %get-tuple-element.78), channel_id=1, source_target_pairs={{0,4},{4,0},{8,12},{12,8},{16,20},{20,16},{24,28},{28,24},{1,5},{5... | collective-permute-start | bytes 245768 | tf_op jit(solution)/shard_map/ppermute | solution.py:381
  107.8 8.8 %collective-permute-start.27 = (bf16[160,256]{1,0:T(8,128)(2,1)S(1)}, bf16[160,256]{1,0:T(8,128)(2,1)S(1)}, u32[]{:S(2)}, u32[]{:S(2)}) collective-permute-start(bf16[160,256]{1,0:T(8,128)(2,1)S(1)} %get-tuple-element.79), channel_id=1, source_target_pairs={{0,8},{4,12},{8,16},{12,20},{16,24},{20,28},{24,0},{28,4},{1,9},{5... | collective-permute-start | bytes 245768 | tf_op jit(solution)/shard_map/ppermute | solution.py:381
  109.0 11.3 %collective-permute-start.28 = (bf16[160,256]{1,0:T(8,128)(2,1)S(1)}, bf16[160,256]{1,0:T(8,128)(2,1)S(1)}, u32[]{:S(2)}, u32[]{:S(2)}) collective-permute-start(bf16[160,256]{1,0:T(8,128)(2,1)S(1)} %get-tuple-element.80), channel_id=1, source_target_pairs={{0,12},{4,8},{8,20},{12,16},{16,28},{20,24},{24,4},{28,0},{1,13},{... | collective-permute-start | bytes 245768 | tf_op jit(solution)/shard_map/ppermute | solution.py:381
  109.1 12.3 %collective-permute-start.29 = (bf16[160,256]{1,0:T(8,128)(2,1)S(1)}, bf16[160,256]{1,0:T(8,128)(2,1)S(1)}, u32[]{:S(2)}, u32[]{:S(2)}) collective-permute-start(bf16[160,256]{1,0:T(8,128)(2,1)S(1)} %get-tuple-element.81), channel_id=1, source_target_pairs={{0,16},{4,20},{8,24},{12,28},{16,0},{20,4},{24,8},{28,12},{1,17},{... | collective-permute-start | bytes 245768 | tf_op jit(solution)/shard_map/ppermute | solution.py:381
  112.2 10.9 %collective-permute-start.30 = (bf16[160,256]{1,0:T(8,128)(2,1)S(1)}, bf16[160,256]{1,0:T(8,128)(2,1)S(1)}, u32[]{:S(2)}, u32[]{:S(2)}) collective-permute-start(bf16[160,256]{1,0:T(8,128)(2,1)S(1)} %get-tuple-element.82), channel_id=1, source_target_pairs={{0,20},{4,16},{8,28},{12,24},{16,4},{20,0},{24,12},{28,8},{1,21},{... | collective-permute-start | bytes 245768 | tf_op jit(solution)/shard_map/ppermute | solution.py:381
  113.1 10.0 %collective-permute-start.31 = (bf16[160,256]{1,0:T(8,128)(2,1)S(1)}, bf16[160,256]{1,0:T(8,128)(2,1)S(1)}, u32[]{:S(2)}, u32[]{:S(2)}) collective-permute-start(bf16[160,256]{1,0:T(8,128)(2,1)S(1)} %get-tuple-element.83), channel_id=1, source_target_pairs={{0,24},{4,28},{8,0},{12,4},{16,8},{20,12},{24,16},{28,20},{1,25},{... | collective-permute-start | bytes 245768 | tf_op jit(solution)/shard_map/ppermute | solution.py:381
  116.7 7.3 %collective-permute-start.32 = (bf16[160,256]{1,0:T(8,128)(2,1)S(1)}, bf16[160,256]{1,0:T(8,128)(2,1)S(1)}, u32[]{:S(2)}, u32[]{:S(2)}) collective-permute-start(bf16[160,256]{1,0:T(8,128)(2,1)S(1)} %get-tuple-element.84), channel_id=1, source_target_pairs={{0,28},{4,24},{8,4},{12,0},{16,12},{20,8},{24,20},{28,16},{1,29},{... | collective-permute-start | bytes 245768 | tf_op jit(solution)/shard_map/ppermute | solution.py:381
  141.3 5.9 %collective-permute-start.33 = (bf16[96,128]{1,0:T(8,128)(2,1)S(1)}, bf16[96,128]{1,0:T(8,128)(2,1)S(1)}, u32[]{:S(2)}, u32[]{:S(2)}) collective-permute-start(bf16[96,128]{1,0:T(8,128)(2,1)S(1)} %get-tuple-element.89.refs_0_), channel_id=1, source_target_pairs={{0,4},{4,0},{8,12},{12,8},{16,20},{20,16},{24,28},{28,24},{1,5},{5... | collective-permute-start | bytes 73736 | tf_op jit(solution)/shard_map/ppermute | solution.py:381
  142.0 8.2 %collective-permute-start.34 = (bf16[96,128]{1,0:T(8,128)(2,1)S(1)}, bf16[96,128]{1,0:T(8,128)(2,1)S(1)}, u32[]{:S(2)}, u32[]{:S(2)}) collective-permute-start(bf16[96,128]{1,0:T(8,128)(2,1)S(1)} %get-tuple-element.90), channel_id=1, source_target_pairs={{0,8},{4,12},{8,16},{12,20},{16,24},{20,28},{24,0},{28,4},{1,9},{5... | collective-permute-start | bytes 73736 | tf_op jit(solution)/shard_map/ppermute | solution.py:381
  142.5 10.0 %collective-permute-start.35 = (bf16[96,128]{1,0:T(8,128)(2,1)S(1)}, bf16[96,128]{1,0:T(8,128)(2,1)S(1)}, u32[]{:S(2)}, u32[]{:S(2)}) collective-permute-start(bf16[96,128]{1,0:T(8,128)(2,1)S(1)} %get-tuple-element.90), channel_id=1, source_target_pairs={{0,12},{4,8},{8,20},{12,16},{16,28},{20,24},{24,4},{28,0},{1,13},{... | collective-permute-start | bytes 73736 | tf_op jit(solution)/shard_map/ppermute | solution.py:381
  144.0 8.5 %collective-permute-start.36 = (bf16[96,128]{1,0:T(8,128)(2,1)S(1)}, bf16[96,128]{1,0:T(8,128)(2,1)S(1)}, u32[]{:S(2)}, u32[]{:S(2)}) collective-permute-start(bf16[96,128]{1,0:T(8,128)(2,1)S(1)} %get-tuple-element.91), channel_id=1, source_target_pairs={{0,16},{4,20},{8,24},{12,28},{16,0},{20,4},{24,8},{28,12},{1,17},{... | collective-permute-start | bytes 73736 | tf_op jit(solution)/shard_map/ppermute | solution.py:381
  147.3 5.9 %collective-permute-start.37 = (bf16[96,128]{1,0:T(8,128)(2,1)S(1)}, bf16[96,128]{1,0:T(8,128)(2,1)S(1)}, u32[]{:S(2)}, u32[]{:S(2)}) collective-permute-start(bf16[96,128]{1,0:T(8,128)(2,1)S(1)} %get-tuple-element.91), channel_id=1, source_target_pairs={{0,20},{4,16},{8,28},{12,24},{16,4},{20,0},{24,12},{28,8},{1,21},{... | collective-permute-start | bytes 73736 | tf_op jit(solution)/shard_map/ppermute | solution.py:381
  147.3 5.9 %collective-permute-start.38 = (bf16[96,128]{1,0:T(8,128)(2,1)S(1)}, bf16[96,128]{1,0:T(8,128)(2,1)S(1)}, u32[]{:S(2)}, u32[]{:S(2)}) collective-permute-start(bf16[96,128]{1,0:T(8,128)(2,1)S(1)} %get-tuple-element.92), channel_id=1, source_target_pairs={{0,24},{4,28},{8,0},{12,4},{16,8},{20,12},{24,16},{28,20},{1,25},{... | collective-permute-start | bytes 73736 | tf_op jit(solution)/shard_map/ppermute | solution.py:381
  (16 other events, 93.6 us)

commit v5 on v3

--- a/solution.py
+++ b/solution.py
@@ -67,9 +67,7 @@
     return ranked_first, ranked_second
 
 
-def pick_kernel(parts, tensor_count, place_ref, routes_ref, logits_ref, tokens_ref, info_ref, *out_refs):
-    info_ref[0:2, :] = routes_ref[...].astype(f32)
-    info_ref[2:4, :] = logits_ref[...]
+def pick_kernel(parts, tensor_count, place_ref, info_ref, tokens_ref, *out_refs):
     first, second = info_ref[0:1, :], info_ref[1:2, :]
     rank_first, rank_second = block_slots(first, second)
     count = first.shape[1]
@@ -81,32 +79,15 @@
         out_ref[...] = mm(hit.astype(f32).astype(bf16), values).astype(bf16)
 
 
-def turn_kernel(*refs):
-    rows = jnp.concatenate([ref[...].astype(f32) for ref in refs[:-1]], axis=0)
-    refs[-1][...] = rows.T.astype(bf16)
-
-
-def turned(values):
-    rows, slots = values.shape
-    main = slots // 128 * 128
-    rest = slots - main
-    if main == 0 or rest == 0 or 128 % rest or rows % (128 // rest):
-        return values.T
-    groups = 128 // rest
-    tall = rows // groups
-    folded = jnp.concatenate(
-        [values[group * tall : (group + 1) * tall, main:] for group in range(groups)], axis=1
-    ).T
-    tail = jnp.concatenate(
-        [folded[group * rest : (group + 1) * rest] for group in range(groups)], axis=1
-    )
-    return jnp.concatenate([values[:, :main].T, tail], axis=0)
+def stack_kernel(*refs):
+    pieces = refs[: (len(refs) - 1) // 2]
+    refs[-1][...] = jnp.concatenate([ref[...].astype(f32) for ref in pieces], axis=0).astype(bf16)
 
 
 def gate_up_kernel(has_keep, order_ref, inputs_ref, gate_ref, up_ref, *rest):
     values = inputs_ref[...]
-    gate = turned(mm(gate_ref[...], values).astype(bf16))
-    up = turned(mm(up_ref[...], values).astype(bf16))
+    gate = mm(values, gate_ref[...], NT).astype(bf16)
+    up = mm(values, up_ref[...], NT).astype(bf16)
     step = pl.program_id(0)
     outs = rest[-(1 + (has_keep == 2)) :]
     for index, ref in enumerate(outs):
@@ -118,7 +99,7 @@
 
 
 def gate_up(order, inputs, gate_weight, up_weight, width, keep, send, after):
-    depth, slots = inputs.shape
+    slots, depth = inputs.shape
     quarter = gate_weight.shape[0] // 4
     gate_weight = gate_weight.reshape(4, quarter, depth)
     up_weight = up_weight.reshape(4, quarter, depth)
@@ -143,7 +124,7 @@
             num_scalar_prefetch=1,
             grid=(2 * count,),
             in_specs=[
-                pl.BlockSpec((depth, slots), lambda s, order: (0, 0)),
+                pl.BlockSpec((slots, depth), lambda s, order: (0, 0)),
                 weight_spec,
                 weight_spec,
             ]
@@ -152,13 +133,17 @@
         ),
         out_shape=[jax.ShapeDtypeStruct((2, 2, slots, width), bf16)] * count,
         compiler_params=params(41),
-        cost_estimate=LIGHT,
+        cost_estimate=pl.CostEstimate(
+            flops=32 * count * slots * depth * width,
+            bytes_accessed=32 * count * width * depth,
+            transcendentals=0,
+        ),
         name=f"gate_up_{chunks[-1] + (send is None)}",
     )(order, inputs, gate_weight, up_weight, *after)
 
 
-def down_kernel(pack, has_old, order_ref, place_ref, own_ref, across_ref, beside_ref, both_ref, down_ref, *rest):
-    pieces = (own_ref, across_ref, beside_ref, both_ref)
+def down_kernel(count, pack, has_old, order_ref, place_ref, *refs):
+    pieces, down_ref, rest = refs[:count], refs[count], refs[count + 1 :]
     old, new = rest[:3] if has_old else (), rest[3 * has_old :]
     packed_refs = ()
     if pack:
@@ -203,7 +188,7 @@
                         ).astype(bf16)
 
 
-def down(order, place, pieces, down_weight, chunk, older, pack=None):
+def down(order, place, pieces, down_weight, chunk, older, first=0, pack=None):
     slots, width = pieces[0].shape
     columns = down_weight.shape[1]
     down_weight = down_weight.reshape(4, -1, columns)
@@ -218,19 +203,19 @@
         packed = (slots, slots + columns // parts)
         out_shape = [jax.ShapeDtypeStruct(packed, bf16)] * parts + out_shape
     return pl.pallas_call(
-        functools.partial(down_kernel, pack, bool(older)),
+        functools.partial(down_kernel, len(pieces), pack, bool(older)),
         grid_spec=pltpu.PrefetchScalarGridSpec(
             num_scalar_prefetch=2,
-            grid=(4,),
-            in_specs=[fixed((slots, width))] * 4
-            + [pl.BlockSpec((None, width, columns), lambda s, order, place: (order[s], chunk, 0))]
+            grid=(len(pieces),),
+            in_specs=[fixed((slots, width))] * len(pieces)
+            + [pl.BlockSpec((None, width, columns), lambda s, order, place: (order[first + s], chunk, 0))]
             + [fixed(value.shape) for value in older],
             out_specs=[fixed(value.shape) for value in out_shape],
         ),
         out_shape=out_shape,
         compiler_params=params(20),
         cost_estimate=LIGHT,
-        name=f"down_{chunk}",
+        name=f"down_{chunk}_{first}",
     )(order, place, *pieces, down_weight, *older)
 
 
@@ -312,7 +297,7 @@
         sums_ref[part] = sums
 
 
-def finish_kernel(ridge, base_ref, zero_ref, one_ref, sums_ref, *out_refs):
+def finish_kernel(ridge, blocks, copies, place_ref, base_ref, zero_ref, one_ref, sums_ref, out_ref):
     sums = jnp.sum(sums_ref[...], axis=0)[0:1, :]
     norm, zero_zero = sums[:, 0:1], sums[:, 1:2]
     zero_one, one_one = sums[:, 2:3], sums[:, 3:4]
@@ -324,22 +309,17 @@
     image = grown * grown * zero_zero - 2.0 * grown * step * zero_one + step * step * one_one
     later = new / (image + ridge * (new + ratio * ratio * norm))
     field = base_ref[...] - (step + later * grown) * zero_ref[...] + (later * step) * one_ref[...]
-    rows = field.shape[0] // len(out_refs)
+    rows = field.shape[0] // blocks
     sideways = field.T.astype(bf16)
-    for block, ref in enumerate(out_refs):
-        ref[...] = sideways[:, block * rows : (block + 1) * rows]
-
-
-def join_kernel(blocks, tensor_count, place_ref, *refs):
-    pieces, (out_ref, rows_ref) = refs[:-2], refs[-2:]
-    lanes = pieces[0].shape[0]
     for back in range(blocks):
-        for aside in range(tensor_count):
-            part = lax.rem(place_ref[0] + blocks - back, blocks) * tensor_count
-            part = part + lax.rem(place_ref[1] + tensor_count - aside, tensor_count)
-            start = pl.multiple_of(part * lanes, 8)
-            rows_ref[pl.ds(start, lanes), :] = pieces[back * tensor_count + aside][...].astype(f32)
-    out_ref[...] = rows_ref[...].T
+        target = lax.rem(place_ref[0] + blocks - back, blocks) * copies
+        for copy in range(copies):
+            out_ref[target + copy] = sideways[:, back * rows : (back + 1) * rows]
+
+
+def join_kernel(pieces_ref, out_ref):
+    rows = jnp.concatenate([pieces_ref[part].astype(f32) for part in range(pieces_ref.shape[0])], axis=0)
+    out_ref[...] = rows.T
 
 
 def single(kernel, out_shape, in_specs, mib, name, scratch=()):
@@ -389,21 +369,25 @@
         return lax.ppermute(values, ("dp", "tensor"), pairs)
 
     shifts = [(ahead, aside) for ahead in range(dp_count) for aside in range(tensor_count)]
-    info, *picked = single(
+    upper = lax.pad(routes.T, jnp.int32(0), ((0, 2, 0), (0, 0, 0))).astype(f32)
+    info = upper + lax.pad(route_logits.T, f32(0), ((2, 0, 0), (0, 0, 0)))
+    picked = single(
         functools.partial(pick_kernel, dp_count, tensor_count),
-        [jax.ShapeDtypeStruct((4, tok_rows), f32)] + [jax.ShapeDtypeStruct((CAP, depth), bf16)] * dp_count,
-        [scalars(), whole(), whole(), whole()],
+        [jax.ShapeDtypeStruct((CAP, depth), bf16)] * dp_count,
+        [scalars(), whole(), whole()],
         16,
         "pick",
-    )(place, routes.T, route_logits.T, tokens)
+    )(place, info, tokens)
     arrived = [shifted(value, ahead) for ahead, value in enumerate(picked)]
+    info = lax.optimization_barrier((info, arrived[1]))[0]
+    infos = [shifted(info, ahead) for ahead in range(dp_count)]
     inputs = single(
-        turn_kernel,
-        jax.ShapeDtypeStruct((depth, slots), bf16),
-        [whole()] * dp_count,
+        stack_kernel,
+        jax.ShapeDtypeStruct((slots, depth), bf16),
+        [whole()] * dp_count + [pl.BlockSpec(memory_space=pl.ANY)] * dp_count,
         16,
-        "turn",
-    )(*arrived)
+        "stack",
+    )(*arrived, *infos)
 
     gate_order = col_index ^ jnp.array([2, 0, 3, 1], jnp.int32)
     down_order = col_index ^ jnp.array([0, 2, 1, 3], jnp.int32)
@@ -421,12 +405,9 @@
 
     nears.append(beside(products(None, 0)[0]))
     for chunk in range(CHUNKS):
-        after = []
+        after = [keeps[-1]] if chunk else []
         if chunk >= 2:
-            after = after + [fars[chunk - 2]]
-        if chunk >= 3:
-            activate(chunk - 3, [])
-            after = after + [owns[chunk - 3]]
+            after.extend([fars[chunk - 2], pairs[chunk - 1]])
         if chunk < last:
             keep, send = products(chunk, chunk + 1, after)
             nears.append(beside(send))
@@ -435,27 +416,23 @@
         keeps.append(keep)
         pairs.append((keep[0].astype(f32) + nears[chunk][0].astype(f32)).astype(bf16))
         fars.append(across(pairs[-1]))
-    info = lax.optimization_barrier((info, owns[0]))[0]
-    infos = [shifted(info, ahead) for ahead in range(dp_count)]
     older, olders = (), []
     for chunk in range(CHUNKS):
         if chunk >= len(owns):
             after = [pairs[last]]
             if chunk >= 2:
                 after.append(olders[chunk - 2][2])
-                after.extend(infos[1:])
             activate(chunk, after)
         own = owns[chunk]
         other = across(own)
-        older = down(
-            down_order,
-            place,
-            (own, other, beside(own), beside(other)),
-            down_weight,
-            chunk,
-            older,
-            (dp_count, tensor_count) if chunk == last else None,
-        )
+        pieces = (own, other, beside(own), beside(other))
+        if chunk < last:
+            older = down(down_order, place, pieces, down_weight, chunk, older)
+        else:
+            older = down(down_order, place, pieces[:3], down_weight, chunk, older)
+            older = down(
+                down_order, place, pieces[3:], down_weight, chunk, older, 3, (dp_count, tensor_count)
+            )
         olders.append(older)
     packed, (_, _, square) = older[:parts], older[parts:]
     spread = [shifted(value, *shift) for value, shift in zip(packed, shifts)]
@@ -486,21 +463,20 @@
     sums = lax.all_to_all(sums, ("dp", "tensor", "col"), split_axis=0, concat_axis=0, tiled=True)
 
     home = single(
-        functools.partial(finish_kernel, ridge),
-        [jax.ShapeDtypeStruct((lanes, tok_rows), bf16)] * dp_count,
-        [whole()] * 4,
+        functools.partial(finish_kernel, ridge, dp_count, tensor_count),
+        jax.ShapeDtypeStruct((parts, lanes, tok_rows), bf16),
+        [scalars()] + [whole()] * 4,
         16,
         "finish",
-    )(base, zero, one, sums)
-    pieces = [shifted(home[-ahead % dp_count], ahead, aside) for ahead, aside in shifts]
+    )(place, base, zero, one, sums)
+    home = lax.all_to_all(home, ("dp", "tensor"), split_axis=0, concat_axis=0, tiled=True)
     return single(
-        functools.partial(join_kernel, dp_count, tensor_count),
+        join_kernel,
         jax.ShapeDtypeStruct((tok_rows, columns), f32),
-        [scalars()] + [whole()] * parts,
+        [whole()],
         16,
         "join",
-        [pltpu.VMEM((columns, tok_rows), f32)],
-    )(place, *pieces)
+    )(home)
 
 
 def spread_copies(values, experts, held_count, copies):

time: 151 us -> 145 us (0.960)
  blocking collectives: 11.8 us -> 23.1 us
  waiting for transfers between devices: 33.1 us -> 22.8 us
  starting transfers between devices: 45.6 us -> 38.1 us
    all_to_all x0 -> x1, blocking collectives: none -> 10.7 us  [one_expert_each(): lax.all_to_all(home, ('dp', 'tensor'), split_axis=0, concat_axis=0, tiled...]
    ppermute x20 -> x13, starting transfers between devices: 35.7 us -> 26.5 us  [shifted(): return lax.ppermute(values, ('dp', 'tensor'), pairs)]
    ppermute x8, waiting for transfers between devices: 19.6 us -> 14.2 us  [across(): return lax.ppermute(values, 'col', [(k, k ^ 2) for k in range(4)])]
    ppermute x20 -> x13, waiting for transfers between devices: 12 us -> 8.56 us  [shifted(): return lax.ppermute(values, ('dp', 'tensor'), pairs)]
    ppermute x8, starting transfers between devices: 7.84 us -> 9.55 us  [across(): return lax.ppermute(values, 'col', [(k, k ^ 2) for k in range(4)])]
    pallas_call x7 -> x8, Pallas kernels: 12.4 us -> 12.5 us  [the longest x5 10.7 us: down(): pl.pallas_call(functools.partial(down_kernel, len(pieces), pack, bool(old...]
  transfers between devices with their start and end apart: 40 -> 33, of which waited for: 13 -> 10; matrix products, arithmetic and copies ran while one was open for 2% -> 2% of each run, Pallas kernels for 25% -> 28%
where the time goes in v5:
time: 145 us; the launch traced here: 144 us
  Pallas kernels  55.1 us (38%)
  starting transfers between devices  38.1 us (26%)
  blocking collectives  23.1 us (16%)
  waiting for transfers between devices  22.8 us (16%)
  other arithmetic  3.3 us (2%)
    pallas_call x5, Pallas kernels, gate_up(): pl.pallas_call(functools.partial(gate_up_kernel, count), grid_spec=pltpu....  34.8 us
    ppermute x13, starting transfers between devices, shifted(): return lax.ppermute(values, ('dp', 'tensor'), pairs)  26.5 us
    ppermute x8, waiting for transfers between devices, across(): return lax.ppermute(values, 'col', [(k, k ^ 2) for k in range(4)])  14.2 us
    all_to_all x1, blocking collectives, one_expert_each(): lax.all_to_all(sums, ('dp', 'tensor', 'col'), split_axis=0, concat_axis=0...  12.4 us
    pallas_call x5, Pallas kernels, down(): pl.pallas_call(functools.partial(down_kernel, len(pieces), pack, bool(old...  10.7 us
    all_to_all x1, blocking collectives, one_expert_each(): lax.all_to_all(home, ('dp', 'tensor'), split_axis=0, concat_axis=0, tiled...  10.7 us
    ppermute x8, starting transfers between devices, across(): return lax.ppermute(values, 'col', [(k, k ^ 2) for k in range(4)])  9.55 us
    ppermute x13, waiting for transfers between devices, shifted(): return lax.ppermute(values, ('dp', 'tensor'), pairs)  8.56 us
  transfers between devices with their start and end apart: 33, of which 10 were waited for; matrix products, arithmetic and copies ran while one was open for 2% of the time, Pallas kernels for 28%

profile of v5, /device:TPU:0, one launch (start us, length us, event | category | flops | bytes accessed | tf_op | source)
XLA Modules:
  0.0 144.4 jit_solution(9979727376399004773)
XLA Ops:
  2.8 3.1 %collective-permute-start = (bf16[40,1536]{1,0:T(8,128)(2,1)S(1)}, bf16[40,1536]{1,0:T(8,128)(2,1)S(1)}, u32[]{:S(2)}, u32[]{:S(2)}) collective-permute-start(bf16[40,1536]{1,0:T(8,128)(2,1)S(1)} %get-tuple-element.48), channel_id=1, source_target_pairs={{0,8},{4,12},{8,16},{12,20},{16,24},{20,28},{24,0},{28,4},{1,9},{5... | collective-permute-start | bytes 368648 | tf_op jit(solution)/shard_map/ppermute | solution.py:369
  5.9 2.6 %collective-permute-start.4 = (bf16[40,1536]{1,0:T(8,128)(2,1)S(1)}, bf16[40,1536]{1,0:T(8,128)(2,1)S(1)}, u32[]{:S(2)}, u32[]{:S(2)}) collective-permute-start(bf16[40,1536]{1,0:T(8,128)(2,1)S(1)} %get-tuple-element.51), channel_id=1, source_target_pairs={{0,16},{4,20},{8,24},{12,28},{16,0},{20,4},{24,8},{28,12},{1,17},{... | collective-permute-start | bytes 368648 | tf_op jit(solution)/shard_map/ppermute | solution.py:369
  9.8 2.3 %collective-permute-done.refs_1_ = bf16[40,1536]{1,0:T(8,128)(2,1)S(1)} collective-permute-done((bf16[40,1536]{1,0:T(8,128)(2,1)S(1)}, bf16[40,1536]{1,0:T(8,128)(2,1)S(1)}, u32[]{:S(2)}, u32[]{:S(2)}) %collective-permute-start) | collective-permute-done | bytes 122912 | tf_op jit(solution)/shard_map/ppermute | solution.py:369
  13.5 4.9 %collective-permute-start.2 = (f32[4,128]{1,0:T(4,128)S(1)}, f32[4,128]{1,0:T(4,128)S(1)}, u32[]{:S(2)}, u32[]{:S(2)}) collective-permute-start(f32[4,128]{1,0:T(4,128)S(1)} %pad_add_fusion.info_ref.refs_4_.refs_0_), channel_id=1, source_target_pairs={{0,16},{4,20},{8,24},{12,28},{16,0},{20,4},{24,8},{28,12},{1,17},{... | collective-permute-start | bytes 6152 | tf_op jit(solution)/shard_map/ppermute | solution.py:369
  18.4 2.0 %collective-permute-start.1 = (f32[4,128]{1,0:T(4,128)S(1)}, f32[4,128]{1,0:T(4,128)S(1)}, u32[]{:S(2)}, u32[]{:S(2)}) collective-permute-start(f32[4,128]{1,0:T(4,128)S(1)} %pad_add_fusion.info_ref.refs_4_.refs_0_), channel_id=1, source_target_pairs={{0,8},{4,12},{8,16},{12,20},{16,24},{20,28},{24,0},{28,4},{1,9},{5... | collective-permute-start | bytes 6152 | tf_op jit(solution)/shard_map/ppermute | solution.py:369
  21.1 2.7 %collective-permute-done.1.refs_5_.refs_1_ = f32[4,128]{1,0:T(4,128)S(1)} collective-permute-done((f32[4,128]{1,0:T(4,128)S(1)}, f32[4,128]{1,0:T(4,128)S(1)}, u32[]{:S(2)}, u32[]{:S(2)}) %collective-permute-start.1) | collective-permute-done | bytes 2080 | tf_op jit(solution)/shard_map/ppermute | solution.py:369
  23.9 4.9 %gate_up_0.1 = bf16[2,2,160,512]{3,2,1,0:T(8,128)(2,1)S(1)} custom-call(s32[4]{0:T(128)S(1)} %broadcast_xor_fusion.order_ref, bf16[160,1536]{1,0:T(8,128)(2,1)S(1)} %stack.13.inputs_ref, bf16[4,2048,1536]{2,1,0:T(8,128)(2,1)} %bitcast.71, bf16[4,2048,1536]{2,1,0:T(8,128)(2,1)} %bitcast.76), custom_call_target="tpu_custom_call" | custom-call | flops 4026531840 | bytes 25165824 | tf_op jit(solution)/shard_map/gate_up_0/pallas_call | solution.py:121
  28.8 8.2 %gate_up_1.1 = (bf16[2,2,160,512]{3,2,1,0:T(8,128)(2,1)S(1)}, bf16[2,2,160,512]{3,2,1,0:T(8,128)(2,1)S(1)}) custom-call(s32[4]{0:T(128)S(1)} %broadcast_xor_fusion.order_ref, bf16[160,1536]{1,0:T(8,128)(2,1)S(1)} %stack.13.inputs_ref, bf16[4,2048,1536]{2,1,0:T(8,128)(2,1)} %bitcast.72, bf16[4,2048,1536]{2,1,0:T(8,128)(2,1)} %bitcast.77), custom_call_target="tpu_custom_call" | custom-call | flops 8053063680 | bytes 50331648 | tf_op jit(solution)/shard_map/gate_up_1/pallas_call | solution.py:121
  37.7 1.6 %collective-permute-start.7 = (bf16[2,160,512]{2,1,0:T(8,128)(2,1)S(1)}, bf16[2,160,512]{2,1,0:T(8,128)(2,1)S(1)}, u32[]{:S(2)}, u32[]{:S(2)}) collective-permute-start(bf16[2,160,512]{2,1,0:T(8,128)(2,1)S(1)} %fusion), channel_id=1, source_target_pairs={{0,2},{1,3},{2,0},{3,1},{4,6},{5,7},{6,4},{7,5},{8,10},{9,11},{10,... | collective-permute-start | bytes 983048 | tf_op jit(solution)/shard_map/ppermute | solution.py:359
  39.2 8.2 %gate_up_2.1 = (bf16[2,2,160,512]{3,2,1,0:T(8,128)(2,1)S(1)}, bf16[2,2,160,512]{3,2,1,0:T(8,128)(2,1)S(1)}) custom-call(s32[4]{0:T(128)S(1)} %broadcast_xor_fusion.order_ref, bf16[160,1536]{1,0:T(8,128)(2,1)S(1)} %stack.13.inputs_ref, bf16[4,2048,1536]{2,1,0:T(8,128)(2,1)} %bitcast.73, bf16[4,2048,1536]{2,1,0:T(8,128)(2,1)} %bitcast.78, ...), custom_call_target="tpu_custom_call" | custom-call | flops 8053063680 | bytes 50331648 | tf_op jit(solution)/shard_map/gate_up_2/pallas_call | solution.py:121
  48.2 8.7 %gate_up_3.1 = (bf16[2,2,160,512]{3,2,1,0:T(8,128)(2,1)S(1)}, bf16[2,2,160,512]{3,2,1,0:T(8,128)(2,1)S(1)}) custom-call(s32[4]{0:T(128)S(1)} %broadcast_xor_fusion.order_ref, bf16[160,1536]{1,0:T(8,128)(2,1)S(1)} %stack.13.inputs_ref, bf16[4,2048,1536]{2,1,0:T(8,128)(2,1)} %bitcast.74, bf16[4,2048,1536]{2,1,0:T(8,128)(2,1)} %bitcast.79, ...), custom_call_target="tpu_custom_call" | custom-call | flops 8053063680 | bytes 50331648 | tf_op jit(solution)/shard_map/gate_up_3/pallas_call | solution.py:121
  57.3 1.6 %collective-permute-start.22 = (bf16[2,160,512]{2,1,0:T(8,128)(2,1)S(1)}, bf16[2,160,512]{2,1,0:T(8,128)(2,1)S(1)}, u32[]{:S(2)}, u32[]{:S(2)}) collective-permute-start(bf16[2,160,512]{2,1,0:T(8,128)(2,1)S(1)} %fusion.2.rest_2_), channel_id=1, source_target_pairs={{0,2},{1,3},{2,0},{3,1},{4,6},{5,7},{6,4},{7,5},{8,10},{9,11},{10,... | collective-permute-start | bytes 983048 | tf_op jit(solution)/shard_map/ppermute | solution.py:359
  58.8 4.9 %gate_up_4.1 = bf16[2,2,160,512]{3,2,1,0:T(8,128)(2,1)S(1)} custom-call(s32[4]{0:T(128)S(1)} %broadcast_xor_fusion.order_ref, bf16[160,1536]{1,0:T(8,128)(2,1)S(1)} %stack.13.inputs_ref, bf16[4,2048,1536]{2,1,0:T(8,128)(2,1)} %bitcast.75, bf16[4,2048,1536]{2,1,0:T(8,128)(2,1)} %bitcast.80, bf16[2,2,160,512]{3,2,1,0:T(8,128)(2,1)S(1)} %get-tuple-element.56.rest_0_, ...), custom_call_target="tpu_custom_call" | custom-call | flops 4026531840 | bytes 25165824 | tf_op jit(solution)/shard_map/gate_up_4/pallas_call | solution.py:121
  66.5 4.7 %collective-permute-done.16.refs_1_ = bf16[160,512]{1,0:T(8,128)(2,1)S(1)} collective-permute-done((bf16[160,512]{1,0:T(8,128)(2,1)S(1)}, bf16[160,512]{1,0:T(8,128)(2,1)S(1)}, u32[]{:S(2)}, u32[]{:S(2)}) %collective-permute-start.16) | collective-permute-done | bytes 163872 | tf_op jit(solution)/shard_map/ppermute | solution.py:359
  71.7 2.5 %collective-permute-done.13.refs_1_ = bf16[160,512]{1,0:T(8,128)(2,1)S(1)} collective-permute-done((bf16[160,512]{1,0:T(8,128)(2,1)S(1)}, bf16[160,512]{1,0:T(8,128)(2,1)S(1)}, u32[]{:S(2)}, u32[]{:S(2)}) %collective-permute-start.13) | collective-permute-done | bytes 163872 | tf_op jit(solution)/shard_map/ppermute | solution.py:359
  74.3 1.5 %collective-permute-start.12 = (bf16[2,160,512]{2,1,0:T(8,128)(2,1)S(1)}, bf16[2,160,512]{2,1,0:T(8,128)(2,1)S(1)}, u32[]{:S(2)}, u32[]{:S(2)}) collective-permute-start(bf16[2,160,512]{2,1,0:T(8,128)(2,1)S(1)} %fusion.3), channel_id=1, source_target_pairs={{0,2},{1,3},{2,0},{3,1},{4,6},{5,7},{6,4},{7,5},{8,10},{9,11},{10,... | collective-permute-start | bytes 983048 | tf_op jit(solution)/shard_map/ppermute | solution.py:359
  75.8 2.3 %down_0_0.1 = (f32[160,768]{1,0:T(8,128)S(1)}, f32[160,160]{1,0:T(8,128)S(1)}, f32[8,768]{1,0:T(8,128)S(1)}) custom-call(s32[4]{0:T(128)S(1)} %broadcast_xor_fusion.1.order_ref, s32[2]{0:T(128)S(1)} %pad_add_fusion.1.place_ref, bf16[160,512]{1,0:T(8,128)(2,1)S(1)} %fusion.9.refs_0_, bf16[160,512]{1,0:T(8,128)(2,1)S(1)} %collective-permute-done.16.refs_1_, ...), custom_call_target="tpu_custom_call" | custom-call | flops 1 | bytes 1 | tf_op jit(solution)/shard_map/down_0_0/pallas_call | solution.py:205
  79.0 2.3 %down_1_0.1 = (f32[160,768]{1,0:T(8,128)S(1)}, f32[160,160]{1,0:T(8,128)S(1)}, f32[8,768]{1,0:T(8,128)S(1)}) custom-call(s32[4]{0:T(128)S(1)} %broadcast_xor_fusion.1.order_ref, s32[2]{0:T(128)S(1)} %pad_add_fusion.1.place_ref, bf16[160,512]{1,0:T(8,128)(2,1)S(1)} %fusion.11.refs_0_, bf16[160,512]{1,0:T(8,128)(2,1)S(1)} %collective-permute-done.13.refs_1_, ...), custom_call_target="tpu_custom_call" | custom-call | flops 1 | bytes 1 | tf_op jit(solution)/shard_map/down_1_0/pallas_call | solution.py:205
  81.3 3.6 %collective-permute-done.12 = bf16[2,160,512]{2,1,0:T(8,128)(2,1)S(1)} collective-permute-done((bf16[2,160,512]{2,1,0:T(8,128)(2,1)S(1)}, bf16[2,160,512]{2,1,0:T(8,128)(2,1)S(1)}, u32[]{:S(2)}, u32[]{:S(2)}) %collective-permute-start.12) | collective-permute-done | bytes 327712 | tf_op jit(solution)/shard_map/ppermute | solution.py:359
  85.1 1.6 %collective-permute-start.19 = (bf16[160,512]{1,0:T(8,128)(2,1)S(1)}, bf16[160,512]{1,0:T(8,128)(2,1)S(1)}, u32[]{:S(2)}, u32[]{:S(2)}) collective-permute-start(bf16[160,512]{1,0:T(8,128)(2,1)S(1)} %fusion.7.refs_0_), channel_id=1, source_target_pairs={{0,2},{1,3},{2,0},{3,1},{4,6},{5,7},{6,4},{7,5},{8,10},{9,11},{10,... | collective-permute-start | bytes 491528 | tf_op jit(solution)/shard_map/ppermute | solution.py:359
  86.7 1.7 %collective-permute-done.23.refs_1_ = bf16[160,512]{1,0:T(8,128)(2,1)S(1)} collective-permute-done((bf16[160,512]{1,0:T(8,128)(2,1)S(1)}, bf16[160,512]{1,0:T(8,128)(2,1)S(1)}, u32[]{:S(2)}, u32[]{:S(2)}) %collective-permute-start.23) | collective-permute-done | bytes 163872 | tf_op jit(solution)/shard_map/ppermute | solution.py:359
  88.9 1.6 %collective-permute-done.19.refs_1_ = bf16[160,512]{1,0:T(8,128)(2,1)S(1)} collective-permute-done((bf16[160,512]{1,0:T(8,128)(2,1)S(1)}, bf16[160,512]{1,0:T(8,128)(2,1)S(1)}, u32[]{:S(2)}, u32[]{:S(2)}) %collective-permute-start.19) | collective-permute-done | bytes 163872 | tf_op jit(solution)/shard_map/ppermute | solution.py:359
  90.6 2.3 %down_2_0.1 = (f32[160,768]{1,0:T(8,128)S(1)}, f32[160,160]{1,0:T(8,128)S(1)}, f32[8,768]{1,0:T(8,128)S(1)}) custom-call(s32[4]{0:T(128)S(1)} %broadcast_xor_fusion.1.order_ref, s32[2]{0:T(128)S(1)} %pad_add_fusion.1.place_ref, bf16[160,512]{1,0:T(8,128)(2,1)S(1)} %fusion.5.refs_0_, bf16[160,512]{1,0:T(8,128)(2,1)S(1)} %collective-permute-done.23.refs_1_, ...), custom_call_target="tpu_custom_call" | custom-call | flops 1 | bytes 1 | tf_op jit(solution)/shard_map/down_2_0/pallas_call | solution.py:205
  92.9 1.9 %down_3_0.1 = (f32[160,768]{1,0:T(8,128)S(1)}, f32[160,160]{1,0:T(8,128)S(1)}, f32[8,768]{1,0:T(8,128)S(1)}) custom-call(s32[4]{0:T(128)S(1)} %broadcast_xor_fusion.1.order_ref, s32[2]{0:T(128)S(1)} %pad_add_fusion.1.place_ref, bf16[160,512]{1,0:T(8,128)(2,1)S(1)} %fusion.7.refs_0_, bf16[160,512]{1,0:T(8,128)(2,1)S(1)} %collective-permute-done.19.refs_1_, ...), custom_call_target="tpu_custom_call" | custom-call | flops 1 | bytes 1 | tf_op jit(solution)/shard_map/down_3_0/pallas_call | solution.py:205
  94.8 1.9 %down_3_3.1 = (bf16[160,256]{1,0:T(8,128)(2,1)S(1)}, bf16[160,256]{1,0:T(8,128)(2,1)S(1)}, bf16[160,256]{1,0:T(8,128)(2,1)S(1)}, bf16[160,256]{1,0:T(8,128)(2,1)...) custom-call(s32[4]{0:T(128)S(1)} %broadcast_xor_fusion.1.order_ref, ...), custom_call_target="tpu_custom_call" | custom-call | flops 1 | bytes 1 | tf_op jit(solution)/shard_map/down_3_3/pallas_call | solution.py:205
  98.4 4.1 %collective-permute-start.29 = (bf16[160,256]{1,0:T(8,128)(2,1)S(1)}, bf16[160,256]{1,0:T(8,128)(2,1)S(1)}, u32[]{:S(2)}, u32[]{:S(2)}) collective-permute-start(bf16[160,256]{1,0:T(8,128)(2,1)S(1)} %get-tuple-element.83), channel_id=1, source_target_pairs={{0,16},{4,20},{8,24},{12,28},{16,0},{20,4},{24,8},{28,12},{1,17},{... | collective-permute-start | bytes 245768 | tf_op jit(solution)/shard_map/ppermute | solution.py:369
  103.5 2.6 %collective-permute-start.31 = (bf16[160,256]{1,0:T(8,128)(2,1)S(1)}, bf16[160,256]{1,0:T(8,128)(2,1)S(1)}, u32[]{:S(2)}, u32[]{:S(2)}) collective-permute-start(bf16[160,256]{1,0:T(8,128)(2,1)S(1)} %get-tuple-element.85), channel_id=1, source_target_pairs={{0,24},{4,28},{8,0},{12,4},{16,8},{20,12},{24,16},{28,20},{1,25},{... | collective-permute-start | bytes 245768 | tf_op jit(solution)/shard_map/ppermute | solution.py:369
  106.1 1.8 %collective-permute-start.32 = (bf16[160,256]{1,0:T(8,128)(2,1)S(1)}, bf16[160,256]{1,0:T(8,128)(2,1)S(1)}, u32[]{:S(2)}, u32[]{:S(2)}) collective-permute-start(bf16[160,256]{1,0:T(8,128)(2,1)S(1)} %get-tuple-element.86), channel_id=1, source_target_pairs={{0,28},{4,24},{8,4},{12,0},{16,12},{20,8},{24,20},{28,16},{1,29},{... | collective-permute-start | bytes 245768 | tf_op jit(solution)/shard_map/ppermute | solution.py:369
  111.8 1.7 %collective-permute-done.30.refs_5_ = bf16[160,256]{1,0:T(8,128)(2,1)S(1)} collective-permute-done((bf16[160,256]{1,0:T(8,128)(2,1)S(1)}, bf16[160,256]{1,0:T(8,128)(2,1)S(1)}, u32[]{:S(2)}, u32[]{:S(2)}) %collective-permute-start.30) | collective-permute-done | bytes 81952 | tf_op jit(solution)/shard_map/ppermute | solution.py:369
  114.2 5.3 %solve.1 = (f32[512,96]{1,0:T(8,128)S(1)}, f32[512,96]{1,0:T(8,128)S(1)}, f32[512,96]{1,0:T(8,128)S(1)}, f32[32,1,128]{2,1,0:T(1,128)S(1)}) custom-call(f32[1]{0:T(128)} %bitcast.2.own_ref, bf16[1280,512]{1,0:T(8,128)(2,1)S(1)} %get-tuple-element.76.hot_ref, bf16[512,1280]{1,0:T(8,128)(2,1)S(1)} %get-tuple-element.77.turned_ref, ...), custom_call_target="tpu_custom_call" | custom-call | flops 1 | bytes 1 | tf_op jit(solution)/shard_map/solve/pallas_call | solution.py:456
  119.6 12.4 %all_to_all.10.sums_ref = f32[32,1,128]{2,1,0:T(1,128)S(1)} all-to-all(f32[32,1,128]{2,1,0:T(1,128)S(1)} %get-tuple-element.90), channel_id=1, replica_groups=mesh['dp'=4,'tensor'=2,'col'=4] {'dp','tensor','col'}, dimensions={0} | all-to-all | bytes 32768 | tf_op jit(solution)/shard_map/all_to_all | solution.py:463
  132.9 10.7 %all_to_all.11.pieces_ref = bf16[8,96,128]{2,1,0:T(8,128)(2,1)S(1)} all-to-all(bf16[8,96,128]{2,1,0:T(8,128)(2,1)S(1)} %finish.1), channel_id=1, replica_groups=mesh['dp'=4,'tensor'=2,'col'=4] {'dp','tensor'}, dimensions={0} | all-to-all | bytes 393216 | tf_op jit(solution)/shard_map/all_to_all | solution.py:472
  (82 shorter events, 21.3 us)
Async XLA Ops:
  2.8 9.3 %collective-permute-start = (bf16[40,1536]{1,0:T(8,128)(2,1)S(1)}, bf16[40,1536]{1,0:T(8,128)(2,1)S(1)}, u32[]{:S(2)}, u32[]{:S(2)}) collective-permute-start(bf16[40,1536]{1,0:T(8,128)(2,1)S(1)} %get-tuple-element.48), channel_id=1, source_target_pairs={{0,8},{4,12},{8,16},{12,20},{16,24},{20,28},{24,0},{28,4},{1,9},{5... | collective-permute-start | bytes 368648 | tf_op jit(solution)/shard_map/ppermute | solution.py:369
  5.9 15.2 %collective-permute-start.4 = (bf16[40,1536]{1,0:T(8,128)(2,1)S(1)}, bf16[40,1536]{1,0:T(8,128)(2,1)S(1)}, u32[]{:S(2)}, u32[]{:S(2)}) collective-permute-start(bf16[40,1536]{1,0:T(8,128)(2,1)S(1)} %get-tuple-element.51), channel_id=1, source_target_pairs={{0,16},{4,20},{8,24},{12,28},{16,0},{20,4},{24,8},{28,12},{1,17},{... | collective-permute-start | bytes 368648 | tf_op jit(solution)/shard_map/ppermute | solution.py:369
  8.5 12.7 %collective-permute-start.5 = (bf16[40,1536]{1,0:T(8,128)(2,1)S(1)}, bf16[40,1536]{1,0:T(8,128)(2,1)S(1)}, u32[]{:S(2)}, u32[]{:S(2)}) collective-permute-start(bf16[40,1536]{1,0:T(8,128)(2,1)S(1)} %get-tuple-element.52), channel_id=1, source_target_pairs={{0,24},{4,28},{8,0},{12,4},{16,8},{20,12},{24,16},{28,20},{1,25},{... | collective-permute-start | bytes 368648 | tf_op jit(solution)/shard_map/ppermute | solution.py:369
  12.2 9.0 %collective-permute-start.3 = (f32[4,128]{1,0:T(4,128)S(1)}, f32[4,128]{1,0:T(4,128)S(1)}, u32[]{:S(2)}, u32[]{:S(2)}) collective-permute-start(f32[4,128]{1,0:T(4,128)S(1)} %pad_add_fusion.info_ref.refs_4_.refs_0_), channel_id=1, source_target_pairs={{0,24},{4,28},{8,0},{12,4},{16,8},{20,12},{24,16},{28,20},{1,25},{... | collective-permute-start | bytes 6152 | tf_op jit(solution)/shard_map/ppermute | solution.py:369
  13.5 7.6 %collective-permute-start.2 = (f32[4,128]{1,0:T(4,128)S(1)}, f32[4,128]{1,0:T(4,128)S(1)}, u32[]{:S(2)}, u32[]{:S(2)}) collective-permute-start(f32[4,128]{1,0:T(4,128)S(1)} %pad_add_fusion.info_ref.refs_4_.refs_0_), channel_id=1, source_target_pairs={{0,16},{4,20},{8,24},{12,28},{16,0},{20,4},{24,8},{28,12},{1,17},{... | collective-permute-start | bytes 6152 | tf_op jit(solution)/shard_map/ppermute | solution.py:369
  18.4 5.4 %collective-permute-start.1 = (f32[4,128]{1,0:T(4,128)S(1)}, f32[4,128]{1,0:T(4,128)S(1)}, u32[]{:S(2)}, u32[]{:S(2)}) collective-permute-start(f32[4,128]{1,0:T(4,128)S(1)} %pad_add_fusion.info_ref.refs_4_.refs_0_), channel_id=1, source_target_pairs={{0,8},{4,12},{8,16},{12,20},{16,24},{20,28},{24,0},{28,4},{1,9},{5... | collective-permute-start | bytes 6152 | tf_op jit(solution)/shard_map/ppermute | solution.py:369
  28.8 8.8 %collective-permute-start.6 = (bf16[2,2,160,512]{3,2,1,0:T(8,128)(2,1)S(1)}, bf16[2,2,160,512]{3,2,1,0:T(8,128)(2,1)S(1)}, u32[]{:S(2)}, u32[]{:S(2)}) collective-permute-start(bf16[2,2,160,512]{3,2,1,0:T(8,128)(2,1)S(1)} %gate_up_0.1), channel_id=1, source_target_pairs={{0,1},{1,0},{2,3},{3,2},{4,5},{5,4},{6,7},{7,6},{8,9},{9,8},{10,11... | collective-permute-start | bytes 1966088 | tf_op jit(solution)/shard_map/ppermute | solution.py:356
  37.0 10.5 %collective-permute-start.8 = (bf16[2,2,160,512]{3,2,1,0:T(8,128)(2,1)S(1)}, bf16[2,2,160,512]{3,2,1,0:T(8,128)(2,1)S(1)}, u32[]{:S(2)}, u32[]{:S(2)}) collective-permute-start(bf16[2,2,160,512]{3,2,1,0:T(8,128)(2,1)S(1)} %get-tuple-element.55), channel_id=1, source_target_pairs={{0,1},{1,0},{2,3},{3,2},{4,5},{5,4},{6,7},{7,6},{8,9},{9,8},{10,11... | collective-permute-start | bytes 1966088 | tf_op jit(solution)/shard_map/ppermute | solution.py:356
  37.7 10.5 %collective-permute-start.7 = (bf16[2,160,512]{2,1,0:T(8,128)(2,1)S(1)}, bf16[2,160,512]{2,1,0:T(8,128)(2,1)S(1)}, u32[]{:S(2)}, u32[]{:S(2)}) collective-permute-start(bf16[2,160,512]{2,1,0:T(8,128)(2,1)S(1)} %fusion), channel_id=1, source_target_pairs={{0,2},{1,3},{2,0},{3,1},{4,6},{5,7},{6,4},{7,5},{8,10},{9,11},{10,... | collective-permute-start | bytes 983048 | tf_op jit(solution)/shard_map/ppermute | solution.py:359
  47.4 9.7 %collective-permute-start.10 = (bf16[2,2,160,512]{3,2,1,0:T(8,128)(2,1)S(1)}, bf16[2,2,160,512]{3,2,1,0:T(8,128)(2,1)S(1)}, u32[]{:S(2)}, u32[]{:S(2)}) collective-permute-start(bf16[2,2,160,512]{3,2,1,0:T(8,128)(2,1)S(1)} %get-tuple-element.57), channel_id=1, source_target_pairs={{0,1},{1,0},{2,3},{3,2},{4,5},{5,4},{6,7},{7,6},{8,9},{9,8},{10,11... | collective-permute-start | bytes 1966088 | tf_op jit(solution)/shard_map/ppermute | solution.py:356
  47.6 11.2 %collective-permute-start.9 = (bf16[2,160,512]{2,1,0:T(8,128)(2,1)S(1)}, bf16[2,160,512]{2,1,0:T(8,128)(2,1)S(1)}, u32[]{:S(2)}, u32[]{:S(2)}) collective-permute-start(bf16[2,160,512]{2,1,0:T(8,128)(2,1)S(1)} %fusion.1.rest_2_), channel_id=1, source_target_pairs={{0,2},{1,3},{2,0},{3,1},{4,6},{5,7},{6,4},{7,5},{8,10},{9,11},{10,... | collective-permute-start | bytes 983048 | tf_op jit(solution)/shard_map/ppermute | solution.py:359
  56.9 6.9 %collective-permute-start.11 = (bf16[2,2,160,512]{3,2,1,0:T(8,128)(2,1)S(1)}, bf16[2,2,160,512]{3,2,1,0:T(8,128)(2,1)S(1)}, u32[]{:S(2)}, u32[]{:S(2)}) collective-permute-start(bf16[2,2,160,512]{3,2,1,0:T(8,128)(2,1)S(1)} %get-tuple-element.58), channel_id=1, source_target_pairs={{0,1},{1,0},{2,3},{3,2},{4,5},{5,4},{6,7},{7,6},{8,9},{9,8},{10,11... | collective-permute-start | bytes 1966088 | tf_op jit(solution)/shard_map/ppermute | solution.py:356
  57.3 20.9 %collective-permute-start.22 = (bf16[2,160,512]{2,1,0:T(8,128)(2,1)S(1)}, bf16[2,160,512]{2,1,0:T(8,128)(2,1)S(1)}, u32[]{:S(2)}, u32[]{:S(2)}) collective-permute-start(bf16[2,160,512]{2,1,0:T(8,128)(2,1)S(1)} %fusion.2.rest_2_), channel_id=1, source_target_pairs={{0,2},{1,3},{2,0},{3,1},{4,6},{5,7},{6,4},{7,5},{8,10},{9,11},{10,... | collective-permute-start | bytes 983048 | tf_op jit(solution)/shard_map/ppermute | solution.py:359
  64.1 11.7 %collective-permute-start.17 = (bf16[160,512]{1,0:T(8,128)(2,1)S(1)}, bf16[160,512]{1,0:T(8,128)(2,1)S(1)}, u32[]{:S(2)}, u32[]{:S(2)}) collective-permute-start(bf16[160,512]{1,0:T(8,128)(2,1)S(1)} %fusion.9.refs_0_), channel_id=1, source_target_pairs={{0,1},{1,0},{2,3},{3,2},{4,5},{5,4},{6,7},{7,6},{8,9},{9,8},{10,11... | collective-permute-start | bytes 491528 | tf_op jit(solution)/shard_map/ppermute | solution.py:356
  64.2 7.1 %collective-permute-start.16 = (bf16[160,512]{1,0:T(8,128)(2,1)S(1)}, bf16[160,512]{1,0:T(8,128)(2,1)S(1)}, u32[]{:S(2)}, u32[]{:S(2)}) collective-permute-start(bf16[160,512]{1,0:T(8,128)(2,1)S(1)} %fusion.9.refs_0_), channel_id=1, source_target_pairs={{0,2},{1,3},{2,0},{3,1},{4,6},{5,7},{6,4},{7,5},{8,10},{9,11},{10,... | collective-permute-start | bytes 491528 | tf_op jit(solution)/shard_map/ppermute | solution.py:359
  65.3 9.0 %collective-permute-start.13 = (bf16[160,512]{1,0:T(8,128)(2,1)S(1)}, bf16[160,512]{1,0:T(8,128)(2,1)S(1)}, u32[]{:S(2)}, u32[]{:S(2)}) collective-permute-start(bf16[160,512]{1,0:T(8,128)(2,1)S(1)} %fusion.11.refs_0_), channel_id=1, source_target_pairs={{0,2},{1,3},{2,0},{3,1},{4,6},{5,7},{6,4},{7,5},{8,10},{9,11},{10,... | collective-permute-start | bytes 491528 | tf_op jit(solution)/shard_map/ppermute | solution.py:359
  71.2 4.6 %collective-permute-start.18 = (bf16[160,512]{1,0:T(8,128)(2,1)S(1)}, bf16[160,512]{1,0:T(8,128)(2,1)S(1)}, u32[]{:S(2)}, u32[]{:S(2)}) collective-permute-start(bf16[160,512]{1,0:T(8,128)(2,1)S(1)} %collective-permute-done.16.refs_1_), channel_id=1, source_target_pairs={{0,1},{1,0},{2,3},{3,2},{4,5},{5,4},{6,7},{7,6},{8,9},{9,8},{10,11... | collective-permute-start | bytes 491528 | tf_op jit(solution)/shard_map/ppermute | solution.py:356
  71.2 7.7 %collective-permute-start.14 = (bf16[160,512]{1,0:T(8,128)(2,1)S(1)}, bf16[160,512]{1,0:T(8,128)(2,1)S(1)}, u32[]{:S(2)}, u32[]{:S(2)}) collective-permute-start(bf16[160,512]{1,0:T(8,128)(2,1)S(1)} %fusion.11.refs_0_), channel_id=1, source_target_pairs={{0,1},{1,0},{2,3},{3,2},{4,5},{5,4},{6,7},{7,6},{8,9},{9,8},{10,11... | collective-permute-start | bytes 491528 | tf_op jit(solution)/shard_map/ppermute | solution.py:356
  74.3 10.6 %collective-permute-start.12 = (bf16[2,160,512]{2,1,0:T(8,128)(2,1)S(1)}, bf16[2,160,512]{2,1,0:T(8,128)(2,1)S(1)}, u32[]{:S(2)}, u32[]{:S(2)}) collective-permute-start(bf16[2,160,512]{2,1,0:T(8,128)(2,1)S(1)} %fusion.3), channel_id=1, source_target_pairs={{0,2},{1,3},{2,0},{3,1},{4,6},{5,7},{6,4},{7,5},{8,10},{9,11},{10,... | collective-permute-start | bytes 983048 | tf_op jit(solution)/shard_map/ppermute | solution.py:359
  75.8 3.2 %collective-permute-start.15 = (bf16[160,512]{1,0:T(8,128)(2,1)S(1)}, bf16[160,512]{1,0:T(8,128)(2,1)S(1)}, u32[]{:S(2)}, u32[]{:S(2)}) collective-permute-start(bf16[160,512]{1,0:T(8,128)(2,1)S(1)} %collective-permute-done.13.refs_1_), channel_id=1, source_target_pairs={{0,1},{1,0},{2,3},{3,2},{4,5},{5,4},{6,7},{7,6},{8,9},{9,8},{10,11... | collective-permute-start | bytes 491528 | tf_op jit(solution)/shard_map/ppermute | solution.py:356
  78.4 10.0 %collective-permute-start.23 = (bf16[160,512]{1,0:T(8,128)(2,1)S(1)}, bf16[160,512]{1,0:T(8,128)(2,1)S(1)}, u32[]{:S(2)}, u32[]{:S(2)}) collective-permute-start(bf16[160,512]{1,0:T(8,128)(2,1)S(1)} %fusion.5.refs_0_), channel_id=1, source_target_pairs={{0,2},{1,3},{2,0},{3,1},{4,6},{5,7},{6,4},{7,5},{8,10},{9,11},{10,... | collective-permute-start | bytes 491528 | tf_op jit(solution)/shard_map/ppermute | solution.py:359
  85.1 5.4 %collective-permute-start.19 = (bf16[160,512]{1,0:T(8,128)(2,1)S(1)}, bf16[160,512]{1,0:T(8,128)(2,1)S(1)}, u32[]{:S(2)}, u32[]{:S(2)}) collective-permute-start(bf16[160,512]{1,0:T(8,128)(2,1)S(1)} %fusion.7.refs_0_), channel_id=1, source_target_pairs={{0,2},{1,3},{2,0},{3,1},{4,6},{5,7},{6,4},{7,5},{8,10},{9,11},{10,... | collective-permute-start | bytes 491528 | tf_op jit(solution)/shard_map/ppermute | solution.py:359
  86.7 3.9 %collective-permute-start.24 = (bf16[160,512]{1,0:T(8,128)(2,1)S(1)}, bf16[160,512]{1,0:T(8,128)(2,1)S(1)}, u32[]{:S(2)}, u32[]{:S(2)}) collective-permute-start(bf16[160,512]{1,0:T(8,128)(2,1)S(1)} %fusion.5.refs_0_), channel_id=1, source_target_pairs={{0,1},{1,0},{2,3},{3,2},{4,5},{5,4},{6,7},{7,6},{8,9},{9,8},{10,11... | collective-permute-start | bytes 491528 | tf_op jit(solution)/shard_map/ppermute | solution.py:356
  88.4 4.5 %collective-permute-start.21 = (bf16[160,512]{1,0:T(8,128)(2,1)S(1)}, bf16[160,512]{1,0:T(8,128)(2,1)S(1)}, u32[]{:S(2)}, u32[]{:S(2)}) collective-permute-start(bf16[160,512]{1,0:T(8,128)(2,1)S(1)} %fusion.7.refs_0_), channel_id=1, source_target_pairs={{0,1},{1,0},{2,3},{3,2},{4,5},{5,4},{6,7},{7,6},{8,9},{9,8},{10,11... | collective-permute-start | bytes 491528 | tf_op jit(solution)/shard_map/ppermute | solution.py:356
  90.6 4.2 %collective-permute-start.20 = (bf16[160,512]{1,0:T(8,128)(2,1)S(1)}, bf16[160,512]{1,0:T(8,128)(2,1)S(1)}, u32[]{:S(2)}, u32[]{:S(2)}) collective-permute-start(bf16[160,512]{1,0:T(8,128)(2,1)S(1)} %collective-permute-done.19.refs_1_), channel_id=1, source_target_pairs={{0,1},{1,0},{2,3},{3,2},{4,5},{5,4},{6,7},{7,6},{8,9},{9,8},{10,11... | collective-permute-start | bytes 491528 | tf_op jit(solution)/shard_map/ppermute | solution.py:356
  96.7 6.8 %collective-permute-start.26 = (bf16[160,256]{1,0:T(8,128)(2,1)S(1)}, bf16[160,256]{1,0:T(8,128)(2,1)S(1)}, u32[]{:S(2)}, u32[]{:S(2)}) collective-permute-start(bf16[160,256]{1,0:T(8,128)(2,1)S(1)} %get-tuple-element.80), channel_id=1, source_target_pairs={{0,4},{4,0},{8,12},{12,8},{16,20},{20,16},{24,28},{28,24},{1,5},{5... | collective-permute-start | bytes 245768 | tf_op jit(solution)/shard_map/ppermute | solution.py:369
  98.2 7.9 %collective-permute-start.27 = (bf16[160,256]{1,0:T(8,128)(2,1)S(1)}, bf16[160,256]{1,0:T(8,128)(2,1)S(1)}, u32[]{:S(2)}, u32[]{:S(2)}) collective-permute-start(bf16[160,256]{1,0:T(8,128)(2,1)S(1)} %get-tuple-element.81), channel_id=1, source_target_pairs={{0,8},{4,12},{8,16},{12,20},{16,24},{20,28},{24,0},{28,4},{1,9},{5... | collective-permute-start | bytes 245768 | tf_op jit(solution)/shard_map/ppermute | solution.py:369
  98.4 12.2 %collective-permute-start.28 = (bf16[160,256]{1,0:T(8,128)(2,1)S(1)}, bf16[160,256]{1,0:T(8,128)(2,1)S(1)}, u32[]{:S(2)}, u32[]{:S(2)}) collective-permute-start(bf16[160,256]{1,0:T(8,128)(2,1)S(1)} %get-tuple-element.82), channel_id=1, source_target_pairs={{0,12},{4,8},{8,20},{12,16},{16,28},{20,24},{24,4},{28,0},{1,13},{... | collective-permute-start | bytes 245768 | tf_op jit(solution)/shard_map/ppermute | solution.py:369
  98.4 13.4 %collective-permute-start.29 = (bf16[160,256]{1,0:T(8,128)(2,1)S(1)}, bf16[160,256]{1,0:T(8,128)(2,1)S(1)}, u32[]{:S(2)}, u32[]{:S(2)}) collective-permute-start(bf16[160,256]{1,0:T(8,128)(2,1)S(1)} %get-tuple-element.83), channel_id=1, source_target_pairs={{0,16},{4,20},{8,24},{12,28},{16,0},{20,4},{24,8},{28,12},{1,17},{... | collective-permute-start | bytes 245768 | tf_op jit(solution)/shard_map/ppermute | solution.py:369
  102.6 10.9 %collective-permute-start.30 = (bf16[160,256]{1,0:T(8,128)(2,1)S(1)}, bf16[160,256]{1,0:T(8,128)(2,1)S(1)}, u32[]{:S(2)}, u32[]{:S(2)}) collective-permute-start(bf16[160,256]{1,0:T(8,128)(2,1)S(1)} %get-tuple-element.84), channel_id=1, source_target_pairs={{0,20},{4,16},{8,28},{12,24},{16,4},{20,0},{24,12},{28,8},{1,21},{... | collective-permute-start | bytes 245768 | tf_op jit(solution)/shard_map/ppermute | solution.py:369
  103.5 10.0 %collective-permute-start.31 = (bf16[160,256]{1,0:T(8,128)(2,1)S(1)}, bf16[160,256]{1,0:T(8,128)(2,1)S(1)}, u32[]{:S(2)}, u32[]{:S(2)}) collective-permute-start(bf16[160,256]{1,0:T(8,128)(2,1)S(1)} %get-tuple-element.85), channel_id=1, source_target_pairs={{0,24},{4,28},{8,0},{12,4},{16,8},{20,12},{24,16},{28,20},{1,25},{... | collective-permute-start | bytes 245768 | tf_op jit(solution)/shard_map/ppermute | solution.py:369
  106.1 8.1 %collective-permute-start.32 = (bf16[160,256]{1,0:T(8,128)(2,1)S(1)}, bf16[160,256]{1,0:T(8,128)(2,1)S(1)}, u32[]{:S(2)}, u32[]{:S(2)}) collective-permute-start(bf16[160,256]{1,0:T(8,128)(2,1)S(1)} %get-tuple-element.86), channel_id=1, source_target_pairs={{0,28},{4,24},{8,4},{12,0},{16,12},{20,8},{24,20},{28,16},{1,29},{... | collective-permute-start | bytes 245768 | tf_op jit(solution)/shard_map/ppermute | solution.py:369
  (7 other events, 105.9 us)

commit v6 on v5

--- a/solution.py
+++ b/solution.py
@@ -73,15 +73,26 @@
     count = first.shape[1]
     rows = lax.broadcasted_iota(jnp.int32, (CAP, count), 0).astype(f32)
     values = tokens_ref[...]
+    logits = info_ref[2:4, :]
+    high = logits.astype(bf16).astype(f32)
+    middle = (logits - high).astype(bf16).astype(f32)
+    extra = jnp.concatenate([info_ref[0:2, :], high, middle, logits - high - middle], axis=0)
+    extra = jnp.concatenate([extra, jnp.zeros((8, values.shape[1] - count), f32)], axis=1)
     for shift, out_ref in enumerate(out_refs):
         expert = (lax.rem(place_ref[0] + shift, parts) * tensor_count + place_ref[1]).astype(f32)
         hit = ((first == expert) & (rank_first == rows)) | ((second == expert) & (rank_second == rows))
-        out_ref[...] = mm(hit.astype(f32).astype(bf16), values).astype(bf16)
+        rows_picked = mm(hit.astype(f32).astype(bf16), values)
+        out_ref[...] = jnp.concatenate([rows_picked, extra], axis=0).astype(bf16)
 
 
 def stack_kernel(*refs):
-    pieces = refs[: (len(refs) - 1) // 2]
-    refs[-1][...] = jnp.concatenate([ref[...].astype(f32) for ref in pieces], axis=0).astype(bf16)
+    pieces, (rows_ref, info_ref) = refs[:-2], refs[-2:]
+    wide = [ref[...].astype(f32) for ref in pieces]
+    rows_ref[...] = jnp.concatenate([value[:CAP] for value in wide], axis=0).astype(bf16)
+    for index, value in enumerate(wide):
+        extra = value[CAP : CAP + 8, : info_ref.shape[2]]
+        info_ref[index, 0:2, :] = extra[0:2]
+        info_ref[index, 2:4, :] = extra[2:4] + extra[4:6] + extra[6:8]
 
 
 def gate_up_kernel(has_keep, order_ref, inputs_ref, gate_ref, up_ref, *rest):
@@ -220,7 +231,7 @@
 
 
 def route_kernel(blocks, tensor_count, kept_ref, place_ref, *refs):
-    infos = refs[:blocks]
+    infos = [refs[0][block] for block in range(blocks)]
     hot_ref, turned_ref, gates_ref, wide_ref = refs[-4:]
     count = infos[0].shape[1]
     slots = blocks * CAP
@@ -373,21 +384,19 @@
     info = upper + lax.pad(route_logits.T, f32(0), ((2, 0, 0), (0, 0, 0)))
     picked = single(
         functools.partial(pick_kernel, dp_count, tensor_count),
-        [jax.ShapeDtypeStruct((CAP, depth), bf16)] * dp_count,
+        [jax.ShapeDtypeStruct((CAP + 8, depth), bf16)] * dp_count,
         [scalars(), whole(), whole()],
         16,
         "pick",
     )(place, info, tokens)
     arrived = [shifted(value, ahead) for ahead, value in enumerate(picked)]
-    info = lax.optimization_barrier((info, arrived[1]))[0]
-    infos = [shifted(info, ahead) for ahead in range(dp_count)]
-    inputs = single(
+    inputs, infos = single(
         stack_kernel,
-        jax.ShapeDtypeStruct((slots, depth), bf16),
-        [whole()] * dp_count + [pl.BlockSpec(memory_space=pl.ANY)] * dp_count,
+        [jax.ShapeDtypeStruct((slots, depth), bf16), jax.ShapeDtypeStruct((dp_count, 4, tok_rows), f32)],
+        [whole()] * dp_count,
         16,
         "stack",
-    )(*arrived, *infos)
+    )(*arrived)
 
     gate_order = col_index ^ jnp.array([2, 0, 3, 1], jnp.int32)
     down_order = col_index ^ jnp.array([0, 2, 1, 3], jnp.int32)
@@ -445,11 +454,11 @@
             jax.ShapeDtypeStruct((total_tokens, total_slots), bf16),
             jax.ShapeDtypeStruct((total_slots, 2), f32),
         ],
-        [scalars(), scalars()] + [whole()] * dp_count + [pl.BlockSpec(memory_space=pl.ANY)],
+        [scalars(), scalars(), whole(), pl.BlockSpec(memory_space=pl.ANY)],
         24,
         "route",
         [pltpu.VMEM((total_slots, total_tokens), f32)],
-    )(kept_experts, place, *infos, square)
+    )(kept_experts, place, infos, square)
     is_kept = jnp.any(kept_experts == own_expert).astype(f32).reshape(1)
     field = jax.ShapeDtypeStruct((total_tokens, lanes), f32)
     everyone = parts * lax.axis_size("col")

time: 145 us -> 141 us (0.972)
  starting transfers between devices: 38.1 us -> 31.6 us
  waiting for transfers between devices: 22.8 us -> 25.3 us
    ppermute x13 -> x10, starting transfers between devices: 26.5 us -> 20 us  [shifted(): return lax.ppermute(values, ('dp', 'tensor'), pairs)]
    ppermute x13 -> x10, waiting for transfers between devices: 8.56 us -> 11.1 us  [shifted(): return lax.ppermute(values, ('dp', 'tensor'), pairs)]
  transfers between devices with their start and end apart: 33 -> 30, of which waited for: 10 -> 10; matrix products, arithmetic and copies ran while one was open for 2% -> 2% of each run, Pallas kernels for 28% -> 29%
where the time goes in v6:
time: 141 us
  Pallas kernels  55.1 us (39%)
  starting transfers between devices  31.6 us (22%)
  waiting for transfers between devices  25.3 us (18%)
  blocking collectives  23.2 us (16%)
  other arithmetic  3.29 us (2%)
    pallas_call x5, Pallas kernels, gate_up(): pl.pallas_call(functools.partial(gate_up_kernel, count), grid_spec=pltpu....  34.8 us
    ppermute x10, starting transfers between devices, shifted(): return lax.ppermute(values, ('dp', 'tensor'), pairs)  20 us
    ppermute x8, waiting for transfers between devices, across(): return lax.ppermute(values, 'col', [(k, k ^ 2) for k in range(4)])  14.2 us
    all_to_all x1, blocking collectives, one_expert_each(): lax.all_to_all(sums, ('dp', 'tensor', 'col'), split_axis=0, concat_axis=0...  12.6 us
    ppermute x10, waiting for transfers between devices, shifted(): return lax.ppermute(values, ('dp', 'tensor'), pairs)  11.1 us
    all_to_all x1, blocking collectives, one_expert_each(): lax.all_to_all(home, ('dp', 'tensor'), split_axis=0, concat_axis=0, tiled...  10.7 us
    pallas_call x5, Pallas kernels, down(): pl.pallas_call(functools.partial(down_kernel, len(pieces), pack, bool(old...  10.7 us
    ppermute x8, starting transfers between devices, across(): return lax.ppermute(values, 'col', [(k, k ^ 2) for k in range(4)])  9.57 us
  transfers between devices with their start and end apart: 30, of which 10 were waited for; matrix products, arithmetic and copies ran while one was open for 2% of the time, Pallas kernels for 29%

profile of v6, /device:TPU:0, one launch (start us, length us, event | category | flops | bytes accessed | tf_op | source)
XLA Modules:
  0.0 140.6 jit_solution(8842789123943827828)
XLA Ops:
  2.8 3.1 %collective-permute-start = (bf16[48,1536]{1,0:T(8,128)(2,1)S(1)}, bf16[48,1536]{1,0:T(8,128)(2,1)S(1)}, u32[]{:S(2)}, u32[]{:S(2)}) collective-permute-start(bf16[48,1536]{1,0:T(8,128)(2,1)S(1)} %get-tuple-element.50), channel_id=1, source_target_pairs={{0,8},{4,12},{8,16},{12,20},{16,24},{20,28},{24,0},{28,4},{1,9},{5... | collective-permute-start | bytes 442376 | tf_op jit(solution)/shard_map/ppermute | solution.py:380
  5.9 2.6 %collective-permute-start.1 = (bf16[48,1536]{1,0:T(8,128)(2,1)S(1)}, bf16[48,1536]{1,0:T(8,128)(2,1)S(1)}, u32[]{:S(2)}, u32[]{:S(2)}) collective-permute-start(bf16[48,1536]{1,0:T(8,128)(2,1)S(1)} %get-tuple-element.51), channel_id=1, source_target_pairs={{0,16},{4,20},{8,24},{12,28},{16,0},{20,4},{24,8},{28,12},{1,17},{... | collective-permute-start | bytes 442376 | tf_op jit(solution)/shard_map/ppermute | solution.py:380
  10.5 2.2 %collective-permute-done.refs_1_ = bf16[48,1536]{1,0:T(8,128)(2,1)S(1)} collective-permute-done((bf16[48,1536]{1,0:T(8,128)(2,1)S(1)}, bf16[48,1536]{1,0:T(8,128)(2,1)S(1)}, u32[]{:S(2)}, u32[]{:S(2)}) %collective-permute-start) | collective-permute-done | bytes 147488 | tf_op jit(solution)/shard_map/ppermute | solution.py:380
  12.7 5.5 %collective-permute-done.1.refs_2_ = bf16[48,1536]{1,0:T(8,128)(2,1)S(1)} collective-permute-done((bf16[48,1536]{1,0:T(8,128)(2,1)S(1)}, bf16[48,1536]{1,0:T(8,128)(2,1)S(1)}, u32[]{:S(2)}, u32[]{:S(2)}) %collective-permute-start.1) | collective-permute-done | bytes 147488 | tf_op jit(solution)/shard_map/ppermute | solution.py:380
  18.2 4.9 %gate_up_0.1 = bf16[2,2,160,512]{3,2,1,0:T(8,128)(2,1)S(1)} custom-call(s32[4]{0:T(128)S(1)} %broadcast_xor_fusion.order_ref, bf16[160,1536]{1,0:T(8,128)(2,1)S(1)} %get-tuple-element.54.inputs_ref, bf16[4,2048,1536]{2,1,0:T(8,128)(2,1)} %bitcast.71, bf16[4,2048,1536]{2,1,0:T(8,128)(2,1)} %bitcast.76), custom_call_target="tpu_custom_call" | custom-call | flops 4026531840 | bytes 25165824 | tf_op jit(solution)/shard_map/gate_up_0/pallas_call | solution.py:132
  23.2 8.2 %gate_up_1.1 = (bf16[2,2,160,512]{3,2,1,0:T(8,128)(2,1)S(1)}, bf16[2,2,160,512]{3,2,1,0:T(8,128)(2,1)S(1)}) custom-call(s32[4]{0:T(128)S(1)} %broadcast_xor_fusion.order_ref, bf16[160,1536]{1,0:T(8,128)(2,1)S(1)} %get-tuple-element.54.inputs_ref, bf16[4,2048,1536]{2,1,0:T(8,128)(2,1)} %bitcast.72, bf16[4,2048,1536]{2,1,0:T(8,128)(2,1)} %bitcast.77), custom_call_target="tpu_custom_call" | custom-call | flops 8053063680 | bytes 50331648 | tf_op jit(solution)/shard_map/gate_up_1/pallas_call | solution.py:132
  32.0 1.6 %collective-permute-start.4 = (bf16[2,160,512]{2,1,0:T(8,128)(2,1)S(1)}, bf16[2,160,512]{2,1,0:T(8,128)(2,1)S(1)}, u32[]{:S(2)}, u32[]{:S(2)}) collective-permute-start(bf16[2,160,512]{2,1,0:T(8,128)(2,1)S(1)} %fusion), channel_id=1, source_target_pairs={{0,2},{1,3},{2,0},{3,1},{4,6},{5,7},{6,4},{7,5},{8,10},{9,11},{10,... | collective-permute-start | bytes 983048 | tf_op jit(solution)/shard_map/ppermute | solution.py:370
  33.6 8.2 %gate_up_2.1 = (bf16[2,2,160,512]{3,2,1,0:T(8,128)(2,1)S(1)}, bf16[2,2,160,512]{3,2,1,0:T(8,128)(2,1)S(1)}) custom-call(s32[4]{0:T(128)S(1)} %broadcast_xor_fusion.order_ref, bf16[160,1536]{1,0:T(8,128)(2,1)S(1)} %get-tuple-element.54.inputs_ref, bf16[4,2048,1536]{2,1,0:T(8,128)(2,1)} %bitcast.73, bf16[4,2048,1536]{2,1,0:T(8,128)(2,1)} %bitcast.78, ...), custom_call_target="tpu_custom_call" | custom-call | flops 8053063680 | bytes 50331648 | tf_op jit(solution)/shard_map/gate_up_2/pallas_call | solution.py:132
  42.6 8.7 %gate_up_3.1 = (bf16[2,2,160,512]{3,2,1,0:T(8,128)(2,1)S(1)}, bf16[2,2,160,512]{3,2,1,0:T(8,128)(2,1)S(1)}) custom-call(s32[4]{0:T(128)S(1)} %broadcast_xor_fusion.order_ref, bf16[160,1536]{1,0:T(8,128)(2,1)S(1)} %get-tuple-element.54.inputs_ref, bf16[4,2048,1536]{2,1,0:T(8,128)(2,1)} %bitcast.74, bf16[4,2048,1536]{2,1,0:T(8,128)(2,1)} %bitcast.79, ...), custom_call_target="tpu_custom_call" | custom-call | flops 8053063680 | bytes 50331648 | tf_op jit(solution)/shard_map/gate_up_3/pallas_call | solution.py:132
  51.6 1.6 %collective-permute-start.19 = (bf16[2,160,512]{2,1,0:T(8,128)(2,1)S(1)}, bf16[2,160,512]{2,1,0:T(8,128)(2,1)S(1)}, u32[]{:S(2)}, u32[]{:S(2)}) collective-permute-start(bf16[2,160,512]{2,1,0:T(8,128)(2,1)S(1)} %fusion.2.rest_2_), channel_id=1, source_target_pairs={{0,2},{1,3},{2,0},{3,1},{4,6},{5,7},{6,4},{7,5},{8,10},{9,11},{10,... | collective-permute-start | bytes 983048 | tf_op jit(solution)/shard_map/ppermute | solution.py:370
  53.2 4.9 %gate_up_4.1 = bf16[2,2,160,512]{3,2,1,0:T(8,128)(2,1)S(1)} custom-call(s32[4]{0:T(128)S(1)} %broadcast_xor_fusion.order_ref, bf16[160,1536]{1,0:T(8,128)(2,1)S(1)} %get-tuple-element.54.inputs_ref, bf16[4,2048,1536]{2,1,0:T(8,128)(2,1)} %bitcast.75, bf16[4,2048,1536]{2,1,0:T(8,128)(2,1)} %bitcast.80, ...), custom_call_target="tpu_custom_call" | custom-call | flops 4026531840 | bytes 25165824 | tf_op jit(solution)/shard_map/gate_up_4/pallas_call | solution.py:132
  60.9 4.7 %collective-permute-done.13.refs_1_ = bf16[160,512]{1,0:T(8,128)(2,1)S(1)} collective-permute-done((bf16[160,512]{1,0:T(8,128)(2,1)S(1)}, bf16[160,512]{1,0:T(8,128)(2,1)S(1)}, u32[]{:S(2)}, u32[]{:S(2)}) %collective-permute-start.13) | collective-permute-done | bytes 163872 | tf_op jit(solution)/shard_map/ppermute | solution.py:370
  66.1 2.5 %collective-permute-done.10.refs_1_ = bf16[160,512]{1,0:T(8,128)(2,1)S(1)} collective-permute-done((bf16[160,512]{1,0:T(8,128)(2,1)S(1)}, bf16[160,512]{1,0:T(8,128)(2,1)S(1)}, u32[]{:S(2)}, u32[]{:S(2)}) %collective-permute-start.10) | collective-permute-done | bytes 163872 | tf_op jit(solution)/shard_map/ppermute | solution.py:370
  68.6 1.5 %collective-permute-start.9 = (bf16[2,160,512]{2,1,0:T(8,128)(2,1)S(1)}, bf16[2,160,512]{2,1,0:T(8,128)(2,1)S(1)}, u32[]{:S(2)}, u32[]{:S(2)}) collective-permute-start(bf16[2,160,512]{2,1,0:T(8,128)(2,1)S(1)} %fusion.3), channel_id=1, source_target_pairs={{0,2},{1,3},{2,0},{3,1},{4,6},{5,7},{6,4},{7,5},{8,10},{9,11},{10,... | collective-permute-start | bytes 983048 | tf_op jit(solution)/shard_map/ppermute | solution.py:370
  70.2 2.3 %down_0_0.1 = (f32[160,768]{1,0:T(8,128)S(1)}, f32[160,160]{1,0:T(8,128)S(1)}, f32[8,768]{1,0:T(8,128)S(1)}) custom-call(s32[4]{0:T(128)S(1)} %broadcast_xor_fusion.1.order_ref, s32[2]{0:T(128)S(1)} %pad_add_fusion.1.place_ref, bf16[160,512]{1,0:T(8,128)(2,1)S(1)} %fusion.9.refs_0_, bf16[160,512]{1,0:T(8,128)(2,1)S(1)} %collective-permute-done.13.refs_1_, ...), custom_call_target="tpu_custom_call" | custom-call | flops 1 | bytes 1 | tf_op jit(solution)/shard_map/down_0_0/pallas_call | solution.py:216
  73.3 2.3 %down_1_0.1 = (f32[160,768]{1,0:T(8,128)S(1)}, f32[160,160]{1,0:T(8,128)S(1)}, f32[8,768]{1,0:T(8,128)S(1)}) custom-call(s32[4]{0:T(128)S(1)} %broadcast_xor_fusion.1.order_ref, s32[2]{0:T(128)S(1)} %pad_add_fusion.1.place_ref, bf16[160,512]{1,0:T(8,128)(2,1)S(1)} %fusion.11.refs_0_, bf16[160,512]{1,0:T(8,128)(2,1)S(1)} %collective-permute-done.10.refs_1_, ...), custom_call_target="tpu_custom_call" | custom-call | flops 1 | bytes 1 | tf_op jit(solution)/shard_map/down_1_0/pallas_call | solution.py:216
  75.6 3.6 %collective-permute-done.9 = bf16[2,160,512]{2,1,0:T(8,128)(2,1)S(1)} collective-permute-done((bf16[2,160,512]{2,1,0:T(8,128)(2,1)S(1)}, bf16[2,160,512]{2,1,0:T(8,128)(2,1)S(1)}, u32[]{:S(2)}, u32[]{:S(2)}) %collective-permute-start.9) | collective-permute-done | bytes 327712 | tf_op jit(solution)/shard_map/ppermute | solution.py:370
  79.5 1.6 %collective-permute-start.16 = (bf16[160,512]{1,0:T(8,128)(2,1)S(1)}, bf16[160,512]{1,0:T(8,128)(2,1)S(1)}, u32[]{:S(2)}, u32[]{:S(2)}) collective-permute-start(bf16[160,512]{1,0:T(8,128)(2,1)S(1)} %fusion.7.refs_0_), channel_id=1, source_target_pairs={{0,2},{1,3},{2,0},{3,1},{4,6},{5,7},{6,4},{7,5},{8,10},{9,11},{10,... | collective-permute-start | bytes 491528 | tf_op jit(solution)/shard_map/ppermute | solution.py:370
  81.1 1.7 %collective-permute-done.20.refs_1_ = bf16[160,512]{1,0:T(8,128)(2,1)S(1)} collective-permute-done((bf16[160,512]{1,0:T(8,128)(2,1)S(1)}, bf16[160,512]{1,0:T(8,128)(2,1)S(1)}, u32[]{:S(2)}, u32[]{:S(2)}) %collective-permute-start.20) | collective-permute-done | bytes 163872 | tf_op jit(solution)/shard_map/ppermute | solution.py:370
  83.3 1.6 %collective-permute-done.16.refs_1_ = bf16[160,512]{1,0:T(8,128)(2,1)S(1)} collective-permute-done((bf16[160,512]{1,0:T(8,128)(2,1)S(1)}, bf16[160,512]{1,0:T(8,128)(2,1)S(1)}, u32[]{:S(2)}, u32[]{:S(2)}) %collective-permute-start.16) | collective-permute-done | bytes 163872 | tf_op jit(solution)/shard_map/ppermute | solution.py:370
  84.9 2.3 %down_2_0.1 = (f32[160,768]{1,0:T(8,128)S(1)}, f32[160,160]{1,0:T(8,128)S(1)}, f32[8,768]{1,0:T(8,128)S(1)}) custom-call(s32[4]{0:T(128)S(1)} %broadcast_xor_fusion.1.order_ref, s32[2]{0:T(128)S(1)} %pad_add_fusion.1.place_ref, bf16[160,512]{1,0:T(8,128)(2,1)S(1)} %fusion.5.refs_0_, bf16[160,512]{1,0:T(8,128)(2,1)S(1)} %collective-permute-done.20.refs_1_, ...), custom_call_target="tpu_custom_call" | custom-call | flops 1 | bytes 1 | tf_op jit(solution)/shard_map/down_2_0/pallas_call | solution.py:216
  87.3 1.9 %down_3_0.1 = (f32[160,768]{1,0:T(8,128)S(1)}, f32[160,160]{1,0:T(8,128)S(1)}, f32[8,768]{1,0:T(8,128)S(1)}) custom-call(s32[4]{0:T(128)S(1)} %broadcast_xor_fusion.1.order_ref, s32[2]{0:T(128)S(1)} %pad_add_fusion.1.place_ref, bf16[160,512]{1,0:T(8,128)(2,1)S(1)} %fusion.7.refs_0_, bf16[160,512]{1,0:T(8,128)(2,1)S(1)} %collective-permute-done.16.refs_1_, ...), custom_call_target="tpu_custom_call" | custom-call | flops 1 | bytes 1 | tf_op jit(solution)/shard_map/down_3_0/pallas_call | solution.py:216
  89.2 1.9 %down_3_3.1 = (bf16[160,256]{1,0:T(8,128)(2,1)S(1)}, bf16[160,256]{1,0:T(8,128)(2,1)S(1)}, bf16[160,256]{1,0:T(8,128)(2,1)S(1)}, bf16[160,256]{1,0:T(8,128)(2,1)...) custom-call(s32[4]{0:T(128)S(1)} %broadcast_xor_fusion.1.order_ref, ...), custom_call_target="tpu_custom_call" | custom-call | flops 1 | bytes 1 | tf_op jit(solution)/shard_map/down_3_3/pallas_call | solution.py:216
  92.6 3.6 %collective-permute-start.24 = (bf16[160,256]{1,0:T(8,128)(2,1)S(1)}, bf16[160,256]{1,0:T(8,128)(2,1)S(1)}, u32[]{:S(2)}, u32[]{:S(2)}) collective-permute-start(bf16[160,256]{1,0:T(8,128)(2,1)S(1)} %get-tuple-element.83), channel_id=1, source_target_pairs={{0,8},{4,12},{8,16},{12,20},{16,24},{20,28},{24,0},{28,4},{1,9},{5... | collective-permute-start | bytes 245768 | tf_op jit(solution)/shard_map/ppermute | solution.py:380
  96.2 1.6 %collective-permute-start.26 = (bf16[160,256]{1,0:T(8,128)(2,1)S(1)}, bf16[160,256]{1,0:T(8,128)(2,1)S(1)}, u32[]{:S(2)}, u32[]{:S(2)}) collective-permute-start(bf16[160,256]{1,0:T(8,128)(2,1)S(1)} %get-tuple-element.85), channel_id=1, source_target_pairs={{0,16},{4,20},{8,24},{12,28},{16,0},{20,4},{24,8},{28,12},{1,17},{... | collective-permute-start | bytes 245768 | tf_op jit(solution)/shard_map/ppermute | solution.py:380
  97.8 2.2 %collective-permute-start.27 = (bf16[160,256]{1,0:T(8,128)(2,1)S(1)}, bf16[160,256]{1,0:T(8,128)(2,1)S(1)}, u32[]{:S(2)}, u32[]{:S(2)}) collective-permute-start(bf16[160,256]{1,0:T(8,128)(2,1)S(1)} %get-tuple-element.86), channel_id=1, source_target_pairs={{0,20},{4,16},{8,28},{12,24},{16,4},{20,0},{24,12},{28,8},{1,21},{... | collective-permute-start | bytes 245768 | tf_op jit(solution)/shard_map/ppermute | solution.py:380
  100.0 3.8 %collective-permute-start.28 = (bf16[160,256]{1,0:T(8,128)(2,1)S(1)}, bf16[160,256]{1,0:T(8,128)(2,1)S(1)}, u32[]{:S(2)}, u32[]{:S(2)}) collective-permute-start(bf16[160,256]{1,0:T(8,128)(2,1)S(1)} %get-tuple-element.87), channel_id=1, source_target_pairs={{0,24},{4,28},{8,0},{12,4},{16,8},{20,12},{24,16},{28,20},{1,25},{... | collective-permute-start | bytes 245768 | tf_op jit(solution)/shard_map/ppermute | solution.py:380
  105.3 1.5 %route.1 = (bf16[1280,512]{1,0:T(8,128)(2,1)S(1)}, bf16[512,1280]{1,0:T(8,128)(2,1)S(1)}, f32[1280,2]{1,0:T(8,128)S(1)}) custom-call(s32[6]{0:T(128)S(1)} %copy-done.1, s32[2]{0:T(128)S(1)} %pad_add_fusion.1.place_ref, f32[4,4,128]{2,1,0:T(4,128)S(1)} %get-tuple-element.53.refs_0_, f32[8,768]{1,0:T(8,128)S(1)} %get-tuple-element.77.refs_1_.square_ref), custom_call_target="tpu_custom_call" | custom-call | flops 1 | bytes 1 | tf_op jit(solution)/shard_map/route/pallas_call | solution.py:450
  107.5 2.7 %collective-permute-done.27.refs_5_ = bf16[160,256]{1,0:T(8,128)(2,1)S(1)} collective-permute-done((bf16[160,256]{1,0:T(8,128)(2,1)S(1)}, bf16[160,256]{1,0:T(8,128)(2,1)S(1)}, u32[]{:S(2)}, u32[]{:S(2)}) %collective-permute-start.27) | collective-permute-done | bytes 81952 | tf_op jit(solution)/shard_map/ppermute | solution.py:380
  110.3 5.3 %solve.1 = (f32[512,96]{1,0:T(8,128)S(1)}, f32[512,96]{1,0:T(8,128)S(1)}, f32[512,96]{1,0:T(8,128)S(1)}, f32[32,1,128]{2,1,0:T(1,128)S(1)}) custom-call(f32[1]{0:T(128)} %bitcast.2.own_ref, bf16[1280,512]{1,0:T(8,128)(2,1)S(1)} %get-tuple-element.78.hot_ref, bf16[512,1280]{1,0:T(8,128)(2,1)S(1)} %get-tuple-element.79.turned_ref, ...), custom_call_target="tpu_custom_call" | custom-call | flops 1 | bytes 1 | tf_op jit(solution)/shard_map/solve/pallas_call | solution.py:465
  115.6 12.6 %all_to_all.10.sums_ref = f32[32,1,128]{2,1,0:T(1,128)S(1)} all-to-all(f32[32,1,128]{2,1,0:T(1,128)S(1)} %get-tuple-element.92), channel_id=1, replica_groups=mesh['dp'=4,'tensor'=2,'col'=4] {'dp','tensor','col'}, dimensions={0} | all-to-all | bytes 32768 | tf_op jit(solution)/shard_map/all_to_all | solution.py:472
  129.1 10.7 %all_to_all.11.pieces_ref = bf16[8,96,128]{2,1,0:T(8,128)(2,1)S(1)} all-to-all(bf16[8,96,128]{2,1,0:T(8,128)(2,1)S(1)} %finish.1), channel_id=1, replica_groups=mesh['dp'=4,'tensor'=2,'col'=4] {'dp','tensor'}, dimensions={0} | all-to-all | bytes 393216 | tf_op jit(solution)/shard_map/all_to_all | solution.py:481
  (76 shorter events, 16.4 us)
Async XLA Ops:
  2.8 9.9 %collective-permute-start = (bf16[48,1536]{1,0:T(8,128)(2,1)S(1)}, bf16[48,1536]{1,0:T(8,128)(2,1)S(1)}, u32[]{:S(2)}, u32[]{:S(2)}) collective-permute-start(bf16[48,1536]{1,0:T(8,128)(2,1)S(1)} %get-tuple-element.50), channel_id=1, source_target_pairs={{0,8},{4,12},{8,16},{12,20},{16,24},{20,28},{24,0},{28,4},{1,9},{5... | collective-permute-start | bytes 442376 | tf_op jit(solution)/shard_map/ppermute | solution.py:380
  5.9 12.3 %collective-permute-start.1 = (bf16[48,1536]{1,0:T(8,128)(2,1)S(1)}, bf16[48,1536]{1,0:T(8,128)(2,1)S(1)}, u32[]{:S(2)}, u32[]{:S(2)}) collective-permute-start(bf16[48,1536]{1,0:T(8,128)(2,1)S(1)} %get-tuple-element.51), channel_id=1, source_target_pairs={{0,16},{4,20},{8,24},{12,28},{16,0},{20,4},{24,8},{28,12},{1,17},{... | collective-permute-start | bytes 442376 | tf_op jit(solution)/shard_map/ppermute | solution.py:380
  8.5 9.7 %collective-permute-start.2 = (bf16[48,1536]{1,0:T(8,128)(2,1)S(1)}, bf16[48,1536]{1,0:T(8,128)(2,1)S(1)}, u32[]{:S(2)}, u32[]{:S(2)}) collective-permute-start(bf16[48,1536]{1,0:T(8,128)(2,1)S(1)} %get-tuple-element.52), channel_id=1, source_target_pairs={{0,24},{4,28},{8,0},{12,4},{16,8},{20,12},{24,16},{28,20},{1,25},{... | collective-permute-start | bytes 442376 | tf_op jit(solution)/shard_map/ppermute | solution.py:380
  23.1 8.8 %collective-permute-start.3 = (bf16[2,2,160,512]{3,2,1,0:T(8,128)(2,1)S(1)}, bf16[2,2,160,512]{3,2,1,0:T(8,128)(2,1)S(1)}, u32[]{:S(2)}, u32[]{:S(2)}) collective-permute-start(bf16[2,2,160,512]{3,2,1,0:T(8,128)(2,1)S(1)} %gate_up_0.1), channel_id=1, source_target_pairs={{0,1},{1,0},{2,3},{3,2},{4,5},{5,4},{6,7},{7,6},{8,9},{9,8},{10,11... | collective-permute-start | bytes 1966088 | tf_op jit(solution)/shard_map/ppermute | solution.py:367
  31.4 10.5 %collective-permute-start.5 = (bf16[2,2,160,512]{3,2,1,0:T(8,128)(2,1)S(1)}, bf16[2,2,160,512]{3,2,1,0:T(8,128)(2,1)S(1)}, u32[]{:S(2)}, u32[]{:S(2)}) collective-permute-start(bf16[2,2,160,512]{3,2,1,0:T(8,128)(2,1)S(1)} %get-tuple-element.57), channel_id=1, source_target_pairs={{0,1},{1,0},{2,3},{3,2},{4,5},{5,4},{6,7},{7,6},{8,9},{9,8},{10,11... | collective-permute-start | bytes 1966088 | tf_op jit(solution)/shard_map/ppermute | solution.py:367
  32.0 10.5 %collective-permute-start.4 = (bf16[2,160,512]{2,1,0:T(8,128)(2,1)S(1)}, bf16[2,160,512]{2,1,0:T(8,128)(2,1)S(1)}, u32[]{:S(2)}, u32[]{:S(2)}) collective-permute-start(bf16[2,160,512]{2,1,0:T(8,128)(2,1)S(1)} %fusion), channel_id=1, source_target_pairs={{0,2},{1,3},{2,0},{3,1},{4,6},{5,7},{6,4},{7,5},{8,10},{9,11},{10,... | collective-permute-start | bytes 983048 | tf_op jit(solution)/shard_map/ppermute | solution.py:370
  41.8 9.7 %collective-permute-start.7 = (bf16[2,2,160,512]{3,2,1,0:T(8,128)(2,1)S(1)}, bf16[2,2,160,512]{3,2,1,0:T(8,128)(2,1)S(1)}, u32[]{:S(2)}, u32[]{:S(2)}) collective-permute-start(bf16[2,2,160,512]{3,2,1,0:T(8,128)(2,1)S(1)} %get-tuple-element.59), channel_id=1, source_target_pairs={{0,1},{1,0},{2,3},{3,2},{4,5},{5,4},{6,7},{7,6},{8,9},{9,8},{10,11... | collective-permute-start | bytes 1966088 | tf_op jit(solution)/shard_map/ppermute | solution.py:367
  42.0 11.2 %collective-permute-start.6 = (bf16[2,160,512]{2,1,0:T(8,128)(2,1)S(1)}, bf16[2,160,512]{2,1,0:T(8,128)(2,1)S(1)}, u32[]{:S(2)}, u32[]{:S(2)}) collective-permute-start(bf16[2,160,512]{2,1,0:T(8,128)(2,1)S(1)} %fusion.1.rest_2_), channel_id=1, source_target_pairs={{0,2},{1,3},{2,0},{3,1},{4,6},{5,7},{6,4},{7,5},{8,10},{9,11},{10,... | collective-permute-start | bytes 983048 | tf_op jit(solution)/shard_map/ppermute | solution.py:370
  42.5 27.6 %slice-start = ((s8[12582912]{0:T(1024)(128)(4,1)}), s8[4194304]{0:T(1024)(128)(4,1)S(1)}, s32[]{:S(2)}) async-start(s8[12582912]{0:T(1024)(128)(4,1)} %bitcast.64), calls=%async_computation.2 | async-start | bytes 8388608
  42.6 27.6 %slice-start.1 = ((s8[12582912]{0:T(1024)(128)(4,1)}), s8[4194304]{0:T(1024)(128)(4,1)S(1)}, s32[]{:S(2)}) async-start(s8[12582912]{0:T(1024)(128)(4,1)} %bitcast.64), calls=%async_computation.3 | async-start | bytes 8388608
  51.2 6.9 %collective-permute-start.8 = (bf16[2,2,160,512]{3,2,1,0:T(8,128)(2,1)S(1)}, bf16[2,2,160,512]{3,2,1,0:T(8,128)(2,1)S(1)}, u32[]{:S(2)}, u32[]{:S(2)}) collective-permute-start(bf16[2,2,160,512]{3,2,1,0:T(8,128)(2,1)S(1)} %get-tuple-element.60), channel_id=1, source_target_pairs={{0,1},{1,0},{2,3},{3,2},{4,5},{5,4},{6,7},{7,6},{8,9},{9,8},{10,11... | collective-permute-start | bytes 1966088 | tf_op jit(solution)/shard_map/ppermute | solution.py:367
  51.6 20.9 %collective-permute-start.19 = (bf16[2,160,512]{2,1,0:T(8,128)(2,1)S(1)}, bf16[2,160,512]{2,1,0:T(8,128)(2,1)S(1)}, u32[]{:S(2)}, u32[]{:S(2)}) collective-permute-start(bf16[2,160,512]{2,1,0:T(8,128)(2,1)S(1)} %fusion.2.rest_2_), channel_id=1, source_target_pairs={{0,2},{1,3},{2,0},{3,1},{4,6},{5,7},{6,4},{7,5},{8,10},{9,11},{10,... | collective-permute-start | bytes 983048 | tf_op jit(solution)/shard_map/ppermute | solution.py:370
  58.4 11.7 %collective-permute-start.14 = (bf16[160,512]{1,0:T(8,128)(2,1)S(1)}, bf16[160,512]{1,0:T(8,128)(2,1)S(1)}, u32[]{:S(2)}, u32[]{:S(2)}) collective-permute-start(bf16[160,512]{1,0:T(8,128)(2,1)S(1)} %fusion.9.refs_0_), channel_id=1, source_target_pairs={{0,1},{1,0},{2,3},{3,2},{4,5},{5,4},{6,7},{7,6},{8,9},{9,8},{10,11... | collective-permute-start | bytes 491528 | tf_op jit(solution)/shard_map/ppermute | solution.py:367
  58.5 7.1 %collective-permute-start.13 = (bf16[160,512]{1,0:T(8,128)(2,1)S(1)}, bf16[160,512]{1,0:T(8,128)(2,1)S(1)}, u32[]{:S(2)}, u32[]{:S(2)}) collective-permute-start(bf16[160,512]{1,0:T(8,128)(2,1)S(1)} %fusion.9.refs_0_), channel_id=1, source_target_pairs={{0,2},{1,3},{2,0},{3,1},{4,6},{5,7},{6,4},{7,5},{8,10},{9,11},{10,... | collective-permute-start | bytes 491528 | tf_op jit(solution)/shard_map/ppermute | solution.py:370
  59.7 9.0 %collective-permute-start.10 = (bf16[160,512]{1,0:T(8,128)(2,1)S(1)}, bf16[160,512]{1,0:T(8,128)(2,1)S(1)}, u32[]{:S(2)}, u32[]{:S(2)}) collective-permute-start(bf16[160,512]{1,0:T(8,128)(2,1)S(1)} %fusion.11.refs_0_), channel_id=1, source_target_pairs={{0,2},{1,3},{2,0},{3,1},{4,6},{5,7},{6,4},{7,5},{8,10},{9,11},{10,... | collective-permute-start | bytes 491528 | tf_op jit(solution)/shard_map/ppermute | solution.py:370
  65.6 4.6 %collective-permute-start.15 = (bf16[160,512]{1,0:T(8,128)(2,1)S(1)}, bf16[160,512]{1,0:T(8,128)(2,1)S(1)}, u32[]{:S(2)}, u32[]{:S(2)}) collective-permute-start(bf16[160,512]{1,0:T(8,128)(2,1)S(1)} %collective-permute-done.13.refs_1_), channel_id=1, source_target_pairs={{0,1},{1,0},{2,3},{3,2},{4,5},{5,4},{6,7},{7,6},{8,9},{9,8},{10,11... | collective-permute-start | bytes 491528 | tf_op jit(solution)/shard_map/ppermute | solution.py:367
  65.6 7.7 %collective-permute-start.11 = (bf16[160,512]{1,0:T(8,128)(2,1)S(1)}, bf16[160,512]{1,0:T(8,128)(2,1)S(1)}, u32[]{:S(2)}, u32[]{:S(2)}) collective-permute-start(bf16[160,512]{1,0:T(8,128)(2,1)S(1)} %fusion.11.refs_0_), channel_id=1, source_target_pairs={{0,1},{1,0},{2,3},{3,2},{4,5},{5,4},{6,7},{7,6},{8,9},{9,8},{10,11... | collective-permute-start | bytes 491528 | tf_op jit(solution)/shard_map/ppermute | solution.py:367
  68.6 10.6 %collective-permute-start.9 = (bf16[2,160,512]{2,1,0:T(8,128)(2,1)S(1)}, bf16[2,160,512]{2,1,0:T(8,128)(2,1)S(1)}, u32[]{:S(2)}, u32[]{:S(2)}) collective-permute-start(bf16[2,160,512]{2,1,0:T(8,128)(2,1)S(1)} %fusion.3), channel_id=1, source_target_pairs={{0,2},{1,3},{2,0},{3,1},{4,6},{5,7},{6,4},{7,5},{8,10},{9,11},{10,... | collective-permute-start | bytes 983048 | tf_op jit(solution)/shard_map/ppermute | solution.py:370
  70.1 3.2 %collective-permute-start.12 = (bf16[160,512]{1,0:T(8,128)(2,1)S(1)}, bf16[160,512]{1,0:T(8,128)(2,1)S(1)}, u32[]{:S(2)}, u32[]{:S(2)}) collective-permute-start(bf16[160,512]{1,0:T(8,128)(2,1)S(1)} %collective-permute-done.10.refs_1_), channel_id=1, source_target_pairs={{0,1},{1,0},{2,3},{3,2},{4,5},{5,4},{6,7},{7,6},{8,9},{9,8},{10,11... | collective-permute-start | bytes 491528 | tf_op jit(solution)/shard_map/ppermute | solution.py:367
  72.7 10.0 %collective-permute-start.20 = (bf16[160,512]{1,0:T(8,128)(2,1)S(1)}, bf16[160,512]{1,0:T(8,128)(2,1)S(1)}, u32[]{:S(2)}, u32[]{:S(2)}) collective-permute-start(bf16[160,512]{1,0:T(8,128)(2,1)S(1)} %fusion.5.refs_0_), channel_id=1, source_target_pairs={{0,2},{1,3},{2,0},{3,1},{4,6},{5,7},{6,4},{7,5},{8,10},{9,11},{10,... | collective-permute-start | bytes 491528 | tf_op jit(solution)/shard_map/ppermute | solution.py:370
  79.5 5.4 %collective-permute-start.16 = (bf16[160,512]{1,0:T(8,128)(2,1)S(1)}, bf16[160,512]{1,0:T(8,128)(2,1)S(1)}, u32[]{:S(2)}, u32[]{:S(2)}) collective-permute-start(bf16[160,512]{1,0:T(8,128)(2,1)S(1)} %fusion.7.refs_0_), channel_id=1, source_target_pairs={{0,2},{1,3},{2,0},{3,1},{4,6},{5,7},{6,4},{7,5},{8,10},{9,11},{10,... | collective-permute-start | bytes 491528 | tf_op jit(solution)/shard_map/ppermute | solution.py:370
  81.1 3.9 %collective-permute-start.21 = (bf16[160,512]{1,0:T(8,128)(2,1)S(1)}, bf16[160,512]{1,0:T(8,128)(2,1)S(1)}, u32[]{:S(2)}, u32[]{:S(2)}) collective-permute-start(bf16[160,512]{1,0:T(8,128)(2,1)S(1)} %fusion.5.refs_0_), channel_id=1, source_target_pairs={{0,1},{1,0},{2,3},{3,2},{4,5},{5,4},{6,7},{7,6},{8,9},{9,8},{10,11... | collective-permute-start | bytes 491528 | tf_op jit(solution)/shard_map/ppermute | solution.py:367
  82.8 2.2 %collective-permute-start.22 = (bf16[160,512]{1,0:T(8,128)(2,1)S(1)}, bf16[160,512]{1,0:T(8,128)(2,1)S(1)}, u32[]{:S(2)}, u32[]{:S(2)}) collective-permute-start(bf16[160,512]{1,0:T(8,128)(2,1)S(1)} %collective-permute-done.20.refs_1_), channel_id=1, source_target_pairs={{0,1},{1,0},{2,3},{3,2},{4,5},{5,4},{6,7},{7,6},{8,9},{9,8},{10,11... | collective-permute-start | bytes 491528 | tf_op jit(solution)/shard_map/ppermute | solution.py:367
  82.8 4.5 %collective-permute-start.18 = (bf16[160,512]{1,0:T(8,128)(2,1)S(1)}, bf16[160,512]{1,0:T(8,128)(2,1)S(1)}, u32[]{:S(2)}, u32[]{:S(2)}) collective-permute-start(bf16[160,512]{1,0:T(8,128)(2,1)S(1)} %fusion.7.refs_0_), channel_id=1, source_target_pairs={{0,1},{1,0},{2,3},{3,2},{4,5},{5,4},{6,7},{7,6},{8,9},{9,8},{10,11... | collective-permute-start | bytes 491528 | tf_op jit(solution)/shard_map/ppermute | solution.py:367
  84.9 4.2 %collective-permute-start.17 = (bf16[160,512]{1,0:T(8,128)(2,1)S(1)}, bf16[160,512]{1,0:T(8,128)(2,1)S(1)}, u32[]{:S(2)}, u32[]{:S(2)}) collective-permute-start(bf16[160,512]{1,0:T(8,128)(2,1)S(1)} %collective-permute-done.16.refs_1_), channel_id=1, source_target_pairs={{0,1},{1,0},{2,3},{3,2},{4,5},{5,4},{6,7},{7,6},{8,9},{9,8},{10,11... | collective-permute-start | bytes 491528 | tf_op jit(solution)/shard_map/ppermute | solution.py:367
  91.1 8.9 %collective-permute-start.23 = (bf16[160,256]{1,0:T(8,128)(2,1)S(1)}, bf16[160,256]{1,0:T(8,128)(2,1)S(1)}, u32[]{:S(2)}, u32[]{:S(2)}) collective-permute-start(bf16[160,256]{1,0:T(8,128)(2,1)S(1)} %get-tuple-element.82), channel_id=1, source_target_pairs={{0,4},{4,0},{8,12},{12,8},{16,20},{20,16},{24,28},{28,24},{1,5},{5... | collective-permute-start | bytes 245768 | tf_op jit(solution)/shard_map/ppermute | solution.py:380
  92.6 11.3 %collective-permute-start.24 = (bf16[160,256]{1,0:T(8,128)(2,1)S(1)}, bf16[160,256]{1,0:T(8,128)(2,1)S(1)}, u32[]{:S(2)}, u32[]{:S(2)}) collective-permute-start(bf16[160,256]{1,0:T(8,128)(2,1)S(1)} %get-tuple-element.83), channel_id=1, source_target_pairs={{0,8},{4,12},{8,16},{12,20},{16,24},{20,28},{24,0},{28,4},{1,9},{5... | collective-permute-start | bytes 245768 | tf_op jit(solution)/shard_map/ppermute | solution.py:380
  96.2 10.7 %collective-permute-start.25 = (bf16[160,256]{1,0:T(8,128)(2,1)S(1)}, bf16[160,256]{1,0:T(8,128)(2,1)S(1)}, u32[]{:S(2)}, u32[]{:S(2)}) collective-permute-start(bf16[160,256]{1,0:T(8,128)(2,1)S(1)} %get-tuple-element.84), channel_id=1, source_target_pairs={{0,12},{4,8},{8,20},{12,16},{16,28},{20,24},{24,4},{28,0},{1,13},{... | collective-permute-start | bytes 245768 | tf_op jit(solution)/shard_map/ppermute | solution.py:380
  96.2 11.3 %collective-permute-start.26 = (bf16[160,256]{1,0:T(8,128)(2,1)S(1)}, bf16[160,256]{1,0:T(8,128)(2,1)S(1)}, u32[]{:S(2)}, u32[]{:S(2)}) collective-permute-start(bf16[160,256]{1,0:T(8,128)(2,1)S(1)} %get-tuple-element.85), channel_id=1, source_target_pairs={{0,16},{4,20},{8,24},{12,28},{16,0},{20,4},{24,8},{28,12},{1,17},{... | collective-permute-start | bytes 245768 | tf_op jit(solution)/shard_map/ppermute | solution.py:380
  97.8 12.3 %collective-permute-start.27 = (bf16[160,256]{1,0:T(8,128)(2,1)S(1)}, bf16[160,256]{1,0:T(8,128)(2,1)S(1)}, u32[]{:S(2)}, u32[]{:S(2)}) collective-permute-start(bf16[160,256]{1,0:T(8,128)(2,1)S(1)} %get-tuple-element.86), channel_id=1, source_target_pairs={{0,20},{4,16},{8,28},{12,24},{16,4},{20,0},{24,12},{28,8},{1,21},{... | collective-permute-start | bytes 245768 | tf_op jit(solution)/shard_map/ppermute | solution.py:380
  100.0 10.2 %collective-permute-start.28 = (bf16[160,256]{1,0:T(8,128)(2,1)S(1)}, bf16[160,256]{1,0:T(8,128)(2,1)S(1)}, u32[]{:S(2)}, u32[]{:S(2)}) collective-permute-start(bf16[160,256]{1,0:T(8,128)(2,1)S(1)} %get-tuple-element.87), channel_id=1, source_target_pairs={{0,24},{4,28},{8,0},{12,4},{16,8},{20,12},{24,16},{28,20},{1,25},{... | collective-permute-start | bytes 245768 | tf_op jit(solution)/shard_map/ppermute | solution.py:380
  103.8 6.4 %collective-permute-start.29 = (bf16[160,256]{1,0:T(8,128)(2,1)S(1)}, bf16[160,256]{1,0:T(8,128)(2,1)S(1)}, u32[]{:S(2)}, u32[]{:S(2)}) collective-permute-start(bf16[160,256]{1,0:T(8,128)(2,1)S(1)} %get-tuple-element.88), channel_id=1, source_target_pairs={{0,28},{4,24},{8,4},{12,0},{16,12},{20,8},{24,20},{28,16},{1,29},{... | collective-permute-start | bytes 245768 | tf_op jit(solution)/shard_map/ppermute | solution.py:380
  (4 other events, 50.4 us)

commit v7 on v6

--- a/solution.py
+++ b/solution.py
@@ -416,7 +416,8 @@
     for chunk in range(CHUNKS):
         after = [keeps[-1]] if chunk else []
         if chunk >= 2:
-            after.extend([fars[chunk - 2], pairs[chunk - 1]])
+            activate(chunk - 2, [pairs[chunk - 1]])
+            after.extend([pairs[chunk - 1], owns[chunk - 2]])
         if chunk < last:
             keep, send = products(chunk, chunk + 1, after)
             nears.append(beside(send))
@@ -434,6 +435,8 @@
             activate(chunk, after)
         own = owns[chunk]
         other = across(own)
+        if chunk + 2 <= last:
+            own, other = lax.optimization_barrier((own, other, pairs[last]))[:2]
         pieces = (own, other, beside(own), beside(other))
         if chunk < last:
             older = down(down_order, place, pieces, down_weight, chunk, older)

time: 141 us -> 138 us (0.979)
  waiting for transfers between devices: 25.3 us -> 22.2 us
    ppermute x8, waiting for transfers between devices: 14.2 us -> 11 us  [across(): return lax.ppermute(values, 'col', [(k, k ^ 2) for k in range(4)])]
  transfers between devices with their start and end apart: 30 -> 30, of which waited for: 10 -> 8; matrix products, arithmetic and copies ran while one was open for 2% -> 2% of each run, Pallas kernels for 29% -> 29%
where the time goes in v7:
time: 138 us
  Pallas kernels  55.4 us (40%)
  starting transfers between devices  31.5 us (23%)
  blocking collectives  23.3 us (17%)
  waiting for transfers between devices  22.2 us (16%)
  other arithmetic  3.3 us (2%)
    pallas_call x5, Pallas kernels, gate_up(): pl.pallas_call(functools.partial(gate_up_kernel, count), grid_spec=pltpu....  35.1 us
    ppermute x10, starting transfers between devices, shifted(): return lax.ppermute(values, ('dp', 'tensor'), pairs)  20 us
    all_to_all x1, blocking collectives, one_expert_each(): lax.all_to_all(sums, ('dp', 'tensor', 'col'), split_axis=0, concat_axis=0...  12.6 us
    ppermute x10, waiting for transfers between devices, shifted(): return lax.ppermute(values, ('dp', 'tensor'), pairs)  11.1 us
    ppermute x8, waiting for transfers between devices, across(): return lax.ppermute(values, 'col', [(k, k ^ 2) for k in range(4)])  11 us
    all_to_all x1, blocking collectives, one_expert_each(): lax.all_to_all(home, ('dp', 'tensor'), split_axis=0, concat_axis=0, tiled...  10.7 us
    pallas_call x5, Pallas kernels, down(): pl.pallas_call(functools.partial(down_kernel, len(pieces), pack, bool(old...  10.6 us
    ppermute x8, starting transfers between devices, across(): return lax.ppermute(values, 'col', [(k, k ^ 2) for k in range(4)])  9.22 us
  transfers between devices with their start and end apart: 30, of which 8 were waited for; matrix products, arithmetic and copies ran while one was open for 2% of the time, Pallas kernels for 29%

profile of v7, /device:TPU:0, one launch (start us, length us, event | category | flops | bytes accessed | tf_op | source)
XLA Modules:
  0.0 137.7 jit_solution(1861397783996559836)
XLA Ops:
  2.8 3.1 %collective-permute-start = (bf16[48,1536]{1,0:T(8,128)(2,1)S(1)}, bf16[48,1536]{1,0:T(8,128)(2,1)S(1)}, u32[]{:S(2)}, u32[]{:S(2)}) collective-permute-start(bf16[48,1536]{1,0:T(8,128)(2,1)S(1)} %get-tuple-element.54), channel_id=1, source_target_pairs={{0,8},{4,12},{8,16},{12,20},{16,24},{20,28},{24,0},{28,4},{1,9},{5... | collective-permute-start | bytes 442376 | tf_op jit(solution)/shard_map/ppermute | solution.py:380
  5.9 2.6 %collective-permute-start.1 = (bf16[48,1536]{1,0:T(8,128)(2,1)S(1)}, bf16[48,1536]{1,0:T(8,128)(2,1)S(1)}, u32[]{:S(2)}, u32[]{:S(2)}) collective-permute-start(bf16[48,1536]{1,0:T(8,128)(2,1)S(1)} %get-tuple-element.55), channel_id=1, source_target_pairs={{0,16},{4,20},{8,24},{12,28},{16,0},{20,4},{24,8},{28,12},{1,17},{... | collective-permute-start | bytes 442376 | tf_op jit(solution)/shard_map/ppermute | solution.py:380
  10.5 2.2 %collective-permute-done.refs_1_ = bf16[48,1536]{1,0:T(8,128)(2,1)S(1)} collective-permute-done((bf16[48,1536]{1,0:T(8,128)(2,1)S(1)}, bf16[48,1536]{1,0:T(8,128)(2,1)S(1)}, u32[]{:S(2)}, u32[]{:S(2)}) %collective-permute-start) | collective-permute-done | bytes 147488 | tf_op jit(solution)/shard_map/ppermute | solution.py:380
  12.7 5.5 %collective-permute-done.1.refs_2_ = bf16[48,1536]{1,0:T(8,128)(2,1)S(1)} collective-permute-done((bf16[48,1536]{1,0:T(8,128)(2,1)S(1)}, bf16[48,1536]{1,0:T(8,128)(2,1)S(1)}, u32[]{:S(2)}, u32[]{:S(2)}) %collective-permute-start.1) | collective-permute-done | bytes 147488 | tf_op jit(solution)/shard_map/ppermute | solution.py:380
  18.2 4.9 %gate_up_0.1 = bf16[2,2,160,512]{3,2,1,0:T(8,128)(2,1)S(1)} custom-call(s32[4]{0:T(128)S(1)} %broadcast_xor_fusion.order_ref, bf16[160,1536]{1,0:T(8,128)(2,1)S(1)} %get-tuple-element.58.inputs_ref, bf16[4,2048,1536]{2,1,0:T(8,128)(2,1)} %bitcast.71, bf16[4,2048,1536]{2,1,0:T(8,128)(2,1)} %bitcast.76), custom_call_target="tpu_custom_call" | custom-call | flops 4026531840 | bytes 25165824 | tf_op jit(solution)/shard_map/gate_up_0/pallas_call | solution.py:132
  23.2 8.2 %gate_up_1.1 = (bf16[2,2,160,512]{3,2,1,0:T(8,128)(2,1)S(1)}, bf16[2,2,160,512]{3,2,1,0:T(8,128)(2,1)S(1)}) custom-call(s32[4]{0:T(128)S(1)} %broadcast_xor_fusion.order_ref, bf16[160,1536]{1,0:T(8,128)(2,1)S(1)} %get-tuple-element.58.inputs_ref, bf16[4,2048,1536]{2,1,0:T(8,128)(2,1)} %bitcast.72, bf16[4,2048,1536]{2,1,0:T(8,128)(2,1)} %bitcast.77), custom_call_target="tpu_custom_call" | custom-call | flops 8053063680 | bytes 50331648 | tf_op jit(solution)/shard_map/gate_up_1/pallas_call | solution.py:132
  32.0 1.6 %collective-permute-start.5 = (bf16[2,160,512]{2,1,0:T(8,128)(2,1)S(1)}, bf16[2,160,512]{2,1,0:T(8,128)(2,1)S(1)}, u32[]{:S(2)}, u32[]{:S(2)}) collective-permute-start(bf16[2,160,512]{2,1,0:T(8,128)(2,1)S(1)} %fusion.1), channel_id=1, source_target_pairs={{0,2},{1,3},{2,0},{3,1},{4,6},{5,7},{6,4},{7,5},{8,10},{9,11},{10,... | collective-permute-start | bytes 983048 | tf_op jit(solution)/shard_map/ppermute | solution.py:370
  33.6 8.2 %gate_up_2.1 = (bf16[2,2,160,512]{3,2,1,0:T(8,128)(2,1)S(1)}, bf16[2,2,160,512]{3,2,1,0:T(8,128)(2,1)S(1)}) custom-call(s32[4]{0:T(128)S(1)} %broadcast_xor_fusion.order_ref, bf16[160,1536]{1,0:T(8,128)(2,1)S(1)} %get-tuple-element.58.inputs_ref, bf16[4,2048,1536]{2,1,0:T(8,128)(2,1)} %bitcast.73, bf16[4,2048,1536]{2,1,0:T(8,128)(2,1)} %bitcast.78, ...), custom_call_target="tpu_custom_call" | custom-call | flops 8053063680 | bytes 50331648 | tf_op jit(solution)/shard_map/gate_up_2/pallas_call | solution.py:132
  42.8 8.2 %gate_up_3.1 = (bf16[2,2,160,512]{3,2,1,0:T(8,128)(2,1)S(1)}, bf16[2,2,160,512]{3,2,1,0:T(8,128)(2,1)S(1)}) custom-call(s32[4]{0:T(128)S(1)} %broadcast_xor_fusion.order_ref, bf16[160,1536]{1,0:T(8,128)(2,1)S(1)} %get-tuple-element.58.inputs_ref, bf16[4,2048,1536]{2,1,0:T(8,128)(2,1)} %bitcast.74, bf16[4,2048,1536]{2,1,0:T(8,128)(2,1)} %bitcast.79, ...), custom_call_target="tpu_custom_call" | custom-call | flops 8053063680 | bytes 50331648 | tf_op jit(solution)/shard_map/gate_up_3/pallas_call | solution.py:132
  51.0 1.6 %collective-permute-start.13 = (bf16[160,512]{1,0:T(8,128)(2,1)S(1)}, bf16[160,512]{1,0:T(8,128)(2,1)S(1)}, u32[]{:S(2)}, u32[]{:S(2)}) collective-permute-start(bf16[160,512]{1,0:T(8,128)(2,1)S(1)} %fusion.11.rest_2_.refs_0_), channel_id=1, source_target_pairs={{0,2},{1,3},{2,0},{3,1},{4,6},{5,7},{6,4},{7,5},{8,10},{9,11},{10,... | collective-permute-start | bytes 491528 | tf_op jit(solution)/shard_map/ppermute | solution.py:370
  53.5 1.6 %collective-permute-start.10 = (bf16[160,512]{1,0:T(8,128)(2,1)S(1)}, bf16[160,512]{1,0:T(8,128)(2,1)S(1)}, u32[]{:S(2)}, u32[]{:S(2)}) collective-permute-start(bf16[160,512]{1,0:T(8,128)(2,1)S(1)} %fusion.9.rest_2_.refs_0_), channel_id=1, source_target_pairs={{0,2},{1,3},{2,0},{3,1},{4,6},{5,7},{6,4},{7,5},{8,10},{9,11},{10,... | collective-permute-start | bytes 491528 | tf_op jit(solution)/shard_map/ppermute | solution.py:370
  55.1 5.6 %gate_up_4.1 = bf16[2,2,160,512]{3,2,1,0:T(8,128)(2,1)S(1)} custom-call(s32[4]{0:T(128)S(1)} %broadcast_xor_fusion.order_ref, bf16[160,1536]{1,0:T(8,128)(2,1)S(1)} %get-tuple-element.58.inputs_ref, bf16[4,2048,1536]{2,1,0:T(8,128)(2,1)} %bitcast.75, bf16[4,2048,1536]{2,1,0:T(8,128)(2,1)} %bitcast.80, ...), custom_call_target="tpu_custom_call" | custom-call | flops 4026531840 | bytes 25165824 | tf_op jit(solution)/shard_map/gate_up_4/pallas_call | solution.py:132
  61.8 6.8 %collective-permute-done.10.refs_1_ = bf16[160,512]{1,0:T(8,128)(2,1)S(1)} collective-permute-done((bf16[160,512]{1,0:T(8,128)(2,1)S(1)}, bf16[160,512]{1,0:T(8,128)(2,1)S(1)}, u32[]{:S(2)}, u32[]{:S(2)}) %collective-permute-start.10) | collective-permute-done | bytes 163872 | tf_op jit(solution)/shard_map/ppermute | solution.py:370
  69.2 2.3 %down_0_0.1 = (f32[160,768]{1,0:T(8,128)S(1)}, f32[160,160]{1,0:T(8,128)S(1)}, f32[8,768]{1,0:T(8,128)S(1)}) custom-call(s32[4]{0:T(128)S(1)} %broadcast_xor_fusion.1.order_ref, s32[2]{0:T(128)S(1)} %pad_add_fusion.1.place_ref, bf16[160,512]{1,0:T(8,128)(2,1)S(1)} %fusion.11.rest_2_.refs_0_, bf16[160,512]{1,0:T(8,128)(2,1)S(1)} %collective-permute-done.13.refs_1_, ...), custom_call_target="tpu_custom_call" | custom-call | flops 1 | bytes 1 | tf_op jit(solution)/shard_map/down_0_0/pallas_call | solution.py:216
  71.7 1.6 %collective-permute-start.20 = (bf16[160,512]{1,0:T(8,128)(2,1)S(1)}, bf16[160,512]{1,0:T(8,128)(2,1)S(1)}, u32[]{:S(2)}, u32[]{:S(2)}) collective-permute-start(bf16[160,512]{1,0:T(8,128)(2,1)S(1)} %fusion.5.refs_0_), channel_id=1, source_target_pairs={{0,2},{1,3},{2,0},{3,1},{4,6},{5,7},{6,4},{7,5},{8,10},{9,11},{10,... | collective-permute-start | bytes 491528 | tf_op jit(solution)/shard_map/ppermute | solution.py:370
  73.3 2.3 %down_1_0.1 = (f32[160,768]{1,0:T(8,128)S(1)}, f32[160,160]{1,0:T(8,128)S(1)}, f32[8,768]{1,0:T(8,128)S(1)}) custom-call(s32[4]{0:T(128)S(1)} %broadcast_xor_fusion.1.order_ref, s32[2]{0:T(128)S(1)} %pad_add_fusion.1.place_ref, bf16[160,512]{1,0:T(8,128)(2,1)S(1)} %fusion.9.rest_2_.refs_0_, bf16[160,512]{1,0:T(8,128)(2,1)S(1)} %collective-permute-done.10.refs_1_, ...), custom_call_target="tpu_custom_call" | custom-call | flops 1 | bytes 1 | tf_op jit(solution)/shard_map/down_1_0/pallas_call | solution.py:216
  75.8 1.4 %collective-permute-start.16 = (bf16[160,512]{1,0:T(8,128)(2,1)S(1)}, bf16[160,512]{1,0:T(8,128)(2,1)S(1)}, u32[]{:S(2)}, u32[]{:S(2)}) collective-permute-start(bf16[160,512]{1,0:T(8,128)(2,1)S(1)} %fusion.7.refs_0_), channel_id=1, source_target_pairs={{0,2},{1,3},{2,0},{3,1},{4,6},{5,7},{6,4},{7,5},{8,10},{9,11},{10,... | collective-permute-start | bytes 491528 | tf_op jit(solution)/shard_map/ppermute | solution.py:370
  77.2 1.4 collective-permute-done.20.refs_1_
  79.1 2.8 %collective-permute-done.16.refs_1_ = bf16[160,512]{1,0:T(8,128)(2,1)S(1)} collective-permute-done((bf16[160,512]{1,0:T(8,128)(2,1)S(1)}, bf16[160,512]{1,0:T(8,128)(2,1)S(1)}, u32[]{:S(2)}, u32[]{:S(2)}) %collective-permute-start.16) | collective-permute-done | bytes 163872 | tf_op jit(solution)/shard_map/ppermute | solution.py:370
  81.9 2.3 %down_2_0.1 = (f32[160,768]{1,0:T(8,128)S(1)}, f32[160,160]{1,0:T(8,128)S(1)}, f32[8,768]{1,0:T(8,128)S(1)}) custom-call(s32[4]{0:T(128)S(1)} %broadcast_xor_fusion.1.order_ref, s32[2]{0:T(128)S(1)} %pad_add_fusion.1.place_ref, bf16[160,512]{1,0:T(8,128)(2,1)S(1)} %fusion.5.refs_0_, bf16[160,512]{1,0:T(8,128)(2,1)S(1)} %collective-permute-done.20.refs_1_, ...), custom_call_target="tpu_custom_call" | custom-call | flops 1 | bytes 1 | tf_op jit(solution)/shard_map/down_2_0/pallas_call | solution.py:216
  84.3 1.9 %down_3_0.1 = (f32[160,768]{1,0:T(8,128)S(1)}, f32[160,160]{1,0:T(8,128)S(1)}, f32[8,768]{1,0:T(8,128)S(1)}) custom-call(s32[4]{0:T(128)S(1)} %broadcast_xor_fusion.1.order_ref, s32[2]{0:T(128)S(1)} %pad_add_fusion.1.place_ref, bf16[160,512]{1,0:T(8,128)(2,1)S(1)} %fusion.7.refs_0_, bf16[160,512]{1,0:T(8,128)(2,1)S(1)} %collective-permute-done.16.refs_1_, ...), custom_call_target="tpu_custom_call" | custom-call | flops 1 | bytes 1 | tf_op jit(solution)/shard_map/down_3_0/pallas_call | solution.py:216
  86.1 1.9 %down_3_3.1 = (bf16[160,256]{1,0:T(8,128)(2,1)S(1)}, bf16[160,256]{1,0:T(8,128)(2,1)S(1)}, bf16[160,256]{1,0:T(8,128)(2,1)S(1)}, bf16[160,256]{1,0:T(8,128)(2,1)...) custom-call(s32[4]{0:T(128)S(1)} %broadcast_xor_fusion.1.order_ref, ...), custom_call_target="tpu_custom_call" | custom-call | flops 1 | bytes 1 | tf_op jit(solution)/shard_map/down_3_3/pallas_call | solution.py:216
  88.1 1.5 %collective-permute-start.23 = (bf16[160,256]{1,0:T(8,128)(2,1)S(1)}, bf16[160,256]{1,0:T(8,128)(2,1)S(1)}, u32[]{:S(2)}, u32[]{:S(2)}) collective-permute-start(bf16[160,256]{1,0:T(8,128)(2,1)S(1)} %get-tuple-element.90), channel_id=1, source_target_pairs={{0,4},{4,0},{8,12},{12,8},{16,20},{20,16},{24,28},{28,24},{1,5},{5... | collective-permute-start | bytes 245768 | tf_op jit(solution)/shard_map/ppermute | solution.py:380
  89.5 3.6 %collective-permute-start.24 = (bf16[160,256]{1,0:T(8,128)(2,1)S(1)}, bf16[160,256]{1,0:T(8,128)(2,1)S(1)}, u32[]{:S(2)}, u32[]{:S(2)}) collective-permute-start(bf16[160,256]{1,0:T(8,128)(2,1)S(1)} %get-tuple-element.91), channel_id=1, source_target_pairs={{0,8},{4,12},{8,16},{12,20},{16,24},{20,28},{24,0},{28,4},{1,9},{5... | collective-permute-start | bytes 245768 | tf_op jit(solution)/shard_map/ppermute | solution.py:380
  93.2 1.6 %collective-permute-start.26 = (bf16[160,256]{1,0:T(8,128)(2,1)S(1)}, bf16[160,256]{1,0:T(8,128)(2,1)S(1)}, u32[]{:S(2)}, u32[]{:S(2)}) collective-permute-start(bf16[160,256]{1,0:T(8,128)(2,1)S(1)} %get-tuple-element.93), channel_id=1, source_target_pairs={{0,16},{4,20},{8,24},{12,28},{16,0},{20,4},{24,8},{28,12},{1,17},{... | collective-permute-start | bytes 245768 | tf_op jit(solution)/shard_map/ppermute | solution.py:380
  94.8 2.2 %collective-permute-start.27 = (bf16[160,256]{1,0:T(8,128)(2,1)S(1)}, bf16[160,256]{1,0:T(8,128)(2,1)S(1)}, u32[]{:S(2)}, u32[]{:S(2)}) collective-permute-start(bf16[160,256]{1,0:T(8,128)(2,1)S(1)} %get-tuple-element.94), channel_id=1, source_target_pairs={{0,20},{4,16},{8,28},{12,24},{16,4},{20,0},{24,12},{28,8},{1,21},{... | collective-permute-start | bytes 245768 | tf_op jit(solution)/shard_map/ppermute | solution.py:380
  97.0 3.8 %collective-permute-start.28 = (bf16[160,256]{1,0:T(8,128)(2,1)S(1)}, bf16[160,256]{1,0:T(8,128)(2,1)S(1)}, u32[]{:S(2)}, u32[]{:S(2)}) collective-permute-start(bf16[160,256]{1,0:T(8,128)(2,1)S(1)} %get-tuple-element.95), channel_id=1, source_target_pairs={{0,24},{4,28},{8,0},{12,4},{16,8},{20,12},{24,16},{28,20},{1,25},{... | collective-permute-start | bytes 245768 | tf_op jit(solution)/shard_map/ppermute | solution.py:380
  102.3 1.5 %route.1 = (bf16[1280,512]{1,0:T(8,128)(2,1)S(1)}, bf16[512,1280]{1,0:T(8,128)(2,1)S(1)}, f32[1280,2]{1,0:T(8,128)S(1)}) custom-call(s32[6]{0:T(128)S(1)} %copy-done.1, s32[2]{0:T(128)S(1)} %pad_add_fusion.1.place_ref, f32[4,4,128]{2,1,0:T(4,128)S(1)} %get-tuple-element.57.refs_0_, f32[8,768]{1,0:T(8,128)S(1)} %get-tuple-element.85.refs_1_.square_ref), custom_call_target="tpu_custom_call" | custom-call | flops 1 | bytes 1 | tf_op jit(solution)/shard_map/route/pallas_call | solution.py:453
  104.5 2.7 %collective-permute-done.27.refs_5_ = bf16[160,256]{1,0:T(8,128)(2,1)S(1)} collective-permute-done((bf16[160,256]{1,0:T(8,128)(2,1)S(1)}, bf16[160,256]{1,0:T(8,128)(2,1)S(1)}, u32[]{:S(2)}, u32[]{:S(2)}) %collective-permute-start.27) | collective-permute-done | bytes 81952 | tf_op jit(solution)/shard_map/ppermute | solution.py:380
  107.3 5.3 %solve.1 = (f32[512,96]{1,0:T(8,128)S(1)}, f32[512,96]{1,0:T(8,128)S(1)}, f32[512,96]{1,0:T(8,128)S(1)}, f32[32,1,128]{2,1,0:T(1,128)S(1)}) custom-call(f32[1]{0:T(128)} %bitcast.2.own_ref, bf16[1280,512]{1,0:T(8,128)(2,1)S(1)} %get-tuple-element.86.hot_ref, bf16[512,1280]{1,0:T(8,128)(2,1)S(1)} %get-tuple-element.87.turned_ref, ...), custom_call_target="tpu_custom_call" | custom-call | flops 1 | bytes 1 | tf_op jit(solution)/shard_map/solve/pallas_call | solution.py:468
  112.6 12.6 %all_to_all.10.sums_ref = f32[32,1,128]{2,1,0:T(1,128)S(1)} all-to-all(f32[32,1,128]{2,1,0:T(1,128)S(1)} %get-tuple-element.100), channel_id=1, replica_groups=mesh['dp'=4,'tensor'=2,'col'=4] {'dp','tensor','col'}, dimensions={0} | all-to-all | bytes 32768 | tf_op jit(solution)/shard_map/all_to_all | solution.py:475
  126.1 10.7 %all_to_all.11.pieces_ref = bf16[8,96,128]{2,1,0:T(8,128)(2,1)S(1)} all-to-all(bf16[8,96,128]{2,1,0:T(8,128)(2,1)S(1)} %finish.1), channel_id=1, replica_groups=mesh['dp'=4,'tensor'=2,'col'=4] {'dp','tensor'}, dimensions={0} | all-to-all | bytes 393216 | tf_op jit(solution)/shard_map/all_to_all | solution.py:484
  (76 shorter events, 13.4 us)
Async XLA Ops:
  2.8 9.9 %collective-permute-start = (bf16[48,1536]{1,0:T(8,128)(2,1)S(1)}, bf16[48,1536]{1,0:T(8,128)(2,1)S(1)}, u32[]{:S(2)}, u32[]{:S(2)}) collective-permute-start(bf16[48,1536]{1,0:T(8,128)(2,1)S(1)} %get-tuple-element.54), channel_id=1, source_target_pairs={{0,8},{4,12},{8,16},{12,20},{16,24},{20,28},{24,0},{28,4},{1,9},{5... | collective-permute-start | bytes 442376 | tf_op jit(solution)/shard_map/ppermute | solution.py:380
  5.9 12.3 %collective-permute-start.1 = (bf16[48,1536]{1,0:T(8,128)(2,1)S(1)}, bf16[48,1536]{1,0:T(8,128)(2,1)S(1)}, u32[]{:S(2)}, u32[]{:S(2)}) collective-permute-start(bf16[48,1536]{1,0:T(8,128)(2,1)S(1)} %get-tuple-element.55), channel_id=1, source_target_pairs={{0,16},{4,20},{8,24},{12,28},{16,0},{20,4},{24,8},{28,12},{1,17},{... | collective-permute-start | bytes 442376 | tf_op jit(solution)/shard_map/ppermute | solution.py:380
  8.5 9.7 %collective-permute-start.2 = (bf16[48,1536]{1,0:T(8,128)(2,1)S(1)}, bf16[48,1536]{1,0:T(8,128)(2,1)S(1)}, u32[]{:S(2)}, u32[]{:S(2)}) collective-permute-start(bf16[48,1536]{1,0:T(8,128)(2,1)S(1)} %get-tuple-element.56), channel_id=1, source_target_pairs={{0,24},{4,28},{8,0},{12,4},{16,8},{20,12},{24,16},{28,20},{1,25},{... | collective-permute-start | bytes 442376 | tf_op jit(solution)/shard_map/ppermute | solution.py:380
  23.1 8.8 %collective-permute-start.4 = (bf16[2,2,160,512]{3,2,1,0:T(8,128)(2,1)S(1)}, bf16[2,2,160,512]{3,2,1,0:T(8,128)(2,1)S(1)}, u32[]{:S(2)}, u32[]{:S(2)}) collective-permute-start(bf16[2,2,160,512]{3,2,1,0:T(8,128)(2,1)S(1)} %gate_up_0.1), channel_id=1, source_target_pairs={{0,1},{1,0},{2,3},{3,2},{4,5},{5,4},{6,7},{7,6},{8,9},{9,8},{10,11... | collective-permute-start | bytes 1966088 | tf_op jit(solution)/shard_map/ppermute | solution.py:367
  31.4 10.5 %collective-permute-start.3 = (bf16[2,2,160,512]{3,2,1,0:T(8,128)(2,1)S(1)}, bf16[2,2,160,512]{3,2,1,0:T(8,128)(2,1)S(1)}, u32[]{:S(2)}, u32[]{:S(2)}) collective-permute-start(bf16[2,2,160,512]{3,2,1,0:T(8,128)(2,1)S(1)} %get-tuple-element.61), channel_id=1, source_target_pairs={{0,1},{1,0},{2,3},{3,2},{4,5},{5,4},{6,7},{7,6},{8,9},{9,8},{10,11... | collective-permute-start | bytes 1966088 | tf_op jit(solution)/shard_map/ppermute | solution.py:367
  32.0 10.5 %collective-permute-start.5 = (bf16[2,160,512]{2,1,0:T(8,128)(2,1)S(1)}, bf16[2,160,512]{2,1,0:T(8,128)(2,1)S(1)}, u32[]{:S(2)}, u32[]{:S(2)}) collective-permute-start(bf16[2,160,512]{2,1,0:T(8,128)(2,1)S(1)} %fusion.1), channel_id=1, source_target_pairs={{0,2},{1,3},{2,0},{3,1},{4,6},{5,7},{6,4},{7,5},{8,10},{9,11},{10,... | collective-permute-start | bytes 983048 | tf_op jit(solution)/shard_map/ppermute | solution.py:370
  41.8 10.7 %collective-permute-start.6 = (bf16[2,2,160,512]{3,2,1,0:T(8,128)(2,1)S(1)}, bf16[2,2,160,512]{3,2,1,0:T(8,128)(2,1)S(1)}, u32[]{:S(2)}, u32[]{:S(2)}) collective-permute-start(bf16[2,2,160,512]{3,2,1,0:T(8,128)(2,1)S(1)} %get-tuple-element.64), channel_id=1, source_target_pairs={{0,1},{1,0},{2,3},{3,2},{4,5},{5,4},{6,7},{7,6},{8,9},{9,8},{10,11... | collective-permute-start | bytes 1966088 | tf_op jit(solution)/shard_map/ppermute | solution.py:367
  42.0 11.3 %collective-permute-start.7 = (bf16[2,160,512]{2,1,0:T(8,128)(2,1)S(1)}, bf16[2,160,512]{2,1,0:T(8,128)(2,1)S(1)}, u32[]{:S(2)}, u32[]{:S(2)}) collective-permute-start(bf16[2,160,512]{2,1,0:T(8,128)(2,1)S(1)} %fusion.rest_1_), channel_id=1, source_target_pairs={{0,2},{1,3},{2,0},{3,1},{4,6},{5,7},{6,4},{7,5},{8,10},{9,11},{10,... | collective-permute-start | bytes 983048 | tf_op jit(solution)/shard_map/ppermute | solution.py:370
  51.0 9.9 %collective-permute-start.13 = (bf16[160,512]{1,0:T(8,128)(2,1)S(1)}, bf16[160,512]{1,0:T(8,128)(2,1)S(1)}, u32[]{:S(2)}, u32[]{:S(2)}) collective-permute-start(bf16[160,512]{1,0:T(8,128)(2,1)S(1)} %fusion.11.rest_2_.refs_0_), channel_id=1, source_target_pairs={{0,2},{1,3},{2,0},{3,1},{4,6},{5,7},{6,4},{7,5},{8,10},{9,11},{10,... | collective-permute-start | bytes 491528 | tf_op jit(solution)/shard_map/ppermute | solution.py:370
  52.6 18.8 %collective-permute-start.19 = (bf16[2,160,512]{2,1,0:T(8,128)(2,1)S(1)}, bf16[2,160,512]{2,1,0:T(8,128)(2,1)S(1)}, u32[]{:S(2)}, u32[]{:S(2)}) collective-permute-start(bf16[2,160,512]{2,1,0:T(8,128)(2,1)S(1)} %fusion.2.rest_1_), channel_id=1, source_target_pairs={{0,2},{1,3},{2,0},{3,1},{4,6},{5,7},{6,4},{7,5},{8,10},{9,11},{10,... | collective-permute-start | bytes 983048 | tf_op jit(solution)/shard_map/ppermute | solution.py:370
  53.2 7.5 %collective-permute-start.8 = (bf16[2,2,160,512]{3,2,1,0:T(8,128)(2,1)S(1)}, bf16[2,2,160,512]{3,2,1,0:T(8,128)(2,1)S(1)}, u32[]{:S(2)}, u32[]{:S(2)}) collective-permute-start(bf16[2,2,160,512]{3,2,1,0:T(8,128)(2,1)S(1)} %get-tuple-element.66), channel_id=1, source_target_pairs={{0,1},{1,0},{2,3},{3,2},{4,5},{5,4},{6,7},{7,6},{8,9},{9,8},{10,11... | collective-permute-start | bytes 1966088 | tf_op jit(solution)/shard_map/ppermute | solution.py:367
  53.4 15.8 %slice-start = ((s8[12582912]{0:T(1024)(128)(4,1)}), s8[4194304]{0:T(1024)(128)(4,1)S(1)}, s32[]{:S(2)}) async-start(s8[12582912]{0:T(1024)(128)(4,1)} %bitcast.64), calls=%async_computation.2 | async-start | bytes 8388608
  53.5 15.1 %collective-permute-start.10 = (bf16[160,512]{1,0:T(8,128)(2,1)S(1)}, bf16[160,512]{1,0:T(8,128)(2,1)S(1)}, u32[]{:S(2)}, u32[]{:S(2)}) collective-permute-start(bf16[160,512]{1,0:T(8,128)(2,1)S(1)} %fusion.9.rest_2_.refs_0_), channel_id=1, source_target_pairs={{0,2},{1,3},{2,0},{3,1},{4,6},{5,7},{6,4},{7,5},{8,10},{9,11},{10,... | collective-permute-start | bytes 491528 | tf_op jit(solution)/shard_map/ppermute | solution.py:370
  60.8 7.8 %collective-permute-start.14 = (bf16[160,512]{1,0:T(8,128)(2,1)S(1)}, bf16[160,512]{1,0:T(8,128)(2,1)S(1)}, u32[]{:S(2)}, u32[]{:S(2)}) collective-permute-start(bf16[160,512]{1,0:T(8,128)(2,1)S(1)} %fusion.11.rest_2_.refs_0_), channel_id=1, source_target_pairs={{0,1},{1,0},{2,3},{3,2},{4,5},{5,4},{6,7},{7,6},{8,9},{9,8},{10,11... | collective-permute-start | bytes 491528 | tf_op jit(solution)/shard_map/ppermute | solution.py:367
  61.1 8.0 %collective-permute-start.15 = (bf16[160,512]{1,0:T(8,128)(2,1)S(1)}, bf16[160,512]{1,0:T(8,128)(2,1)S(1)}, u32[]{:S(2)}, u32[]{:S(2)}) collective-permute-start(bf16[160,512]{1,0:T(8,128)(2,1)S(1)} %collective-permute-done.13.refs_1_), channel_id=1, source_target_pairs={{0,1},{1,0},{2,3},{3,2},{4,5},{5,4},{6,7},{7,6},{8,9},{9,8},{10,11... | collective-permute-start | bytes 491528 | tf_op jit(solution)/shard_map/ppermute | solution.py:367
  61.4 14.1 %collective-permute-start.9 = (bf16[2,160,512]{2,1,0:T(8,128)(2,1)S(1)}, bf16[2,160,512]{2,1,0:T(8,128)(2,1)S(1)}, u32[]{:S(2)}, u32[]{:S(2)}) collective-permute-start(bf16[2,160,512]{2,1,0:T(8,128)(2,1)S(1)} %fusion.3), channel_id=1, source_target_pairs={{0,2},{1,3},{2,0},{3,1},{4,6},{5,7},{6,4},{7,5},{8,10},{9,11},{10,... | collective-permute-start | bytes 983048 | tf_op jit(solution)/shard_map/ppermute | solution.py:370
  68.6 4.6 %collective-permute-start.11 = (bf16[160,512]{1,0:T(8,128)(2,1)S(1)}, bf16[160,512]{1,0:T(8,128)(2,1)S(1)}, u32[]{:S(2)}, u32[]{:S(2)}) collective-permute-start(bf16[160,512]{1,0:T(8,128)(2,1)S(1)} %fusion.9.rest_2_.refs_0_), channel_id=1, source_target_pairs={{0,1},{1,0},{2,3},{3,2},{4,5},{5,4},{6,7},{7,6},{8,9},{9,8},{10,11... | collective-permute-start | bytes 491528 | tf_op jit(solution)/shard_map/ppermute | solution.py:367
  68.6 4.6 %collective-permute-start.12 = (bf16[160,512]{1,0:T(8,128)(2,1)S(1)}, bf16[160,512]{1,0:T(8,128)(2,1)S(1)}, u32[]{:S(2)}, u32[]{:S(2)}) collective-permute-start(bf16[160,512]{1,0:T(8,128)(2,1)S(1)} %collective-permute-done.10.refs_1_), channel_id=1, source_target_pairs={{0,1},{1,0},{2,3},{3,2},{4,5},{5,4},{6,7},{7,6},{8,9},{9,8},{10,11... | collective-permute-start | bytes 491528 | tf_op jit(solution)/shard_map/ppermute | solution.py:367
  71.7 6.9 %collective-permute-start.20 = (bf16[160,512]{1,0:T(8,128)(2,1)S(1)}, bf16[160,512]{1,0:T(8,128)(2,1)S(1)}, u32[]{:S(2)}, u32[]{:S(2)}) collective-permute-start(bf16[160,512]{1,0:T(8,128)(2,1)S(1)} %fusion.5.refs_0_), channel_id=1, source_target_pairs={{0,2},{1,3},{2,0},{3,1},{4,6},{5,7},{6,4},{7,5},{8,10},{9,11},{10,... | collective-permute-start | bytes 491528 | tf_op jit(solution)/shard_map/ppermute | solution.py:370
  75.8 6.1 %collective-permute-start.16 = (bf16[160,512]{1,0:T(8,128)(2,1)S(1)}, bf16[160,512]{1,0:T(8,128)(2,1)S(1)}, u32[]{:S(2)}, u32[]{:S(2)}) collective-permute-start(bf16[160,512]{1,0:T(8,128)(2,1)S(1)} %fusion.7.refs_0_), channel_id=1, source_target_pairs={{0,2},{1,3},{2,0},{3,1},{4,6},{5,7},{6,4},{7,5},{8,10},{9,11},{10,... | collective-permute-start | bytes 491528 | tf_op jit(solution)/shard_map/ppermute | solution.py:370
  77.2 4.7 %collective-permute-start.21 = (bf16[160,512]{1,0:T(8,128)(2,1)S(1)}, bf16[160,512]{1,0:T(8,128)(2,1)S(1)}, u32[]{:S(2)}, u32[]{:S(2)}) collective-permute-start(bf16[160,512]{1,0:T(8,128)(2,1)S(1)} %fusion.5.refs_0_), channel_id=1, source_target_pairs={{0,1},{1,0},{2,3},{3,2},{4,5},{5,4},{6,7},{7,6},{8,9},{9,8},{10,11... | collective-permute-start | bytes 491528 | tf_op jit(solution)/shard_map/ppermute | solution.py:367
  78.6 3.4 %collective-permute-start.22 = (bf16[160,512]{1,0:T(8,128)(2,1)S(1)}, bf16[160,512]{1,0:T(8,128)(2,1)S(1)}, u32[]{:S(2)}, u32[]{:S(2)}) collective-permute-start(bf16[160,512]{1,0:T(8,128)(2,1)S(1)} %collective-permute-done.20.refs_1_), channel_id=1, source_target_pairs={{0,1},{1,0},{2,3},{3,2},{4,5},{5,4},{6,7},{7,6},{8,9},{9,8},{10,11... | collective-permute-start | bytes 491528 | tf_op jit(solution)/shard_map/ppermute | solution.py:367
  78.6 5.7 %collective-permute-start.18 = (bf16[160,512]{1,0:T(8,128)(2,1)S(1)}, bf16[160,512]{1,0:T(8,128)(2,1)S(1)}, u32[]{:S(2)}, u32[]{:S(2)}) collective-permute-start(bf16[160,512]{1,0:T(8,128)(2,1)S(1)} %fusion.7.refs_0_), channel_id=1, source_target_pairs={{0,1},{1,0},{2,3},{3,2},{4,5},{5,4},{6,7},{7,6},{8,9},{9,8},{10,11... | collective-permute-start | bytes 491528 | tf_op jit(solution)/shard_map/ppermute | solution.py:367
  81.9 4.2 %collective-permute-start.17 = (bf16[160,512]{1,0:T(8,128)(2,1)S(1)}, bf16[160,512]{1,0:T(8,128)(2,1)S(1)}, u32[]{:S(2)}, u32[]{:S(2)}) collective-permute-start(bf16[160,512]{1,0:T(8,128)(2,1)S(1)} %collective-permute-done.16.refs_1_), channel_id=1, source_target_pairs={{0,1},{1,0},{2,3},{3,2},{4,5},{5,4},{6,7},{7,6},{8,9},{9,8},{10,11... | collective-permute-start | bytes 491528 | tf_op jit(solution)/shard_map/ppermute | solution.py:367
  84.2 16.8 %copy-start.1 = (s32[6]{0:T(128)S(1)}, s32[6]{0:T(128)}, u32[]{:S(2)}) copy-start(s32[6]{0:T(128)} %kept_ref.1) | copy-start | bytes 76
  88.1 8.9 %collective-permute-start.23 = (bf16[160,256]{1,0:T(8,128)(2,1)S(1)}, bf16[160,256]{1,0:T(8,128)(2,1)S(1)}, u32[]{:S(2)}, u32[]{:S(2)}) collective-permute-start(bf16[160,256]{1,0:T(8,128)(2,1)S(1)} %get-tuple-element.90), channel_id=1, source_target_pairs={{0,4},{4,0},{8,12},{12,8},{16,20},{20,16},{24,28},{28,24},{1,5},{5... | collective-permute-start | bytes 245768 | tf_op jit(solution)/shard_map/ppermute | solution.py:380
  89.5 11.3 %collective-permute-start.24 = (bf16[160,256]{1,0:T(8,128)(2,1)S(1)}, bf16[160,256]{1,0:T(8,128)(2,1)S(1)}, u32[]{:S(2)}, u32[]{:S(2)}) collective-permute-start(bf16[160,256]{1,0:T(8,128)(2,1)S(1)} %get-tuple-element.91), channel_id=1, source_target_pairs={{0,8},{4,12},{8,16},{12,20},{16,24},{20,28},{24,0},{28,4},{1,9},{5... | collective-permute-start | bytes 245768 | tf_op jit(solution)/shard_map/ppermute | solution.py:380
  93.2 10.7 %collective-permute-start.25 = (bf16[160,256]{1,0:T(8,128)(2,1)S(1)}, bf16[160,256]{1,0:T(8,128)(2,1)S(1)}, u32[]{:S(2)}, u32[]{:S(2)}) collective-permute-start(bf16[160,256]{1,0:T(8,128)(2,1)S(1)} %get-tuple-element.92), channel_id=1, source_target_pairs={{0,12},{4,8},{8,20},{12,16},{16,28},{20,24},{24,4},{28,0},{1,13},{... | collective-permute-start | bytes 245768 | tf_op jit(solution)/shard_map/ppermute | solution.py:380
  93.2 11.3 %collective-permute-start.26 = (bf16[160,256]{1,0:T(8,128)(2,1)S(1)}, bf16[160,256]{1,0:T(8,128)(2,1)S(1)}, u32[]{:S(2)}, u32[]{:S(2)}) collective-permute-start(bf16[160,256]{1,0:T(8,128)(2,1)S(1)} %get-tuple-element.93), channel_id=1, source_target_pairs={{0,16},{4,20},{8,24},{12,28},{16,0},{20,4},{24,8},{28,12},{1,17},{... | collective-permute-start | bytes 245768 | tf_op jit(solution)/shard_map/ppermute | solution.py:380
  94.8 12.3 %collective-permute-start.27 = (bf16[160,256]{1,0:T(8,128)(2,1)S(1)}, bf16[160,256]{1,0:T(8,128)(2,1)S(1)}, u32[]{:S(2)}, u32[]{:S(2)}) collective-permute-start(bf16[160,256]{1,0:T(8,128)(2,1)S(1)} %get-tuple-element.94), channel_id=1, source_target_pairs={{0,20},{4,16},{8,28},{12,24},{16,4},{20,0},{24,12},{28,8},{1,21},{... | collective-permute-start | bytes 245768 | tf_op jit(solution)/shard_map/ppermute | solution.py:380
  97.0 10.2 %collective-permute-start.28 = (bf16[160,256]{1,0:T(8,128)(2,1)S(1)}, bf16[160,256]{1,0:T(8,128)(2,1)S(1)}, u32[]{:S(2)}, u32[]{:S(2)}) collective-permute-start(bf16[160,256]{1,0:T(8,128)(2,1)S(1)} %get-tuple-element.95), channel_id=1, source_target_pairs={{0,24},{4,28},{8,0},{12,4},{16,8},{20,12},{24,16},{28,20},{1,25},{... | collective-permute-start | bytes 245768 | tf_op jit(solution)/shard_map/ppermute | solution.py:380
  100.8 6.4 %collective-permute-start.29 = (bf16[160,256]{1,0:T(8,128)(2,1)S(1)}, bf16[160,256]{1,0:T(8,128)(2,1)S(1)}, u32[]{:S(2)}, u32[]{:S(2)}) collective-permute-start(bf16[160,256]{1,0:T(8,128)(2,1)S(1)} %get-tuple-element.96), channel_id=1, source_target_pairs={{0,28},{4,24},{8,4},{12,0},{16,12},{20,8},{24,20},{28,16},{1,29},{... | collective-permute-start | bytes 245768 | tf_op jit(solution)/shard_map/ppermute | solution.py:380
  (4 other events, 40.2 us)

commit v8 on v7

--- a/solution.py
+++ b/solution.py
@@ -199,10 +199,10 @@
                         ).astype(bf16)
 
 
-def down(order, place, pieces, down_weight, chunk, older, first=0, pack=None):
+def down(order, place, pieces, down_weight, first, older, pack=None):
     slots, width = pieces[0].shape
     columns = down_weight.shape[1]
-    down_weight = down_weight.reshape(4, -1, columns)
+    down_weight = down_weight.reshape(-1, width, columns)
 
     def fixed(shape):
         return pl.BlockSpec(shape, lambda s, order, place: (0,) * len(shape))
@@ -219,14 +219,18 @@
             num_scalar_prefetch=2,
             grid=(len(pieces),),
             in_specs=[fixed((slots, width))] * len(pieces)
-            + [pl.BlockSpec((None, width, columns), lambda s, order, place: (order[first + s], chunk, 0))]
+            + [pl.BlockSpec((None, width, columns), lambda s, order, place: (order[first + s], 0, 0))]
             + [fixed(value.shape) for value in older],
             out_specs=[fixed(value.shape) for value in out_shape],
         ),
         out_shape=out_shape,
         compiler_params=params(20),
-        cost_estimate=LIGHT,
-        name=f"down_{chunk}_{first}",
+        cost_estimate=pl.CostEstimate(
+            flops=8 * len(pieces) * slots * width * columns,
+            bytes_accessed=8 * len(pieces) * width * columns,
+            transcendentals=0,
+        ),
+        name=f"down_{first}",
     )(order, place, *pieces, down_weight, *older)
 
 
@@ -399,7 +403,8 @@
     )(*arrived)
 
     gate_order = col_index ^ jnp.array([2, 0, 3, 1], jnp.int32)
-    down_order = col_index ^ jnp.array([0, 2, 1, 3], jnp.int32)
+    near_first = jnp.array([0, 2, 1, 3] * CHUNKS, jnp.int32)
+    down_order = (col_index ^ near_first) * CHUNKS + jnp.arange(4 * CHUNKS, dtype=jnp.int32) // 4
 
     def products(keep, send, after=()):
         return gate_up(gate_order, inputs, gate_weight, up_weight, width, keep, send, after)
@@ -426,7 +431,7 @@
         keeps.append(keep)
         pairs.append((keep[0].astype(f32) + nears[chunk][0].astype(f32)).astype(bf16))
         fars.append(across(pairs[-1]))
-    older, olders = (), []
+    older, olders, queue, counts = (), [], [], []
     for chunk in range(CHUNKS):
         if chunk >= len(owns):
             after = [pairs[last]]
@@ -437,15 +442,19 @@
         other = across(own)
         if chunk + 2 <= last:
             own, other = lax.optimization_barrier((own, other, pairs[last]))[:2]
-        pieces = (own, other, beside(own), beside(other))
-        if chunk < last:
-            older = down(down_order, place, pieces, down_weight, chunk, older)
+        queue.extend((own, other, beside(own), beside(other)))
+        done = sum(counts)
+        if chunk < last - 1:
+            counts.append(4)
+        elif chunk == last - 1:
+            counts.append(3)
         else:
-            older = down(down_order, place, pieces[:3], down_weight, chunk, older)
-            older = down(
-                down_order, place, pieces[3:], down_weight, chunk, older, 3, (dp_count, tensor_count)
-            )
-        olders.append(older)
+            counts.extend([4, 1])
+        for count in counts[len(olders) :]:
+            pack = (dp_count, tensor_count) if done + count == 4 * CHUNKS else None
+            older = down(down_order, place, queue[done : done + count], down_weight, done, older, pack)
+            olders.append(older)
+            done += count
     packed, (_, _, square) = older[:parts], older[parts:]
     spread = [shifted(value, *shift) for value, shift in zip(packed, shifts)]
 

time: 138 us -> 136 us (0.986)
  transfers between devices with their start and end apart: 30 -> 30, of which waited for: 8 -> 8; matrix products, arithmetic and copies ran while one was open for 2% -> 2% of each run, Pallas kernels for 29% -> 30%
where the time goes in v8:
time: 136 us
  Pallas kernels  55.4 us (41%)
  starting transfers between devices  31 us (23%)
  blocking collectives  22.7 us (17%)
  waiting for transfers between devices  21.4 us (16%)
  other arithmetic  3.29 us (2%)
    pallas_call x5, Pallas kernels, gate_up(): pl.pallas_call(functools.partial(gate_up_kernel, count), grid_spec=pltpu....  35.1 us
    ppermute x10, starting transfers between devices, shifted(): return lax.ppermute(values, ('dp', 'tensor'), pairs)  20 us
    all_to_all x1, blocking collectives, one_expert_each(): lax.all_to_all(sums, ('dp', 'tensor', 'col'), split_axis=0, concat_axis=0...  12.1 us
    ppermute x10, waiting for transfers between devices, shifted(): return lax.ppermute(values, ('dp', 'tensor'), pairs)  11.1 us
    all_to_all x1, blocking collectives, one_expert_each(): lax.all_to_all(home, ('dp', 'tensor'), split_axis=0, concat_axis=0, tiled...  10.7 us
    pallas_call x5, Pallas kernels, down(): pl.pallas_call(functools.partial(down_kernel, len(pieces), pack, bool(old...  10.6 us
    ppermute x8, waiting for transfers between devices, across(): return lax.ppermute(values, 'col', [(k, k ^ 2) for k in range(4)])  10.3 us
    ppermute x8, starting transfers between devices, across(): return lax.ppermute(values, 'col', [(k, k ^ 2) for k in range(4)])  9.18 us
  transfers between devices with their start and end apart: 30, of which 8 were waited for; matrix products, arithmetic and copies ran while one was open for 2% of the time, Pallas kernels for 30%

profile of v8, /device:TPU:0, one launch (start us, length us, event | category | flops | bytes accessed | tf_op | source)
XLA Modules:
  0.0 135.8 jit_solution(9859142227655571100)
XLA Ops:
  2.8 3.1 %collective-permute-start = (bf16[48,1536]{1,0:T(8,128)(2,1)S(1)}, bf16[48,1536]{1,0:T(8,128)(2,1)S(1)}, u32[]{:S(2)}, u32[]{:S(2)}) collective-permute-start(bf16[48,1536]{1,0:T(8,128)(2,1)S(1)} %get-tuple-element.54), channel_id=1, source_target_pairs={{0,8},{4,12},{8,16},{12,20},{16,24},{20,28},{24,0},{28,4},{1,9},{5... | collective-permute-start | bytes 442376 | tf_op jit(solution)/shard_map/ppermute | solution.py:384
  5.9 2.6 %collective-permute-start.1 = (bf16[48,1536]{1,0:T(8,128)(2,1)S(1)}, bf16[48,1536]{1,0:T(8,128)(2,1)S(1)}, u32[]{:S(2)}, u32[]{:S(2)}) collective-permute-start(bf16[48,1536]{1,0:T(8,128)(2,1)S(1)} %get-tuple-element.55), channel_id=1, source_target_pairs={{0,16},{4,20},{8,24},{12,28},{16,0},{20,4},{24,8},{28,12},{1,17},{... | collective-permute-start | bytes 442376 | tf_op jit(solution)/shard_map/ppermute | solution.py:384
  8.5 1.3 collective-permute-start.2
  10.5 2.2 %collective-permute-done.refs_1_ = bf16[48,1536]{1,0:T(8,128)(2,1)S(1)} collective-permute-done((bf16[48,1536]{1,0:T(8,128)(2,1)S(1)}, bf16[48,1536]{1,0:T(8,128)(2,1)S(1)}, u32[]{:S(2)}, u32[]{:S(2)}) %collective-permute-start) | collective-permute-done | bytes 147488 | tf_op jit(solution)/shard_map/ppermute | solution.py:384
  12.7 5.5 %collective-permute-done.1.refs_2_ = bf16[48,1536]{1,0:T(8,128)(2,1)S(1)} collective-permute-done((bf16[48,1536]{1,0:T(8,128)(2,1)S(1)}, bf16[48,1536]{1,0:T(8,128)(2,1)S(1)}, u32[]{:S(2)}, u32[]{:S(2)}) %collective-permute-start.1) | collective-permute-done | bytes 147488 | tf_op jit(solution)/shard_map/ppermute | solution.py:384
  18.2 4.9 %gate_up_0.1 = bf16[2,2,160,512]{3,2,1,0:T(8,128)(2,1)S(1)} custom-call(s32[4]{0:T(128)S(1)} %broadcast_xor_fusion.order_ref, bf16[160,1536]{1,0:T(8,128)(2,1)S(1)} %get-tuple-element.58.inputs_ref, bf16[4,2048,1536]{2,1,0:T(8,128)(2,1)} %bitcast.71, bf16[4,2048,1536]{2,1,0:T(8,128)(2,1)} %bitcast.76), custom_call_target="tpu_custom_call" | custom-call | flops 4026531840 | bytes 25165824 | tf_op jit(solution)/shard_map/gate_up_0/pallas_call | solution.py:132
  23.2 8.2 %gate_up_1.1 = (bf16[2,2,160,512]{3,2,1,0:T(8,128)(2,1)S(1)}, bf16[2,2,160,512]{3,2,1,0:T(8,128)(2,1)S(1)}) custom-call(s32[4]{0:T(128)S(1)} %broadcast_xor_fusion.order_ref, bf16[160,1536]{1,0:T(8,128)(2,1)S(1)} %get-tuple-element.58.inputs_ref, bf16[4,2048,1536]{2,1,0:T(8,128)(2,1)} %bitcast.72, bf16[4,2048,1536]{2,1,0:T(8,128)(2,1)} %bitcast.77), custom_call_target="tpu_custom_call" | custom-call | flops 8053063680 | bytes 50331648 | tf_op jit(solution)/shard_map/gate_up_1/pallas_call | solution.py:132
  32.0 1.6 %collective-permute-start.5 = (bf16[2,160,512]{2,1,0:T(8,128)(2,1)S(1)}, bf16[2,160,512]{2,1,0:T(8,128)(2,1)S(1)}, u32[]{:S(2)}, u32[]{:S(2)}) collective-permute-start(bf16[2,160,512]{2,1,0:T(8,128)(2,1)S(1)} %fusion.1), channel_id=1, source_target_pairs={{0,2},{1,3},{2,0},{3,1},{4,6},{5,7},{6,4},{7,5},{8,10},{9,11},{10,... | collective-permute-start | bytes 983048 | tf_op jit(solution)/shard_map/ppermute | solution.py:374
  33.6 8.2 %gate_up_2.1 = (bf16[2,2,160,512]{3,2,1,0:T(8,128)(2,1)S(1)}, bf16[2,2,160,512]{3,2,1,0:T(8,128)(2,1)S(1)}) custom-call(s32[4]{0:T(128)S(1)} %broadcast_xor_fusion.order_ref, bf16[160,1536]{1,0:T(8,128)(2,1)S(1)} %get-tuple-element.58.inputs_ref, bf16[4,2048,1536]{2,1,0:T(8,128)(2,1)} %bitcast.73, bf16[4,2048,1536]{2,1,0:T(8,128)(2,1)} %bitcast.78, ...), custom_call_target="tpu_custom_call" | custom-call | flops 8053063680 | bytes 50331648 | tf_op jit(solution)/shard_map/gate_up_2/pallas_call | solution.py:132
  42.8 8.2 %gate_up_3.1 = (bf16[2,2,160,512]{3,2,1,0:T(8,128)(2,1)S(1)}, bf16[2,2,160,512]{3,2,1,0:T(8,128)(2,1)S(1)}) custom-call(s32[4]{0:T(128)S(1)} %broadcast_xor_fusion.order_ref, bf16[160,1536]{1,0:T(8,128)(2,1)S(1)} %get-tuple-element.58.inputs_ref, bf16[4,2048,1536]{2,1,0:T(8,128)(2,1)} %bitcast.74, bf16[4,2048,1536]{2,1,0:T(8,128)(2,1)} %bitcast.79, ...), custom_call_target="tpu_custom_call" | custom-call | flops 8053063680 | bytes 50331648 | tf_op jit(solution)/shard_map/gate_up_3/pallas_call | solution.py:132
  51.0 1.6 %collective-permute-start.13 = (bf16[160,512]{1,0:T(8,128)(2,1)S(1)}, bf16[160,512]{1,0:T(8,128)(2,1)S(1)}, u32[]{:S(2)}, u32[]{:S(2)}) collective-permute-start(bf16[160,512]{1,0:T(8,128)(2,1)S(1)} %fusion.11.rest_2_.refs_0_), channel_id=1, source_target_pairs={{0,2},{1,3},{2,0},{3,1},{4,6},{5,7},{6,4},{7,5},{8,10},{9,11},{10,... | collective-permute-start | bytes 491528 | tf_op jit(solution)/shard_map/ppermute | solution.py:374
  53.5 1.6 %collective-permute-start.10 = (bf16[160,512]{1,0:T(8,128)(2,1)S(1)}, bf16[160,512]{1,0:T(8,128)(2,1)S(1)}, u32[]{:S(2)}, u32[]{:S(2)}) collective-permute-start(bf16[160,512]{1,0:T(8,128)(2,1)S(1)} %fusion.9.rest_2_.refs_0_), channel_id=1, source_target_pairs={{0,2},{1,3},{2,0},{3,1},{4,6},{5,7},{6,4},{7,5},{8,10},{9,11},{10,... | collective-permute-start | bytes 491528 | tf_op jit(solution)/shard_map/ppermute | solution.py:374
  55.1 5.7 %gate_up_4.1 = bf16[2,2,160,512]{3,2,1,0:T(8,128)(2,1)S(1)} custom-call(s32[4]{0:T(128)S(1)} %broadcast_xor_fusion.order_ref, bf16[160,1536]{1,0:T(8,128)(2,1)S(1)} %get-tuple-element.58.inputs_ref, bf16[4,2048,1536]{2,1,0:T(8,128)(2,1)} %bitcast.75, bf16[4,2048,1536]{2,1,0:T(8,128)(2,1)} %bitcast.80, ...), custom_call_target="tpu_custom_call" | custom-call | flops 4026531840 | bytes 25165824 | tf_op jit(solution)/shard_map/gate_up_4/pallas_call | solution.py:132
  61.8 6.8 %collective-permute-done.10.refs_1_ = bf16[160,512]{1,0:T(8,128)(2,1)S(1)} collective-permute-done((bf16[160,512]{1,0:T(8,128)(2,1)S(1)}, bf16[160,512]{1,0:T(8,128)(2,1)S(1)}, u32[]{:S(2)}, u32[]{:S(2)}) %collective-permute-start.10) | collective-permute-done | bytes 163872 | tf_op jit(solution)/shard_map/ppermute | solution.py:374
  69.1 2.3 %down_0.1 = (f32[160,768]{1,0:T(8,128)S(1)}, f32[160,160]{1,0:T(8,128)S(1)}, f32[8,768]{1,0:T(8,128)S(1)}) custom-call(s32[16]{0:T(128)S(1)} %fusion.12.order_ref, s32[2]{0:T(128)S(1)} %pad_add_fusion.1.place_ref, bf16[160,512]{1,0:T(8,128)(2,1)S(1)} %fusion.11.rest_2_.refs_0_, bf16[160,512]{1,0:T(8,128)(2,1)S(1)} %collective-permute-done.13.refs_1_, ...), custom_call_target="tpu_custom_call" | custom-call | flops 2013265920 | bytes 12582912 | tf_op jit(solution)/shard_map/down_0/pallas_call | solution.py:216
  71.7 1.6 %collective-permute-start.19 = (bf16[160,512]{1,0:T(8,128)(2,1)S(1)}, bf16[160,512]{1,0:T(8,128)(2,1)S(1)}, u32[]{:S(2)}, u32[]{:S(2)}) collective-permute-start(bf16[160,512]{1,0:T(8,128)(2,1)S(1)} %fusion.5.refs_0_), channel_id=1, source_target_pairs={{0,2},{1,3},{2,0},{3,1},{4,6},{5,7},{6,4},{7,5},{8,10},{9,11},{10,... | collective-permute-start | bytes 491528 | tf_op jit(solution)/shard_map/ppermute | solution.py:374
  73.3 2.3 %down_4.1 = (f32[160,768]{1,0:T(8,128)S(1)}, f32[160,160]{1,0:T(8,128)S(1)}, f32[8,768]{1,0:T(8,128)S(1)}) custom-call(s32[16]{0:T(128)S(1)} %fusion.12.order_ref, s32[2]{0:T(128)S(1)} %pad_add_fusion.1.place_ref, bf16[160,512]{1,0:T(8,128)(2,1)S(1)} %fusion.9.rest_2_.refs_0_, bf16[160,512]{1,0:T(8,128)(2,1)S(1)} %collective-permute-done.10.refs_1_, ...), custom_call_target="tpu_custom_call" | custom-call | flops 2013265920 | bytes 12582912 | tf_op jit(solution)/shard_map/down_4/pallas_call | solution.py:216
  75.8 1.4 %collective-permute-start.16 = (bf16[160,512]{1,0:T(8,128)(2,1)S(1)}, bf16[160,512]{1,0:T(8,128)(2,1)S(1)}, u32[]{:S(2)}, u32[]{:S(2)}) collective-permute-start(bf16[160,512]{1,0:T(8,128)(2,1)S(1)} %fusion.7.refs_1_), channel_id=1, source_target_pairs={{0,2},{1,3},{2,0},{3,1},{4,6},{5,7},{6,4},{7,5},{8,10},{9,11},{10,... | collective-permute-start | bytes 491528 | tf_op jit(solution)/shard_map/ppermute | solution.py:374
  78.4 1.9 %down_8.1 = (f32[160,768]{1,0:T(8,128)S(1)}, f32[160,160]{1,0:T(8,128)S(1)}, f32[8,768]{1,0:T(8,128)S(1)}) custom-call(s32[16]{0:T(128)S(1)} %fusion.12.order_ref, s32[2]{0:T(128)S(1)} %pad_add_fusion.1.place_ref, bf16[160,512]{1,0:T(8,128)(2,1)S(1)} %fusion.5.refs_0_, bf16[160,512]{1,0:T(8,128)(2,1)S(1)} %collective-permute-done.19.refs_1_, ...), custom_call_target="tpu_custom_call" | custom-call | flops 1509949440 | bytes 9437184 | tf_op jit(solution)/shard_map/down_8/pallas_call | solution.py:216
  80.3 2.2 %collective-permute-done.16.refs_2_ = bf16[160,512]{1,0:T(8,128)(2,1)S(1)} collective-permute-done((bf16[160,512]{1,0:T(8,128)(2,1)S(1)}, bf16[160,512]{1,0:T(8,128)(2,1)S(1)}, u32[]{:S(2)}, u32[]{:S(2)}) %collective-permute-start.16) | collective-permute-done | bytes 163872 | tf_op jit(solution)/shard_map/ppermute | solution.py:374
  82.5 2.3 %down_11.1 = (f32[160,768]{1,0:T(8,128)S(1)}, f32[160,160]{1,0:T(8,128)S(1)}, f32[8,768]{1,0:T(8,128)S(1)}) custom-call(s32[16]{0:T(128)S(1)} %fusion.12.order_ref, s32[2]{0:T(128)S(1)} %pad_add_fusion.1.place_ref, bf16[160,512]{1,0:T(8,128)(2,1)S(1)} %collective-permute-done.20.refs_0_, bf16[160,512]{1,0:T(8,128)(2,1)S(1)} %fusion.7.refs_1_, ...), custom_call_target="tpu_custom_call" | custom-call | flops 2013265920 | bytes 12582912 | tf_op jit(solution)/shard_map/down_11/pallas_call | solution.py:216
  84.8 1.9 %down_15.1 = (bf16[160,256]{1,0:T(8,128)(2,1)S(1)}, bf16[160,256]{1,0:T(8,128)(2,1)S(1)}, bf16[160,256]{1,0:T(8,128)(2,1)S(1)}, bf16[160,256]{1,0:T(8,128)(2,1)S...) custom-call(s32[16]{0:T(128)S(1)} %fusion.12.order_ref, ...), custom_call_target="tpu_custom_call" | custom-call | flops 503316480 | bytes 3145728 | tf_op jit(solution)/shard_map/down_15/pallas_call | solution.py:216
  86.7 1.5 %collective-permute-start.23 = (bf16[160,256]{1,0:T(8,128)(2,1)S(1)}, bf16[160,256]{1,0:T(8,128)(2,1)S(1)}, u32[]{:S(2)}, u32[]{:S(2)}) collective-permute-start(bf16[160,256]{1,0:T(8,128)(2,1)S(1)} %get-tuple-element.90), channel_id=1, source_target_pairs={{0,4},{4,0},{8,12},{12,8},{16,20},{20,16},{24,28},{28,24},{1,5},{5... | collective-permute-start | bytes 245768 | tf_op jit(solution)/shard_map/ppermute | solution.py:384
  88.2 3.6 %collective-permute-start.24 = (bf16[160,256]{1,0:T(8,128)(2,1)S(1)}, bf16[160,256]{1,0:T(8,128)(2,1)S(1)}, u32[]{:S(2)}, u32[]{:S(2)}) collective-permute-start(bf16[160,256]{1,0:T(8,128)(2,1)S(1)} %get-tuple-element.91), channel_id=1, source_target_pairs={{0,8},{4,12},{8,16},{12,20},{16,24},{20,28},{24,0},{28,4},{1,9},{5... | collective-permute-start | bytes 245768 | tf_op jit(solution)/shard_map/ppermute | solution.py:384
  91.8 1.6 %collective-permute-start.26 = (bf16[160,256]{1,0:T(8,128)(2,1)S(1)}, bf16[160,256]{1,0:T(8,128)(2,1)S(1)}, u32[]{:S(2)}, u32[]{:S(2)}) collective-permute-start(bf16[160,256]{1,0:T(8,128)(2,1)S(1)} %get-tuple-element.93), channel_id=1, source_target_pairs={{0,16},{4,20},{8,24},{12,28},{16,0},{20,4},{24,8},{28,12},{1,17},{... | collective-permute-start | bytes 245768 | tf_op jit(solution)/shard_map/ppermute | solution.py:384
  93.5 2.2 %collective-permute-start.27 = (bf16[160,256]{1,0:T(8,128)(2,1)S(1)}, bf16[160,256]{1,0:T(8,128)(2,1)S(1)}, u32[]{:S(2)}, u32[]{:S(2)}) collective-permute-start(bf16[160,256]{1,0:T(8,128)(2,1)S(1)} %get-tuple-element.94), channel_id=1, source_target_pairs={{0,20},{4,16},{8,28},{12,24},{16,4},{20,0},{24,12},{28,8},{1,21},{... | collective-permute-start | bytes 245768 | tf_op jit(solution)/shard_map/ppermute | solution.py:384
  95.7 3.8 %collective-permute-start.28 = (bf16[160,256]{1,0:T(8,128)(2,1)S(1)}, bf16[160,256]{1,0:T(8,128)(2,1)S(1)}, u32[]{:S(2)}, u32[]{:S(2)}) collective-permute-start(bf16[160,256]{1,0:T(8,128)(2,1)S(1)} %get-tuple-element.95), channel_id=1, source_target_pairs={{0,24},{4,28},{8,0},{12,4},{16,8},{20,12},{24,16},{28,20},{1,25},{... | collective-permute-start | bytes 245768 | tf_op jit(solution)/shard_map/ppermute | solution.py:384
  101.0 1.5 %route.1 = (bf16[1280,512]{1,0:T(8,128)(2,1)S(1)}, bf16[512,1280]{1,0:T(8,128)(2,1)S(1)}, f32[1280,2]{1,0:T(8,128)S(1)}) custom-call(s32[6]{0:T(128)S(1)} %copy-done.1, s32[2]{0:T(128)S(1)} %pad_add_fusion.1.place_ref, f32[4,4,128]{2,1,0:T(4,128)S(1)} %get-tuple-element.57.refs_0_, f32[8,768]{1,0:T(8,128)S(1)} %get-tuple-element.85.refs_1_.square_ref), custom_call_target="tpu_custom_call" | custom-call | flops 1 | bytes 1 | tf_op jit(solution)/shard_map/route/pallas_call | solution.py:462
  103.2 2.7 %collective-permute-done.27.refs_5_ = bf16[160,256]{1,0:T(8,128)(2,1)S(1)} collective-permute-done((bf16[160,256]{1,0:T(8,128)(2,1)S(1)}, bf16[160,256]{1,0:T(8,128)(2,1)S(1)}, u32[]{:S(2)}, u32[]{:S(2)}) %collective-permute-start.27) | collective-permute-done | bytes 81952 | tf_op jit(solution)/shard_map/ppermute | solution.py:384
  105.9 5.4 %solve.1 = (f32[512,96]{1,0:T(8,128)S(1)}, f32[512,96]{1,0:T(8,128)S(1)}, f32[512,96]{1,0:T(8,128)S(1)}, f32[32,1,128]{2,1,0:T(1,128)S(1)}) custom-call(f32[1]{0:T(128)} %bitcast.2.own_ref, bf16[1280,512]{1,0:T(8,128)(2,1)S(1)} %get-tuple-element.86.hot_ref, bf16[512,1280]{1,0:T(8,128)(2,1)S(1)} %get-tuple-element.87.turned_ref, ...), custom_call_target="tpu_custom_call" | custom-call | flops 1 | bytes 1 | tf_op jit(solution)/shard_map/solve/pallas_call | solution.py:477
  111.3 12.1 %all_to_all.10.sums_ref = f32[32,1,128]{2,1,0:T(1,128)S(1)} all-to-all(f32[32,1,128]{2,1,0:T(1,128)S(1)} %get-tuple-element.100), channel_id=1, replica_groups=mesh['dp'=4,'tensor'=2,'col'=4] {'dp','tensor','col'}, dimensions={0} | all-to-all | bytes 32768 | tf_op jit(solution)/shard_map/all_to_all | solution.py:484
  124.2 10.7 %all_to_all.11.pieces_ref = bf16[8,96,128]{2,1,0:T(8,128)(2,1)S(1)} all-to-all(bf16[8,96,128]{2,1,0:T(8,128)(2,1)S(1)} %finish.1), channel_id=1, replica_groups=mesh['dp'=4,'tensor'=2,'col'=4] {'dp','tensor'}, dimensions={0} | all-to-all | bytes 393216 | tf_op jit(solution)/shard_map/all_to_all | solution.py:493
  (76 shorter events, 12.7 us)
Async XLA Ops:
  2.8 9.9 %collective-permute-start = (bf16[48,1536]{1,0:T(8,128)(2,1)S(1)}, bf16[48,1536]{1,0:T(8,128)(2,1)S(1)}, u32[]{:S(2)}, u32[]{:S(2)}) collective-permute-start(bf16[48,1536]{1,0:T(8,128)(2,1)S(1)} %get-tuple-element.54), channel_id=1, source_target_pairs={{0,8},{4,12},{8,16},{12,20},{16,24},{20,28},{24,0},{28,4},{1,9},{5... | collective-permute-start | bytes 442376 | tf_op jit(solution)/shard_map/ppermute | solution.py:384
  5.9 12.3 %collective-permute-start.1 = (bf16[48,1536]{1,0:T(8,128)(2,1)S(1)}, bf16[48,1536]{1,0:T(8,128)(2,1)S(1)}, u32[]{:S(2)}, u32[]{:S(2)}) collective-permute-start(bf16[48,1536]{1,0:T(8,128)(2,1)S(1)} %get-tuple-element.55), channel_id=1, source_target_pairs={{0,16},{4,20},{8,24},{12,28},{16,0},{20,4},{24,8},{28,12},{1,17},{... | collective-permute-start | bytes 442376 | tf_op jit(solution)/shard_map/ppermute | solution.py:384
  8.5 9.7 %collective-permute-start.2 = (bf16[48,1536]{1,0:T(8,128)(2,1)S(1)}, bf16[48,1536]{1,0:T(8,128)(2,1)S(1)}, u32[]{:S(2)}, u32[]{:S(2)}) collective-permute-start(bf16[48,1536]{1,0:T(8,128)(2,1)S(1)} %get-tuple-element.56), channel_id=1, source_target_pairs={{0,24},{4,28},{8,0},{12,4},{16,8},{20,12},{24,16},{28,20},{1,25},{... | collective-permute-start | bytes 442376 | tf_op jit(solution)/shard_map/ppermute | solution.py:384
  23.1 8.8 %collective-permute-start.4 = (bf16[2,2,160,512]{3,2,1,0:T(8,128)(2,1)S(1)}, bf16[2,2,160,512]{3,2,1,0:T(8,128)(2,1)S(1)}, u32[]{:S(2)}, u32[]{:S(2)}) collective-permute-start(bf16[2,2,160,512]{3,2,1,0:T(8,128)(2,1)S(1)} %gate_up_0.1), channel_id=1, source_target_pairs={{0,1},{1,0},{2,3},{3,2},{4,5},{5,4},{6,7},{7,6},{8,9},{9,8},{10,11... | collective-permute-start | bytes 1966088 | tf_op jit(solution)/shard_map/ppermute | solution.py:371
  31.4 10.5 %collective-permute-start.3 = (bf16[2,2,160,512]{3,2,1,0:T(8,128)(2,1)S(1)}, bf16[2,2,160,512]{3,2,1,0:T(8,128)(2,1)S(1)}, u32[]{:S(2)}, u32[]{:S(2)}) collective-permute-start(bf16[2,2,160,512]{3,2,1,0:T(8,128)(2,1)S(1)} %get-tuple-element.61), channel_id=1, source_target_pairs={{0,1},{1,0},{2,3},{3,2},{4,5},{5,4},{6,7},{7,6},{8,9},{9,8},{10,11... | collective-permute-start | bytes 1966088 | tf_op jit(solution)/shard_map/ppermute | solution.py:371
  32.0 10.5 %collective-permute-start.5 = (bf16[2,160,512]{2,1,0:T(8,128)(2,1)S(1)}, bf16[2,160,512]{2,1,0:T(8,128)(2,1)S(1)}, u32[]{:S(2)}, u32[]{:S(2)}) collective-permute-start(bf16[2,160,512]{2,1,0:T(8,128)(2,1)S(1)} %fusion.1), channel_id=1, source_target_pairs={{0,2},{1,3},{2,0},{3,1},{4,6},{5,7},{6,4},{7,5},{8,10},{9,11},{10,... | collective-permute-start | bytes 983048 | tf_op jit(solution)/shard_map/ppermute | solution.py:374
  41.8 10.7 %collective-permute-start.6 = (bf16[2,2,160,512]{3,2,1,0:T(8,128)(2,1)S(1)}, bf16[2,2,160,512]{3,2,1,0:T(8,128)(2,1)S(1)}, u32[]{:S(2)}, u32[]{:S(2)}) collective-permute-start(bf16[2,2,160,512]{3,2,1,0:T(8,128)(2,1)S(1)} %get-tuple-element.64), channel_id=1, source_target_pairs={{0,1},{1,0},{2,3},{3,2},{4,5},{5,4},{6,7},{7,6},{8,9},{9,8},{10,11... | collective-permute-start | bytes 1966088 | tf_op jit(solution)/shard_map/ppermute | solution.py:371
  42.0 11.2 %collective-permute-start.7 = (bf16[2,160,512]{2,1,0:T(8,128)(2,1)S(1)}, bf16[2,160,512]{2,1,0:T(8,128)(2,1)S(1)}, u32[]{:S(2)}, u32[]{:S(2)}) collective-permute-start(bf16[2,160,512]{2,1,0:T(8,128)(2,1)S(1)} %fusion.rest_1_), channel_id=1, source_target_pairs={{0,2},{1,3},{2,0},{3,1},{4,6},{5,7},{6,4},{7,5},{8,10},{9,11},{10,... | collective-permute-start | bytes 983048 | tf_op jit(solution)/shard_map/ppermute | solution.py:374
  51.0 9.9 %collective-permute-start.13 = (bf16[160,512]{1,0:T(8,128)(2,1)S(1)}, bf16[160,512]{1,0:T(8,128)(2,1)S(1)}, u32[]{:S(2)}, u32[]{:S(2)}) collective-permute-start(bf16[160,512]{1,0:T(8,128)(2,1)S(1)} %fusion.11.rest_2_.refs_0_), channel_id=1, source_target_pairs={{0,2},{1,3},{2,0},{3,1},{4,6},{5,7},{6,4},{7,5},{8,10},{9,11},{10,... | collective-permute-start | bytes 491528 | tf_op jit(solution)/shard_map/ppermute | solution.py:374
  52.6 18.8 %collective-permute-start.18 = (bf16[2,160,512]{2,1,0:T(8,128)(2,1)S(1)}, bf16[2,160,512]{2,1,0:T(8,128)(2,1)S(1)}, u32[]{:S(2)}, u32[]{:S(2)}) collective-permute-start(bf16[2,160,512]{2,1,0:T(8,128)(2,1)S(1)} %fusion.2.rest_1_), channel_id=1, source_target_pairs={{0,2},{1,3},{2,0},{3,1},{4,6},{5,7},{6,4},{7,5},{8,10},{9,11},{10,... | collective-permute-start | bytes 983048 | tf_op jit(solution)/shard_map/ppermute | solution.py:374
  53.2 7.5 %collective-permute-start.8 = (bf16[2,2,160,512]{3,2,1,0:T(8,128)(2,1)S(1)}, bf16[2,2,160,512]{3,2,1,0:T(8,128)(2,1)S(1)}, u32[]{:S(2)}, u32[]{:S(2)}) collective-permute-start(bf16[2,2,160,512]{3,2,1,0:T(8,128)(2,1)S(1)} %get-tuple-element.66), channel_id=1, source_target_pairs={{0,1},{1,0},{2,3},{3,2},{4,5},{5,4},{6,7},{7,6},{8,9},{9,8},{10,11... | collective-permute-start | bytes 1966088 | tf_op jit(solution)/shard_map/ppermute | solution.py:371
  53.3 15.8 %slice-start = ((s8[12582912]{0:T(1024)(128)(4,1)}), s8[4194304]{0:T(1024)(128)(4,1)S(1)}, s32[]{:S(2)}) async-start(s8[12582912]{0:T(1024)(128)(4,1)} %bitcast.64), calls=%async_computation.2 | async-start | bytes 8388608
  53.5 15.1 %collective-permute-start.10 = (bf16[160,512]{1,0:T(8,128)(2,1)S(1)}, bf16[160,512]{1,0:T(8,128)(2,1)S(1)}, u32[]{:S(2)}, u32[]{:S(2)}) collective-permute-start(bf16[160,512]{1,0:T(8,128)(2,1)S(1)} %fusion.9.rest_2_.refs_0_), channel_id=1, source_target_pairs={{0,2},{1,3},{2,0},{3,1},{4,6},{5,7},{6,4},{7,5},{8,10},{9,11},{10,... | collective-permute-start | bytes 491528 | tf_op jit(solution)/shard_map/ppermute | solution.py:374
  60.8 7.8 %collective-permute-start.14 = (bf16[160,512]{1,0:T(8,128)(2,1)S(1)}, bf16[160,512]{1,0:T(8,128)(2,1)S(1)}, u32[]{:S(2)}, u32[]{:S(2)}) collective-permute-start(bf16[160,512]{1,0:T(8,128)(2,1)S(1)} %fusion.11.rest_2_.refs_0_), channel_id=1, source_target_pairs={{0,1},{1,0},{2,3},{3,2},{4,5},{5,4},{6,7},{7,6},{8,9},{9,8},{10,11... | collective-permute-start | bytes 491528 | tf_op jit(solution)/shard_map/ppermute | solution.py:371
  61.1 8.0 %collective-permute-start.15 = (bf16[160,512]{1,0:T(8,128)(2,1)S(1)}, bf16[160,512]{1,0:T(8,128)(2,1)S(1)}, u32[]{:S(2)}, u32[]{:S(2)}) collective-permute-start(bf16[160,512]{1,0:T(8,128)(2,1)S(1)} %collective-permute-done.13.refs_1_), channel_id=1, source_target_pairs={{0,1},{1,0},{2,3},{3,2},{4,5},{5,4},{6,7},{7,6},{8,9},{9,8},{10,11... | collective-permute-start | bytes 491528 | tf_op jit(solution)/shard_map/ppermute | solution.py:371
  61.4 14.1 %collective-permute-start.9 = (bf16[2,160,512]{2,1,0:T(8,128)(2,1)S(1)}, bf16[2,160,512]{2,1,0:T(8,128)(2,1)S(1)}, u32[]{:S(2)}, u32[]{:S(2)}) collective-permute-start(bf16[2,160,512]{2,1,0:T(8,128)(2,1)S(1)} %fusion.3), channel_id=1, source_target_pairs={{0,2},{1,3},{2,0},{3,1},{4,6},{5,7},{6,4},{7,5},{8,10},{9,11},{10,... | collective-permute-start | bytes 983048 | tf_op jit(solution)/shard_map/ppermute | solution.py:374
  68.6 4.7 %collective-permute-start.11 = (bf16[160,512]{1,0:T(8,128)(2,1)S(1)}, bf16[160,512]{1,0:T(8,128)(2,1)S(1)}, u32[]{:S(2)}, u32[]{:S(2)}) collective-permute-start(bf16[160,512]{1,0:T(8,128)(2,1)S(1)} %fusion.9.rest_2_.refs_0_), channel_id=1, source_target_pairs={{0,1},{1,0},{2,3},{3,2},{4,5},{5,4},{6,7},{7,6},{8,9},{9,8},{10,11... | collective-permute-start | bytes 491528 | tf_op jit(solution)/shard_map/ppermute | solution.py:371
  68.6 4.7 %collective-permute-start.12 = (bf16[160,512]{1,0:T(8,128)(2,1)S(1)}, bf16[160,512]{1,0:T(8,128)(2,1)S(1)}, u32[]{:S(2)}, u32[]{:S(2)}) collective-permute-start(bf16[160,512]{1,0:T(8,128)(2,1)S(1)} %collective-permute-done.10.refs_1_), channel_id=1, source_target_pairs={{0,1},{1,0},{2,3},{3,2},{4,5},{5,4},{6,7},{7,6},{8,9},{9,8},{10,11... | collective-permute-start | bytes 491528 | tf_op jit(solution)/shard_map/ppermute | solution.py:371
  71.7 6.7 %collective-permute-start.19 = (bf16[160,512]{1,0:T(8,128)(2,1)S(1)}, bf16[160,512]{1,0:T(8,128)(2,1)S(1)}, u32[]{:S(2)}, u32[]{:S(2)}) collective-permute-start(bf16[160,512]{1,0:T(8,128)(2,1)S(1)} %fusion.5.refs_0_), channel_id=1, source_target_pairs={{0,2},{1,3},{2,0},{3,1},{4,6},{5,7},{6,4},{7,5},{8,10},{9,11},{10,... | collective-permute-start | bytes 491528 | tf_op jit(solution)/shard_map/ppermute | solution.py:374
  73.3 5.2 %collective-permute-start.22 = (bf16[160,512]{1,0:T(8,128)(2,1)S(1)}, bf16[160,512]{1,0:T(8,128)(2,1)S(1)}, u32[]{:S(2)}, u32[]{:S(2)}) collective-permute-start(bf16[160,512]{1,0:T(8,128)(2,1)S(1)} %fusion.5.refs_0_), channel_id=1, source_target_pairs={{0,1},{1,0},{2,3},{3,2},{4,5},{5,4},{6,7},{7,6},{8,9},{9,8},{10,11... | collective-permute-start | bytes 491528 | tf_op jit(solution)/shard_map/ppermute | solution.py:371
  75.8 6.7 %collective-permute-start.16 = (bf16[160,512]{1,0:T(8,128)(2,1)S(1)}, bf16[160,512]{1,0:T(8,128)(2,1)S(1)}, u32[]{:S(2)}, u32[]{:S(2)}) collective-permute-start(bf16[160,512]{1,0:T(8,128)(2,1)S(1)} %fusion.7.refs_1_), channel_id=1, source_target_pairs={{0,2},{1,3},{2,0},{3,1},{4,6},{5,7},{6,4},{7,5},{8,10},{9,11},{10,... | collective-permute-start | bytes 491528 | tf_op jit(solution)/shard_map/ppermute | solution.py:374
  77.2 5.3 %collective-permute-start.21 = (bf16[160,512]{1,0:T(8,128)(2,1)S(1)}, bf16[160,512]{1,0:T(8,128)(2,1)S(1)}, u32[]{:S(2)}, u32[]{:S(2)}) collective-permute-start(bf16[160,512]{1,0:T(8,128)(2,1)S(1)} %fusion.7.refs_1_), channel_id=1, source_target_pairs={{0,1},{1,0},{2,3},{3,2},{4,5},{5,4},{6,7},{7,6},{8,9},{9,8},{10,11... | collective-permute-start | bytes 491528 | tf_op jit(solution)/shard_map/ppermute | solution.py:371
  78.4 4.1 %collective-permute-start.20 = (bf16[160,512]{1,0:T(8,128)(2,1)S(1)}, bf16[160,512]{1,0:T(8,128)(2,1)S(1)}, u32[]{:S(2)}, u32[]{:S(2)}) collective-permute-start(bf16[160,512]{1,0:T(8,128)(2,1)S(1)} %collective-permute-done.19.refs_1_), channel_id=1, source_target_pairs={{0,1},{1,0},{2,3},{3,2},{4,5},{5,4},{6,7},{7,6},{8,9},{9,8},{10,11... | collective-permute-start | bytes 491528 | tf_op jit(solution)/shard_map/ppermute | solution.py:371
  82.5 2.3 %collective-permute-start.17 = (bf16[160,512]{1,0:T(8,128)(2,1)S(1)}, bf16[160,512]{1,0:T(8,128)(2,1)S(1)}, u32[]{:S(2)}, u32[]{:S(2)}) collective-permute-start(bf16[160,512]{1,0:T(8,128)(2,1)S(1)} %collective-permute-done.16.refs_2_), channel_id=1, source_target_pairs={{0,1},{1,0},{2,3},{3,2},{4,5},{5,4},{6,7},{7,6},{8,9},{9,8},{10,11... | collective-permute-start | bytes 491528 | tf_op jit(solution)/shard_map/ppermute | solution.py:371
  82.5 17.2 %copy-start.1 = (s32[6]{0:T(128)S(1)}, s32[6]{0:T(128)}, u32[]{:S(2)}) copy-start(s32[6]{0:T(128)} %kept_ref.1) | copy-start | bytes 76
  86.7 8.9 %collective-permute-start.23 = (bf16[160,256]{1,0:T(8,128)(2,1)S(1)}, bf16[160,256]{1,0:T(8,128)(2,1)S(1)}, u32[]{:S(2)}, u32[]{:S(2)}) collective-permute-start(bf16[160,256]{1,0:T(8,128)(2,1)S(1)} %get-tuple-element.90), channel_id=1, source_target_pairs={{0,4},{4,0},{8,12},{12,8},{16,20},{20,16},{24,28},{28,24},{1,5},{5... | collective-permute-start | bytes 245768 | tf_op jit(solution)/shard_map/ppermute | solution.py:384
  88.2 11.3 %collective-permute-start.24 = (bf16[160,256]{1,0:T(8,128)(2,1)S(1)}, bf16[160,256]{1,0:T(8,128)(2,1)S(1)}, u32[]{:S(2)}, u32[]{:S(2)}) collective-permute-start(bf16[160,256]{1,0:T(8,128)(2,1)S(1)} %get-tuple-element.91), channel_id=1, source_target_pairs={{0,8},{4,12},{8,16},{12,20},{16,24},{20,28},{24,0},{28,4},{1,9},{5... | collective-permute-start | bytes 245768 | tf_op jit(solution)/shard_map/ppermute | solution.py:384
  91.8 10.7 %collective-permute-start.25 = (bf16[160,256]{1,0:T(8,128)(2,1)S(1)}, bf16[160,256]{1,0:T(8,128)(2,1)S(1)}, u32[]{:S(2)}, u32[]{:S(2)}) collective-permute-start(bf16[160,256]{1,0:T(8,128)(2,1)S(1)} %get-tuple-element.92), channel_id=1, source_target_pairs={{0,12},{4,8},{8,20},{12,16},{16,28},{20,24},{24,4},{28,0},{1,13},{... | collective-permute-start | bytes 245768 | tf_op jit(solution)/shard_map/ppermute | solution.py:384
  91.8 11.3 %collective-permute-start.26 = (bf16[160,256]{1,0:T(8,128)(2,1)S(1)}, bf16[160,256]{1,0:T(8,128)(2,1)S(1)}, u32[]{:S(2)}, u32[]{:S(2)}) collective-permute-start(bf16[160,256]{1,0:T(8,128)(2,1)S(1)} %get-tuple-element.93), channel_id=1, source_target_pairs={{0,16},{4,20},{8,24},{12,28},{16,0},{20,4},{24,8},{28,12},{1,17},{... | collective-permute-start | bytes 245768 | tf_op jit(solution)/shard_map/ppermute | solution.py:384
  93.5 12.3 %collective-permute-start.27 = (bf16[160,256]{1,0:T(8,128)(2,1)S(1)}, bf16[160,256]{1,0:T(8,128)(2,1)S(1)}, u32[]{:S(2)}, u32[]{:S(2)}) collective-permute-start(bf16[160,256]{1,0:T(8,128)(2,1)S(1)} %get-tuple-element.94), channel_id=1, source_target_pairs={{0,20},{4,16},{8,28},{12,24},{16,4},{20,0},{24,12},{28,8},{1,21},{... | collective-permute-start | bytes 245768 | tf_op jit(solution)/shard_map/ppermute | solution.py:384
  95.7 10.2 %collective-permute-start.28 = (bf16[160,256]{1,0:T(8,128)(2,1)S(1)}, bf16[160,256]{1,0:T(8,128)(2,1)S(1)}, u32[]{:S(2)}, u32[]{:S(2)}) collective-permute-start(bf16[160,256]{1,0:T(8,128)(2,1)S(1)} %get-tuple-element.95), channel_id=1, source_target_pairs={{0,24},{4,28},{8,0},{12,4},{16,8},{20,12},{24,16},{28,20},{1,25},{... | collective-permute-start | bytes 245768 | tf_op jit(solution)/shard_map/ppermute | solution.py:384
  99.5 6.4 %collective-permute-start.29 = (bf16[160,256]{1,0:T(8,128)(2,1)S(1)}, bf16[160,256]{1,0:T(8,128)(2,1)S(1)}, u32[]{:S(2)}, u32[]{:S(2)}) collective-permute-start(bf16[160,256]{1,0:T(8,128)(2,1)S(1)} %get-tuple-element.96), channel_id=1, source_target_pairs={{0,28},{4,24},{8,4},{12,0},{16,12},{20,8},{24,20},{28,16},{1,29},{... | collective-permute-start | bytes 245768 | tf_op jit(solution)/shard_map/ppermute | solution.py:384
  (4 other events, 40.2 us)

commit v9 on v8

--- a/solution.py
+++ b/solution.py
@@ -282,8 +282,9 @@
     hot, turned = hot_ref[...], turned_ref[...]
     kept, dropped = gates_ref[:, 0:1], gates_ref[:, 1:2]
     values = jnp.concatenate([packed_refs[e][:, slots:].astype(f32) for e in range(E)], axis=0)
-    base = mm_wide(turned, dropped * values)
-    output = mm_wide(turned, kept * values)
+    lanes = values.shape[1]
+    both = mm_wide(turned, jnp.concatenate([dropped * values, kept * values], axis=1))
+    base, output = both[:, :lanes], both[:, lanes:]
 
     def apply(field):
         spread = kept * mm_wide(hot, field)

time: 136 us -> 136 us (level)
  no operation moved by 1% of the time
where the time goes in v9:
time: 136 us
  Pallas kernels  55.8 us (41%)
  starting transfers between devices  31 us (23%)
  blocking collectives  22.7 us (17%)
  waiting for transfers between devices  21.4 us (16%)
  other arithmetic  3.29 us (2%)
    pallas_call x5, Pallas kernels, gate_up(): pl.pallas_call(functools.partial(gate_up_kernel, count), grid_spec=pltpu....  35.1 us
    ppermute x10, starting transfers between devices, shifted(): return lax.ppermute(values, ('dp', 'tensor'), pairs)  20 us
    all_to_all x1, blocking collectives, one_expert_each(): lax.all_to_all(sums, ('dp', 'tensor', 'col'), split_axis=0, concat_axis=0...  12.1 us
    ppermute x10, waiting for transfers between devices, shifted(): return lax.ppermute(values, ('dp', 'tensor'), pairs)  11.1 us
    all_to_all x1, blocking collectives, one_expert_each(): lax.all_to_all(home, ('dp', 'tensor'), split_axis=0, concat_axis=0, tiled...  10.7 us
    pallas_call x5, Pallas kernels, down(): pl.pallas_call(functools.partial(down_kernel, len(pieces), pack, bool(old...  10.6 us
    ppermute x8, waiting for transfers between devices, across(): return lax.ppermute(values, 'col', [(k, k ^ 2) for k in range(4)])  10.3 us
    ppermute x8, starting transfers between devices, across(): return lax.ppermute(values, 'col', [(k, k ^ 2) for k in range(4)])  9.18 us
  transfers between devices with their start and end apart: 30, of which 8 were waited for; matrix products, arithmetic and copies ran while one was open for 2% of the time, Pallas kernels for 30%

profile of v9, /device:TPU:0, one launch (start us, length us, event | category | flops | bytes accessed | tf_op | source)
XLA Modules:
  0.0 136.2 jit_solution(8572424687026480741)
XLA Ops:
  2.8 3.1 %collective-permute-start = (bf16[48,1536]{1,0:T(8,128)(2,1)S(1)}, bf16[48,1536]{1,0:T(8,128)(2,1)S(1)}, u32[]{:S(2)}, u32[]{:S(2)}) collective-permute-start(bf16[48,1536]{1,0:T(8,128)(2,1)S(1)} %get-tuple-element.54), channel_id=1, source_target_pairs={{0,8},{4,12},{8,16},{12,20},{16,24},{20,28},{24,0},{28,4},{1,9},{5... | collective-permute-start | bytes 442376 | tf_op jit(solution)/shard_map/ppermute | solution.py:385
  5.9 2.6 %collective-permute-start.1 = (bf16[48,1536]{1,0:T(8,128)(2,1)S(1)}, bf16[48,1536]{1,0:T(8,128)(2,1)S(1)}, u32[]{:S(2)}, u32[]{:S(2)}) collective-permute-start(bf16[48,1536]{1,0:T(8,128)(2,1)S(1)} %get-tuple-element.55), channel_id=1, source_target_pairs={{0,16},{4,20},{8,24},{12,28},{16,0},{20,4},{24,8},{28,12},{1,17},{... | collective-permute-start | bytes 442376 | tf_op jit(solution)/shard_map/ppermute | solution.py:385
  8.5 1.3 collective-permute-start.2
  10.5 2.2 %collective-permute-done.refs_1_ = bf16[48,1536]{1,0:T(8,128)(2,1)S(1)} collective-permute-done((bf16[48,1536]{1,0:T(8,128)(2,1)S(1)}, bf16[48,1536]{1,0:T(8,128)(2,1)S(1)}, u32[]{:S(2)}, u32[]{:S(2)}) %collective-permute-start) | collective-permute-done | bytes 147488 | tf_op jit(solution)/shard_map/ppermute | solution.py:385
  12.7 5.5 %collective-permute-done.1.refs_2_ = bf16[48,1536]{1,0:T(8,128)(2,1)S(1)} collective-permute-done((bf16[48,1536]{1,0:T(8,128)(2,1)S(1)}, bf16[48,1536]{1,0:T(8,128)(2,1)S(1)}, u32[]{:S(2)}, u32[]{:S(2)}) %collective-permute-start.1) | collective-permute-done | bytes 147488 | tf_op jit(solution)/shard_map/ppermute | solution.py:385
  18.2 4.9 %gate_up_0.1 = bf16[2,2,160,512]{3,2,1,0:T(8,128)(2,1)S(1)} custom-call(s32[4]{0:T(128)S(1)} %broadcast_xor_fusion.order_ref, bf16[160,1536]{1,0:T(8,128)(2,1)S(1)} %get-tuple-element.58.inputs_ref, bf16[4,2048,1536]{2,1,0:T(8,128)(2,1)} %bitcast.71, bf16[4,2048,1536]{2,1,0:T(8,128)(2,1)} %bitcast.76), custom_call_target="tpu_custom_call" | custom-call | flops 4026531840 | bytes 25165824 | tf_op jit(solution)/shard_map/gate_up_0/pallas_call | solution.py:132
  23.2 8.2 %gate_up_1.1 = (bf16[2,2,160,512]{3,2,1,0:T(8,128)(2,1)S(1)}, bf16[2,2,160,512]{3,2,1,0:T(8,128)(2,1)S(1)}) custom-call(s32[4]{0:T(128)S(1)} %broadcast_xor_fusion.order_ref, bf16[160,1536]{1,0:T(8,128)(2,1)S(1)} %get-tuple-element.58.inputs_ref, bf16[4,2048,1536]{2,1,0:T(8,128)(2,1)} %bitcast.72, bf16[4,2048,1536]{2,1,0:T(8,128)(2,1)} %bitcast.77), custom_call_target="tpu_custom_call" | custom-call | flops 8053063680 | bytes 50331648 | tf_op jit(solution)/shard_map/gate_up_1/pallas_call | solution.py:132
  32.0 1.6 %collective-permute-start.5 = (bf16[2,160,512]{2,1,0:T(8,128)(2,1)S(1)}, bf16[2,160,512]{2,1,0:T(8,128)(2,1)S(1)}, u32[]{:S(2)}, u32[]{:S(2)}) collective-permute-start(bf16[2,160,512]{2,1,0:T(8,128)(2,1)S(1)} %fusion.1), channel_id=1, source_target_pairs={{0,2},{1,3},{2,0},{3,1},{4,6},{5,7},{6,4},{7,5},{8,10},{9,11},{10,... | collective-permute-start | bytes 983048 | tf_op jit(solution)/shard_map/ppermute | solution.py:375
  33.6 8.2 %gate_up_2.1 = (bf16[2,2,160,512]{3,2,1,0:T(8,128)(2,1)S(1)}, bf16[2,2,160,512]{3,2,1,0:T(8,128)(2,1)S(1)}) custom-call(s32[4]{0:T(128)S(1)} %broadcast_xor_fusion.order_ref, bf16[160,1536]{1,0:T(8,128)(2,1)S(1)} %get-tuple-element.58.inputs_ref, bf16[4,2048,1536]{2,1,0:T(8,128)(2,1)} %bitcast.73, bf16[4,2048,1536]{2,1,0:T(8,128)(2,1)} %bitcast.78, ...), custom_call_target="tpu_custom_call" | custom-call | flops 8053063680 | bytes 50331648 | tf_op jit(solution)/shard_map/gate_up_2/pallas_call | solution.py:132
  42.8 8.2 %gate_up_3.1 = (bf16[2,2,160,512]{3,2,1,0:T(8,128)(2,1)S(1)}, bf16[2,2,160,512]{3,2,1,0:T(8,128)(2,1)S(1)}) custom-call(s32[4]{0:T(128)S(1)} %broadcast_xor_fusion.order_ref, bf16[160,1536]{1,0:T(8,128)(2,1)S(1)} %get-tuple-element.58.inputs_ref, bf16[4,2048,1536]{2,1,0:T(8,128)(2,1)} %bitcast.74, bf16[4,2048,1536]{2,1,0:T(8,128)(2,1)} %bitcast.79, ...), custom_call_target="tpu_custom_call" | custom-call | flops 8053063680 | bytes 50331648 | tf_op jit(solution)/shard_map/gate_up_3/pallas_call | solution.py:132
  51.0 1.6 %collective-permute-start.13 = (bf16[160,512]{1,0:T(8,128)(2,1)S(1)}, bf16[160,512]{1,0:T(8,128)(2,1)S(1)}, u32[]{:S(2)}, u32[]{:S(2)}) collective-permute-start(bf16[160,512]{1,0:T(8,128)(2,1)S(1)} %fusion.11.rest_2_.refs_0_), channel_id=1, source_target_pairs={{0,2},{1,3},{2,0},{3,1},{4,6},{5,7},{6,4},{7,5},{8,10},{9,11},{10,... | collective-permute-start | bytes 491528 | tf_op jit(solution)/shard_map/ppermute | solution.py:375
  53.5 1.6 %collective-permute-start.10 = (bf16[160,512]{1,0:T(8,128)(2,1)S(1)}, bf16[160,512]{1,0:T(8,128)(2,1)S(1)}, u32[]{:S(2)}, u32[]{:S(2)}) collective-permute-start(bf16[160,512]{1,0:T(8,128)(2,1)S(1)} %fusion.9.rest_2_.refs_0_), channel_id=1, source_target_pairs={{0,2},{1,3},{2,0},{3,1},{4,6},{5,7},{6,4},{7,5},{8,10},{9,11},{10,... | collective-permute-start | bytes 491528 | tf_op jit(solution)/shard_map/ppermute | solution.py:375
  55.1 5.7 %gate_up_4.1 = bf16[2,2,160,512]{3,2,1,0:T(8,128)(2,1)S(1)} custom-call(s32[4]{0:T(128)S(1)} %broadcast_xor_fusion.order_ref, bf16[160,1536]{1,0:T(8,128)(2,1)S(1)} %get-tuple-element.58.inputs_ref, bf16[4,2048,1536]{2,1,0:T(8,128)(2,1)} %bitcast.75, bf16[4,2048,1536]{2,1,0:T(8,128)(2,1)} %bitcast.80, ...), custom_call_target="tpu_custom_call" | custom-call | flops 4026531840 | bytes 25165824 | tf_op jit(solution)/shard_map/gate_up_4/pallas_call | solution.py:132
  61.8 6.8 %collective-permute-done.10.refs_1_ = bf16[160,512]{1,0:T(8,128)(2,1)S(1)} collective-permute-done((bf16[160,512]{1,0:T(8,128)(2,1)S(1)}, bf16[160,512]{1,0:T(8,128)(2,1)S(1)}, u32[]{:S(2)}, u32[]{:S(2)}) %collective-permute-start.10) | collective-permute-done | bytes 163872 | tf_op jit(solution)/shard_map/ppermute | solution.py:375
  69.1 2.3 %down_0.1 = (f32[160,768]{1,0:T(8,128)S(1)}, f32[160,160]{1,0:T(8,128)S(1)}, f32[8,768]{1,0:T(8,128)S(1)}) custom-call(s32[16]{0:T(128)S(1)} %fusion.12.order_ref, s32[2]{0:T(128)S(1)} %pad_add_fusion.1.place_ref, bf16[160,512]{1,0:T(8,128)(2,1)S(1)} %fusion.11.rest_2_.refs_0_, bf16[160,512]{1,0:T(8,128)(2,1)S(1)} %collective-permute-done.13.refs_1_, ...), custom_call_target="tpu_custom_call" | custom-call | flops 2013265920 | bytes 12582912 | tf_op jit(solution)/shard_map/down_0/pallas_call | solution.py:216
  71.7 1.6 %collective-permute-start.19 = (bf16[160,512]{1,0:T(8,128)(2,1)S(1)}, bf16[160,512]{1,0:T(8,128)(2,1)S(1)}, u32[]{:S(2)}, u32[]{:S(2)}) collective-permute-start(bf16[160,512]{1,0:T(8,128)(2,1)S(1)} %fusion.5.refs_0_), channel_id=1, source_target_pairs={{0,2},{1,3},{2,0},{3,1},{4,6},{5,7},{6,4},{7,5},{8,10},{9,11},{10,... | collective-permute-start | bytes 491528 | tf_op jit(solution)/shard_map/ppermute | solution.py:375
  73.3 2.3 %down_4.1 = (f32[160,768]{1,0:T(8,128)S(1)}, f32[160,160]{1,0:T(8,128)S(1)}, f32[8,768]{1,0:T(8,128)S(1)}) custom-call(s32[16]{0:T(128)S(1)} %fusion.12.order_ref, s32[2]{0:T(128)S(1)} %pad_add_fusion.1.place_ref, bf16[160,512]{1,0:T(8,128)(2,1)S(1)} %fusion.9.rest_2_.refs_0_, bf16[160,512]{1,0:T(8,128)(2,1)S(1)} %collective-permute-done.10.refs_1_, ...), custom_call_target="tpu_custom_call" | custom-call | flops 2013265920 | bytes 12582912 | tf_op jit(solution)/shard_map/down_4/pallas_call | solution.py:216
  75.8 1.4 %collective-permute-start.16 = (bf16[160,512]{1,0:T(8,128)(2,1)S(1)}, bf16[160,512]{1,0:T(8,128)(2,1)S(1)}, u32[]{:S(2)}, u32[]{:S(2)}) collective-permute-start(bf16[160,512]{1,0:T(8,128)(2,1)S(1)} %fusion.7.refs_1_), channel_id=1, source_target_pairs={{0,2},{1,3},{2,0},{3,1},{4,6},{5,7},{6,4},{7,5},{8,10},{9,11},{10,... | collective-permute-start | bytes 491528 | tf_op jit(solution)/shard_map/ppermute | solution.py:375
  78.4 1.9 %down_8.1 = (f32[160,768]{1,0:T(8,128)S(1)}, f32[160,160]{1,0:T(8,128)S(1)}, f32[8,768]{1,0:T(8,128)S(1)}) custom-call(s32[16]{0:T(128)S(1)} %fusion.12.order_ref, s32[2]{0:T(128)S(1)} %pad_add_fusion.1.place_ref, bf16[160,512]{1,0:T(8,128)(2,1)S(1)} %fusion.5.refs_0_, bf16[160,512]{1,0:T(8,128)(2,1)S(1)} %collective-permute-done.19.refs_1_, ...), custom_call_target="tpu_custom_call" | custom-call | flops 1509949440 | bytes 9437184 | tf_op jit(solution)/shard_map/down_8/pallas_call | solution.py:216
  80.3 2.2 %collective-permute-done.16.refs_2_ = bf16[160,512]{1,0:T(8,128)(2,1)S(1)} collective-permute-done((bf16[160,512]{1,0:T(8,128)(2,1)S(1)}, bf16[160,512]{1,0:T(8,128)(2,1)S(1)}, u32[]{:S(2)}, u32[]{:S(2)}) %collective-permute-start.16) | collective-permute-done | bytes 163872 | tf_op jit(solution)/shard_map/ppermute | solution.py:375
  82.5 2.3 %down_11.1 = (f32[160,768]{1,0:T(8,128)S(1)}, f32[160,160]{1,0:T(8,128)S(1)}, f32[8,768]{1,0:T(8,128)S(1)}) custom-call(s32[16]{0:T(128)S(1)} %fusion.12.order_ref, s32[2]{0:T(128)S(1)} %pad_add_fusion.1.place_ref, bf16[160,512]{1,0:T(8,128)(2,1)S(1)} %collective-permute-done.20.refs_0_, bf16[160,512]{1,0:T(8,128)(2,1)S(1)} %fusion.7.refs_1_, ...), custom_call_target="tpu_custom_call" | custom-call | flops 2013265920 | bytes 12582912 | tf_op jit(solution)/shard_map/down_11/pallas_call | solution.py:216
  84.8 1.9 %down_15.1 = (bf16[160,256]{1,0:T(8,128)(2,1)S(1)}, bf16[160,256]{1,0:T(8,128)(2,1)S(1)}, bf16[160,256]{1,0:T(8,128)(2,1)S(1)}, bf16[160,256]{1,0:T(8,128)(2,1)S...) custom-call(s32[16]{0:T(128)S(1)} %fusion.12.order_ref, ...), custom_call_target="tpu_custom_call" | custom-call | flops 503316480 | bytes 3145728 | tf_op jit(solution)/shard_map/down_15/pallas_call | solution.py:216
  86.7 1.5 %collective-permute-start.23 = (bf16[160,256]{1,0:T(8,128)(2,1)S(1)}, bf16[160,256]{1,0:T(8,128)(2,1)S(1)}, u32[]{:S(2)}, u32[]{:S(2)}) collective-permute-start(bf16[160,256]{1,0:T(8,128)(2,1)S(1)} %get-tuple-element.90), channel_id=1, source_target_pairs={{0,4},{4,0},{8,12},{12,8},{16,20},{20,16},{24,28},{28,24},{1,5},{5... | collective-permute-start | bytes 245768 | tf_op jit(solution)/shard_map/ppermute | solution.py:385
  88.2 3.6 %collective-permute-start.24 = (bf16[160,256]{1,0:T(8,128)(2,1)S(1)}, bf16[160,256]{1,0:T(8,128)(2,1)S(1)}, u32[]{:S(2)}, u32[]{:S(2)}) collective-permute-start(bf16[160,256]{1,0:T(8,128)(2,1)S(1)} %get-tuple-element.91), channel_id=1, source_target_pairs={{0,8},{4,12},{8,16},{12,20},{16,24},{20,28},{24,0},{28,4},{1,9},{5... | collective-permute-start | bytes 245768 | tf_op jit(solution)/shard_map/ppermute | solution.py:385
  91.8 1.6 %collective-permute-start.26 = (bf16[160,256]{1,0:T(8,128)(2,1)S(1)}, bf16[160,256]{1,0:T(8,128)(2,1)S(1)}, u32[]{:S(2)}, u32[]{:S(2)}) collective-permute-start(bf16[160,256]{1,0:T(8,128)(2,1)S(1)} %get-tuple-element.93), channel_id=1, source_target_pairs={{0,16},{4,20},{8,24},{12,28},{16,0},{20,4},{24,8},{28,12},{1,17},{... | collective-permute-start | bytes 245768 | tf_op jit(solution)/shard_map/ppermute | solution.py:385
  93.5 2.2 %collective-permute-start.27 = (bf16[160,256]{1,0:T(8,128)(2,1)S(1)}, bf16[160,256]{1,0:T(8,128)(2,1)S(1)}, u32[]{:S(2)}, u32[]{:S(2)}) collective-permute-start(bf16[160,256]{1,0:T(8,128)(2,1)S(1)} %get-tuple-element.94), channel_id=1, source_target_pairs={{0,20},{4,16},{8,28},{12,24},{16,4},{20,0},{24,12},{28,8},{1,21},{... | collective-permute-start | bytes 245768 | tf_op jit(solution)/shard_map/ppermute | solution.py:385
  95.7 3.8 %collective-permute-start.28 = (bf16[160,256]{1,0:T(8,128)(2,1)S(1)}, bf16[160,256]{1,0:T(8,128)(2,1)S(1)}, u32[]{:S(2)}, u32[]{:S(2)}) collective-permute-start(bf16[160,256]{1,0:T(8,128)(2,1)S(1)} %get-tuple-element.95), channel_id=1, source_target_pairs={{0,24},{4,28},{8,0},{12,4},{16,8},{20,12},{24,16},{28,20},{1,25},{... | collective-permute-start | bytes 245768 | tf_op jit(solution)/shard_map/ppermute | solution.py:385
  101.0 1.5 %route.1 = (bf16[1280,512]{1,0:T(8,128)(2,1)S(1)}, bf16[512,1280]{1,0:T(8,128)(2,1)S(1)}, f32[1280,2]{1,0:T(8,128)S(1)}) custom-call(s32[6]{0:T(128)S(1)} %copy-done.1, s32[2]{0:T(128)S(1)} %pad_add_fusion.1.place_ref, f32[4,4,128]{2,1,0:T(4,128)S(1)} %get-tuple-element.57.refs_0_, f32[8,768]{1,0:T(8,128)S(1)} %get-tuple-element.85.refs_1_.square_ref), custom_call_target="tpu_custom_call" | custom-call | flops 1 | bytes 1 | tf_op jit(solution)/shard_map/route/pallas_call | solution.py:463
  103.2 2.7 %collective-permute-done.27.refs_5_ = bf16[160,256]{1,0:T(8,128)(2,1)S(1)} collective-permute-done((bf16[160,256]{1,0:T(8,128)(2,1)S(1)}, bf16[160,256]{1,0:T(8,128)(2,1)S(1)}, u32[]{:S(2)}, u32[]{:S(2)}) %collective-permute-start.27) | collective-permute-done | bytes 81952 | tf_op jit(solution)/shard_map/ppermute | solution.py:385
  105.9 5.8 %solve.1 = (f32[512,96]{1,0:T(8,128)S(1)}, f32[512,96]{1,0:T(8,128)S(1)}, f32[512,96]{1,0:T(8,128)S(1)}, f32[32,1,128]{2,1,0:T(1,128)S(1)}) custom-call(f32[1]{0:T(128)} %bitcast.2.own_ref, bf16[1280,512]{1,0:T(8,128)(2,1)S(1)} %get-tuple-element.86.hot_ref, bf16[512,1280]{1,0:T(8,128)(2,1)S(1)} %get-tuple-element.87.turned_ref, ...), custom_call_target="tpu_custom_call" | custom-call | flops 1 | bytes 1 | tf_op jit(solution)/shard_map/solve/pallas_call | solution.py:478
  111.7 12.1 %all_to_all.10.sums_ref = f32[32,1,128]{2,1,0:T(1,128)S(1)} all-to-all(f32[32,1,128]{2,1,0:T(1,128)S(1)} %get-tuple-element.100), channel_id=1, replica_groups=mesh['dp'=4,'tensor'=2,'col'=4] {'dp','tensor','col'}, dimensions={0} | all-to-all | bytes 32768 | tf_op jit(solution)/shard_map/all_to_all | solution.py:485
  124.6 10.7 %all_to_all.11.pieces_ref = bf16[8,96,128]{2,1,0:T(8,128)(2,1)S(1)} all-to-all(bf16[8,96,128]{2,1,0:T(8,128)(2,1)S(1)} %finish.1), channel_id=1, replica_groups=mesh['dp'=4,'tensor'=2,'col'=4] {'dp','tensor'}, dimensions={0} | all-to-all | bytes 393216 | tf_op jit(solution)/shard_map/all_to_all | solution.py:494
  (76 shorter events, 12.7 us)
Async XLA Ops:
  2.8 9.9 %collective-permute-start = (bf16[48,1536]{1,0:T(8,128)(2,1)S(1)}, bf16[48,1536]{1,0:T(8,128)(2,1)S(1)}, u32[]{:S(2)}, u32[]{:S(2)}) collective-permute-start(bf16[48,1536]{1,0:T(8,128)(2,1)S(1)} %get-tuple-element.54), channel_id=1, source_target_pairs={{0,8},{4,12},{8,16},{12,20},{16,24},{20,28},{24,0},{28,4},{1,9},{5... | collective-permute-start | bytes 442376 | tf_op jit(solution)/shard_map/ppermute | solution.py:385
  5.9 12.3 %collective-permute-start.1 = (bf16[48,1536]{1,0:T(8,128)(2,1)S(1)}, bf16[48,1536]{1,0:T(8,128)(2,1)S(1)}, u32[]{:S(2)}, u32[]{:S(2)}) collective-permute-start(bf16[48,1536]{1,0:T(8,128)(2,1)S(1)} %get-tuple-element.55), channel_id=1, source_target_pairs={{0,16},{4,20},{8,24},{12,28},{16,0},{20,4},{24,8},{28,12},{1,17},{... | collective-permute-start | bytes 442376 | tf_op jit(solution)/shard_map/ppermute | solution.py:385
  8.5 9.7 %collective-permute-start.2 = (bf16[48,1536]{1,0:T(8,128)(2,1)S(1)}, bf16[48,1536]{1,0:T(8,128)(2,1)S(1)}, u32[]{:S(2)}, u32[]{:S(2)}) collective-permute-start(bf16[48,1536]{1,0:T(8,128)(2,1)S(1)} %get-tuple-element.56), channel_id=1, source_target_pairs={{0,24},{4,28},{8,0},{12,4},{16,8},{20,12},{24,16},{28,20},{1,25},{... | collective-permute-start | bytes 442376 | tf_op jit(solution)/shard_map/ppermute | solution.py:385
  23.1 8.8 %collective-permute-start.4 = (bf16[2,2,160,512]{3,2,1,0:T(8,128)(2,1)S(1)}, bf16[2,2,160,512]{3,2,1,0:T(8,128)(2,1)S(1)}, u32[]{:S(2)}, u32[]{:S(2)}) collective-permute-start(bf16[2,2,160,512]{3,2,1,0:T(8,128)(2,1)S(1)} %gate_up_0.1), channel_id=1, source_target_pairs={{0,1},{1,0},{2,3},{3,2},{4,5},{5,4},{6,7},{7,6},{8,9},{9,8},{10,11... | collective-permute-start | bytes 1966088 | tf_op jit(solution)/shard_map/ppermute | solution.py:372
  31.4 10.5 %collective-permute-start.3 = (bf16[2,2,160,512]{3,2,1,0:T(8,128)(2,1)S(1)}, bf16[2,2,160,512]{3,2,1,0:T(8,128)(2,1)S(1)}, u32[]{:S(2)}, u32[]{:S(2)}) collective-permute-start(bf16[2,2,160,512]{3,2,1,0:T(8,128)(2,1)S(1)} %get-tuple-element.61), channel_id=1, source_target_pairs={{0,1},{1,0},{2,3},{3,2},{4,5},{5,4},{6,7},{7,6},{8,9},{9,8},{10,11... | collective-permute-start | bytes 1966088 | tf_op jit(solution)/shard_map/ppermute | solution.py:372
  32.0 10.5 %collective-permute-start.5 = (bf16[2,160,512]{2,1,0:T(8,128)(2,1)S(1)}, bf16[2,160,512]{2,1,0:T(8,128)(2,1)S(1)}, u32[]{:S(2)}, u32[]{:S(2)}) collective-permute-start(bf16[2,160,512]{2,1,0:T(8,128)(2,1)S(1)} %fusion.1), channel_id=1, source_target_pairs={{0,2},{1,3},{2,0},{3,1},{4,6},{5,7},{6,4},{7,5},{8,10},{9,11},{10,... | collective-permute-start | bytes 983048 | tf_op jit(solution)/shard_map/ppermute | solution.py:375
  41.8 10.7 %collective-permute-start.6 = (bf16[2,2,160,512]{3,2,1,0:T(8,128)(2,1)S(1)}, bf16[2,2,160,512]{3,2,1,0:T(8,128)(2,1)S(1)}, u32[]{:S(2)}, u32[]{:S(2)}) collective-permute-start(bf16[2,2,160,512]{3,2,1,0:T(8,128)(2,1)S(1)} %get-tuple-element.64), channel_id=1, source_target_pairs={{0,1},{1,0},{2,3},{3,2},{4,5},{5,4},{6,7},{7,6},{8,9},{9,8},{10,11... | collective-permute-start | bytes 1966088 | tf_op jit(solution)/shard_map/ppermute | solution.py:372
  42.0 11.2 %collective-permute-start.7 = (bf16[2,160,512]{2,1,0:T(8,128)(2,1)S(1)}, bf16[2,160,512]{2,1,0:T(8,128)(2,1)S(1)}, u32[]{:S(2)}, u32[]{:S(2)}) collective-permute-start(bf16[2,160,512]{2,1,0:T(8,128)(2,1)S(1)} %fusion.rest_1_), channel_id=1, source_target_pairs={{0,2},{1,3},{2,0},{3,1},{4,6},{5,7},{6,4},{7,5},{8,10},{9,11},{10,... | collective-permute-start | bytes 983048 | tf_op jit(solution)/shard_map/ppermute | solution.py:375
  51.0 9.9 %collective-permute-start.13 = (bf16[160,512]{1,0:T(8,128)(2,1)S(1)}, bf16[160,512]{1,0:T(8,128)(2,1)S(1)}, u32[]{:S(2)}, u32[]{:S(2)}) collective-permute-start(bf16[160,512]{1,0:T(8,128)(2,1)S(1)} %fusion.11.rest_2_.refs_0_), channel_id=1, source_target_pairs={{0,2},{1,3},{2,0},{3,1},{4,6},{5,7},{6,4},{7,5},{8,10},{9,11},{10,... | collective-permute-start | bytes 491528 | tf_op jit(solution)/shard_map/ppermute | solution.py:375
  52.6 18.8 %collective-permute-start.18 = (bf16[2,160,512]{2,1,0:T(8,128)(2,1)S(1)}, bf16[2,160,512]{2,1,0:T(8,128)(2,1)S(1)}, u32[]{:S(2)}, u32[]{:S(2)}) collective-permute-start(bf16[2,160,512]{2,1,0:T(8,128)(2,1)S(1)} %fusion.2.rest_1_), channel_id=1, source_target_pairs={{0,2},{1,3},{2,0},{3,1},{4,6},{5,7},{6,4},{7,5},{8,10},{9,11},{10,... | collective-permute-start | bytes 983048 | tf_op jit(solution)/shard_map/ppermute | solution.py:375
  53.2 7.5 %collective-permute-start.8 = (bf16[2,2,160,512]{3,2,1,0:T(8,128)(2,1)S(1)}, bf16[2,2,160,512]{3,2,1,0:T(8,128)(2,1)S(1)}, u32[]{:S(2)}, u32[]{:S(2)}) collective-permute-start(bf16[2,2,160,512]{3,2,1,0:T(8,128)(2,1)S(1)} %get-tuple-element.66), channel_id=1, source_target_pairs={{0,1},{1,0},{2,3},{3,2},{4,5},{5,4},{6,7},{7,6},{8,9},{9,8},{10,11... | collective-permute-start | bytes 1966088 | tf_op jit(solution)/shard_map/ppermute | solution.py:372
  53.3 15.8 %slice-start = ((s8[12582912]{0:T(1024)(128)(4,1)}), s8[4194304]{0:T(1024)(128)(4,1)S(1)}, s32[]{:S(2)}) async-start(s8[12582912]{0:T(1024)(128)(4,1)} %bitcast.64), calls=%async_computation.2 | async-start | bytes 8388608
  53.5 15.1 %collective-permute-start.10 = (bf16[160,512]{1,0:T(8,128)(2,1)S(1)}, bf16[160,512]{1,0:T(8,128)(2,1)S(1)}, u32[]{:S(2)}, u32[]{:S(2)}) collective-permute-start(bf16[160,512]{1,0:T(8,128)(2,1)S(1)} %fusion.9.rest_2_.refs_0_), channel_id=1, source_target_pairs={{0,2},{1,3},{2,0},{3,1},{4,6},{5,7},{6,4},{7,5},{8,10},{9,11},{10,... | collective-permute-start | bytes 491528 | tf_op jit(solution)/shard_map/ppermute | solution.py:375
  60.8 7.8 %collective-permute-start.14 = (bf16[160,512]{1,0:T(8,128)(2,1)S(1)}, bf16[160,512]{1,0:T(8,128)(2,1)S(1)}, u32[]{:S(2)}, u32[]{:S(2)}) collective-permute-start(bf16[160,512]{1,0:T(8,128)(2,1)S(1)} %fusion.11.rest_2_.refs_0_), channel_id=1, source_target_pairs={{0,1},{1,0},{2,3},{3,2},{4,5},{5,4},{6,7},{7,6},{8,9},{9,8},{10,11... | collective-permute-start | bytes 491528 | tf_op jit(solution)/shard_map/ppermute | solution.py:372
  61.1 8.0 %collective-permute-start.15 = (bf16[160,512]{1,0:T(8,128)(2,1)S(1)}, bf16[160,512]{1,0:T(8,128)(2,1)S(1)}, u32[]{:S(2)}, u32[]{:S(2)}) collective-permute-start(bf16[160,512]{1,0:T(8,128)(2,1)S(1)} %collective-permute-done.13.refs_1_), channel_id=1, source_target_pairs={{0,1},{1,0},{2,3},{3,2},{4,5},{5,4},{6,7},{7,6},{8,9},{9,8},{10,11... | collective-permute-start | bytes 491528 | tf_op jit(solution)/shard_map/ppermute | solution.py:372
  61.4 14.1 %collective-permute-start.9 = (bf16[2,160,512]{2,1,0:T(8,128)(2,1)S(1)}, bf16[2,160,512]{2,1,0:T(8,128)(2,1)S(1)}, u32[]{:S(2)}, u32[]{:S(2)}) collective-permute-start(bf16[2,160,512]{2,1,0:T(8,128)(2,1)S(1)} %fusion.3), channel_id=1, source_target_pairs={{0,2},{1,3},{2,0},{3,1},{4,6},{5,7},{6,4},{7,5},{8,10},{9,11},{10,... | collective-permute-start | bytes 983048 | tf_op jit(solution)/shard_map/ppermute | solution.py:375
  68.6 4.7 %collective-permute-start.11 = (bf16[160,512]{1,0:T(8,128)(2,1)S(1)}, bf16[160,512]{1,0:T(8,128)(2,1)S(1)}, u32[]{:S(2)}, u32[]{:S(2)}) collective-permute-start(bf16[160,512]{1,0:T(8,128)(2,1)S(1)} %fusion.9.rest_2_.refs_0_), channel_id=1, source_target_pairs={{0,1},{1,0},{2,3},{3,2},{4,5},{5,4},{6,7},{7,6},{8,9},{9,8},{10,11... | collective-permute-start | bytes 491528 | tf_op jit(solution)/shard_map/ppermute | solution.py:372
  68.6 4.7 %collective-permute-start.12 = (bf16[160,512]{1,0:T(8,128)(2,1)S(1)}, bf16[160,512]{1,0:T(8,128)(2,1)S(1)}, u32[]{:S(2)}, u32[]{:S(2)}) collective-permute-start(bf16[160,512]{1,0:T(8,128)(2,1)S(1)} %collective-permute-done.10.refs_1_), channel_id=1, source_target_pairs={{0,1},{1,0},{2,3},{3,2},{4,5},{5,4},{6,7},{7,6},{8,9},{9,8},{10,11... | collective-permute-start | bytes 491528 | tf_op jit(solution)/shard_map/ppermute | solution.py:372
  71.7 6.7 %collective-permute-start.19 = (bf16[160,512]{1,0:T(8,128)(2,1)S(1)}, bf16[160,512]{1,0:T(8,128)(2,1)S(1)}, u32[]{:S(2)}, u32[]{:S(2)}) collective-permute-start(bf16[160,512]{1,0:T(8,128)(2,1)S(1)} %fusion.5.refs_0_), channel_id=1, source_target_pairs={{0,2},{1,3},{2,0},{3,1},{4,6},{5,7},{6,4},{7,5},{8,10},{9,11},{10,... | collective-permute-start | bytes 491528 | tf_op jit(solution)/shard_map/ppermute | solution.py:375
  73.3 5.2 %collective-permute-start.22 = (bf16[160,512]{1,0:T(8,128)(2,1)S(1)}, bf16[160,512]{1,0:T(8,128)(2,1)S(1)}, u32[]{:S(2)}, u32[]{:S(2)}) collective-permute-start(bf16[160,512]{1,0:T(8,128)(2,1)S(1)} %fusion.5.refs_0_), channel_id=1, source_target_pairs={{0,1},{1,0},{2,3},{3,2},{4,5},{5,4},{6,7},{7,6},{8,9},{9,8},{10,11... | collective-permute-start | bytes 491528 | tf_op jit(solution)/shard_map/ppermute | solution.py:372
  75.8 6.7 %collective-permute-start.16 = (bf16[160,512]{1,0:T(8,128)(2,1)S(1)}, bf16[160,512]{1,0:T(8,128)(2,1)S(1)}, u32[]{:S(2)}, u32[]{:S(2)}) collective-permute-start(bf16[160,512]{1,0:T(8,128)(2,1)S(1)} %fusion.7.refs_1_), channel_id=1, source_target_pairs={{0,2},{1,3},{2,0},{3,1},{4,6},{5,7},{6,4},{7,5},{8,10},{9,11},{10,... | collective-permute-start | bytes 491528 | tf_op jit(solution)/shard_map/ppermute | solution.py:375
  77.2 5.3 %collective-permute-start.21 = (bf16[160,512]{1,0:T(8,128)(2,1)S(1)}, bf16[160,512]{1,0:T(8,128)(2,1)S(1)}, u32[]{:S(2)}, u32[]{:S(2)}) collective-permute-start(bf16[160,512]{1,0:T(8,128)(2,1)S(1)} %fusion.7.refs_1_), channel_id=1, source_target_pairs={{0,1},{1,0},{2,3},{3,2},{4,5},{5,4},{6,7},{7,6},{8,9},{9,8},{10,11... | collective-permute-start | bytes 491528 | tf_op jit(solution)/shard_map/ppermute | solution.py:372
  78.4 4.1 %collective-permute-start.20 = (bf16[160,512]{1,0:T(8,128)(2,1)S(1)}, bf16[160,512]{1,0:T(8,128)(2,1)S(1)}, u32[]{:S(2)}, u32[]{:S(2)}) collective-permute-start(bf16[160,512]{1,0:T(8,128)(2,1)S(1)} %collective-permute-done.19.refs_1_), channel_id=1, source_target_pairs={{0,1},{1,0},{2,3},{3,2},{4,5},{5,4},{6,7},{7,6},{8,9},{9,8},{10,11... | collective-permute-start | bytes 491528 | tf_op jit(solution)/shard_map/ppermute | solution.py:372
  82.5 2.3 %collective-permute-start.17 = (bf16[160,512]{1,0:T(8,128)(2,1)S(1)}, bf16[160,512]{1,0:T(8,128)(2,1)S(1)}, u32[]{:S(2)}, u32[]{:S(2)}) collective-permute-start(bf16[160,512]{1,0:T(8,128)(2,1)S(1)} %collective-permute-done.16.refs_2_), channel_id=1, source_target_pairs={{0,1},{1,0},{2,3},{3,2},{4,5},{5,4},{6,7},{7,6},{8,9},{9,8},{10,11... | collective-permute-start | bytes 491528 | tf_op jit(solution)/shard_map/ppermute | solution.py:372
  82.5 17.2 %copy-start.1 = (s32[6]{0:T(128)S(1)}, s32[6]{0:T(128)}, u32[]{:S(2)}) copy-start(s32[6]{0:T(128)} %kept_ref.1) | copy-start | bytes 76
  86.7 8.9 %collective-permute-start.23 = (bf16[160,256]{1,0:T(8,128)(2,1)S(1)}, bf16[160,256]{1,0:T(8,128)(2,1)S(1)}, u32[]{:S(2)}, u32[]{:S(2)}) collective-permute-start(bf16[160,256]{1,0:T(8,128)(2,1)S(1)} %get-tuple-element.90), channel_id=1, source_target_pairs={{0,4},{4,0},{8,12},{12,8},{16,20},{20,16},{24,28},{28,24},{1,5},{5... | collective-permute-start | bytes 245768 | tf_op jit(solution)/shard_map/ppermute | solution.py:385
  88.2 11.3 %collective-permute-start.24 = (bf16[160,256]{1,0:T(8,128)(2,1)S(1)}, bf16[160,256]{1,0:T(8,128)(2,1)S(1)}, u32[]{:S(2)}, u32[]{:S(2)}) collective-permute-start(bf16[160,256]{1,0:T(8,128)(2,1)S(1)} %get-tuple-element.91), channel_id=1, source_target_pairs={{0,8},{4,12},{8,16},{12,20},{16,24},{20,28},{24,0},{28,4},{1,9},{5... | collective-permute-start | bytes 245768 | tf_op jit(solution)/shard_map/ppermute | solution.py:385
  91.8 10.7 %collective-permute-start.25 = (bf16[160,256]{1,0:T(8,128)(2,1)S(1)}, bf16[160,256]{1,0:T(8,128)(2,1)S(1)}, u32[]{:S(2)}, u32[]{:S(2)}) collective-permute-start(bf16[160,256]{1,0:T(8,128)(2,1)S(1)} %get-tuple-element.92), channel_id=1, source_target_pairs={{0,12},{4,8},{8,20},{12,16},{16,28},{20,24},{24,4},{28,0},{1,13},{... | collective-permute-start | bytes 245768 | tf_op jit(solution)/shard_map/ppermute | solution.py:385
  91.8 11.3 %collective-permute-start.26 = (bf16[160,256]{1,0:T(8,128)(2,1)S(1)}, bf16[160,256]{1,0:T(8,128)(2,1)S(1)}, u32[]{:S(2)}, u32[]{:S(2)}) collective-permute-start(bf16[160,256]{1,0:T(8,128)(2,1)S(1)} %get-tuple-element.93), channel_id=1, source_target_pairs={{0,16},{4,20},{8,24},{12,28},{16,0},{20,4},{24,8},{28,12},{1,17},{... | collective-permute-start | bytes 245768 | tf_op jit(solution)/shard_map/ppermute | solution.py:385
  93.5 12.3 %collective-permute-start.27 = (bf16[160,256]{1,0:T(8,128)(2,1)S(1)}, bf16[160,256]{1,0:T(8,128)(2,1)S(1)}, u32[]{:S(2)}, u32[]{:S(2)}) collective-permute-start(bf16[160,256]{1,0:T(8,128)(2,1)S(1)} %get-tuple-element.94), channel_id=1, source_target_pairs={{0,20},{4,16},{8,28},{12,24},{16,4},{20,0},{24,12},{28,8},{1,21},{... | collective-permute-start | bytes 245768 | tf_op jit(solution)/shard_map/ppermute | solution.py:385
  95.7 10.2 %collective-permute-start.28 = (bf16[160,256]{1,0:T(8,128)(2,1)S(1)}, bf16[160,256]{1,0:T(8,128)(2,1)S(1)}, u32[]{:S(2)}, u32[]{:S(2)}) collective-permute-start(bf16[160,256]{1,0:T(8,128)(2,1)S(1)} %get-tuple-element.95), channel_id=1, source_target_pairs={{0,24},{4,28},{8,0},{12,4},{16,8},{20,12},{24,16},{28,20},{1,25},{... | collective-permute-start | bytes 245768 | tf_op jit(solution)/shard_map/ppermute | solution.py:385
  99.5 6.4 %collective-permute-start.29 = (bf16[160,256]{1,0:T(8,128)(2,1)S(1)}, bf16[160,256]{1,0:T(8,128)(2,1)S(1)}, u32[]{:S(2)}, u32[]{:S(2)}) collective-permute-start(bf16[160,256]{1,0:T(8,128)(2,1)S(1)} %get-tuple-element.96), channel_id=1, source_target_pairs={{0,28},{4,24},{8,4},{12,0},{16,12},{20,8},{24,20},{28,16},{1,29},{... | collective-permute-start | bytes 245768 | tf_op jit(solution)/shard_map/ppermute | solution.py:385
  (4 other events, 40.2 us)
